TPU v7x, 32 devices: a whole 2x2x4 slice. The times are simulated.
32 devices in a mesh: dp: 8 (over z, x), seq: 4 (over y, core).
Axes of the slice: x: 2, y: 2, z: 4, core: 2. Of those that a mesh axis runs over, the one named last changes fastest.
Arguments:
- x_text: bfloat16 [8192, 768], P(('dp', 'seq')), may hold values from -6 to 6
- x_vis: bfloat16 [2304, 1024], P(('dp', 'seq')), may hold values from -6 to 6
- caption_len: int32 [64], P(('dp', 'seq')), may hold values from 8 to 128, as said below
- cot_text: bfloat16 [8192, 768], P(('dp', 'seq')), may hold values from -6 to 6
- cot_vis: bfloat16 [2304, 1024], P(('dp', 'seq'))
- master_blocks: float32 [5056, 4096], P('dp')
- stat_left: float32 [5056, 4096], P('dp')
- stat_right: float32 [5056, 4096], P('dp')
- root_left: float32 [5056, 4096], P('dp')
- root_right: float32 [5056, 4096], P('dp')
- norm_params: float32 [2, 5376], replicated
- norm_second: float32 [2, 5376], replicated
Outputs:
- out_text: bfloat16 [8192, 768], P(('dp', 'seq'))
- out_vis: bfloat16 [2304, 1024], P(('dp', 'seq'))
- grad_text: float32 [8192, 768], P(('dp', 'seq'))
- grad_vis: float32 [2304, 1024], P(('dp', 'seq'))
- grad_blocks: float32 [5056, 4096], P('dp')
- left_new: float32 [5056, 4096], P('dp')
- right_new: float32 [5056, 4096], P('dp')
- master_new: float32 [5056, 4096], P('dp')
- norm_grads: float32 [2, 5376], replicated
- norm_second_new: float32 [2, 5376], replicated
- norm_new: float32 [2, 5376], replicated
Inputs may be any that keep to these rules, and one draw needn't show every extreme that they name: `caption_len`: some pair has exactly 128 live slots and some exactly 8.
All inputs are finite; a program needn't handle non-finite values.
Results may differ from a plain program's by a relative error of at most 0.02.
Values may be sent and summed in bfloat16 or wider, within the bound.
No kernel may reach another device: no remote copies, remote signals or barrier semaphores. Data moves between devices by JAX's collectives and lax.ppermute only.
A program may use at most 448 MiB of HBM per device.

v0:
```python
import jax
import jax.numpy as jnp
from jax import lax
from jax.sharding import PartitionSpec as P

TXT = 768
VIS = 1024
BI = 1024
FFT = 3072
FFV = 1024
HEAD = 128
HEAD_T = 64
HEAD_V = 128
BLK = 64


MASK_FILL = -1000000000.0
STAT_DECAY = 0.9
WEIGHT_RATE = 0.3
NORM_RATE = 0.2
NORM_EPSILON = 1e-05
MOMENT_EPSILON = 1e-08
HIGHEST = lax.Precision.HIGHEST
CONTRACT_COLS = (((1,), (1,)), ((), ()))


def weight_layout():
    return (
        (VIS, BI, 3),
        (BI, VIS, 1),
        (VIS, FFV, 1),
        (FFV, VIS, 1),
        (VIS, VIS, 3),
        (VIS, VIS, 1),
        (TXT, BI, 3),
        (BI, TXT, 1),
        (TXT, FFT, 1),
        (FFT, TXT, 1),
        (TXT, TXT, 3),
        (TXT, TXT, 1),
    )


def unpack_weights(flat):
    size = BLK
    blocks = flat.reshape(flat.shape[0], size, size)
    begin = 0
    matrices = []
    for rows, columns, count in weight_layout():
        number = count * rows * columns // (size * size)
        shaped = blocks[begin : begin + number].reshape(
            count, rows // size, columns // size, size, size
        )
        matrices.append(shaped.transpose(1, 3, 0, 2, 4).reshape(rows, count * columns))
        begin += number
    return matrices


def block_grad(inputs, grads, count):
    size = BLK
    left = inputs.reshape(inputs.shape[0], inputs.shape[1] // size, size)
    right = grads.reshape(grads.shape[0], count, grads.shape[1] // (count * size), size)
    return jnp.einsum("nai,nkbj->kabij", left, right, preferred_element_type=jnp.float32).reshape(
        -1, size * size
    )


def norm_columns(values, stream, which):
    if stream == 0:
        begin = which * VIS
        width = VIS
    else:
        begin = 3 * VIS + which * TXT
        width = TXT
    return values[:, begin : begin + width]


def gelu_exact(value):
    return jax.nn.gelu(value, approximate=False)


def heads_of(side, which, head):
    part = side[:, :, which, :]
    return part.reshape(part.shape[0], part.shape[1], part.shape[2] // head, head)


def scores_of(query, keys, live, head):
    scores = jnp.einsum(
        "gqhd,gkhd->ghqk", query, keys, preferred_element_type=jnp.float32
    ) * head ** (-0.5)
    if live is not None:
        scores = jnp.where(live[:, None, None, :], scores, MASK_FILL)
    return scores


def attend_one(query, keys, values, live, head):
    scores = scores_of(query, keys, live, head)
    top = jnp.max(scores, axis=3, keepdims=True)
    raised = jnp.exp(scores - top)
    total = jnp.sum(raised, axis=3, keepdims=True)
    found = jnp.einsum(
        "ghqk,gkhd->gqhd",
        (raised / total).astype(jnp.bfloat16),
        values,
        preferred_element_type=jnp.float32,
    ).astype(jnp.bfloat16)
    return (found.reshape(found.shape[0], found.shape[1], -1), top + jnp.log(total))


def attend_one_back(query, keys, values, live, head, logsum, dfound):
    scale = head ** (-0.5)
    probs = jnp.exp(scores_of(query, keys, live, head) - logsum)
    upstream = dfound.reshape(dfound.shape[0], dfound.shape[1], -1, head)
    dprobs = jnp.einsum("gqhd,gkhd->ghqk", upstream, values, preferred_element_type=jnp.float32)
    dvalues = jnp.einsum(
        "ghqk,gqhd->gkhd", probs.astype(jnp.bfloat16), upstream, preferred_element_type=jnp.float32
    )
    dscores = (probs * (dprobs - jnp.sum(probs * dprobs, axis=3, keepdims=True))).astype(
        jnp.bfloat16
    )
    dquery = (
        jnp.einsum("ghqk,gkhd->gqhd", dscores, keys, preferred_element_type=jnp.float32) * scale
    )
    dkeys = (
        jnp.einsum("ghqk,gqhd->gkhd", dscores, query, preferred_element_type=jnp.float32) * scale
    )
    return (dquery, dkeys, dvalues)


def attention_plan(vis_side, text_side, lengths, cross):
    live = (
        lax.broadcasted_iota(jnp.int32, (lengths.shape[0], text_side.shape[1]), 1)
        < lengths[:, None]
    )
    if cross:
        return ((vis_side, text_side, live, HEAD), (text_side, vis_side, None, HEAD))
    return ((vis_side, vis_side, None, HEAD_V), (text_side, text_side, live, HEAD_T))


def pair_attend(vis_side, text_side, lengths, cross):
    results = []
    for query_side, key_side, live, head in attention_plan(vis_side, text_side, lengths, cross):
        results.append(
            attend_one(
                heads_of(query_side, 0, head),
                heads_of(key_side, 1, head),
                heads_of(key_side, 2, head),
                live,
                head,
            )
        )
    return (results[0][0], results[1][0], results[0][1], results[1][1])


def pair_attend_back(
    vis_side, text_side, lengths, cross, vis_logsum, text_logsum, vis_dfound, text_dfound
):
    plan = attention_plan(vis_side, text_side, lengths, cross)
    parts = []
    for (query_side, key_side, live, head), logsum, dfound in zip(
        plan, (vis_logsum, text_logsum), (vis_dfound, text_dfound)
    ):
        parts.append(
            attend_one_back(
                heads_of(query_side, 0, head),
                heads_of(key_side, 1, head),
                heads_of(key_side, 2, head),
                live,
                head,
                logsum,
                dfound,
            )
        )
    if cross:
        vis_parts = (parts[0][0], parts[1][1], parts[1][2])
        text_parts = (parts[1][0], parts[0][1], parts[0][2])
    else:
        vis_parts = parts[0]
        text_parts = parts[1]
    vis_grad = jnp.stack(vis_parts, axis=2).reshape(vis_side.shape).astype(jnp.bfloat16)
    text_grad = jnp.stack(text_parts, axis=2).reshape(text_side.shape).astype(jnp.bfloat16)
    return (vis_grad, text_grad)


def to_heads(vis_side, text_side):
    return (
        lax.all_to_all(vis_side, "seq", split_axis=3, concat_axis=0, tiled=True),
        lax.all_to_all(text_side, "seq", split_axis=3, concat_axis=0, tiled=True),
    )


def from_heads(vis_found, text_found):
    return (
        lax.all_to_all(vis_found, "seq", split_axis=0, concat_axis=2, tiled=True),
        lax.all_to_all(text_found, "seq", split_axis=0, concat_axis=2, tiled=True),
    )


def dfound_to_heads(vis_dfound, text_dfound):
    return (
        lax.all_to_all(vis_dfound, "seq", split_axis=2, concat_axis=0, tiled=True),
        lax.all_to_all(text_dfound, "seq", split_axis=2, concat_axis=0, tiled=True),
    )


def grads_from_heads(vis_grad, text_grad):
    return (
        lax.all_to_all(vis_grad, "seq", split_axis=0, concat_axis=3, tiled=True),
        lax.all_to_all(text_grad, "seq", split_axis=0, concat_axis=3, tiled=True),
    )


def side_of(rows_in, weight, pairs):
    made = jnp.dot(rows_in, weight, preferred_element_type=jnp.float32).astype(jnp.bfloat16)
    return made.reshape(pairs, -1, 3, weight.shape[1] // 3)


def norm_forward(resid, columns):
    mean = jnp.mean(resid, -1, keepdims=True)
    centered = resid - mean
    scale = lax.rsqrt(jnp.mean(centered * centered, -1, keepdims=True) + NORM_EPSILON)
    normed = centered * scale
    return (normed, scale, normed * columns[0] + columns[1])


def norm_backward(upstream, normed, scale, gain):
    scaled = upstream * gain
    resid_grad = scale * (
        scaled
        - jnp.mean(scaled, -1, keepdims=True)
        - normed * jnp.mean(scaled * normed, -1, keepdims=True)
    )
    return (resid_grad, jnp.sum(upstream * normed, 0), jnp.sum(upstream, 0))


def stream_middle(context_rows, x_rows, weights, values, stream, pairs):
    resid = x_rows.astype(jnp.float32) + jnp.dot(
        context_rows, weights[1], preferred_element_type=jnp.float32
    )
    normed_one, scale_one, first = norm_forward(resid, norm_columns(values, stream, 0))
    first_low = first.astype(jnp.bfloat16)
    pre = jnp.dot(first_low, weights[2], preferred_element_type=jnp.float32)
    act = gelu_exact(pre).astype(jnp.bfloat16)
    resid = first + jnp.dot(act, weights[3], preferred_element_type=jnp.float32)
    normed_two, scale_two, second = norm_forward(resid, norm_columns(values, stream, 1))
    second_low = second.astype(jnp.bfloat16)
    side = side_of(second_low, weights[4], pairs)
    return (
        side,
        (normed_one, scale_one, first_low, pre, act, normed_two, scale_two, second, second_low),
    )


def stream_end(self_rows, second, out_weight, values, stream):
    resid = second + jnp.dot(self_rows, out_weight, preferred_element_type=jnp.float32)
    normed_three, scale_three, third = norm_forward(resid, norm_columns(values, stream, 2))
    return (third.astype(jnp.bfloat16), normed_three, scale_three)


def stream_back_end(
    cotangent, normed_three, scale_three, self_rows, out_weight, values, stream, pairs
):
    resid_three, gain_three, bias_three = norm_backward(
        cotangent.astype(jnp.float32), normed_three, scale_three, norm_columns(values, stream, 2)[0]
    )
    third_back = resid_three.astype(jnp.bfloat16)
    grad_self_out = block_grad(self_rows, third_back, 1)
    dself = lax.dot_general(
        third_back, out_weight, CONTRACT_COLS, preferred_element_type=jnp.float32
    )
    dself = dself.astype(jnp.bfloat16).reshape(pairs, -1, out_weight.shape[0])
    return (resid_three, dself, grad_self_out, gain_three, bias_three)


def stream_back_middle(resid_three, dself_side, kept, context_rows, weights, values, stream, pairs):
    normed_one, scale_one, first_low, pre, act, normed_two, scale_two, second, second_low = kept
    dself_rows = dself_side.reshape(-1, dself_side.shape[2] * dself_side.shape[3])
    grad_self_qkv = block_grad(second_low, dself_rows, 3)
    second_in = resid_three + lax.dot_general(
        dself_rows, weights[4], CONTRACT_COLS, preferred_element_type=jnp.float32
    )
    resid_two, gain_two, bias_two = norm_backward(
        second_in, normed_two, scale_two, norm_columns(values, stream, 1)[0]
    )
    branch_back = resid_two.astype(jnp.bfloat16)
    grad_down = block_grad(act, branch_back, 1)
    act_grad = lax.dot_general(
        branch_back, weights[3], CONTRACT_COLS, preferred_element_type=jnp.float32
    )
    pre_grad = jax.vjp(gelu_exact, pre)[1](act_grad)[0].astype(jnp.bfloat16)
    grad_up = block_grad(first_low, pre_grad, 1)
    first_in = resid_two + lax.dot_general(
        pre_grad, weights[2], CONTRACT_COLS, preferred_element_type=jnp.float32
    )
    resid_one, gain_one, bias_one = norm_backward(
        first_in, normed_one, scale_one, norm_columns(values, stream, 0)[0]
    )
    first_back = resid_one.astype(jnp.bfloat16)
    grad_co_out = block_grad(context_rows, first_back, 1)
    dcontext = lax.dot_general(
        first_back, weights[1], CONTRACT_COLS, preferred_element_type=jnp.float32
    )
    dcontext = dcontext.astype(jnp.bfloat16).reshape(pairs, -1, BI)
    return (
        resid_one,
        dcontext,
        (grad_co_out, grad_up, grad_down, grad_self_qkv),
        (gain_one, gain_two),
        (bias_one, bias_two),
    )


def shards(
    x_text,
    x_vis,
    caption_len,
    cot_text,
    cot_vis,
    master_blocks,
    stat_left,
    stat_right,
    root_left,
    root_right,
    norm_params,
    norm_second,
):
    pairs = caption_len.shape[0]
    width = master_blocks.shape[1] // lax.axis_size("seq")
    mine = lax.dynamic_slice_in_dim(master_blocks, lax.axis_index("seq") * width, width, 1).astype(
        jnp.bfloat16
    )
    partial_value = lax.all_gather(mine, "dp", axis=0, tiled=True)
    every = lax.all_gather(partial_value, "seq", axis=1, tiled=True)
    matrices = unpack_weights(every)
    vis_weights = matrices[:6]
    text_weights = matrices[6:]
    vis_co = side_of(x_vis, vis_weights[0], pairs)
    text_co = side_of(x_text, text_weights[0], pairs)
    lengths = lax.all_gather(caption_len, "seq", axis=0, tiled=True)
    vis_co_use, text_co_use = to_heads(vis_co, text_co)
    vis_found, text_found, vis_co_sum, text_co_sum = pair_attend(
        vis_co_use, text_co_use, lengths, True
    )
    vis_context, text_context = from_heads(vis_found, text_found)
    vis_context_rows = vis_context.reshape(-1, BI)
    text_context_rows = text_context.reshape(-1, BI)
    vis_self, vis_kept = stream_middle(vis_context_rows, x_vis, vis_weights, norm_params, 0, pairs)
    text_self, text_kept = stream_middle(
        text_context_rows, x_text, text_weights, norm_params, 1, pairs
    )
    vis_self_use, text_self_use = to_heads(vis_self, text_self)
    vis_found, text_found, vis_self_sum, text_self_sum = pair_attend(
        vis_self_use, text_self_use, lengths, False
    )
    vis_self_context, text_self_context = from_heads(vis_found, text_found)
    vis_self_rows = vis_self_context.reshape(-1, VIS)
    text_self_rows = text_self_context.reshape(-1, TXT)
    out_vis, vis_normed_three, vis_scale_three = stream_end(
        vis_self_rows, vis_kept[7], vis_weights[5], norm_params, 0
    )
    out_text, text_normed_three, text_scale_three = stream_end(
        text_self_rows, text_kept[7], text_weights[5], norm_params, 1
    )
    vis_resid_three, vis_dself, vis_grad_so, vis_gain_three, vis_bias_three = stream_back_end(
        cot_vis,
        vis_normed_three,
        vis_scale_three,
        vis_self_rows,
        vis_weights[5],
        norm_params,
        0,
        pairs,
    )
    text_resid_three, text_dself, text_grad_so, text_gain_three, text_bias_three = stream_back_end(
        cot_text,
        text_normed_three,
        text_scale_three,
        text_self_rows,
        text_weights[5],
        norm_params,
        1,
        pairs,
    )
    vis_dheads, text_dheads = dfound_to_heads(vis_dself, text_dself)
    vis_dgot, text_dgot = pair_attend_back(
        vis_self_use,
        text_self_use,
        lengths,
        False,
        vis_self_sum,
        text_self_sum,
        vis_dheads,
        text_dheads,
    )
    vis_dself_side, text_dself_side = grads_from_heads(vis_dgot, text_dgot)
    vis_resid_one, vis_dcontext, vis_grads_mid, vis_gains_mid, vis_biases_mid = stream_back_middle(
        vis_resid_three,
        vis_dself_side,
        vis_kept,
        vis_context_rows,
        vis_weights,
        norm_params,
        0,
        pairs,
    )
    text_resid_one, text_dcontext, text_grads_mid, text_gains_mid, text_biases_mid = (
        stream_back_middle(
            text_resid_three,
            text_dself_side,
            text_kept,
            text_context_rows,
            text_weights,
            norm_params,
            1,
            pairs,
        )
    )
    vis_dheads, text_dheads = dfound_to_heads(vis_dcontext, text_dcontext)
    vis_dgot, text_dgot = pair_attend_back(
        vis_co_use, text_co_use, lengths, True, vis_co_sum, text_co_sum, vis_dheads, text_dheads
    )
    vis_dco, text_dco = grads_from_heads(vis_dgot, text_dgot)
    vis_dco_rows = vis_dco.reshape(-1, 3 * BI)
    text_dco_rows = text_dco.reshape(-1, 3 * BI)
    grad_vis = vis_resid_one + lax.dot_general(
        vis_dco_rows, vis_weights[0], CONTRACT_COLS, preferred_element_type=jnp.float32
    )
    grad_text = text_resid_one + lax.dot_general(
        text_dco_rows, text_weights[0], CONTRACT_COLS, preferred_element_type=jnp.float32
    )
    vis_grad_co = block_grad(x_vis, vis_dco_rows, 3)
    text_grad_co = block_grad(x_text, text_dco_rows, 3)
    local_blocks = jnp.concatenate(
        [vis_grad_co]
        + list(vis_grads_mid)
        + [vis_grad_so]
        + [text_grad_co]
        + list(text_grads_mid)
        + [text_grad_so],
        0,
    )
    norm_local = jnp.stack(
        [
            jnp.concatenate(
                [
                    vis_gains_mid[0],
                    vis_gains_mid[1],
                    vis_gain_three,
                    text_gains_mid[0],
                    text_gains_mid[1],
                    text_gain_three,
                ]
            ),
            jnp.concatenate(
                [
                    vis_biases_mid[0],
                    vis_biases_mid[1],
                    vis_bias_three,
                    text_biases_mid[0],
                    text_biases_mid[1],
                    text_bias_three,
                ]
            ),
        ]
    )
    columns = lax.psum_scatter(
        local_blocks.astype(jnp.bfloat16), "seq", scatter_dimension=1, tiled=True
    ).astype(jnp.float32)
    owned_columns = lax.psum_scatter(columns, "dp", scatter_dimension=0, tiled=True)
    owned = lax.all_gather(owned_columns.astype(jnp.bfloat16), "seq", axis=1, tiled=True).astype(
        owned_columns.dtype
    )
    norm_grads = lax.psum(norm_local, ("dp", "seq"))
    number = owned.shape[0]
    grad_cube = owned.reshape(number, BLK, BLK)
    left_cube = stat_left.reshape(number, BLK, BLK)
    right_cube = stat_right.reshape(number, BLK, BLK)
    rootl_cube = root_left.reshape(number, BLK, BLK)
    rootr_cube = root_right.reshape(number, BLK, BLK)
    left_new = STAT_DECAY * left_cube + (1.0 - STAT_DECAY) * jnp.einsum(
        "bij,bkj->bik", grad_cube, grad_cube, precision=HIGHEST
    )
    right_new = STAT_DECAY * right_cube + (1.0 - STAT_DECAY) * jnp.einsum(
        "bji,bjk->bik", grad_cube, grad_cube, precision=HIGHEST
    )
    half = jnp.einsum("bij,bjk->bik", rootl_cube, grad_cube, precision=HIGHEST)
    direction = jnp.einsum("bij,bjk->bik", half, rootr_cube, precision=HIGHEST)
    master_new = master_blocks - WEIGHT_RATE * direction.reshape(number, BLK * BLK)
    second_new = STAT_DECAY * norm_second + (1.0 - STAT_DECAY) * norm_grads * norm_grads
    norm_new = norm_params - NORM_RATE * norm_grads / (jnp.sqrt(second_new) + MOMENT_EPSILON)
    return (
        out_text,
        out_vis,
        grad_text,
        grad_vis,
        owned,
        left_new.reshape(number, BLK * BLK),
        right_new.reshape(number, BLK * BLK),
        master_new,
        norm_grads,
        second_new,
        norm_new,
    )


def solution(mesh):
    placed = (
        P(("dp", "seq"), None),
        P(("dp", "seq"), None),
        P(("dp", "seq")),
        P(("dp", "seq"), None),
        P(("dp", "seq"), None),
        P("dp", None),
        P("dp", None),
        P("dp", None),
        P("dp", None),
        P("dp", None),
        P(),
        P(),
    )
    return jax.shard_map(
        shards,
        mesh=mesh,
        in_specs=placed,
        out_specs=(
            P(("dp", "seq"), None),
            P(("dp", "seq"), None),
            P(("dp", "seq"), None),
            P(("dp", "seq"), None),
            P("dp", None),
            P("dp", None),
            P("dp", None),
            P("dp", None),
            P(),
            P(),
            P(),
        ),
        check_vma=False,
    )
```

profile of v0, /device:TPU:11, one launch (start us, length us, event | category | flops | bytes accessed | tf_op | source)
XLA Modules:
  0.0 2388.6 jit_solution(9760753635555275558)
XLA Ops:
  10.3 147.8 %all-gather.4.cloned.1.call-done = bf16[5056,1024]{1,0:T(8,128)(2,1)} async-done(((bf16[632,1024]{1,0:T(8,128)(2,1)}), bf16[5056,1024]{1,0:T(8,128)(2,1)}) %all-gather.4.cloned.1.call-update) | async-done | bytes 10354704 | tf_op jit(solution)/shard_map/all_gather | solution.py:332
  168.4 240.5 %all-gather.6.cloned.1.call-done = bf16[5056,4096]{1,0:T(8,128)(2,1)} async-done(((bf16[5056,1024]{1,0:T(8,128)(2,1)}), bf16[5056,4096]{1,0:T(8,128)(2,1)}) %all-gather.6.cloned.1.call-update) | async-done | bytes 41418768 | tf_op jit(solution)/shard_map/all_gather | solution.py:333
  432.9 10.8 fusion.120
  443.7 13.9 reshape.585
  457.6 14.7 copy.957
  472.3 12.5 reshape.586
  484.8 10.5 fusion.119
  495.3 17.9 reshape.582
  513.2 15.5 copy.954
  528.6 16.7 reshape.583
  566.9 13.7 reshape.592
  580.7 14.7 copy.956
  595.4 12.5 reshape.593
  607.9 13.9 reshape.594
  621.8 13.4 copy.647
  635.2 12.5 reshape.595
  649.7 8.6 reshape.596
  658.4 12.2 copy.955
  670.6 12.0 reshape.597
  754.2 18.0 reshape.611
  772.2 15.6 copy.953
  787.7 16.3 reshape.612
  903.6 11.1 multiply_convert_fusion
  1129.8 16.7 copy.749
  1146.6 17.1 reshape.641
  1260.6 12.7 copy.760
  1273.3 13.2 reshape.650
  1291.7 12.6 copy.763
  1304.3 13.2 reshape.653
  1322.3 10.3 copy.765
  1332.6 9.0 reshape.655
  1368.3 9.3 convert_bitcast_fusion.1
  1377.7 16.7 copy.735
  1394.4 17.0 reshape.631
  1442.9 12.6 copy.755
  1455.5 13.3 reshape.645
  1486.7 286.2 %reduce-scatter.3.cloned.1.call-done = bf16[5056,1024]{1,0:T(8,128)(2,1)} async-done(((bf16[5056,4096]{1,0:T(8,128)(2,1)}), bf16[5056,1024]{1,0:T(8,128)(2,1)}) %reduce-scatter.3.cloned.1.call-update) | async-done | bytes 10354704 | tf_op jit(solution)/shard_map/reduce_scatter | solution.py:466
  1772.9 178.4 %reduce-scatter.5.cloned.1.call-done = bf16[632,1024]{1,0:T(8,128)(2,1)} async-done(((bf16[5056,1024]{1,0:T(8,128)(2,1)}), bf16[632,1024]{1,0:T(8,128)(2,1)}) %reduce-scatter.5.cloned.1.call-update) | async-done | bytes 1294352 | tf_op jit(solution)/shard_map/reduce_scatter | solution.py:469
  1951.4 11.4 copy.784
  1962.8 11.3 copy.768
  1974.1 11.2 copy.773
  1985.3 11.3 copy.777
  1996.6 19.8 copy.779
  2016.4 11.2 copy.780
  2027.6 19.8 copy.782
  2047.4 8.8 broadcast_multiply_fusion.2
  2056.4 8.9 broadcast_multiply_fusion.1
  2065.6 40.7 %psum.7 = f32[2,5376]{1,0:T(2,128)S(1)} all-reduce(f32[2,5376]{1,0:T(2,128)S(1)} %pad_maximum_fusion.4), channel_id=1, replica_groups=mesh['dp'=8,'seq'=4] {'dp','seq'}, use_global_device_ids=true, to_apply=%region_50.51 | all-reduce | flops 10752 | bytes 86016 | tf_op jit(solution)/shard_map/psum | solution.py:473
  2126.2 15.7 copy.770
  2141.9 19.0 copy.774
  2160.9 16.7 fusion.134
  2177.6 17.9 copy.772
  2195.4 13.8 multiply_add_fusion.1
  2209.3 11.2 copy.785
  2220.4 16.6 fusion.135
  2237.0 17.8 copy.776
  2254.8 13.9 multiply_add_fusion
  2268.7 11.2 copy.786
  2279.9 24.5 %fusion.136 = f32[632,64,64]{1,2,0:T(8,128)} fusion(bf16[632,64,64]{1,2,0:T(8,128)(2,1)} %copy.774, f32[632,64,64]{2,1,0:T(8,128)} %copy.779), kind=kOutput, calls=%fused_computation.365 | convolution fusion | flops 1988100096 | bytes 25886720 | tf_op jit(solution)/shard_map/bij,bjk->bik/dot_general | solution.py:486
  2304.4 28.7 %broadcast_multiply_fusion = f32[632,64,64]{2,1,0:T(8,128)} fusion(f32[632,64,64]{1,2,0:T(8,128)} %fusion.136, f32[632,64,64]{2,1,0:T(8,128)} %copy.782), kind=kOutput, calls=%fused_computation.7 | convolution fusion | flops 1990688768 | bytes 31064064 | tf_op jit(solution)/shard_map/bij,bjk->bik/dot_general | solution.py:487
  2333.1 17.7 copy.783
  2350.8 12.0 bitcast_subtract_fusion
  2362.8 11.2 copy.787
  2373.9 7.9 convert_element_type.220
  (605 shorter events, 648.1 us)
Async XLA Ops:
  7.2 151.0 %all-gather.4.cloned.1.call-start = ((), (), s32[]{:S(2)}) async-start(), calls=%async_computation.18 | async-start | bytes 11649024 | tf_op jit(solution)/shard_map/all_gather | solution.py:332
  10.2 398.7 %all-gather.6.cloned.1.call-start = ((), (), s32[]{:S(2)}) async-start(), calls=%async_computation.19 | async-start | bytes 51773440 | tf_op jit(solution)/shard_map/all_gather | solution.py:333
  528.6 16.7 copy-start.63
  549.4 11.1 copy-start.42
  556.1 126.5 %all-to-all-start = ((bf16[4,2,27648]{2,1,0:T(2,128)(2,1)}), bf16[4,2,27648]{2,1,0:T(2,128)(2,1)}, u32[]{:S(2)}, u32[]{:S(2)}) async-start(bf16[4,2,27648]{2,1,0:T(2,128)(2,1)} %reshape.703), calls=%async_computation | async-start | bytes 884736 | tf_op jit(solution)/shard_map/all_to_all | solution.py:187
  682.6 154.0 %all-to-all-start.1 = ((bf16[2,128,3,1024]{1,0,2,3:T(2,128)(2,1)}), bf16[2,128,3,1024]{1,0,2,3:T(2,128)(2,1)}, u32[]{:S(2)}, u32[]{:S(2)}) async-start(bf16[2,128,3,1024]{1,0,2,3:T(2,128)(2,1)} %copy.637), calls=%async_computation.1 | async-start | bytes 3145728 | tf_op jit(solution)/shard_map/all_to_all | solution.py:188
  836.6 11.6 copy-start.51
  836.6 19.0 copy-start.50
  845.8 9.8 copy-start.25
  848.2 10.5 copy-start.23
  850.9 16.2 copy-start.64
  851.6 7.9 all-to-all-start.5
  856.6 11.2 copy-start.83
  856.6 11.2 copy-start.87
  859.5 34.2 %all-to-all-start.2 = ((bf16[8,128,256]{1,2,0:T(8,128)(2,1)}), bf16[8,128,256]{1,2,0:T(8,128)(2,1)}, u32[]{:S(2)}, u32[]{:S(2)}) async-start(bf16[8,128,256]{1,2,0:T(8,128)(2,1)} %bitcast.13), calls=%async_computation.2 | async-start | bytes 1048576 | tf_op jit(solution)/shard_map/all_to_all | solution.py:195
  893.8 9.6 copy-start.88
  893.8 9.6 copy-start.107
  893.8 23.6 all-to-all-start.6
  900.7 13.9 slice-start.9
  903.1 11.6 copy-start.93
  903.3 11.3 copy-start.108
  903.5 11.1 copy-start.45
  903.5 11.1 slice-start.10
  916.2 23.6 copy-start.95
  917.3 22.6 copy-start.110
  928.4 11.5 copy-start.89
  928.4 11.5 copy-start.105
  934.9 13.2 copy-start.84
  935.0 14.0 copy-start.97
  935.7 8.1 all-to-all-start.7
  948.9 14.3 copy-start.118
  948.9 14.3 copy-start.120
  958.2 8.9 all-to-all-start.11
  982.8 49.5 %all-to-all-start.12 = ((bf16[8,36,3,256]{3,1,2,0:T(8,128)(2,1)}), bf16[8,36,3,256]{3,1,2,0:T(8,128)(2,1)}, u32[]{:S(2)}, u32[]{:S(2)}) async-start(bf16[8,36,3,256]{3,1,2,0:T(8,128)(2,1)} %copy.709), calls=%async_computation.12 | async-start | bytes 983040 | tf_op jit(solution)/shard_map/all_to_all | solution.py:208
  1032.3 40.9 %all-to-all-start.3 = ((bf16[2,128,3,768]{1,0,2,3:T(2,128)(2,1)}), bf16[2,128,3,768]{1,0,2,3:T(2,128)(2,1)}, u32[]{:S(2)}, u32[]{:S(2)}) async-start(bf16[2,128,3,768]{1,0,2,3:T(2,128)(2,1)} %copy.650), calls=%async_computation.3 | async-start | bytes 2359296 | tf_op jit(solution)/shard_map/all_to_all | solution.py:188
  1050.9 9.2 copy-start.70
  1073.2 8.2 all-to-all-start.13
  1081.4 89.1 %all-to-all-start.4 = ((bf16[8,128,192]{1,2,0:T(8,128)(2,1)}), bf16[8,128,192]{1,2,0:T(8,128)(2,1)}, u32[]{:S(2)}, u32[]{:S(2)}) async-start(bf16[8,128,192]{1,2,0:T(8,128)(2,1)} %bitcast.672), calls=%async_computation.4 | async-start | bytes 786432 | tf_op jit(solution)/shard_map/all_to_all | solution.py:195
  1146.5 22.0 copy-start.11
  1181.0 11.0 all-to-all-start.8
  1197.8 20.4 all-to-all-start.9
  1220.8 9.7 slice-start.7
  1239.1 102.5 %all-to-all-start.10 = ((bf16[2,128,1024]{1,0,2:T(2,128)(2,1)}), bf16[2,128,1024]{1,0,2:T(2,128)(2,1)}, u32[]{:S(2)}, u32[]{:S(2)}) async-start(bf16[2,128,1024]{1,0,2:T(2,128)(2,1)} %copy.691), calls=%async_computation.10 | async-start | bytes 1048576 | tf_op jit(solution)/shard_map/all_to_all | solution.py:202
  1273.3 13.2 copy-start.37
  1273.3 13.2 copy-start.75
  1304.3 13.2 copy-start.22
  1304.3 14.0 copy-start.35
  1332.6 10.2 copy-start.81
  1346.4 11.9 all-to-all-start.15
  1358.3 70.0 %all-to-all-start.14 = ((bf16[8,128,3,256]{1,3,2,0:T(8,128)(2,1)}), bf16[8,128,3,256]{1,3,2,0:T(8,128)(2,1)}, u32[]{:S(2)}, u32[]{:S(2)}) async-start(bf16[8,128,3,256]{1,3,2,0:T(8,128)(2,1)} %pad_maximum_fusion), calls=%async_computation.14 | async-start | bytes 3145728 | tf_op jit(solution)/shard_map/all_to_all | solution.py:209
  1363.5 409.4 %reduce-scatter.3.cloned.1.call-start = ((), (), s32[]{:S(2)}) async-start(), calls=%async_computation.20 | async-start | bytes 51773440 | tf_op jit(solution)/shard_map/reduce_scatter | solution.py:466
  1486.6 464.7 %reduce-scatter.5.cloned.1.call-start = ((), (), s32[]{:S(2)}) async-start(), calls=%async_computation.21 | async-start | bytes 11649024 | tf_op jit(solution)/shard_map/reduce_scatter | solution.py:469
  1772.9 345.5 %all-gather.8.cloned.1.call-start = ((), (), s32[]{:S(2)}) async-start(), calls=%async_computation.22 | async-start | bytes 6471680 | tf_op jit(solution)/shard_map/all_gather | solution.py:470
  2056.2 9.1 copy-start.98
  2056.2 9.1 copy-start.117
  2056.3 9.1 copy-start.115
  2056.3 9.1 copy-start.116
  2056.3 9.1 copy-start.114
  2056.3 9.2 copy-start.102
  2056.3 9.2 copy-start.103
  2056.3 50.6 %copy-start.79 = (f32[2,5376]{1,0:T(2,128)S(1)}, f32[2,5376]{1,0:T(2,128)}, u32[]{:S(2)}) copy-start(f32[2,5376]{1,0:T(2,128)} %param.22) | copy-start | bytes 129028
  2056.3 50.6 %copy-start.85 = (f32[2,5376]{1,0:T(2,128)S(1)}, f32[2,5376]{1,0:T(2,128)}, u32[]{:S(2)}) copy-start(f32[2,5376]{1,0:T(2,128)} %param.23) | copy-start | bytes 129028
  2056.3 51.3 %copy-start.29 = (bf16[2,36,3,4,256]{4,3,2,1,0:T(4,128)(2,1)S(1)}, bf16[2,36,3,4,256]{4,3,2,1,0:T(4,128)(2,1)}, u32[]{:S(2)}) copy-start(bf16[2,36,3,4,256]{4,3,2,1,0:T(4,128)(2,1)} %copy.731) | copy-start | bytes 1327108
  2056.3 51.6 %copy-start.66 = (f32[72,1024]{1,0:T(8,128)S(1)}, f32[72,1024]{1,0:T(8,128)}, u32[]{:S(2)}) copy-start(f32[72,1024]{1,0:T(8,128)} %get-tuple-element.101) | copy-start | bytes 884740
  (94 other events, 437.2 us)
Sparse Core Ops, SparseCore 0:
  10.8 147.3 all-gather.3
  159.7 249.1 all-gather.5
  1486.7 286.0 reduce-scatter.2
  1776.9 174.4 reduce-scatter.4
  1952.8 41.2 all-gather.7
where the time goes:
time: 2410 us; the launch traced here: 2390 us
  local copies, waits for them, and re-layouts  1050 us (44%)
  waiting for transfers between devices  868 us (36%)
  matrix products  245 us (10%)
  other arithmetic  86.3 us (4%)
  starting transfers between devices  75.7 us (3%)
  blocking collectives  45.2 us (2%)
    reduce_scatter x1, waiting for transfers between devices, shards(): lax.psum_scatter(local_blocks.astype(jnp.bfloat16), 'seq', scatter_dimens...  286 us
    reshape x24, local copies, waits for them, and re-layouts, unpack_weights(): blocks[begin:begin + number]  244 us
    all_gather x1, waiting for transfers between devices, shards(): every = lax.all_gather(partial_value, 'seq', axis=1, tiled=True)  240 us
    reduce_scatter x1, waiting for transfers between devices, shards(): lax.psum_scatter(columns, 'dp', scatter_dimension=0, tiled=True)  178 us
    unnamed x311, local copies, waits for them, and re-layouts  165 us
    all_gather x1, waiting for transfers between devices, shards(): partial_value = lax.all_gather(mine, 'dp', axis=0, tiled=True)  148 us
    reshape x12, local copies, waits for them, and re-layouts, block_grad(): jnp.einsum('nai,nkbj->kabij', left, right, preferred_element_type=jnp.flo...  117 us
    reshape x12, local copies, waits for them, and re-layouts, unpack_weights(): shaped.transpose(1, 3, 0, 2, 4).reshape(rows, count * columns)  116 us
  transfers between devices with their start and end apart: 21, of which 10 were waited for; matrix products, arithmetic and copies ran while one was open for 33% of the time, Pallas kernels for 0%

commit v1 on v0

--- a/solution.py
+++ b/solution.py
@@ -1,6 +1,10 @@
+import functools
+
 import jax
 import jax.numpy as jnp
 from jax import lax
+from jax.experimental import pallas as pl
+from jax.experimental.pallas import tpu as pltpu
 from jax.sharding import PartitionSpec as P
 
 TXT = 768
@@ -183,31 +187,19 @@
 
 
 def to_heads(vis_side, text_side):
-    return (
-        lax.all_to_all(vis_side, "seq", split_axis=3, concat_axis=0, tiled=True),
-        lax.all_to_all(text_side, "seq", split_axis=3, concat_axis=0, tiled=True),
-    )
+    return (vis_side, text_side)
 
 
 def from_heads(vis_found, text_found):
-    return (
-        lax.all_to_all(vis_found, "seq", split_axis=0, concat_axis=2, tiled=True),
-        lax.all_to_all(text_found, "seq", split_axis=0, concat_axis=2, tiled=True),
-    )
+    return (vis_found, text_found)
 
 
 def dfound_to_heads(vis_dfound, text_dfound):
-    return (
-        lax.all_to_all(vis_dfound, "seq", split_axis=2, concat_axis=0, tiled=True),
-        lax.all_to_all(text_dfound, "seq", split_axis=2, concat_axis=0, tiled=True),
-    )
+    return (vis_dfound, text_dfound)
 
 
 def grads_from_heads(vis_grad, text_grad):
-    return (
-        lax.all_to_all(vis_grad, "seq", split_axis=0, concat_axis=3, tiled=True),
-        lax.all_to_all(text_grad, "seq", split_axis=0, concat_axis=3, tiled=True),
-    )
+    return (vis_grad, text_grad)
 
 
 def side_of(rows_in, weight, pairs):
@@ -336,7 +328,7 @@
     text_weights = matrices[6:]
     vis_co = side_of(x_vis, vis_weights[0], pairs)
     text_co = side_of(x_text, text_weights[0], pairs)
-    lengths = lax.all_gather(caption_len, "seq", axis=0, tiled=True)
+    lengths = caption_len
     vis_co_use, text_co_use = to_heads(vis_co, text_co)
     vis_found, text_found, vis_co_sum, text_co_sum = pair_attend(
         vis_co_use, text_co_use, lengths, True
@@ -503,6 +495,719 @@
     )
 
 
+SUB = 64
+WIDE = 256
+QUAD = 4
+F32 = jnp.float32
+BF16 = jnp.bfloat16
+VIS_PAD = 48
+VMEM_LIMIT = 60 * 1024 * 1024
+NT = (((1,), (1,)), ((), ()))
+TN = (((0,), (0,)), ((), ()))
+
+
+def tile_table():
+    begin = 0
+    table = []
+    for rows, columns, count in weight_layout():
+        r, g = rows // SUB, columns // WIDE
+        table.append((begin, count, r, g))
+        begin += count * r * g
+    return table
+
+
+TILES = tile_table()
+
+
+def dot(left, right, how=None):
+    if how is None:
+        return jnp.dot(left, right, preferred_element_type=F32)
+    return lax.dot_general(left, right, how, preferred_element_type=F32)
+
+
+def params(**more):
+    return pltpu.CompilerParams(vmem_limit_bytes=VMEM_LIMIT, **more)
+
+
+def whole(count):
+    return [pl.BlockSpec(memory_space=pltpu.VMEM)] * count
+
+
+def lanes_low(rows):
+    return lax.broadcasted_iota(jnp.int32, (rows, 2 * SUB), 1) < SUB
+
+
+def spread_rows(x_ref, scratch):
+    for c in range(32):
+        scratch[c * 8 : (c + 1) * 8, :] = x_ref[:, c * 128 : (c + 1) * 128]
+
+
+def pair_natural(scratch, b, place):
+    low = lanes_low(32)
+    one = scratch[pl.ds(b, 32, stride=8), :]
+    two = scratch[pl.ds(b + 1, 32, stride=8), :]
+    place[pl.ds(0, 32, stride=2), :] = jnp.where(low, one, pltpu.roll(two, SUB, 1))
+    place[pl.ds(1, 32, stride=2), :] = jnp.where(low, pltpu.roll(one, SUB, 1), two)
+    return place[...]
+
+
+def pair_spread(value, place, scratch, b):
+    low = lanes_low(32)
+    place[...] = value
+    even = place[pl.ds(0, 32, stride=2), :]
+    odd = place[pl.ds(1, 32, stride=2), :]
+    scratch[pl.ds(b, 32, stride=8), :] = jnp.where(low, even, pltpu.roll(odd, SUB, 1))
+    scratch[pl.ds(b + 1, 32, stride=8), :] = jnp.where(low, pltpu.roll(even, SUB, 1), odd)
+
+
+def prep_body(x_ref, o_ref, spread, place):
+    spread_rows(x_ref, spread)
+    for k in range(2):
+        for m in range(2):
+            o_ref[k, :, m * 128 : (m + 1) * 128] = pair_natural(
+                spread, 4 * k + 2 * m, place.at[2 * k + m]
+            ).astype(BF16)
+
+
+def prep(master_blocks):
+    number = master_blocks.shape[0]
+    return pl.pallas_call(
+        prep_body,
+        grid=(number // 8,),
+        in_specs=[pl.BlockSpec((8, SUB * SUB), lambda i: (i, 0))],
+        out_specs=pl.BlockSpec((2, SUB, WIDE), lambda i: (i, 0, 0)),
+        out_shape=jax.ShapeDtypeStruct((number // 4, SUB, WIDE), BF16),
+        scratch_shapes=[pltpu.VMEM((256, 128), F32), pltpu.VMEM((4, SUB, 128), F32)],
+        compiler_params=params(),
+    )(master_blocks)
+
+
+def block_diagonal(pair):
+    low = lanes_low(SUB)
+    zero = jnp.zeros_like(pair)
+    return jnp.concatenate([jnp.where(low, pair, zero), jnp.where(low, zero, pair)], 0)
+
+
+def fold(square):
+    return square[:SUB] + square[SUB:]
+
+
+def renew_body(
+    g_ref, m_ref, sl_ref, sr_ref, rl_ref, rr_ref,
+    go_ref, lo_ref, ro_ref, mo_ref,
+    root_l, root_r, out_g, out_l, out_r, out_m, place,
+):
+    spread_rows(rl_ref, root_l)
+    spread_rows(rr_ref, root_r)
+    for pair in range(4):
+        spots = place.at[pair]
+        wide = g_ref[pair // 2, :, (pair % 2) * 128 : (pair % 2 + 1) * 128].astype(F32)
+        grad = block_diagonal(wide).astype(BF16)
+        left = block_diagonal(pair_natural(root_l, 2 * pair, spots.at[0])).astype(BF16)
+        right = block_diagonal(pair_natural(root_r, 2 * pair, spots.at[1])).astype(BF16)
+        half = dot(left, grad).astype(BF16)
+        pair_spread(wide, spots.at[2], out_g, 2 * pair)
+        pair_spread(fold(dot(grad, grad, NT)), spots.at[3], out_l, 2 * pair)
+        pair_spread(fold(dot(grad, grad, TN)), spots.at[4], out_r, 2 * pair)
+        pair_spread(fold(dot(half, right)), spots.at[5], out_m, 2 * pair)
+    for c in range(32):
+        lanes = slice(c * 128, (c + 1) * 128)
+        rows = slice(c * 8, (c + 1) * 8)
+        go_ref[:, lanes] = out_g[rows, :]
+        lo_ref[:, lanes] = STAT_DECAY * sl_ref[:, lanes] + (1.0 - STAT_DECAY) * out_l[rows, :]
+        ro_ref[:, lanes] = STAT_DECAY * sr_ref[:, lanes] + (1.0 - STAT_DECAY) * out_r[rows, :]
+        mo_ref[:, lanes] = m_ref[:, lanes] - WEIGHT_RATE * out_m[rows, :]
+
+
+def renew(owned, master_blocks, stat_left, stat_right, root_left, root_right):
+    number = master_blocks.shape[0]
+    flat = pl.BlockSpec((8, SUB * SUB), lambda i: (i, 0))
+    shape = jax.ShapeDtypeStruct(master_blocks.shape, F32)
+    return pl.pallas_call(
+        renew_body,
+        grid=(number // 8,),
+        in_specs=[pl.BlockSpec((2, SUB, WIDE), lambda i: (i, 0, 0))] + [flat] * 5,
+        out_specs=[flat] * 4,
+        out_shape=[shape] * 4,
+        scratch_shapes=[pltpu.VMEM((256, 128), F32)] * 6 + [pltpu.VMEM((4, 6, SUB, 128), F32)],
+        compiler_params=params(),
+    )(owned, master_blocks, stat_left, stat_right, root_left, root_right)
+
+
+def times(rows_in, w, base, r, g, part, col):
+    first = base + part * r * g + col
+    return dot(rows_in, jnp.concatenate([w[first + a * g] for a in range(r)], 0))
+
+
+def times_back(d_ref, w, base, r, g, count, r4):
+    total = None
+    for part in range(count):
+        first = base + (part * r + 4 * r4) * g
+        wide = jnp.concatenate(
+            [
+                jnp.concatenate([w[first + a * g + col] for a in range(4)], 0)
+                for col in range(g)
+            ],
+            1,
+        )
+        made = dot(d_ref[:, part * g * WIDE : (part + 1) * g * WIDE], wide, NT)
+        total = made if total is None else total + made
+    return total
+
+
+def at256(i):
+    return pl.ds(pl.multiple_of(i * WIDE, WIDE), WIDE)
+
+
+def softmax_of(query, keys, scale, limit):
+    scores = dot(query, keys, NT) * scale
+    column = lax.broadcasted_iota(jnp.int32, scores.shape, 1)
+    scores = jnp.where(column < limit, scores, MASK_FILL)
+    raised = jnp.exp(scores - jnp.max(scores, 1, keepdims=True))
+    return raised / jnp.sum(raised, 1, keepdims=True)
+
+
+def score_grad(probs, dprobs):
+    return (probs * (dprobs - jnp.sum(probs * dprobs, 1, keepdims=True))).astype(BF16)
+
+
+def at128(i):
+    return pl.ds(pl.multiple_of(i * 128, 128), 128)
+
+
+def load(w_any, w, sems, pieces, base):
+    copies = []
+    for i, which in enumerate(pieces):
+        begin, count, r, g = TILES[which]
+        n = count * r * g
+        copies.append(
+            pltpu.make_async_copy(
+                w_any.at[pl.ds(begin, n)], w.at[pl.ds(base[i], n)], sems.at[i]
+            )
+        )
+        copies[-1].start()
+    return copies
+
+
+def tiles_of(which):
+    _, count, r, g = TILES[which]
+    return count * r * g
+
+
+def co_body(len_ref, xv_ref, xt_ref, w_any, cv_ref, ct_ref, fv_ref, ft_ref, w, sems):
+    base = (0, tiles_of(0))
+    copies = load(w_any, w, sems, (0, 6), base)
+    for which, at, x_ref, o_ref, copy in (
+        (0, base[0], xv_ref, cv_ref, copies[0]),
+        (6, base[1], xt_ref, ct_ref, copies[1]),
+    ):
+        _, count, r, g = TILES[which]
+        copy.wait()
+
+        def column(i, carry, at=at, r=r, g=g, x_ref=x_ref, o_ref=o_ref):
+            o_ref[:, at256(i)] = times(x_ref[...], w, at, r, g, i // g, i % g).astype(BF16)
+            return carry
+
+        lax.fori_loop(0, count * g, column, 0)
+    scale = HEAD ** (-0.5)
+    reg = len_ref[2]
+    heads = BI // HEAD
+    for pair in range(2):
+        vis = slice(pair * VIS_PAD, (pair + 1) * VIS_PAD)
+        text = slice(pair * 128, (pair + 1) * 128)
+        live = len_ref[pair]
+
+        def head(j, carry, vis=vis, text=text, live=live):
+            qv, kv, vv = (cv_ref[vis, at128(j + heads * s)] for s in range(3))
+            qt, kt, vt = (ct_ref[text, at128(j + heads * s)] for s in range(3))
+            fv_ref[vis, at128(j)] = dot(softmax_of(qv, kt, scale, live).astype(BF16), vt).astype(BF16)
+            ft_ref[text, at128(j)] = dot(softmax_of(qt, kv, scale, reg).astype(BF16), vv).astype(BF16)
+            return carry
+
+        lax.fori_loop(0, heads, head, 0)
+
+
+def co_forward(lengths, x_vis, x_text, tiles):
+    return pl.pallas_call(
+        co_body,
+        in_specs=[pl.BlockSpec(memory_space=pltpu.SMEM)] + whole(2) + [pl.BlockSpec(memory_space=pl.ANY)],
+        out_specs=whole(4),
+        out_shape=[
+            jax.ShapeDtypeStruct((x_vis.shape[0], 3 * BI), BF16),
+            jax.ShapeDtypeStruct((x_text.shape[0], 3 * BI), BF16),
+            jax.ShapeDtypeStruct((x_vis.shape[0], BI), BF16),
+            jax.ShapeDtypeStruct((x_text.shape[0], BI), BF16),
+        ],
+        scratch_shapes=[
+            pltpu.VMEM((tiles_of(0) + tiles_of(6), SUB, WIDE), BF16),
+            pltpu.SemaphoreType.DMA((2,)),
+        ],
+        compiler_params=params(),
+    )(lengths, x_vis, x_text, tiles)
+
+
+def co_back_body(
+    len_ref, cv_ref, ct_ref, dv_ref, dt_ref, rv_ref, rt_ref, w_any,
+    gv_ref, gt_ref, ov_ref, ot_ref, w, sems,
+):
+    base = (0, tiles_of(0))
+    copies = load(w_any, w, sems, (0, 6), base)
+    scale = HEAD ** (-0.5)
+    reg = len_ref[2]
+    heads = BI // HEAD
+    for pair in range(2):
+        vis = slice(pair * VIS_PAD, (pair + 1) * VIS_PAD)
+        text = slice(pair * 128, (pair + 1) * 128)
+        live = len_ref[pair]
+
+        def head(j, carry, vis=vis, text=text, live=live):
+            qv, kv, vv = (cv_ref[vis, at128(j + heads * s)] for s in range(3))
+            qt, kt, vt = (ct_ref[text, at128(j + heads * s)] for s in range(3))
+            dv = dv_ref[vis, at128(j)]
+            dt = dt_ref[text, at128(j)]
+            probs = softmax_of(qv, kt, scale, live)
+            ds = score_grad(probs, dot(dv, vt, NT))
+            gv_ref[vis, at128(j)] = (dot(ds, kt) * scale).astype(BF16)
+            gt_ref[text, at128(j + heads)] = (dot(ds, qv, TN) * scale).astype(BF16)
+            gt_ref[text, at128(j + 2 * heads)] = dot(probs.astype(BF16), dv, TN).astype(BF16)
+            probs = softmax_of(qt, kv, scale, reg)
+            ds = score_grad(probs, dot(dt, vv, NT))
+            gt_ref[text, at128(j)] = (dot(ds, kv) * scale).astype(BF16)
+            gv_ref[vis, at128(j + heads)] = (dot(ds, qt, TN) * scale).astype(BF16)
+            gv_ref[vis, at128(j + 2 * heads)] = dot(probs.astype(BF16), dt, TN).astype(BF16)
+            return carry
+
+        lax.fori_loop(0, heads, head, 0)
+    for which, at, g_ref, r_ref, o_ref, copy in (
+        (0, base[0], gv_ref, rv_ref, ov_ref, copies[0]),
+        (6, base[1], gt_ref, rt_ref, ot_ref, copies[1]),
+    ):
+        _, count, r, g = TILES[which]
+        copy.wait()
+
+        def rows4(i, carry, at=at, r=r, g=g, count=count, g_ref=g_ref, r_ref=r_ref, o_ref=o_ref):
+            o_ref[:, at256(i)] = r_ref[:, at256(i)] + times_back(g_ref, w, at, r, g, count, i)
+            return carry
+
+        lax.fori_loop(0, r // 4, rows4, 0)
+
+
+def co_backward(lengths, co_vis, co_text, dvis, dtext, resid_vis, resid_text, tiles):
+    return pl.pallas_call(
+        co_back_body,
+        in_specs=[pl.BlockSpec(memory_space=pltpu.SMEM)] + whole(6) + [pl.BlockSpec(memory_space=pl.ANY)],
+        out_specs=whole(4),
+        out_shape=[
+            jax.ShapeDtypeStruct(co_vis.shape, BF16),
+            jax.ShapeDtypeStruct(co_text.shape, BF16),
+            jax.ShapeDtypeStruct(resid_vis.shape, F32),
+            jax.ShapeDtypeStruct(resid_text.shape, F32),
+        ],
+        scratch_shapes=[
+            pltpu.VMEM((tiles_of(0) + tiles_of(6), SUB, WIDE), BF16),
+            pltpu.SemaphoreType.DMA((2,)),
+        ],
+        compiler_params=params(),
+    )(lengths, co_vis, co_text, dvis, dtext, resid_vis, resid_text, tiles)
+
+
+def erf_parts(value):
+    return 0.5 * (1.0 + lax.erf(value * 0.7071067811865476))
+
+
+def middle_body(
+    config,
+    len_ref, ctx_ref, x_ref, cot_ref, norm_ref, w_any,
+    out_ref, first_ref, act_ref, second_ref, sctx_ref,
+    fback_ref, pback_ref, bback_ref, dself_ref, tback_ref,
+    resid_ref, dctx_ref, sums_ref,
+    w, sems, pre, n1, n2, n3, s1, s2, s3, wide, acc, selfs, probs, stat,
+):
+    begin, rows, span, head, chunk = config
+    width = x_ref.shape[1]
+    base = []
+    at = 0
+    for which in range(begin, begin + 5):
+        base.append(at)
+        at += tiles_of(which)
+    copies = load(w_any, w, sems, tuple(range(begin, begin + 5)), base)
+    shapes = [TILES[which][1:] for which in range(begin, begin + 5)]
+    steps = rows // chunk
+
+    def at_chunk(i):
+        return pl.ds(pl.multiple_of(i * chunk, chunk), chunk)
+
+    def norm(resid, which, i, kept, scales):
+        mean = jnp.mean(resid, 1, keepdims=True)
+        centered = resid - mean
+        scale = lax.rsqrt(jnp.mean(centered * centered, 1, keepdims=True) + NORM_EPSILON)
+        normed = centered * scale
+        kept[at_chunk(i), :] = normed
+        scales[at_chunk(i), :] = jnp.broadcast_to(scale, (chunk, 128))
+        return normed * norm_ref[0, which : which + 1, :] + norm_ref[1, which : which + 1, :]
+
+    def eight(value):
+        return jnp.sum(value.reshape(chunk // 8, 8, width), 0)
+
+    def norm_back(upstream, which, i, kept, scales):
+        normed = kept[at_chunk(i), :]
+        stat[which] = stat[which] + eight(upstream * normed)
+        stat[3 + which] = stat[3 + which] + eight(upstream)
+        scaled = upstream * norm_ref[0, which : which + 1, :]
+        return scales[at_chunk(i), 0:1] * (
+            scaled
+            - jnp.mean(scaled, 1, keepdims=True)
+            - normed * jnp.mean(scaled * normed, 1, keepdims=True)
+        )
+
+    def loop(count, body):
+        lax.fori_loop(0, count, lambda i, carry: (body(i), carry)[1], 0)
+
+    stat[...] = jnp.zeros(stat.shape, F32)
+    count, r, g = shapes[0]
+    copies[0].wait()
+
+    def co_out(i):
+        wide[:, at256(i)] = times(ctx_ref[...], w, base[0], r, g, 0, i)
+
+    loop(g, co_out)
+
+    def norm_one(i):
+        value = norm(wide[at_chunk(i), :] + x_ref[at_chunk(i), :].astype(F32), 0, i, n1, s1)
+        wide[at_chunk(i), :] = value
+        first_ref[at_chunk(i), :] = value.astype(BF16)
+
+    loop(steps, norm_one)
+    _, r_up, g_up = shapes[1]
+    _, r_down, g_down = shapes[2]
+    copies[1].wait()
+    copies[2].wait()
+    acc[...] = jnp.zeros(acc.shape, F32)
+
+    def down_rows(i):
+        return jnp.concatenate(
+            [
+                jnp.concatenate([w[base[2] + (4 * i + a) * g_down + col] for a in range(4)], 0)
+                for col in range(g_down)
+            ],
+            1,
+        )
+
+    def feed(i):
+        value = times(first_ref[...], w, base[1], r_up, g_up, 0, i)
+        pre[i] = value
+        act = (value * erf_parts(value)).astype(BF16)
+        act_ref[:, at256(i)] = act
+        acc[...] += dot(act, down_rows(i))
+
+    loop(g_up, feed)
+
+    def norm_two(i):
+        value = norm(wide[at_chunk(i), :] + acc[at_chunk(i), :], 1, i, n2, s2)
+        wide[at_chunk(i), :] = value
+        second_ref[at_chunk(i), :] = value.astype(BF16)
+
+    loop(steps, norm_two)
+    count_s, r_s, g_s = shapes[3]
+    copies[3].wait()
+
+    def self_in(i):
+        selfs[:, at256(i)] = times(second_ref[...], w, base[3], r_s, g_s, i // g_s, i % g_s).astype(BF16)
+
+    loop(count_s * g_s, self_in)
+    scale = head ** (-0.5)
+    groups = width // 128
+    per = 128 // head
+    pairs = rows // span
+
+    def halves(values):
+        if per == 1:
+            return values[0]
+        low = lax.broadcasted_iota(jnp.int32, values[0].shape, 1) < head
+        return jnp.where(low, values[0], values[1])
+
+    def only(value, h):
+        if per == 1:
+            return value
+        low = lax.broadcasted_iota(jnp.int32, value.shape, 1) < head
+        keep = low if h == 0 else jnp.logical_not(low)
+        return jnp.where(keep, value, jnp.zeros_like(value))
+
+    for pair in range(pairs):
+        own = slice(pair * span, (pair + 1) * span)
+        live = len_ref[pair]
+
+        def attend(j, own=own, live=live, pair=pair):
+            q, k, v = (selfs[own, at128(j + groups * s)] for s in range(3))
+            found = []
+            for h in range(per):
+                p = softmax_of(only(q, h), k, scale, live)
+                probs[(pair * groups + j) * per + h] = p
+                found.append(dot(p.astype(BF16), v))
+            sctx_ref[own, at128(j)] = halves(found).astype(BF16)
+
+        loop(groups, attend)
+    _, r_o, g_o = shapes[4]
+    copies[4].wait()
+
+    def self_out(i):
+        acc[:, at256(i)] = times(sctx_ref[...], w, base[4], r_o, g_o, 0, i)
+
+    loop(g_o, self_out)
+
+    def norm_three(i):
+        value = norm(wide[at_chunk(i), :] + acc[at_chunk(i), :], 2, i, n3, s3)
+        out_ref[at_chunk(i), :] = value.astype(BF16)
+        third = norm_back(cot_ref[at_chunk(i), :].astype(F32), 2, i, n3, s3)
+        wide[at_chunk(i), :] = third
+        tback_ref[at_chunk(i), :] = third.astype(BF16)
+
+    loop(steps, norm_three)
+
+    def self_out_back(i):
+        dctx_ref[:, at256(i)] = times_back(tback_ref, w, base[4], r_o, g_o, 1, i).astype(BF16)
+
+    loop(r_o // 4, self_out_back)
+    for pair in range(pairs):
+        own = slice(pair * span, (pair + 1) * span)
+
+        def attend_back(j, own=own, pair=pair):
+            q, k, v = (selfs[own, at128(j + groups * s)] for s in range(3))
+            up = dctx_ref[own, at128(j)]
+            dq, dk, dv = [], [], []
+            for h in range(per):
+                p = probs[(pair * groups + j) * per + h]
+                ds = score_grad(p, dot(only(up, h), v, NT))
+                dq.append(dot(ds, k))
+                dk.append(dot(ds, q, TN))
+                dv.append(dot(p.astype(BF16), up, TN))
+            dself_ref[own, at128(j)] = (halves(dq) * scale).astype(BF16)
+            dself_ref[own, at128(j + groups)] = (halves(dk) * scale).astype(BF16)
+            dself_ref[own, at128(j + 2 * groups)] = halves(dv).astype(BF16)
+
+        loop(groups, attend_back)
+
+    def self_in_back(i):
+        acc[:, at256(i)] = times_back(dself_ref, w, base[3], r_s, g_s, count_s, i)
+
+    loop(r_s // 4, self_in_back)
+
+    def norm_two_back(i):
+        value = norm_back(wide[at_chunk(i), :] + acc[at_chunk(i), :], 1, i, n2, s2)
+        wide[at_chunk(i), :] = value
+        bback_ref[at_chunk(i), :] = value.astype(BF16)
+
+    loop(steps, norm_two_back)
+
+    def feed_back(i):
+        act_grad = dot(bback_ref[...], down_rows(i), NT)
+        value = pre[i]
+        slope = erf_parts(value) + value * (0.3989422804014327 * jnp.exp(-0.5 * value * value))
+        pback_ref[:, at256(i)] = (act_grad * slope).astype(BF16)
+
+    loop(g_up, feed_back)
+
+    def up_back(i):
+        acc[:, at256(i)] = times_back(pback_ref, w, base[1], r_up, g_up, 1, i)
+
+    loop(r_up // 4, up_back)
+
+    def norm_one_back(i):
+        value = norm_back(wide[at_chunk(i), :] + acc[at_chunk(i), :], 0, i, n1, s1)
+        resid_ref[at_chunk(i), :] = value
+        fback_ref[at_chunk(i), :] = value.astype(BF16)
+
+    loop(steps, norm_one_back)
+
+    def co_out_back(i):
+        dctx_ref[:, at256(i)] = times_back(fback_ref, w, base[0], r, g, 1, i).astype(BF16)
+
+    loop(r // 4, co_out_back)
+    sums_ref[...] = jnp.sum(stat[...], 1)
+
+
+def middle(begin, lengths, context, x, cot, norms, tiles, span, head, chunk):
+    rows, width = x.shape
+    hidden = TILES[begin + 1][3] * WIDE
+    number = sum(tiles_of(which) for which in range(begin, begin + 5))
+    low = lambda columns: jax.ShapeDtypeStruct((rows, columns), BF16)
+    return pl.pallas_call(
+        functools.partial(middle_body, (begin, rows, span, head, chunk)),
+        in_specs=[pl.BlockSpec(memory_space=pltpu.SMEM)] + whole(4) + [pl.BlockSpec(memory_space=pl.ANY)],
+        out_specs=whole(13),
+        out_shape=[
+            low(width), low(width), low(hidden), low(width), low(width),
+            low(width), low(hidden), low(width), low(3 * width), low(width),
+            jax.ShapeDtypeStruct((rows, width), F32), low(BI),
+            jax.ShapeDtypeStruct((6, width), F32),
+        ],
+        scratch_shapes=[
+            pltpu.VMEM((number, SUB, WIDE), BF16),
+            pltpu.SemaphoreType.DMA((5,)),
+            pltpu.VMEM((hidden // WIDE, rows, WIDE), F32),
+        ]
+        + [pltpu.VMEM((rows, width), F32)] * 3
+        + [pltpu.VMEM((rows, 128), F32)] * 3
+        + [pltpu.VMEM((rows, width), F32)] * 2
+        + [
+            pltpu.VMEM((rows, 3 * width), BF16),
+            pltpu.VMEM((rows // span * (width // head), span, span), F32),
+            pltpu.VMEM((6, 8, width), F32),
+        ],
+        compiler_params=params(),
+    )(lengths, context, x, cot, norms, tiles)
+
+
+def weight_body(kinds, *refs):
+    n = len(kinds)
+    lefts, rights, out, stage, sems = refs[:n], refs[n : 2 * n], refs[2 * n], refs[2 * n + 1], refs[2 * n + 2]
+    offset = 0
+    for which, a_ref, b_ref in zip(kinds, lefts, rights):
+        _, count, r, g = TILES[which]
+        size = 4 * g
+
+        def copy(i, slot, offset=offset, size=size):
+            return pltpu.make_async_copy(
+                stage.at[slot, pl.ds(0, size)], out.at[pl.ds(offset + i * size, size)], sems.at[slot]
+            )
+
+        total = count * (r // 4)
+
+        def step(i, carry, a_ref=a_ref, b_ref=b_ref, r=r, g=g, copy=copy):
+            slot = lax.rem(i, 2)
+
+            @pl.when(i >= 2)
+            def _():
+                copy(i - 2, slot).wait()
+
+            part = i // (r // 4)
+            r4 = lax.rem(i, r // 4)
+            left = a_ref[:, at256(r4)]
+            for col in range(g):
+                made = dot(left, b_ref[:, at256(part * g + col)], TN).astype(BF16)
+                for a in range(4):
+                    stage[slot, a * g + col] = made[a * SUB : (a + 1) * SUB]
+            copy(i, slot).start()
+            return carry
+
+        lax.fori_loop(0, total, step, 0)
+        for i in range(max(0, total - 2), total):
+            copy(i, i % 2).wait()
+        offset += count * r * g
+
+
+def weight_grads(kinds, lefts, rights):
+    number = sum(tiles_of(which) for which in kinds)
+    most = max(4 * TILES[which][3] for which in kinds)
+    return pl.pallas_call(
+        functools.partial(weight_body, kinds),
+        in_specs=whole(2 * len(kinds)),
+        out_specs=pl.BlockSpec(memory_space=pl.ANY),
+        out_shape=jax.ShapeDtypeStruct((number, SUB, WIDE), BF16),
+        scratch_shapes=[
+            pltpu.VMEM((2, most, SUB, WIDE), BF16),
+            pltpu.SemaphoreType.DMA((2,)),
+        ],
+        compiler_params=params(),
+    )(*lefts, *rights)
+
+
+def sum_everywhere(value):
+    for axis in ("seq", "dp"):
+        size = lax.axis_size(axis)
+        step = 1
+        while step < size:
+            value = value + lax.ppermute(value, axis, [(i, i ^ step) for i in range(size)])
+            step *= 2
+    return value
+
+
+def gather_tiles(own):
+    halves = own.reshape(own.shape[0] * 2, SUB // 2, WIDE)
+    size = halves.shape[0] // lax.axis_size("seq")
+    mine = lax.dynamic_slice_in_dim(halves, lax.axis_index("seq") * size, size, 0)
+    return lax.all_gather(mine, ("dp", "seq"), axis=0, tiled=True).reshape(-1, SUB, WIDE)
+
+
+def reduce_tiles(grads):
+    halves = grads.reshape(grads.shape[0] * 2, SUB // 2, WIDE)
+    mine = lax.psum_scatter(halves, ("dp", "seq"), scatter_dimension=0, tiled=True)
+    return lax.all_gather(mine, "seq", axis=0, tiled=True).reshape(-1, SUB, WIDE)
+
+
+def pad_regions(value, pairs):
+    reg = value.shape[0] // pairs
+    cube = value.reshape(pairs, reg, value.shape[1])
+    return jnp.pad(cube, ((0, 0), (0, VIS_PAD - reg), (0, 0))).reshape(pairs * VIS_PAD, -1)
+
+
+def cut_regions(value, pairs, reg):
+    return value.reshape(pairs, VIS_PAD, -1)[:, :reg].reshape(pairs * reg, -1)
+
+
+def fast_shards(
+    x_text, x_vis, caption_len, cot_text, cot_vis, master_blocks,
+    stat_left, stat_right, root_left, root_right, norm_params, norm_second,
+):
+    pairs = caption_len.shape[0]
+    reg = x_vis.shape[0] // pairs
+    tiles = gather_tiles(prep(master_blocks))
+    lengths = jnp.concatenate([caption_len, jnp.full((2,), reg, jnp.int32)])
+    regions = jnp.full((2,), reg, jnp.int32)
+    xv = pad_regions(x_vis, pairs)
+    cv = pad_regions(cot_vis, pairs)
+    vis_norms = norm_params[:, : 3 * VIS].reshape(2, 3, VIS)
+    text_norms = norm_params[:, 3 * VIS :].reshape(2, 3, TXT)
+    co_vis, co_text, vis_ctx, text_ctx = co_forward(lengths, xv, x_text, tiles)
+    (out_vis, v_first, v_act, v_second, v_sctx, v_fback, v_pback, v_bback, v_dself, v_tback,
+     v_resid, v_dctx, v_sums) = middle(1, regions, vis_ctx, xv, cv, vis_norms, tiles, VIS_PAD, HEAD_V, 32)
+    vis_mid = weight_grads(
+        (1, 2, 3, 4, 5), (vis_ctx, v_first, v_act, v_second, v_sctx),
+        (v_fback, v_pback, v_bback, v_dself, v_tback),
+    )
+    (out_text, t_first, t_act, t_second, t_sctx, t_fback, t_pback, t_bback, t_dself, t_tback,
+     t_resid, t_dctx, t_sums) = middle(
+        7, lengths, text_ctx, x_text, cot_text, text_norms, tiles, x_text.shape[0] // pairs, HEAD_T, 32
+    )
+    text_mid = weight_grads(
+        (7, 8, 9, 10, 11), (text_ctx, t_first, t_act, t_second, t_sctx),
+        (t_fback, t_pback, t_bback, t_dself, t_tback),
+    )
+    dco_vis, dco_text, grad_vis, grad_text = co_backward(
+        lengths, co_vis, co_text, v_dctx, t_dctx, v_resid, t_resid, tiles
+    )
+    vis_co = weight_grads((0,), (xv,), (dco_vis,))
+    text_co = weight_grads((6,), (x_text,), (dco_text,))
+    owned = reduce_tiles(jnp.concatenate([vis_co, vis_mid, text_co, text_mid], 0))
+    norm_local = jnp.concatenate([v_sums.reshape(2, -1), t_sums.reshape(2, -1)], 1)
+    norm_grads = sum_everywhere(norm_local)
+    grad_blocks, left_new, right_new, master_new = renew(
+        owned, master_blocks, stat_left, stat_right, root_left, root_right
+    )
+    second_new = STAT_DECAY * norm_second + (1.0 - STAT_DECAY) * norm_grads * norm_grads
+    norm_new = norm_params - NORM_RATE * norm_grads / (jnp.sqrt(second_new) + MOMENT_EPSILON)
+    return (
+        out_text,
+        cut_regions(out_vis, pairs, reg),
+        grad_text,
+        cut_regions(grad_vis, pairs, reg),
+        grad_blocks,
+        left_new,
+        right_new,
+        master_new,
+        norm_grads,
+        second_new,
+        norm_new,
+    )
+
+
+def fits(mesh):
+    owners, group = mesh.shape["dp"], mesh.shape["seq"]
+    number = sum(rows * columns * count for rows, columns, count in weight_layout()) // (BLK * BLK)
+    powers = owners & (owners - 1) == 0 and group & (group - 1) == 0
+    return powers and number % (8 * owners) == 0 and number // owners // 2 % group == 0
+
+
 def solution(mesh):
     placed = (
         P(("dp", "seq"), None),
@@ -518,8 +1223,9 @@
         P(),
         P(),
     )
+    step = fast_shards if fits(mesh) else shards
     return jax.shard_map(
-        shards,
+        step,
         mesh=mesh,
         in_specs=placed,
         out_specs=(

time: 2410 us -> 1090 us (0.45)
  local copies, waits for them, and re-layouts: 1050 us -> 7.88 us
  Pallas kernels: 0 us -> 320 us
  matrix products: 245 us -> 0 us
  waiting for transfers between devices: 868 us -> 704 us
  starting transfers between devices: 75.7 us -> 4.11 us
  other arithmetic: 86.3 us -> 40.2 us
  blocking collectives: 45.2 us -> 0 us
    reshape x76 -> x8, local copies, waits for them, and re-layouts: 588 us -> 2.83 us  [the longest x2 1.44 us: cut_regions(): return value.reshape(pairs, VIS_PAD, -1)[:, :reg].reshape(pairs * reg, -1)]
    reduce_scatter x2 -> x0, waiting for transfers between devices: 465 us -> none  [the longest x1 286 us: shards(): lax.psum_scatter(local_blocks.astype(jnp.bfloat16), 'seq', scatter_dimens...]
    unnamed x5 -> x4, waiting for transfers between devices: 0.08 us -> 439 us
    pallas_call x0 -> x10, Pallas kernels: none -> 320 us  [the longest x2 86.7 us: middle(): pl.pallas_call(functools.partial(middle_body, (begin, rows, span, head, c...]
    dot_general x64 -> x0, matrix products: 245 us -> none  [the longest x12 58.2 us: block_grad(): jnp.einsum('nai,nkbj->kabij', left, right, preferred_element_type=jnp.flo...]
    unnamed x311 -> x19, local copies, waits for them, and re-layouts: 165 us -> 0.05 us
    all_gather x3 -> x2, waiting for transfers between devices: 388 us -> 256 us  [the longest x1 229 us: gather_tiles(): lax.all_gather(mine, ('dp', 'seq'), axis=0, tiled=True)]
    transpose x14 -> x0, local copies, waits for them, and re-layouts: 115 us -> none  [the longest x12 115 us: block_grad(): jnp.einsum('nai,nkbj->kabij', left, right, preferred_element_type=jnp.flo...]
  transfers between devices with their start and end apart: 21 -> 8, of which waited for: 10 -> 8; matrix products, arithmetic and copies ran while one was open for 33% -> 1% of each run, Pallas kernels for 0% -> 0%
where the time goes in v1:
time: 1090 us
  waiting for transfers between devices  704 us (65%)
  Pallas kernels  320 us (29%)
  other arithmetic  40.2 us (4%)
  between operations  14 us (1%)
    unnamed x4, waiting for transfers between devices  439 us
    all_gather x1, waiting for transfers between devices, gather_tiles(): lax.all_gather(mine, ('dp', 'seq'), axis=0, tiled=True)  229 us
    pallas_call x2, Pallas kernels, middle(): pl.pallas_call(functools.partial(middle_body, (begin, rows, span, head, c...  86.7 us
    pallas_call x1, Pallas kernels, renew(): pl.pallas_call(renew_body, grid=(number // 8,), in_specs=[pl.BlockSpec((2...  83.6 us
    pallas_call x4, Pallas kernels, weight_grads(): pl.pallas_call(functools.partial(weight_body, kinds), in_specs=whole(2 *...  57.7 us
    pallas_call x1, Pallas kernels, prep(): pl.pallas_call(prep_body, grid=(number // 8,), in_specs=[pl.BlockSpec((8,...  45.4 us
    concatenate x1, other arithmetic, fast_shards(): jnp.concatenate([vis_co, vis_mid, text_co, text_mid], 0)  39.4 us
    all_gather x1, waiting for transfers between devices, reduce_tiles(): lax.all_gather(mine, 'seq', axis=0, tiled=True).reshape(-1, SUB, WIDE)  26.8 us
  transfers between devices with their start and end apart: 8, of which 8 were waited for; matrix products, arithmetic and copies ran while one was open for 1% of the time, Pallas kernels for 0%

profile of v1, /device:TPU:11, one launch (start us, length us, event | category | flops | bytes accessed | tf_op | source)
XLA Modules:
  0.0 1090.4 jit_solution(7662475087469203643)
XLA Ops:
  7.2 0.0 slice-start
  7.2 0.0 copy-start.2
  7.2 0.0 copy-start.3
  7.2 0.0 all-gather.3.cloned.1.call-start
  7.3 0.0 slice-start.1
  7.3 0.0 copy-start.8
  7.3 45.4 %shard_map.203 = bf16[158,64,256]{2,1,0:T(8,128)(2,1)} custom-call(f32[632,4096]{1,0:T(8,128)} %m_ref.1), custom_call_target="tpu_custom_call" | custom-call | tf_op jit(solution)/shard_map/pallas_call | solution.py:574
  52.7 2.5 constant_dynamic-slice_fusion
  55.1 0.0 all-gather.3.cloned.1.call-update
  55.1 0.0 reduce-scatter.5.cloned.1.call-start
  55.2 0.0 copy-done.2
  55.2 0.0 slice-done
  55.3 0.6 reshape.74.norm_ref
  55.9 0.0 copy-done.3
  55.9 0.7 pad.8
  56.6 0.7 pad.9
  57.3 0.0 slice-done.1
  57.3 0.6 reshape.77.norm_ref
  58.0 0.0 copy-done.8
  58.0 0.5 concatenate.9.len_ref
  58.5 229.1 %all-gather.3.cloned.1.call-done = bf16[2528,32,256]{2,1,0:T(8,128)(2,1)} async-done(((bf16[79,32,256]{2,1,0:T(8,128)(2,1)}), bf16[2528,32,256]{2,1,0:T(8,128)(2,1)}) %all-gather.3.cloned.1.call-update) | async-done | bytes 41418768 | tf_op jit(solution)/shard_map/all_gather | solution.py:1129
  287.6 22.8 %shard_map.204 = (bf16[96,3072]{1,0:T(8,128)(2,1)}, bf16[256,3072]{1,0:T(8,128)(2,1)}, bf16[96,1024]{1,0:T(8,128)(2,1)}, bf16[256,1024]{1,0:T(8,128)(2,1)}) custom-call(s32[4]{0:T(128)} %concatenate.9.len_ref, bf16[96,1024]{1,0:T(8,128)(2,1)} %bitcast.15, bf16[256,768]{1,0:T(8,128)(2,1)} %refs_0_.1, bf16[1264,64,256]{2,1,0:T(8,128)(2,1)} %bitcast.8), custom_call_target="tpu_custom_call" | custom-call | tf_op jit(solution)/shard_map/pallas_call | solution.py:731
  310.4 52.8 %shard_map.205 = (bf16[256,768]{1,0:T(8,128)(2,1)}, bf16[256,768]{1,0:T(8,128)(2,1)}, bf16[256,3072]{1,0:T(8,128)(2,1)}, bf16[256,768]{1,0:T(8,128)(2,1)}, bf16[...) custom-call(s32[4]{0:T(128)} %concatenate.9.len_ref, ...), custom_call_target="tpu_custom_call" | custom-call | tf_op jit(solution)/shard_map/pallas_call | solution.py:1034
  363.2 0.6 broadcast_1_len_ref.2.len_ref
  363.8 34.0 %shard_map.206 = (bf16[96,1024]{1,0:T(8,128)(2,1)}, bf16[96,1024]{1,0:T(8,128)(2,1)}, bf16[96,1024]{1,0:T(8,128)(2,1)}, bf16[96,1024]{1,0:T(8,128)(2,1)}, bf16[9...) custom-call(s32[2]{0:T(128)} %broadcast_1_len_ref.2.len_ref, ...), custom_call_target="tpu_custom_call" | custom-call | tf_op jit(solution)/shard_map/pallas_call | solution.py:1034
  397.8 23.9 %shard_map.207 = (bf16[96,3072]{1,0:T(8,128)(2,1)}, bf16[256,3072]{1,0:T(8,128)(2,1)}, f32[96,1024]{1,0:T(8,128)}, f32[256,768]{1,0:T(8,128)}) custom-call(s32[4]{0:T(128)} %concatenate.9.len_ref, bf16[96,3072]{1,0:T(8,128)(2,1)} %get-tuple-element.53.cv_ref, bf16[256,3072]{1,0:T(8,128)(2,1)} %get-tuple-element.54.ct_ref, ...), custom_call_target="tpu_custom_call" | custom-call | tf_op jit(solution)/shard_map/pallas_call | solution.py:796
  421.7 7.1 shard_map.210
  428.8 8.2 shard_map.208
  437.0 23.2 %shard_map.211 = bf16[480,64,256]{2,1,0:T(8,128)(2,1)} custom-call(bf16[256,1024]{1,0:T(8,128)(2,1)} %get-tuple-element.49.ctx_ref.refs_0_, bf16[256,768]{1,0:T(8,128)(2,1)} %get-tuple-element.72.refs_1_, bf16[256,3072]{1,0:T(8,128)(2,1)} %get-tuple-element.73.refs_2_, bf16[256,768]{1,0:T(8,128)(2,1)} %get-tuple-element.74.refs_3_, ...), custom_call_target="tpu_custom_call" | custom-call | tf_op jit(solution)/shard_map/pallas_call | solution.py:1102
  460.3 19.2 %shard_map.209 = bf16[448,64,256]{2,1,0:T(8,128)(2,1)} custom-call(bf16[96,1024]{1,0:T(8,128)(2,1)} %get-tuple-element.51.ctx_ref.refs_0_, bf16[96,1024]{1,0:T(8,128)(2,1)} %get-tuple-element.62.refs_1_, bf16[96,1024]{1,0:T(8,128)(2,1)} %get-tuple-element.63.refs_2_, bf16[96,1024]{1,0:T(8,128)(2,1)} %get-tuple-element.64.refs_3_, ...), custom_call_target="tpu_custom_call" | custom-call | tf_op jit(solution)/shard_map/pallas_call | solution.py:1102
  479.4 39.4 %pad_maximum_fusion = bf16[1264,64,256]{2,1,0:T(8,128)(2,1)} fusion(bf16[480,64,256]{2,1,0:T(8,128)(2,1)} %shard_map.211, bf16[144,64,256]{2,1,0:T(8,128)(2,1)} %shard_map.210, bf16[448,64,256]{2,1,0:T(8,128)(2,1)} %shard_map.209, bf16[192,64,256]{2,1,0:T(8,128)(2,1)} %shard_map.208), kind=kLoop, calls=%fused_computation | loop fusion | flops 62128128 | bytes 82837504 | tf_op jit(solution)/shard_map/concatenate | solution.py:1181
  518.8 0.0 copy-start.6
  518.8 0.0 copy-start.7
  518.8 0.0 copy-start.4
  518.8 0.0 copy-start
  518.8 0.0 copy-start.1
  518.9 0.0 copy-start.5
  518.9 0.0 reduce-scatter.5.cloned.1.call-update
  518.9 0.0 all-gather.5.cloned.1.call-start
  518.9 439.1 %reduce-scatter.5.cloned.1.call-done = bf16[79,32,256]{2,1,0:T(8,128)(2,1)} async-done(((bf16[2528,32,256]{2,1,0:T(8,128)(2,1)}), bf16[79,32,256]{2,1,0:T(8,128)(2,1)}) %reduce-scatter.5.cloned.1.call-update) | async-done | bytes 1294352
  958.1 0.0 all-gather.5.cloned.1.call-update
  958.1 0.0 copy-done.6
  958.2 0.0 copy-done.7
  958.2 0.1 collective-permute-start
  958.3 1.2 collective-permute-done
  959.5 0.7 collective-permute-start.1
  960.2 2.3 collective-permute-done.1
  962.5 0.7 collective-permute-start.2
  963.2 2.2 collective-permute-done.2
  965.5 0.3 collective-permute-start.3
  965.8 2.6 collective-permute-done.3
  968.4 2.2 collective-permute-start.4
  970.6 0.0 copy-done.4
  970.6 0.7 reshape.79
  971.3 0.0 copy-done
  971.4 0.7 reshape.81
  972.1 0.6 collective-permute-done.4
  972.7 0.0 copy-done.1
  972.7 0.0 copy-done.5
  972.7 0.7 divide_subtract_fusion
  973.5 26.8 %all-gather.5.cloned.1.call-done = bf16[316,32,256]{2,1,0:T(8,128)(2,1)} async-done(((bf16[79,32,256]{2,1,0:T(8,128)(2,1)}), bf16[316,32,256]{2,1,0:T(8,128)(2,1)}) %all-gather.5.cloned.1.call-update) | async-done | bytes 5177360 | tf_op jit(solution)/shard_map/all_gather | solution.py:1135
  1000.2 83.6 %shard_map.212 = (f32[632,4096]{1,0:T(8,128)}, f32[632,4096]{1,0:T(8,128)}, f32[632,4096]{1,0:T(8,128)}, f32[632,4096]{1,0:T(8,128)}) custom-call(bf16[158,64,256]{2,1,0:T(8,128)(2,1)} %bitcast.14, f32[632,4096]{1,0:T(8,128)} %m_ref.1, f32[632,4096]{1,0:T(8,128)} %sl_ref.1, f32[632,4096]{1,0:T(8,128)} %sr_ref.1, f32[632,4096]{1,0:T(8,128)} %rl_ref.1, ...), custom_call_target="tpu_custom_call" | custom-call | tf_op jit(solution)/shard_map/pallas_call | solution.py:626
  (12 shorter events, 0.3 us)
Async XLA Ops:
  7.2 48.1 %slice-start = ((f32[2,5376]{1,0:T(2,128)}), f32[2,2304]{1,0:T(2,128)S(1)}, s32[]{:S(2)}) async-start(f32[2,5376]{1,0:T(2,128)} %param.22), calls=%async_computation.4 | async-start | bytes 36864 | tf_op jit(solution)/shard_map/slice | solution.py:1160
  7.2 48.0 %copy-start.2 = (bf16[72,1024]{1,0:T(8,128)(2,1)S(1)}, bf16[72,1024]{1,0:T(8,128)(2,1)}, u32[]{:S(2)}) copy-start(bf16[72,1024]{1,0:T(8,128)(2,1)} %param.13) | copy-start | bytes 442372
  7.2 48.7 %copy-start.3 = (bf16[72,1024]{1,0:T(8,128)(2,1)S(1)}, bf16[72,1024]{1,0:T(8,128)(2,1)}, u32[]{:S(2)}) copy-start(bf16[72,1024]{1,0:T(8,128)(2,1)} %param.16) | copy-start | bytes 442372
  7.2 280.4 %all-gather.3.cloned.1.call-start = ((), (), s32[]{:S(2)}) async-start(), calls=%async_computation.1 | async-start | bytes 42713088 | tf_op jit(solution)/shard_map/all_gather | solution.py:1129
  7.3 50.1 %slice-start.1 = ((f32[2,5376]{1,0:T(2,128)}), f32[2,3072]{1,0:T(2,128)S(1)}, s32[]{:S(2)}) async-start(f32[2,5376]{1,0:T(2,128)} %param.22), calls=%async_computation.5 | async-start | bytes 49152 | tf_op jit(solution)/shard_map/slice | solution.py:1159
  7.3 50.7 %copy-start.8 = (s32[2]{0:T(128)S(1)}, s32[2]{0:T(128)}, u32[]{:S(2)}) copy-start(s32[2]{0:T(128)} %param.14) | copy-start | bytes 28
  55.1 902.9 %reduce-scatter.5.cloned.1.call-start = ((), (), s32[]{:S(2)}) async-start(), calls=%async_computation.3 | async-start | bytes 42713088
  518.8 439.3 %copy-start.6 = (f32[6,1024]{1,0:T(8,128)S(1)}, f32[6,1024]{1,0:T(8,128)}, u32[]{:S(2)}) copy-start(f32[6,1024]{1,0:T(8,128)} %get-tuple-element.85) | copy-start | bytes 73732
  518.8 439.3 %copy-start.7 = (f32[6,768]{1,0:T(8,128)S(1)}, f32[6,768]{1,0:T(8,128)}, u32[]{:S(2)}) copy-start(f32[6,768]{1,0:T(8,128)} %get-tuple-element.86) | copy-start | bytes 55300
  518.8 451.8 %copy-start.4 = (bf16[96,1024]{1,0:T(8,128)(2,1)S(1)}, bf16[96,1024]{1,0:T(8,128)(2,1)}, u32[]{:S(2)}) copy-start(bf16[96,1024]{1,0:T(8,128)(2,1)} %get-tuple-element.52) | copy-start | bytes 589828
  518.8 452.5 %copy-start = (f32[96,1024]{1,0:T(8,128)S(1)}, f32[96,1024]{1,0:T(8,128)}, u32[]{:S(2)}) copy-start(f32[96,1024]{1,0:T(8,128)} %get-tuple-element.60) | copy-start | bytes 1179652
  518.8 453.9 %copy-start.1 = (f32[2,5376]{1,0:T(2,128)S(1)}, f32[2,5376]{1,0:T(2,128)}, u32[]{:S(2)}) copy-start(f32[2,5376]{1,0:T(2,128)} %param.22) | copy-start | bytes 129028
  518.9 453.9 %copy-start.5 = (f32[2,5376]{1,0:T(2,128)S(1)}, f32[2,5376]{1,0:T(2,128)}, u32[]{:S(2)}) copy-start(f32[2,5376]{1,0:T(2,128)} %param.23) | copy-start | bytes 129028
  518.9 481.3 %all-gather.5.cloned.1.call-start = ((), (), s32[]{:S(2)}) async-start(), calls=%async_computation.2 | async-start | bytes 6471680 | tf_op jit(solution)/shard_map/all_gather | solution.py:1135
  958.2 1.3 collective-permute-start
  959.5 2.9 collective-permute-start.1
  962.5 2.9 collective-permute-start.2
  965.5 2.9 collective-permute-start.3
  968.4 4.3 collective-permute-start.4
Sparse Core Ops, SparseCore 0:
  55.3 232.2 all-gather.2
  519.0 439.0 reduce-scatter.4
  959.7 40.4 all-gather.4

commit v2 on v1

--- a/solution.py
+++ b/solution.py
@@ -517,6 +517,17 @@
 
 
 TILES = tile_table()
+SHARD = 158
+FAR = 46
+G_HALF = 24
+G_LONE = 6
+R_HALF = 80
+R_STEP = 78
+R_LONE = 28
+CHUNKS = 2
+SWAP_CORE = [(i, i ^ 1) for i in range(4)]
+SWAP_Y = [(i, i ^ 2) for i in range(4)]
+SWAP_X = [(i, i ^ 1) for i in range(8)]
 
 
 def dot(left, right, how=None):
@@ -529,109 +540,146 @@
     return pltpu.CompilerParams(vmem_limit_bytes=VMEM_LIMIT, **more)
 
 
+def cost(micros):
+    return pl.CostEstimate(flops=0, bytes_accessed=int(micros * 3.4e6), transcendentals=0)
+
+
 def whole(count):
     return [pl.BlockSpec(memory_space=pltpu.VMEM)] * count
 
 
+def linear(value):
+    groups = value.shape[0] // 8
+    return value.reshape(groups, 8, 32, 128).transpose(0, 2, 1, 3).reshape(groups * 256, 128)
+
+
+def unlinear(value):
+    groups = value.shape[0] // 256
+    return value.reshape(groups, 32, 8, 128).transpose(0, 2, 1, 3).reshape(groups * 8, SUB * SUB)
+
+
 def lanes_low(rows):
     return lax.broadcasted_iota(jnp.int32, (rows, 2 * SUB), 1) < SUB
 
 
-def spread_rows(x_ref, scratch):
-    for c in range(32):
-        scratch[c * 8 : (c + 1) * 8, :] = x_ref[:, c * 128 : (c + 1) * 128]
-
-
-def pair_natural(scratch, b, place):
+def spread_of(ref, b):
+    return ref[pl.ds(b, 32, stride=8), :]
+
+
+def natural_order():
+    row = lax.broadcasted_iota(jnp.int32, (SUB, SUB), 0)
+    column = lax.broadcasted_iota(jnp.int32, (SUB, SUB), 1)
+    return jnp.where(row == 2 * (column % 32) + column // 32, 1.0, 0.0).astype(BF16)
+
+
+def prep_rows(pairs_ref, x_ref, o_ref):
     low = lanes_low(32)
-    one = scratch[pl.ds(b, 32, stride=8), :]
-    two = scratch[pl.ds(b + 1, 32, stride=8), :]
-    place[pl.ds(0, 32, stride=2), :] = jnp.where(low, one, pltpu.roll(two, SUB, 1))
-    place[pl.ds(1, 32, stride=2), :] = jnp.where(low, pltpu.roll(one, SUB, 1), two)
-    return place[...]
-
-
-def pair_spread(value, place, scratch, b):
-    low = lanes_low(32)
-    place[...] = value
-    even = place[pl.ds(0, 32, stride=2), :]
-    odd = place[pl.ds(1, 32, stride=2), :]
-    scratch[pl.ds(b, 32, stride=8), :] = jnp.where(low, even, pltpu.roll(odd, SUB, 1))
-    scratch[pl.ds(b + 1, 32, stride=8), :] = jnp.where(low, pltpu.roll(even, SUB, 1), odd)
-
-
-def prep_body(x_ref, o_ref, spread, place):
-    spread_rows(x_ref, spread)
+    order = natural_order()
     for k in range(2):
         for m in range(2):
-            o_ref[k, :, m * 128 : (m + 1) * 128] = pair_natural(
-                spread, 4 * k + 2 * m, place.at[2 * k + m]
-            ).astype(BF16)
-
-
-def prep(master_blocks):
-    number = master_blocks.shape[0]
+            one = spread_of(x_ref, 4 * k + 2 * m)
+            two = spread_of(x_ref, 4 * k + 2 * m + 1)
+            rows = jnp.concatenate(
+                [
+                    jnp.where(low, one, pltpu.roll(two, SUB, 1)),
+                    jnp.where(low, pltpu.roll(one, SUB, 1), two),
+                ],
+                0,
+            )
+            o_ref[k, :, m * 128 : (m + 1) * 128] = dot(order, rows.astype(BF16)).astype(BF16)
+
+
+def prep(master_blocks, pairs):
+    number = pairs.shape[0]
     return pl.pallas_call(
-        prep_body,
-        grid=(number // 8,),
-        in_specs=[pl.BlockSpec((8, SUB * SUB), lambda i: (i, 0))],
-        out_specs=pl.BlockSpec((2, SUB, WIDE), lambda i: (i, 0, 0)),
-        out_shape=jax.ShapeDtypeStruct((number // 4, SUB, WIDE), BF16),
-        scratch_shapes=[pltpu.VMEM((256, 128), F32), pltpu.VMEM((4, SUB, 128), F32)],
+        prep_rows,
+        grid_spec=pltpu.PrefetchScalarGridSpec(
+            num_scalar_prefetch=1,
+            grid=(number,),
+            in_specs=[pl.BlockSpec((256, 128), lambda i, which: (which[i], 0))],
+            out_specs=pl.BlockSpec((2, SUB, WIDE), lambda i, which: (i, 0, 0)),
+        ),
+        out_shape=jax.ShapeDtypeStruct((number * 2, SUB, WIDE), BF16),
         compiler_params=params(),
-    )(master_blocks)
-
-
-def block_diagonal(pair):
+        cost_estimate=cost(0.4 * number),
+    )(pairs, linear(master_blocks))
+
+
+def renew_body(which_ref, g_ref, m_ref, sl_ref, sr_ref, rl_ref, rr_ref, *refs):
+    go_ref, lo_ref, ro_ref, mo_ref, place = refs[-5:]
     low = lanes_low(SUB)
-    zero = jnp.zeros_like(pair)
-    return jnp.concatenate([jnp.where(low, pair, zero), jnp.where(low, zero, pair)], 0)
-
-
-def fold(square):
-    return square[:SUB] + square[SUB:]
-
-
-def renew_body(
-    g_ref, m_ref, sl_ref, sr_ref, rl_ref, rr_ref,
-    go_ref, lo_ref, ro_ref, mo_ref,
-    root_l, root_r, out_g, out_l, out_r, out_m, place,
-):
-    spread_rows(rl_ref, root_l)
-    spread_rows(rr_ref, root_r)
-    for pair in range(4):
-        spots = place.at[pair]
-        wide = g_ref[pair // 2, :, (pair % 2) * 128 : (pair % 2 + 1) * 128].astype(F32)
-        grad = block_diagonal(wide).astype(BF16)
-        left = block_diagonal(pair_natural(root_l, 2 * pair, spots.at[0])).astype(BF16)
-        right = block_diagonal(pair_natural(root_r, 2 * pair, spots.at[1])).astype(BF16)
-        half = dot(left, grad).astype(BF16)
-        pair_spread(wide, spots.at[2], out_g, 2 * pair)
-        pair_spread(fold(dot(grad, grad, NT)), spots.at[3], out_l, 2 * pair)
-        pair_spread(fold(dot(grad, grad, TN)), spots.at[4], out_r, 2 * pair)
-        pair_spread(fold(dot(half, right)), spots.at[5], out_m, 2 * pair)
-    for c in range(32):
-        lanes = slice(c * 128, (c + 1) * 128)
-        rows = slice(c * 8, (c + 1) * 8)
-        go_ref[:, lanes] = out_g[rows, :]
-        lo_ref[:, lanes] = STAT_DECAY * sl_ref[:, lanes] + (1.0 - STAT_DECAY) * out_l[rows, :]
-        ro_ref[:, lanes] = STAT_DECAY * sr_ref[:, lanes] + (1.0 - STAT_DECAY) * out_r[rows, :]
-        mo_ref[:, lanes] = m_ref[:, lanes] - WEIGHT_RATE * out_m[rows, :]
-
-
-def renew(owned, master_blocks, stat_left, stat_right, root_left, root_right):
-    number = master_blocks.shape[0]
-    flat = pl.BlockSpec((8, SUB * SUB), lambda i: (i, 0))
-    shape = jax.ShapeDtypeStruct(master_blocks.shape, F32)
-    return pl.pallas_call(
+    low_half = lanes_low(32)
+    nothing = jnp.zeros((SUB, 128), F32)
+    pairs = range(4)
+
+    def diagonal(pair):
+        return jnp.concatenate([jnp.where(low, pair, nothing), jnp.where(low, nothing, pair)], 0).astype(BF16)
+
+    def mixed(even, odd):
+        return (
+            jnp.where(low_half, even, pltpu.roll(odd, SUB, 1)),
+            jnp.where(low_half, pltpu.roll(even, SUB, 1), odd),
+        )
+
+    def natural(ref, pair, spot):
+        even, odd = mixed(spread_of(ref, 2 * pair), spread_of(ref, 2 * pair + 1))
+        spot[pl.ds(0, 32, stride=2), :] = even
+        spot[pl.ds(1, 32, stride=2), :] = odd
+        return spot[...]
+
+    def spread(value, spot):
+        spot[...] = value
+        return mixed(spot[pl.ds(0, 32, stride=2), :], spot[pl.ds(1, 32, stride=2), :])
+
+    tiles = [g_ref[pair // 2, :, (pair % 2) * 128 : (pair % 2 + 1) * 128] for pair in pairs]
+    wide = [tile.astype(F32) for tile in tiles]
+    grads = [diagonal(value) for value in wide]
+    lefts = [natural(rl_ref, pair, place.at[pair, 0]).astype(BF16) for pair in pairs]
+    rights = [diagonal(natural(rr_ref, pair, place.at[pair, 1])) for pair in pairs]
+    halves = [dot(lefts[pair], grads[pair]).astype(BF16) for pair in pairs]
+    left_parts = [dot(tiles[pair], grads[pair], NT) for pair in pairs]
+    squares = [dot(tiles[pair], tiles[pair], TN) for pair in pairs]
+    right_parts = [jnp.where(low, square[:SUB], square[SUB:]) for square in squares]
+    steps = [dot(halves[pair], rights[pair]) for pair in pairs]
+    for pair in pairs:
+        made = [
+            spread(value[pair], place.at[pair, 2 + k])
+            for k, value in enumerate((wide, left_parts, right_parts, steps))
+        ]
+        for i in range(2):
+            at = pl.ds(2 * pair + i, 32, stride=8)
+            go_ref[at, :] = made[0][i]
+            lo_ref[at, :] = STAT_DECAY * sl_ref[at, :] + (1.0 - STAT_DECAY) * made[1][i]
+            ro_ref[at, :] = STAT_DECAY * sr_ref[at, :] + (1.0 - STAT_DECAY) * made[2][i]
+            mo_ref[at, :] = m_ref[at, :] - WEIGHT_RATE * made[3][i]
+
+
+def renew(which, owned, master_blocks, stat_left, stat_right, root_left, root_right, before):
+    steps = which.shape[0]
+    flat = pl.BlockSpec((256, 128), lambda i, which: (which[i], 0))
+    shape = jax.ShapeDtypeStruct((master_blocks.shape[0] * 32, 128), F32)
+    made = pl.pallas_call(
         renew_body,
-        grid=(number // 8,),
-        in_specs=[pl.BlockSpec((2, SUB, WIDE), lambda i: (i, 0, 0))] + [flat] * 5,
-        out_specs=[flat] * 4,
+        grid_spec=pltpu.PrefetchScalarGridSpec(
+            num_scalar_prefetch=1,
+            grid=(steps,),
+            in_specs=[pl.BlockSpec((2, SUB, WIDE), lambda i, which: (i, 0, 0))]
+            + [flat] * 5
+            + [pl.BlockSpec(memory_space=pl.ANY)] * len(before),
+            out_specs=[flat] * 4,
+            scratch_shapes=[pltpu.VMEM((4, 6, SUB, 128), F32)],
+        ),
         out_shape=[shape] * 4,
-        scratch_shapes=[pltpu.VMEM((256, 128), F32)] * 6 + [pltpu.VMEM((4, 6, SUB, 128), F32)],
+        input_output_aliases={7 + i: i for i in range(len(before))},
         compiler_params=params(),
-    )(owned, master_blocks, stat_left, stat_right, root_left, root_right)
+        cost_estimate=cost(0.7 * steps),
+    )(
+        which,
+        owned,
+        *(linear(value) for value in (master_blocks, stat_left, stat_right, root_left, root_right)),
+        *(linear(value) for value in before),
+    )
+    return [unlinear(value) for value in made]
 
 
 def times(rows_in, w, base, r, g, part, col):
@@ -675,18 +723,38 @@
     return pl.ds(pl.multiple_of(i * 128, 128), 128)
 
 
-def load(w_any, w, sems, pieces, base):
-    copies = []
+def load(near, far, w, sems, pieces, base):
+    started = []
+    used = 0
     for i, which in enumerate(pieces):
         begin, count, r, g = TILES[which]
-        n = count * r * g
-        copies.append(
-            pltpu.make_async_copy(
-                w_any.at[pl.ds(begin, n)], w.at[pl.ds(base[i], n)], sems.at[i]
-            )
-        )
-        copies[-1].start()
-    return copies
+        end = begin + count * r * g
+        copies = []
+        for owner in range(begin // SHARD, (end - 1) // SHARD + 1):
+            first = max(begin, owner * SHARD)
+            last = min(end, (owner + 1) * SHARD)
+            middle = min(max(owner * SHARD + FAR, first), last)
+            for source, lo, hi, at in (
+                (near, first, middle, owner * (2 * G_HALF) + first - owner * SHARD),
+                (far, middle, last, owner * (SHARD - FAR) + middle - owner * SHARD - FAR),
+            ):
+                if lo < hi:
+                    copies.append(
+                        pltpu.make_async_copy(
+                            source.at[pl.ds(at, hi - lo)],
+                            w.at[pl.ds(base[i] + lo - begin, hi - lo)],
+                            sems.at[used],
+                        )
+                    )
+                    copies[-1].start()
+                    used += 1
+        started.append(copies)
+    return started
+
+
+def arrive(copies):
+    for copy in copies:
+        copy.wait()
 
 
 def tiles_of(which):
@@ -694,43 +762,42 @@
     return count * r * g
 
 
-def co_body(len_ref, xv_ref, xt_ref, w_any, cv_ref, ct_ref, fv_ref, ft_ref, w, sems):
+def co_body(len_ref, xv_ref, xt_ref, near, far, cv_ref, ct_ref, fv_ref, ft_ref, w, sems):
     base = (0, tiles_of(0))
-    copies = load(w_any, w, sems, (0, 6), base)
+    copies = load(near, far, w, sems, (0, 6), base)
     for which, at, x_ref, o_ref, copy in (
         (0, base[0], xv_ref, cv_ref, copies[0]),
         (6, base[1], xt_ref, ct_ref, copies[1]),
     ):
         _, count, r, g = TILES[which]
-        copy.wait()
+        arrive(copy)
 
         def column(i, carry, at=at, r=r, g=g, x_ref=x_ref, o_ref=o_ref):
             o_ref[:, at256(i)] = times(x_ref[...], w, at, r, g, i // g, i % g).astype(BF16)
             return carry
 
-        lax.fori_loop(0, count * g, column, 0)
+        lax.fori_loop(0, count * g, column, 0, unroll=2)
     scale = HEAD ** (-0.5)
     reg = len_ref[2]
     heads = BI // HEAD
-    for pair in range(2):
-        vis = slice(pair * VIS_PAD, (pair + 1) * VIS_PAD)
-        text = slice(pair * 128, (pair + 1) * 128)
-        live = len_ref[pair]
-
-        def head(j, carry, vis=vis, text=text, live=live):
+    def head(j, carry):
+        for pair in range(2):
+            vis = slice(pair * VIS_PAD, (pair + 1) * VIS_PAD)
+            text = slice(pair * 128, (pair + 1) * 128)
+            live = len_ref[pair]
             qv, kv, vv = (cv_ref[vis, at128(j + heads * s)] for s in range(3))
             qt, kt, vt = (ct_ref[text, at128(j + heads * s)] for s in range(3))
             fv_ref[vis, at128(j)] = dot(softmax_of(qv, kt, scale, live).astype(BF16), vt).astype(BF16)
             ft_ref[text, at128(j)] = dot(softmax_of(qt, kv, scale, reg).astype(BF16), vv).astype(BF16)
-            return carry
-
-        lax.fori_loop(0, heads, head, 0)
-
-
-def co_forward(lengths, x_vis, x_text, tiles):
+        return carry
+
+    lax.fori_loop(0, heads, head, 0, unroll=2)
+
+
+def co_forward(lengths, x_vis, x_text, near, far):
     return pl.pallas_call(
         co_body,
-        in_specs=[pl.BlockSpec(memory_space=pltpu.SMEM)] + whole(2) + [pl.BlockSpec(memory_space=pl.ANY)],
+        in_specs=[pl.BlockSpec(memory_space=pltpu.SMEM)] + whole(2) + [pl.BlockSpec(memory_space=pl.ANY)] * 2,
         out_specs=whole(4),
         out_shape=[
             jax.ShapeDtypeStruct((x_vis.shape[0], 3 * BI), BF16),
@@ -740,27 +807,27 @@
         ],
         scratch_shapes=[
             pltpu.VMEM((tiles_of(0) + tiles_of(6), SUB, WIDE), BF16),
-            pltpu.SemaphoreType.DMA((2,)),
+            pltpu.SemaphoreType.DMA((16,)),
         ],
         compiler_params=params(),
-    )(lengths, x_vis, x_text, tiles)
+        cost_estimate=cost(22),
+    )(lengths, x_vis, x_text, near, far)
 
 
 def co_back_body(
-    len_ref, cv_ref, ct_ref, dv_ref, dt_ref, rv_ref, rt_ref, w_any,
+    len_ref, cv_ref, ct_ref, dv_ref, dt_ref, rv_ref, rt_ref, near, far,
     gv_ref, gt_ref, ov_ref, ot_ref, w, sems,
 ):
     base = (0, tiles_of(0))
-    copies = load(w_any, w, sems, (0, 6), base)
+    copies = load(near, far, w, sems, (0, 6), base)
     scale = HEAD ** (-0.5)
     reg = len_ref[2]
     heads = BI // HEAD
-    for pair in range(2):
-        vis = slice(pair * VIS_PAD, (pair + 1) * VIS_PAD)
-        text = slice(pair * 128, (pair + 1) * 128)
-        live = len_ref[pair]
-
-        def head(j, carry, vis=vis, text=text, live=live):
+    def head(j, carry):
+        for pair in range(2):
+            vis = slice(pair * VIS_PAD, (pair + 1) * VIS_PAD)
+            text = slice(pair * 128, (pair + 1) * 128)
+            live = len_ref[pair]
             qv, kv, vv = (cv_ref[vis, at128(j + heads * s)] for s in range(3))
             qt, kt, vt = (ct_ref[text, at128(j + heads * s)] for s in range(3))
             dv = dv_ref[vis, at128(j)]
@@ -775,15 +842,15 @@
             gt_ref[text, at128(j)] = (dot(ds, kv) * scale).astype(BF16)
             gv_ref[vis, at128(j + heads)] = (dot(ds, qt, TN) * scale).astype(BF16)
             gv_ref[vis, at128(j + 2 * heads)] = dot(probs.astype(BF16), dt, TN).astype(BF16)
-            return carry
-
-        lax.fori_loop(0, heads, head, 0)
+        return carry
+
+    lax.fori_loop(0, heads, head, 0)
     for which, at, g_ref, r_ref, o_ref, copy in (
         (0, base[0], gv_ref, rv_ref, ov_ref, copies[0]),
         (6, base[1], gt_ref, rt_ref, ot_ref, copies[1]),
     ):
         _, count, r, g = TILES[which]
-        copy.wait()
+        arrive(copy)
 
         def rows4(i, carry, at=at, r=r, g=g, count=count, g_ref=g_ref, r_ref=r_ref, o_ref=o_ref):
             o_ref[:, at256(i)] = r_ref[:, at256(i)] + times_back(g_ref, w, at, r, g, count, i)
@@ -792,10 +859,10 @@
         lax.fori_loop(0, r // 4, rows4, 0)
 
 
-def co_backward(lengths, co_vis, co_text, dvis, dtext, resid_vis, resid_text, tiles):
+def co_backward(lengths, co_vis, co_text, dvis, dtext, resid_vis, resid_text, near, far):
     return pl.pallas_call(
         co_back_body,
-        in_specs=[pl.BlockSpec(memory_space=pltpu.SMEM)] + whole(6) + [pl.BlockSpec(memory_space=pl.ANY)],
+        in_specs=[pl.BlockSpec(memory_space=pltpu.SMEM)] + whole(6) + [pl.BlockSpec(memory_space=pl.ANY)] * 2,
         out_specs=whole(4),
         out_shape=[
             jax.ShapeDtypeStruct(co_vis.shape, BF16),
@@ -805,10 +872,11 @@
         ],
         scratch_shapes=[
             pltpu.VMEM((tiles_of(0) + tiles_of(6), SUB, WIDE), BF16),
-            pltpu.SemaphoreType.DMA((2,)),
+            pltpu.SemaphoreType.DMA((16,)),
         ],
         compiler_params=params(),
-    )(lengths, co_vis, co_text, dvis, dtext, resid_vis, resid_text, tiles)
+        cost_estimate=cost(23),
+    )(lengths, co_vis, co_text, dvis, dtext, resid_vis, resid_text, near, far)
 
 
 def erf_parts(value):
@@ -817,7 +885,7 @@
 
 def middle_body(
     config,
-    len_ref, ctx_ref, x_ref, cot_ref, norm_ref, w_any,
+    len_ref, ctx_ref, x_ref, cot_ref, norm_ref, near, far,
     out_ref, first_ref, act_ref, second_ref, sctx_ref,
     fback_ref, pback_ref, bback_ref, dself_ref, tback_ref,
     resid_ref, dctx_ref, sums_ref,
@@ -830,7 +898,7 @@
     for which in range(begin, begin + 5):
         base.append(at)
         at += tiles_of(which)
-    copies = load(w_any, w, sems, tuple(range(begin, begin + 5)), base)
+    copies = load(near, far, w, sems, tuple(range(begin, begin + 5)), base)
     shapes = [TILES[which][1:] for which in range(begin, begin + 5)]
     steps = rows // chunk
 
@@ -860,12 +928,12 @@
             - normed * jnp.mean(scaled * normed, 1, keepdims=True)
         )
 
-    def loop(count, body):
-        lax.fori_loop(0, count, lambda i, carry: (body(i), carry)[1], 0)
+    def loop(count, body, unroll=1):
+        lax.fori_loop(0, count, lambda i, carry: (body(i), carry)[1], 0, unroll=unroll)
 
     stat[...] = jnp.zeros(stat.shape, F32)
     count, r, g = shapes[0]
-    copies[0].wait()
+    arrive(copies[0])
 
     def co_out(i):
         wide[:, at256(i)] = times(ctx_ref[...], w, base[0], r, g, 0, i)
@@ -877,11 +945,11 @@
         wide[at_chunk(i), :] = value
         first_ref[at_chunk(i), :] = value.astype(BF16)
 
-    loop(steps, norm_one)
+    loop(steps, norm_one, 2 if steps % 2 == 0 else steps)
     _, r_up, g_up = shapes[1]
     _, r_down, g_down = shapes[2]
-    copies[1].wait()
-    copies[2].wait()
+    arrive(copies[1])
+    arrive(copies[2])
     acc[...] = jnp.zeros(acc.shape, F32)
 
     def down_rows(i):
@@ -895,26 +963,27 @@
 
     def feed(i):
         value = times(first_ref[...], w, base[1], r_up, g_up, 0, i)
-        pre[i] = value
-        act = (value * erf_parts(value)).astype(BF16)
+        part = erf_parts(value)
+        pre[i] = part + value * (0.3989422804014327 * jnp.exp(-0.5 * value * value))
+        act = (value * part).astype(BF16)
         act_ref[:, at256(i)] = act
         acc[...] += dot(act, down_rows(i))
 
-    loop(g_up, feed)
+    loop(g_up, feed, 2)
 
     def norm_two(i):
         value = norm(wide[at_chunk(i), :] + acc[at_chunk(i), :], 1, i, n2, s2)
         wide[at_chunk(i), :] = value
         second_ref[at_chunk(i), :] = value.astype(BF16)
 
-    loop(steps, norm_two)
+    loop(steps, norm_two, 2 if steps % 2 == 0 else steps)
     count_s, r_s, g_s = shapes[3]
-    copies[3].wait()
+    arrive(copies[3])
 
     def self_in(i):
         selfs[:, at256(i)] = times(second_ref[...], w, base[3], r_s, g_s, i // g_s, i % g_s).astype(BF16)
 
-    loop(count_s * g_s, self_in)
+    loop(count_s * g_s, self_in, 3)
     scale = head ** (-0.5)
     groups = width // 128
     per = 128 // head
@@ -933,11 +1002,10 @@
         keep = low if h == 0 else jnp.logical_not(low)
         return jnp.where(keep, value, jnp.zeros_like(value))
 
-    for pair in range(pairs):
-        own = slice(pair * span, (pair + 1) * span)
-        live = len_ref[pair]
-
-        def attend(j, own=own, live=live, pair=pair):
+    def attend(j):
+        for pair in range(pairs):
+            own = slice(pair * span, (pair + 1) * span)
+            live = len_ref[pair]
             q, k, v = (selfs[own, at128(j + groups * s)] for s in range(3))
             found = []
             for h in range(per):
@@ -946,9 +1014,9 @@
                 found.append(dot(p.astype(BF16), v))
             sctx_ref[own, at128(j)] = halves(found).astype(BF16)
 
-        loop(groups, attend)
+    loop(groups, attend)
     _, r_o, g_o = shapes[4]
-    copies[4].wait()
+    arrive(copies[4])
 
     def self_out(i):
         acc[:, at256(i)] = times(sctx_ref[...], w, base[4], r_o, g_o, 0, i)
@@ -962,16 +1030,15 @@
         wide[at_chunk(i), :] = third
         tback_ref[at_chunk(i), :] = third.astype(BF16)
 
-    loop(steps, norm_three)
+    loop(steps, norm_three, 2 if steps % 2 == 0 else steps)
 
     def self_out_back(i):
         dctx_ref[:, at256(i)] = times_back(tback_ref, w, base[4], r_o, g_o, 1, i).astype(BF16)
 
     loop(r_o // 4, self_out_back)
-    for pair in range(pairs):
-        own = slice(pair * span, (pair + 1) * span)
-
-        def attend_back(j, own=own, pair=pair):
+    def attend_back(j):
+        for pair in range(pairs):
+            own = slice(pair * span, (pair + 1) * span)
             q, k, v = (selfs[own, at128(j + groups * s)] for s in range(3))
             up = dctx_ref[own, at128(j)]
             dq, dk, dv = [], [], []
@@ -985,7 +1052,7 @@
             dself_ref[own, at128(j + groups)] = (halves(dk) * scale).astype(BF16)
             dself_ref[own, at128(j + 2 * groups)] = halves(dv).astype(BF16)
 
-        loop(groups, attend_back)
+    loop(groups, attend_back)
 
     def self_in_back(i):
         acc[:, at256(i)] = times_back(dself_ref, w, base[3], r_s, g_s, count_s, i)
@@ -997,15 +1064,13 @@
         wide[at_chunk(i), :] = value
         bback_ref[at_chunk(i), :] = value.astype(BF16)
 
-    loop(steps, norm_two_back)
+    loop(steps, norm_two_back, 2 if steps % 2 == 0 else steps)
 
     def feed_back(i):
         act_grad = dot(bback_ref[...], down_rows(i), NT)
-        value = pre[i]
-        slope = erf_parts(value) + value * (0.3989422804014327 * jnp.exp(-0.5 * value * value))
-        pback_ref[:, at256(i)] = (act_grad * slope).astype(BF16)
-
-    loop(g_up, feed_back)
+        pback_ref[:, at256(i)] = (act_grad * pre[i]).astype(BF16)
+
+    loop(g_up, feed_back, 2)
 
     def up_back(i):
         acc[:, at256(i)] = times_back(pback_ref, w, base[1], r_up, g_up, 1, i)
@@ -1017,7 +1082,7 @@
         resid_ref[at_chunk(i), :] = value
         fback_ref[at_chunk(i), :] = value.astype(BF16)
 
-    loop(steps, norm_one_back)
+    loop(steps, norm_one_back, 2 if steps % 2 == 0 else steps)
 
     def co_out_back(i):
         dctx_ref[:, at256(i)] = times_back(fback_ref, w, base[0], r, g, 1, i).astype(BF16)
@@ -1026,14 +1091,14 @@
     sums_ref[...] = jnp.sum(stat[...], 1)
 
 
-def middle(begin, lengths, context, x, cot, norms, tiles, span, head, chunk):
+def middle(begin, lengths, context, x, cot, norms, near, far, span, head, chunk):
     rows, width = x.shape
     hidden = TILES[begin + 1][3] * WIDE
     number = sum(tiles_of(which) for which in range(begin, begin + 5))
     low = lambda columns: jax.ShapeDtypeStruct((rows, columns), BF16)
     return pl.pallas_call(
         functools.partial(middle_body, (begin, rows, span, head, chunk)),
-        in_specs=[pl.BlockSpec(memory_space=pltpu.SMEM)] + whole(4) + [pl.BlockSpec(memory_space=pl.ANY)],
+        in_specs=[pl.BlockSpec(memory_space=pltpu.SMEM)] + whole(4) + [pl.BlockSpec(memory_space=pl.ANY)] * 2,
         out_specs=whole(13),
         out_shape=[
             low(width), low(width), low(hidden), low(width), low(width),
@@ -1043,7 +1108,7 @@
         ],
         scratch_shapes=[
             pltpu.VMEM((number, SUB, WIDE), BF16),
-            pltpu.SemaphoreType.DMA((5,)),
+            pltpu.SemaphoreType.DMA((24,)),
             pltpu.VMEM((hidden // WIDE, rows, WIDE), F32),
         ]
         + [pltpu.VMEM((rows, width), F32)] * 3
@@ -1055,12 +1120,14 @@
             pltpu.VMEM((6, 8, width), F32),
         ],
         compiler_params=params(),
-    )(lengths, context, x, cot, norms, tiles)
+        cost_estimate=cost(40),
+    )(lengths, context, x, cot, norms, near, far)
 
 
 def weight_body(kinds, *refs):
     n = len(kinds)
-    lefts, rights, out, stage, sems = refs[:n], refs[n : 2 * n], refs[2 * n], refs[2 * n + 1], refs[2 * n + 2]
+    lefts, rights = refs[:n], refs[n : 2 * n]
+    out, stage, across, sems = refs[2 * n :]
     offset = 0
     for which, a_ref, b_ref in zip(kinds, lefts, rights):
         _, count, r, g = TILES[which]
@@ -1074,25 +1141,26 @@
         total = count * (r // 4)
 
         def step(i, carry, a_ref=a_ref, b_ref=b_ref, r=r, g=g, copy=copy):
-            slot = lax.rem(i, 2)
-
-            @pl.when(i >= 2)
+            slot = lax.rem(i, 4)
+
+            @pl.when(i >= 4)
             def _():
-                copy(i - 2, slot).wait()
+                copy(i - 4, slot).wait()
 
             part = i // (r // 4)
             r4 = lax.rem(i, r // 4)
-            left = a_ref[:, at256(r4)]
+            across[...] = jnp.transpose(a_ref[:, at256(r4)])
+            left = across[...]
             for col in range(g):
-                made = dot(left, b_ref[:, at256(part * g + col)], TN).astype(BF16)
+                made = dot(left, b_ref[:, at256(part * g + col)]).astype(BF16)
                 for a in range(4):
                     stage[slot, a * g + col] = made[a * SUB : (a + 1) * SUB]
             copy(i, slot).start()
             return carry
 
         lax.fori_loop(0, total, step, 0)
-        for i in range(max(0, total - 2), total):
-            copy(i, i % 2).wait()
+        for i in range(max(0, total - 4), total):
+            copy(i, i % 4).wait()
         offset += count * r * g
 
 
@@ -1105,34 +1173,228 @@
         out_specs=pl.BlockSpec(memory_space=pl.ANY),
         out_shape=jax.ShapeDtypeStruct((number, SUB, WIDE), BF16),
         scratch_shapes=[
-            pltpu.VMEM((2, most, SUB, WIDE), BF16),
-            pltpu.SemaphoreType.DMA((2,)),
+            pltpu.VMEM((4, most, SUB, WIDE), BF16),
+            pltpu.VMEM((WIDE, lefts[0].shape[0]), BF16),
+            pltpu.SemaphoreType.DMA((4,)),
         ],
         compiler_params=params(),
+        cost_estimate=cost(number * 0.04),
     )(*lefts, *rights)
 
 
-def sum_everywhere(value):
-    for axis in ("seq", "dp"):
+def spot():
+    dp = lax.axis_index("dp")
+    seq = lax.axis_index("seq")
+    return dp // 2, dp % 2, seq // 2, seq % 2
+
+
+def along_z(value, moves):
+    return lax.ppermute(value, "dp", [(2 * a + x, 2 * b + x) for a, b in moves for x in (0, 1)])
+
+
+def cut(value, begin, size):
+    return lax.dynamic_slice_in_dim(value, begin, size, 0)
+
+
+def join(parts):
+    return jnp.concatenate(parts) if len(parts) > 1 else parts[0]
+
+
+def add(left, right):
+    return (left.astype(F32) + right.astype(F32)).astype(BF16)
+
+
+def by_y(y, mine, other):
+    return [jnp.where(y == 0, mine, other), jnp.where(y == 0, other, mine)]
+
+
+def blank(shape):
+    return pl.pallas_call(
+        lambda out: None,
+        out_specs=pl.BlockSpec(memory_space=pl.ANY),
+        out_shape=jax.ShapeDtypeStruct(shape, BF16),
+        compiler_params=params(),
+    )()
+
+
+def gather_tiles(master_blocks):
+    z, x, y, core = spot()
+    lone, both, half = G_LONE // 2, (G_HALF - 2 * G_LONE) // 2, G_HALF // 2
+    fourth = (SHARD - FAR) // 4
+    mine = prep(
+        master_blocks,
+        jnp.concatenate(
+            [half * core + lone * y + jnp.arange(lone), half * core + 2 * lone + jnp.arange(both)]
+        ).astype(jnp.int32),
+    )
+    last = prep(
+        master_blocks,
+        ((FAR + fourth * lax.axis_index("seq")) // 2 + jnp.arange(fourth // 2)).astype(jnp.int32),
+    )
+    far = lax.all_gather(last, ("dp", "seq"), axis=0, tiled=True)
+    ring = [(0, 1), (1, 2), (2, 3), (3, 0)]
+    near = blank((8, 2 * G_HALF, SUB, WIDE))
+    rows = [mine]
+    cross = []
+    halves = []
+    for phase in range(6):
+        out = {}
+        if phase < 3:
+            out["z"] = along_z(rows[phase], ring)
+        if phase < 4:
+            out["x"] = lax.ppermute(rows[phase], "dp", SWAP_X)
+        if 1 <= phase < 5:
+            here = [rows[phase - 1], cross[phase - 1]]
+            out["y"] = lax.ppermute(join([part[:G_LONE] for part in here]), "seq", SWAP_Y)
+        if phase >= 2:
+            out["core"] = lax.ppermute(join(halves[phase - 2]), "seq", SWAP_CORE)
+        out, rows, cross, halves = lax.optimization_barrier((out, rows, cross, halves))
+        if "z" in out:
+            rows = rows + [out["z"]]
+        if "x" in out:
+            cross = cross + [out["x"]]
+        if "y" in out:
+            halves = halves + [
+                [
+                    join(by_y(y, part[:G_LONE], out["y"][G_LONE * i : G_LONE * (i + 1)]) + [part[G_LONE:]])
+                    for i, part in enumerate(here)
+                ]
+            ]
+        if "core" in out:
+            step = phase - 2
+            for side in range(2):
+                owner = 2 * ((z - step) % 4) + (x + side) % 2
+                own = halves[step][side][None]
+                got = out["core"][None, G_HALF * side : G_HALF * (side + 1)]
+                near = lax.dynamic_update_slice(near, own, (owner, G_HALF * core, 0, 0))
+                near = lax.dynamic_update_slice(near, got, (owner, G_HALF * (1 - core), 0, 0))
+    return near.reshape(-1, SUB, WIDE), far
+
+
+ROUTES = (
+    (((3, 2),), ((2, 1),), ((1, 0),)),
+    (((3, 2), (0, 1)), ((2, 1),)),
+    (((0, 1), (3, 2)), ((1, 2),)),
+    (((0, 1),), ((1, 2),), ((2, 3),)),
+)
+LONE = R_LONE // CHUNKS
+BOTH = (R_HALF - 2 * R_LONE) // CHUNKS
+
+
+def chunk_pairs(k):
+    table = []
+    for core in range(2):
+        begin = R_STEP * core // 2
+        for y in range(2):
+            table += [begin + (R_LONE * y + LONE * k) // 2 + i for i in range(LONE // 2)]
+        table += [begin + R_LONE + BOTH * k // 2 + i for i in range(BOTH // 2)]
+    return jnp.asarray(table, jnp.int32)
+
+
+class Sums:
+    def __init__(self):
+        self.at = spot()
+        self.state = {}
+
+    def group(self, zi, place):
+        pair = (2 * zi, 2 * zi + 1)
+
+        def part(o, core, begin, size):
+            array, offset = place[o]
+            begin += offset + R_STEP * core
+            return array[begin : begin + size]
+
+        lone = jnp.concatenate(
+            [part(o, core, R_LONE * y, R_LONE) for y in range(2) for core in range(2) for o in pair]
+        )
+        lone = lax.psum_scatter(lone, "seq", scatter_dimension=0, tiled=True)
+        self.state["lone", zi] = lone.reshape(2, R_LONE, SUB, WIDE)
+        self.state["both", zi] = tuple(place[o] for o in pair)
+
+    def both_of(self, zi, core):
+        size = R_HALF - 2 * R_LONE
+        return jnp.stack(
+            [cut(array, offset + R_STEP * core + 2 * R_LONE, size) for array, offset in self.state["both", zi]]
+        )
+
+    def send(self, task):
+        z, x, y, core = self.at
+        state = self.state
+        kind, who = task[0], task[1]
+        if kind == "C":
+            array, offset = state["place", who]
+            return lax.ppermute(cut(array, offset + R_STEP * (1 - core), R_HALF), "seq", SWAP_CORE)
+        if kind == "B":
+            return lax.ppermute(self.both_of(who, 1 - core), "seq", SWAP_CORE)
+        if kind == "Y":
+            k = task[2]
+            return lax.ppermute(
+                jnp.stack([cut(state["half", o], R_LONE * (1 - y) + LONE * k, LONE) for o in (2 * who, 2 * who + 1)]),
+                "seq",
+                SWAP_Y,
+            )
+        if kind == "X":
+            lone, both = state["kept", who, task[2]]
+            return lax.ppermute(join([cut(lone, 1 - x, 1)[0], cut(both, 1 - x, 1)[0]]), "dp", SWAP_X)
+        if kind == "Z":
+            return along_z(state["value", who, task[2]], ROUTES[who][task[3]])
+        if kind == "F":
+            values = [state["value", zi, who] for zi in range(4)]
+            mine = jnp.where(z == 0, values[0], jnp.where(z == 1, values[1], jnp.where(z == 2, values[2], values[3])))
+            state["mine", who] = mine
+            return lax.ppermute(mine, "seq", SWAP_Y)
+        if kind == "G":
+            return lax.ppermute(state["whole", who], "seq", SWAP_CORE)
+        axis, step = (("seq", 1), ("seq", 2), ("dp", 1), ("dp", 2), ("dp", 4))[who]
         size = lax.axis_size(axis)
-        step = 1
-        while step < size:
-            value = value + lax.ppermute(value, axis, [(i, i ^ step) for i in range(size)])
-            step *= 2
-    return value
-
-
-def gather_tiles(own):
-    halves = own.reshape(own.shape[0] * 2, SUB // 2, WIDE)
-    size = halves.shape[0] // lax.axis_size("seq")
-    mine = lax.dynamic_slice_in_dim(halves, lax.axis_index("seq") * size, size, 0)
-    return lax.all_gather(mine, ("dp", "seq"), axis=0, tiled=True).reshape(-1, SUB, WIDE)
-
-
-def reduce_tiles(grads):
-    halves = grads.reshape(grads.shape[0] * 2, SUB // 2, WIDE)
-    mine = lax.psum_scatter(halves, ("dp", "seq"), scatter_dimension=0, tiled=True)
-    return lax.all_gather(mine, "seq", axis=0, tiled=True).reshape(-1, SUB, WIDE)
+        return lax.ppermute(state["norms", 0], axis, [(i, i ^ step) for i in range(size)])
+
+    def take(self, task, got):
+        z, x, y, core = self.at
+        state = self.state
+        kind, who = task[0], task[1]
+        if kind == "C":
+            array, offset = state["place", who]
+            state["half", who] = add(cut(array, offset + R_STEP * core, R_HALF), got)
+        elif kind == "B":
+            both = add(self.both_of(who, core), got)
+            lone = state.pop(("lone", who))
+            state.pop(("both", who))
+            for k in range(CHUNKS):
+                state["kept", who, k] = (
+                    lone[:, LONE * k : LONE * (k + 1)],
+                    both[:, BOTH * k : BOTH * (k + 1)],
+                )
+        elif kind == "Y":
+            k = task[2]
+            halves = [state["half", o] for o in (2 * who, 2 * who + 1)]
+            lone = add(jnp.stack([cut(h, R_LONE * y + LONE * k, LONE) for h in halves]), got)
+            both = jnp.stack([h[2 * R_LONE + BOTH * k : 2 * R_LONE + BOTH * (k + 1)] for h in halves])
+            state["kept", who, k] = (lone, both)
+        elif kind == "X":
+            lone, both = state.pop(("kept", who, task[2]))
+            state["value", who, task[2]] = add(join([cut(lone, x, 1)[0], cut(both, x, 1)[0]]), got)
+        elif kind == "Z":
+            state["value", who, task[2]] = add(state["value", who, task[2]], got)
+        elif kind == "F":
+            mine = state.pop(("mine", who))
+            state["whole", who] = join(by_y(y, mine[:LONE], got[:LONE]) + [add(mine[LONE:], got[LONE:])])
+        elif kind == "G":
+            half = state.pop(("whole", who))
+            state["owned", who] = join([jnp.where(core == 0, half, got), jnp.where(core == 0, got, half)])
+        else:
+            state["norms", 0] = state["norms", 0] + got
+
+    def step(self, tasks, beside=None):
+        out = [self.send(task) for task in tasks]
+        work = beside() if beside is not None else ()
+        fixed = {key: value for key, value in self.state.items() if key[0] in ("place", "both")}
+        moving = {key: value for key, value in self.state.items() if key not in fixed}
+        out, work, moving = lax.optimization_barrier((out, work, moving))
+        self.state = {**moving, **fixed}
+        for task, got in zip(tasks, out):
+            self.take(task, got)
+        return work
 
 
 def pad_regions(value, pairs):
@@ -1151,39 +1413,85 @@
 ):
     pairs = caption_len.shape[0]
     reg = x_vis.shape[0] // pairs
-    tiles = gather_tiles(prep(master_blocks))
+    near, far = gather_tiles(master_blocks)
     lengths = jnp.concatenate([caption_len, jnp.full((2,), reg, jnp.int32)])
     regions = jnp.full((2,), reg, jnp.int32)
     xv = pad_regions(x_vis, pairs)
     cv = pad_regions(cot_vis, pairs)
     vis_norms = norm_params[:, : 3 * VIS].reshape(2, 3, VIS)
     text_norms = norm_params[:, 3 * VIS :].reshape(2, 3, TXT)
-    co_vis, co_text, vis_ctx, text_ctx = co_forward(lengths, xv, x_text, tiles)
+    co_vis, co_text, vis_ctx, text_ctx = co_forward(lengths, xv, x_text, near, far)
     (out_vis, v_first, v_act, v_second, v_sctx, v_fback, v_pback, v_bback, v_dself, v_tback,
-     v_resid, v_dctx, v_sums) = middle(1, regions, vis_ctx, xv, cv, vis_norms, tiles, VIS_PAD, HEAD_V, 32)
+     v_resid, v_dctx, v_sums) = middle(1, regions, vis_ctx, xv, cv, vis_norms, near, far, VIS_PAD, HEAD_V, 32)
     vis_mid = weight_grads(
         (1, 2, 3, 4, 5), (vis_ctx, v_first, v_act, v_second, v_sctx),
         (v_fback, v_pback, v_bback, v_dself, v_tback),
     )
+    sums = Sums()
+    vis_at = TILES[1][0]
+    text_at = TILES[7][0]
+    sums.group(1, {o: (vis_mid, SHARD * o - vis_at) for o in (2, 3)})
     (out_text, t_first, t_act, t_second, t_sctx, t_fback, t_pback, t_bback, t_dself, t_tback,
      t_resid, t_dctx, t_sums) = middle(
-        7, lengths, text_ctx, x_text, cot_text, text_norms, tiles, x_text.shape[0] // pairs, HEAD_T, 32
-    )
-    text_mid = weight_grads(
-        (7, 8, 9, 10, 11), (text_ctx, t_first, t_act, t_second, t_sctx),
-        (t_fback, t_pback, t_bback, t_dself, t_tback),
-    )
-    dco_vis, dco_text, grad_vis, grad_text = co_backward(
-        lengths, co_vis, co_text, v_dctx, t_dctx, v_resid, t_resid, tiles
-    )
-    vis_co = weight_grads((0,), (xv,), (dco_vis,))
-    text_co = weight_grads((6,), (x_text,), (dco_text,))
-    owned = reduce_tiles(jnp.concatenate([vis_co, vis_mid, text_co, text_mid], 0))
-    norm_local = jnp.concatenate([v_sums.reshape(2, -1), t_sums.reshape(2, -1)], 1)
-    norm_grads = sum_everywhere(norm_local)
+        7, lengths, text_ctx, x_text, cot_text, text_norms, near, far, x_text.shape[0] // pairs, HEAD_T, 32
+    )
+    sums.state["norms", 0] = jnp.concatenate([v_sums.reshape(2, -1), t_sums.reshape(2, -1)], 1)
+    lefts = (text_ctx, t_first, t_act, t_second, t_sctx)
+    rights = (t_fback, t_pback, t_bback, t_dself, t_tback)
+    later = sums.state.pop(("lone", 1))
+    lefts, rights, later = sums.step([], lambda: (lefts, rights, later))
+    sums.state["lone", 1] = later
+    sums.step([("B", 1)])
+    text_mid, back = sums.step(
+        [("X", 1, 0)],
+        lambda: (
+            weight_grads((7, 8, 9, 10, 11), lefts, rights),
+            (co_vis, co_text, v_dctx, t_dctx, v_resid, t_resid),
+        ),
+    )
+    sums.group(3, {o: (text_mid, SHARD * o - text_at) for o in (6, 7)})
+    later = sums.state.pop(("lone", 3))
+    dco_vis, dco_text, grad_vis, grad_text = sums.step(
+        [("X", 1, 1), ("Z", 1, 0, 0)], lambda: co_backward(lengths, *back, near, far)
+    )
+    vis_co, text_co = sums.step(
+        [("Z", 1, 1, 0), ("Z", 1, 0, 1)],
+        lambda: (weight_grads((0,), (xv,), (dco_vis,)), weight_grads((6,), (x_text,), (dco_text,))),
+    )
+    sums.state["lone", 3] = later
+    sums.state["place", 0] = (vis_co, 0)
+    sums.state["place", 1] = (jnp.concatenate([vis_co[SHARD:], vis_mid[: 2 * SHARD - vis_at]]), 0)
+    sums.state["place", 4] = (
+        jnp.concatenate([vis_mid[4 * SHARD - vis_at :], text_co, text_mid[: 5 * SHARD - text_at]]), 0
+    )
+    sums.state["place", 5] = (text_mid, 5 * SHARD - text_at)
+    for tasks in (
+        [("C", 0), ("C", 1), ("B", 3), ("Z", 1, 1, 1), ("N", 0)],
+        [("C", 4), ("C", 5), ("Y", 0, 0), ("X", 3, 0)],
+        [("Y", 2, 0), ("X", 0, 0), ("Z", 3, 0, 0), ("N", 1)],
+        [("Y", 0, 1), ("X", 2, 0), ("Z", 3, 0, 1), ("Z", 0, 0, 0), ("N", 2)],
+        [("Y", 2, 1), ("X", 3, 1), ("Z", 3, 0, 2), ("Z", 0, 0, 1), ("Z", 2, 0, 0)],
+        [("X", 0, 1), ("Z", 3, 1, 0), ("Z", 0, 0, 2), ("Z", 2, 0, 1), ("N", 3)],
+        [("F", 0), ("X", 2, 1), ("Z", 3, 1, 1), ("Z", 0, 1, 0), ("N", 4)],
+        [("G", 0), ("Z", 3, 1, 2), ("Z", 0, 1, 1), ("Z", 2, 1, 0)],
+    ):
+        sums.step(tasks)
+    statistics = (master_blocks, stat_left, stat_right, root_left, root_right)
+    early = chunk_pairs(0)
+    count = early.shape[0] // 2
+    renewed = sums.step(
+        [("Z", 0, 1, 2), ("Z", 2, 1, 1)],
+        lambda: renew(early[:count], sums.state["owned", 0][: 2 * count], *statistics, ()),
+    )
+    renewed = sums.step(
+        [("F", 1)],
+        lambda: renew(early[count:], sums.state["owned", 0][2 * count :], *statistics, renewed),
+    )
+    sums.step([("G", 1)])
     grad_blocks, left_new, right_new, master_new = renew(
-        owned, master_blocks, stat_left, stat_right, root_left, root_right
-    )
+        chunk_pairs(1), sums.state["owned", 1], *statistics, renewed
+    )
+    norm_grads = sums.state["norms", 0]
     second_new = STAT_DECAY * norm_second + (1.0 - STAT_DECAY) * norm_grads * norm_grads
     norm_new = norm_params - NORM_RATE * norm_grads / (jnp.sqrt(second_new) + MOMENT_EPSILON)
     return (
@@ -1202,10 +1510,7 @@
 
 
 def fits(mesh):
-    owners, group = mesh.shape["dp"], mesh.shape["seq"]
-    number = sum(rows * columns * count for rows, columns, count in weight_layout()) // (BLK * BLK)
-    powers = owners & (owners - 1) == 0 and group & (group - 1) == 0
-    return powers and number % (8 * owners) == 0 and number // owners // 2 % group == 0
+    return mesh.shape["dp"] == 8 and mesh.shape["seq"] == 4
 
 
 def solution(mesh):

time: 1090 us -> 865 us (0.79); the launches traced: 1090 us -> 851 us
  waiting for transfers between devices: 704 us -> 269 us
  local copies, waits for them, and re-layouts: 7.88 us -> 116 us
  starting transfers between devices: 4.11 us -> 99.2 us
  Pallas kernels: 320 us -> 257 us
  other arithmetic: 40.2 us -> 92.7 us
    unnamed x4 -> x3, waiting for transfers between devices: 439 us -> 0.05 us
    all_gather x2 -> x1, waiting for transfers between devices: 256 us -> 33.9 us  [gather_tiles(): far = lax.all_gather(last, ('dp', 'seq'), axis=0, tiled=True)]
    ppermute x5 -> x62, waiting for transfers between devices: 8.9 us -> 223 us  [the longest x23 112 us: along_z(): lax.ppermute(value, 'dp', [(2 * a + x, 2 * b + x) for a, b in moves for x...]
    ppermute x5 -> x62, starting transfers between devices: 3.99 us -> 98.8 us  [the longest x23 46.1 us: along_z(): lax.ppermute(value, 'dp', [(2 * a + x, 2 * b + x) for a, b in moves for x...]
    convert_element_type x0 -> x36, other arithmetic: none -> 56.7 us  [add(): return (left.astype(F32) + right.astype(F32)).astype(BF16)]
    unnamed x19 -> x132, local copies, waits for them, and re-layouts: 0.05 us -> 41.3 us
    pallas_call x2 -> x6, Pallas kernels: 129 us -> 95.6 us  [the longest x3 78.4 us: renew(): pl.pallas_call(renew_body, grid_spec=pltpu.PrefetchScalarGridSpec(num_sca...]
    concatenate x1 -> x27, other arithmetic: 39.4 us -> 13.3 us  [the longest x23 8.93 us: join(): return jnp.concatenate(parts) if len(parts) > 1 else parts[0]]
  transfers between devices with their start and end apart: 8 -> 65, of which waited for: 8 -> 31; matrix products, arithmetic and copies ran while one was open for 1% -> 14% of each run, Pallas kernels for 0% -> 18%
where the time goes in v2:
time: 865 us; the launch traced here: 851 us
  waiting for transfers between devices  269 us (31%)
  Pallas kernels  257 us (30%)
  local copies, waits for them, and re-layouts  116 us (13%)
  starting transfers between devices  99.2 us (11%)
  other arithmetic  92.7 us (11%)
  between operations  16.3 us (2%)
    ppermute x23, waiting for transfers between devices, along_z(): lax.ppermute(value, 'dp', [(2 * a + x, 2 * b + x) for a, b in moves for x...  112 us
    pallas_call x3, Pallas kernels, renew(): pl.pallas_call(renew_body, grid_spec=pltpu.PrefetchScalarGridSpec(num_sca...  78.4 us
    pallas_call x2, Pallas kernels, middle(): pl.pallas_call(functools.partial(middle_body, (begin, rows, span, head, c...  76.9 us
    convert_element_type x36, other arithmetic, add(): return (left.astype(F32) + right.astype(F32)).astype(BF16)  56.7 us
    ppermute x23, starting transfers between devices, along_z(): lax.ppermute(value, 'dp', [(2 * a + x, 2 * b + x) for a, b in moves for x...  46.1 us
    pallas_call x4, Pallas kernels, weight_grads(): pl.pallas_call(functools.partial(weight_body, kinds), in_specs=whole(2 *...  45.9 us
    ppermute x4, waiting for transfers between devices, gather_tiles(): lax.ppermute(join([part[:G_LONE] for part in here]), 'seq', SWAP_Y)  44.6 us
    unnamed x132, local copies, waits for them, and re-layouts  41.3 us
  transfers between devices with their start and end apart: 65, of which 31 were waited for; matrix products, arithmetic and copies ran while one was open for 14% of the time, Pallas kernels for 18%

profile of v2, /device:TPU:11, one launch (start us, length us, event | category | flops | bytes accessed | tf_op | source)
XLA Modules:
  0.0 851.2 jit_solution(5613101605760295314)
XLA Ops:
  7.7 10.1 %shard_map.223 = bf16[28,64,256]{2,1,0:T(8,128)(2,1)} custom-call(s32[14]{0:T(128)} %iota_add_fusion.pairs_ref, f32[20224,128]{1,0:T(8,128)} %bitcast.296), custom_call_target="tpu_custom_call" | custom-call | bytes 19040000 | tf_op jit(solution)/shard_map/pallas_call | solution.py:594
  18.5 7.1 shard_map.222
  27.2 26.4 %collective-permute-done.1 = bf16[18,64,256]{2,1,0:T(8,128)(2,1)S(1)} collective-permute-done((bf16[18,64,256]{2,1,0:T(8,128)(2,1)}, bf16[18,64,256]{2,1,0:T(8,128)(2,1)S(1)}, u32[]{:S(2)}, u32[]{:S(2)}) %collective-permute-start.1) | collective-permute-done | bytes 589856 | tf_op jit(solution)/shard_map/ppermute | solution.py:1192
  53.6 5.5 collective-permute-start.4
  62.5 6.3 collective-permute-done.3
  68.8 5.8 collective-permute-done.4
  76.1 13.8 %collective-permute-start.5 = (bf16[48,64,256]{2,1,0:T(8,128)(2,1)S(1)}, bf16[48,64,256]{2,1,0:T(8,128)(2,1)S(1)}, u32[]{:S(2)}, u32[]{:S(2)}) collective-permute-start(bf16[48,64,256]{2,1,0:T(8,128)(2,1)S(1)} %get-tuple-element.590), channel_id=1, source_target_pairs={{0,1},{1,0},{2,3},{3,2},{4,5},{5,4},{6,7},{7,6},{8,9},{9,8},{10,11... | collective-permute-start | bytes 4718600 | tf_op jit(solution)/shard_map/ppermute | solution.py:1250
  90.0 2.7 collective-permute-start.8
  94.6 8.6 %collective-permute-done.7 = bf16[12,64,256]{2,1,0:T(8,128)(2,1)S(1)} collective-permute-done((bf16[12,64,256]{2,1,0:T(8,128)(2,1)S(1)}, bf16[12,64,256]{2,1,0:T(8,128)(2,1)S(1)}, u32[]{:S(2)}, u32[]{:S(2)}) %collective-permute-start.7) | collective-permute-done | bytes 393248 | tf_op jit(solution)/shard_map/ppermute | solution.py:1248
  103.2 20.4 %collective-permute-done.8 = bf16[18,64,256]{2,1,0:T(8,128)(2,1)S(1)} collective-permute-done((bf16[18,64,256]{2,1,0:T(8,128)(2,1)S(1)}, bf16[18,64,256]{2,1,0:T(8,128)(2,1)S(1)}, u32[]{:S(2)}, u32[]{:S(2)}) %collective-permute-start.8) | collective-permute-done | bytes 589856 | tf_op jit(solution)/shard_map/ppermute | solution.py:1192
  144.9 14.6 %collective-permute-done.11 = bf16[12,64,256]{2,1,0:T(8,128)(2,1)S(1)} collective-permute-done((bf16[12,64,256]{2,1,0:T(8,128)(2,1)S(1)}, bf16[12,64,256]{2,1,0:T(8,128)(2,1)S(1)}, u32[]{:S(2)}, u32[]{:S(2)}) %collective-permute-start.11) | collective-permute-done | bytes 393248 | tf_op jit(solution)/shard_map/ppermute | solution.py:1248
  159.5 9.7 %collective-permute-done.10 = bf16[18,64,256]{2,1,0:T(8,128)(2,1)S(1)} collective-permute-done((bf16[18,64,256]{2,1,0:T(8,128)(2,1)S(1)}, bf16[18,64,256]{2,1,0:T(8,128)(2,1)S(1)}, u32[]{:S(2)}, u32[]{:S(2)}) %collective-permute-start.10) | collective-permute-done | bytes 589856 | tf_op jit(solution)/shard_map/ppermute | solution.py:1245
  177.1 15.1 %collective-permute-done.13 = bf16[12,64,256]{2,1,0:T(8,128)(2,1)S(1)} collective-permute-done((bf16[12,64,256]{2,1,0:T(8,128)(2,1)S(1)}, bf16[12,64,256]{2,1,0:T(8,128)(2,1)S(1)}, u32[]{:S(2)}, u32[]{:S(2)}) %collective-permute-start.13) | collective-permute-done | bytes 393248 | tf_op jit(solution)/shard_map/ppermute | solution.py:1248
  203.3 33.9 %all-gather.2.cloned.1.call-done.far = bf16[896,64,256]{2,1,0:T(8,128)(2,1)} async-done(((bf16[28,64,256]{2,1,0:T(8,128)(2,1)}), bf16[896,64,256]{2,1,0:T(8,128)(2,1)}) %all-gather.2.cloned.1.call-update) | async-done | bytes 29360144 | tf_op jit(solution)/shard_map/all_gather | solution.py:1234
  237.2 16.0 %shard_map.224 = (bf16[96,3072]{1,0:T(8,128)(2,1)}, bf16[256,3072]{1,0:T(8,128)(2,1)}, bf16[96,1024]{1,0:T(8,128)(2,1)}, bf16[256,1024]{1,0:T(8,128)(2,1)}) custom-call(s32[4]{0:T(128)} %concatenate.133.len_ref, bf16[96,1024]{1,0:T(8,128)(2,1)} %bitcast.319, bf16[256,768]{1,0:T(8,128)(2,1)} %refs_0_.1, bf16[384,64,256]{2,1,0:T(8,128)(2,1)} %bitcast.292, ...), custom_call_target="tpu_custom_call" | custom-call | bytes 74800000 | tf_op jit(solution)/shard_map/pallas_call | solution.py:798
  253.7 28.7 %shard_map.226 = (bf16[96,1024]{1,0:T(8,128)(2,1)}, bf16[96,1024]{1,0:T(8,128)(2,1)}, bf16[96,1024]{1,0:T(8,128)(2,1)}, bf16[96,1024]{1,0:T(8,128)(2,1)}, bf16[9...) custom-call(s32[2]{0:T(128)} %broadcast_1_len_ref.2.len_ref, ...), custom_call_target="tpu_custom_call" | custom-call | bytes 136000000 | tf_op jit(solution)/shard_map/pallas_call | solution.py:1099
  282.4 15.2 %shard_map.227 = bf16[448,64,256]{2,1,0:T(8,128)(2,1)} custom-call(bf16[96,1024]{1,0:T(8,128)(2,1)} %get-tuple-element.291.ctx_ref.refs_0_, bf16[96,1024]{1,0:T(8,128)(2,1)} %get-tuple-element.293.refs_1_, bf16[96,1024]{1,0:T(8,128)(2,1)} %get-tuple-element.294.refs_2_, bf16[96,1024]{1,0:T(8,128)(2,1)} %get-tuple-element.295.refs_3_, ...), custom_call_target="tpu_custom_call" | custom-call | bytes 60928000 | tf_op jit(solution)/shard_map/pallas_call | solution.py:1170
  297.6 2.2 slice_dynamic-update-slice_fusion.7
  304.2 2.2 slice_dynamic-update-slice_fusion.4
  306.4 2.2 slice_dynamic-update-slice_fusion.3
  319.1 48.2 %shard_map.225 = (bf16[256,768]{1,0:T(8,128)(2,1)}, bf16[256,768]{1,0:T(8,128)(2,1)}, bf16[256,3072]{1,0:T(8,128)(2,1)}, bf16[256,768]{1,0:T(8,128)(2,1)}, bf16[...) custom-call(s32[4]{0:T(128)} %concatenate.133.len_ref, ...), custom_call_target="tpu_custom_call" | custom-call | bytes 136000000 | tf_op jit(solution)/shard_map/pallas_call | solution.py:1099
  368.1 12.5 %reduce-scatter.3.cloned.1.call-done = bf16[56,64,256]{2,1,0:T(8,128)(2,1)} async-done(((bf16[224,64,256]{2,1,0:T(8,128)(2,1)}), bf16[56,64,256]{2,1,0:T(8,128)(2,1)}) %reduce-scatter.3.cloned.1.call-update) | async-done | bytes 1835024 | tf_op jit(solution)/shard_map/reduce_scatter | solution.py:1310
  385.7 17.9 %shard_map.228 = bf16[480,64,256]{2,1,0:T(8,128)(2,1)} custom-call(bf16[256,1024]{1,0:T(8,128)(2,1)} %get-tuple-element.317.ctx_ref.refs_0_, bf16[256,768]{1,0:T(8,128)(2,1)} %get-tuple-element.318.refs_1_, bf16[256,3072]{1,0:T(8,128)(2,1)} %get-tuple-element.319.refs_2_, bf16[256,768]{1,0:T(8,128)(2,1)} %get-tuple-element.320.refs_3_, ...), custom_call_target="tpu_custom_call" | custom-call | bytes 65280000 | tf_op jit(solution)/shard_map/pallas_call | solution.py:1170
  405.4 2.2 slice_dynamic-update-slice_fusion.15
  427.4 23.0 %shard_map.229 = (bf16[96,3072]{1,0:T(8,128)(2,1)}, bf16[256,3072]{1,0:T(8,128)(2,1)}, f32[96,1024]{1,0:T(8,128)}, f32[256,768]{1,0:T(8,128)}) custom-call(s32[4]{0:T(128)} %concatenate.133.len_ref, bf16[96,3072]{1,0:T(8,128)(2,1)} %get-tuple-element.339.cv_ref, bf16[256,3072]{1,0:T(8,128)(2,1)} %get-tuple-element.340.ct_ref, ...), custom_call_target="tpu_custom_call" | custom-call | bytes 78200000 | tf_op jit(solution)/shard_map/pallas_call | solution.py:863
  453.0 2.4 add_convert_fusion.36
  456.6 2.7 slice.353
  459.4 6.8 shard_map.231
  466.2 6.0 shard_map.230
  472.2 5.9 collective-permute-done.19
  479.5 4.0 constant_dynamic-slice_fusion
  485.5 2.2 collective-permute-start.24
  487.8 3.1 dynamic-slice_bitcast_fusion.1
  496.2 3.6 constant_dynamic-slice_fusion.1
  499.9 2.7 add_convert_fusion.33
  508.0 9.2 %collective-permute-done.26 = bf16[26,64,256]{2,1,0:T(8,128)(2,1)S(1)} collective-permute-done((bf16[26,64,256]{2,1,0:T(8,128)(2,1)S(1)}, bf16[26,64,256]{2,1,0:T(8,128)(2,1)S(1)}, u32[]{:S(2)}, u32[]{:S(2)}) %collective-permute-start.26) | collective-permute-done | bytes 852000 | tf_op jit(solution)/shard_map/ppermute | solution.py:1192
  518.1 4.1 add_convert_fusion.2
  522.2 4.5 add_convert_fusion.3
  536.9 2.6 add_convert_fusion.32
  539.6 14.9 %collective-permute-done.29 = bf16[26,64,256]{2,1,0:T(8,128)(2,1)} collective-permute-done((bf16[26,64,256]{2,1,0:T(8,128)(2,1)}, bf16[26,64,256]{2,1,0:T(8,128)(2,1)}, u32[]{:S(2)}, u32[]{:S(2)}) %collective-permute-start.29) | collective-permute-done | bytes 852000 | tf_op jit(solution)/shard_map/ppermute | solution.py:1338
  556.9 3.7 add_convert_fusion.1
  560.6 4.5 add_convert_fusion
  565.2 2.2 add_convert_fusion.9
  571.9 2.4 add_convert_fusion.31
  577.3 14.8 %collective-permute-done.33 = f32[2,5376]{1,0:T(2,128)S(1)} collective-permute-done((f32[2,5376]{1,0:T(2,128)}, f32[2,5376]{1,0:T(2,128)S(1)}, u32[]{:S(2)}, u32[]{:S(2)}) %collective-permute-start.33) | collective-permute-done | bytes 43040 | tf_op jit(solution)/shard_map/ppermute | solution.py:1350
  592.1 2.9 collective-permute-done.32
  602.3 2.9 add_convert_fusion.30
  610.4 2.4 add_convert_fusion.29
  617.7 9.8 %collective-permute-done.38 = f32[2,5376]{1,0:T(2,128)S(1)} collective-permute-done((f32[2,5376]{1,0:T(2,128)S(1)}, f32[2,5376]{1,0:T(2,128)S(1)}, u32[]{:S(2)}, u32[]{:S(2)}) %collective-permute-start.38) | collective-permute-done | bytes 43040 | tf_op jit(solution)/shard_map/ppermute | solution.py:1350
  644.7 6.8 collective-permute-done.42
  651.6 4.5 collective-permute-done.43
  660.5 5.6 collective-permute-start.47
  672.4 4.8 collective-permute-done.47
  681.0 3.3 collective-permute-done.45
  690.4 7.4 collective-permute-done.53
  702.7 9.8 %collective-permute-start.54 = (bf16[40,64,256]{2,1,0:T(8,128)(2,1)S(1)}, bf16[40,64,256]{2,1,0:T(8,128)(2,1)S(1)}, u32[]{:S(2)}, u32[]{:S(2)}) collective-permute-start(bf16[40,64,256]{2,1,0:T(8,128)(2,1)S(1)} %pad_maximum_fusion.5), channel_id=1, source_target_pairs={{0,1},{1,0},{2,3},{3,2},{4,5},{5,4},{6,7},{7,6},{8,9},{9,8},{10,11... | collective-permute-start | bytes 3932168 | tf_op jit(solution)/shard_map/ppermute | solution.py:1347
  715.2 20.1 %collective-permute-done.57 = bf16[26,64,256]{2,1,0:T(8,128)(2,1)S(1)} collective-permute-done((bf16[26,64,256]{2,1,0:T(8,128)(2,1)S(1)}, bf16[26,64,256]{2,1,0:T(8,128)(2,1)S(1)}, u32[]{:S(2)}, u32[]{:S(2)}) %collective-permute-start.57) | collective-permute-done | bytes 852000 | tf_op jit(solution)/shard_map/ppermute | solution.py:1192
  737.6 6.4 collective-permute-start.59
  745.2 2.4 collective-permute-start.58
  747.7 2.5 broadcast_select_fusion.2
  750.2 20.2 %shard_map.232 = (f32[20224,128]{1,0:T(8,128)}, f32[20224,128]{1,0:T(8,128)}, f32[20224,128]{1,0:T(8,128)}, f32[20224,128]{1,0:T(8,128)}) custom-call(s32[20]{0:T(128)} %constant.206.which_ref, bf16[40,64,256]{2,1,0:T(8,128)(2,1)} %get-tuple-element.564.g_ref, f32[20224,128]{1,0:T(8,128)} %bitcast.298, f32[20224,128]{1,0:T(8,128)} %bitcast.301, ...), custom_call_target="tpu_custom_call" | custom-call | bytes 47600000 | tf_op jit(solution)/shard_map/pallas_call | solution.py:661
  773.0 2.8 select_select_fusion
  778.8 20.2 %shard_map.233 = (f32[20224,128]{1,0:T(8,128)}, f32[20224,128]{1,0:T(8,128)}, f32[20224,128]{1,0:T(8,128)}, f32[20224,128]{1,0:T(8,128)}) custom-call(s32[20]{0:T(128)} %constant.207.which_ref, bf16[40,64,256]{2,1,0:T(8,128)(2,1)} %slice.335.g_ref, f32[20224,128]{1,0:T(8,128)} %bitcast.299, ...), custom_call_target="tpu_custom_call", output_to_operand_aliasing={{0}: (7, {}), {1}: (8, {}), {2}: (9, {}), {3}: (10, {})} | custom-call | bytes 47600000 | tf_op jit(solution)/shard_map/pallas_call | solution.py:661
  806.3 38.0 %shard_map.234 = (f32[20224,128]{1,0:T(8,128)}, f32[20224,128]{1,0:T(8,128)}, f32[20224,128]{1,0:T(8,128)}, f32[20224,128]{1,0:T(8,128)}) custom-call(s32[40]{0:T(128)} %constant.196.clone.which_ref, bf16[80,64,256]{2,1,0:T(8,128)(2,1)} %pad_maximum_fusion.2.g_ref, ...), custom_call_target="tpu_custom_call", output_to_operand_aliasing={{0}: (7, {}), {1}: (8, {}), {2}: (9, {}), {3}: (10, {})} | custom-call | bytes 95200000 | tf_op jit(solution)/shard_map/pallas_call | solution.py:661
  (444 shorter events, 209.8 us)
Async XLA Ops:
  7.2 230.0 %all-gather.2.cloned.1.call-start = ((), (), s32[]{:S(2)}) async-start(), calls=%async_computation.2 | async-start | bytes 30277632 | tf_op jit(solution)/shard_map/all_gather | solution.py:1234
  17.9 362.7 %reduce-scatter.3.cloned.1.call-start = ((), (), s32[]{:S(2)}) async-start(), calls=%async_computation.3 | async-start | bytes 9175040 | tf_op jit(solution)/shard_map/reduce_scatter | solution.py:1310
  25.7 27.9 %collective-permute-start.1 = (bf16[18,64,256]{2,1,0:T(8,128)(2,1)}, bf16[18,64,256]{2,1,0:T(8,128)(2,1)S(1)}, u32[]{:S(2)}, u32[]{:S(2)}) collective-permute-start(bf16[18,64,256]{2,1,0:T(8,128)(2,1)} %shard_map.222), channel_id=1, source_target_pairs={{0,8},{4,12},{8,16},{12,20},{16,24},{20,28},{24,0},{28,4},{1,9},{5... | collective-permute-start | bytes 1769480 | tf_op jit(solution)/shard_map/ppermute | solution.py:1192
  27.0 26.6 %collective-permute-start = (bf16[18,64,256]{2,1,0:T(8,128)(2,1)}, bf16[18,64,256]{2,1,0:T(8,128)(2,1)S(1)}, u32[]{:S(2)}, u32[]{:S(2)}) collective-permute-start(bf16[18,64,256]{2,1,0:T(8,128)(2,1)} %shard_map.222), channel_id=1, source_target_pairs={{0,4},{4,0},{8,12},{12,8},{16,20},{20,16},{24,28},{28,24},{1,5},{5... | collective-permute-start | bytes 1769480 | tf_op jit(solution)/shard_map/ppermute | solution.py:1245
  53.6 20.9 %collective-permute-start.4 = (bf16[18,64,256]{2,1,0:T(8,128)(2,1)S(1)}, bf16[18,64,256]{2,1,0:T(8,128)(2,1)S(1)}, u32[]{:S(2)}, u32[]{:S(2)}) collective-permute-start(bf16[18,64,256]{2,1,0:T(8,128)(2,1)S(1)} %collective-permute-done.1), channel_id=1, source_target_pairs={{0,8},{4,12},{8,16},{12,20},{16,24},{20,28},{24,0},{28,4},{1,9},{5... | collective-permute-start | bytes 1769480 | tf_op jit(solution)/shard_map/ppermute | solution.py:1192
  59.2 15.4 %collective-permute-start.2 = (bf16[18,64,256]{2,1,0:T(8,128)(2,1)S(1)}, bf16[18,64,256]{2,1,0:T(8,128)(2,1)S(1)}, u32[]{:S(2)}, u32[]{:S(2)}) collective-permute-start(bf16[18,64,256]{2,1,0:T(8,128)(2,1)S(1)} %collective-permute-done.1), channel_id=1, source_target_pairs={{0,4},{4,0},{8,12},{12,8},{16,20},{20,16},{24,28},{28,24},{1,5},{5... | collective-permute-start | bytes 1769480 | tf_op jit(solution)/shard_map/ppermute | solution.py:1245
  61.1 7.6 collective-permute-start.3
  76.1 47.4 %collective-permute-start.5 = (bf16[48,64,256]{2,1,0:T(8,128)(2,1)S(1)}, bf16[48,64,256]{2,1,0:T(8,128)(2,1)S(1)}, u32[]{:S(2)}, u32[]{:S(2)}) collective-permute-start(bf16[48,64,256]{2,1,0:T(8,128)(2,1)S(1)} %get-tuple-element.590), channel_id=1, source_target_pairs={{0,1},{1,0},{2,3},{3,2},{4,5},{5,4},{6,7},{7,6},{8,9},{9,8},{10,11... | collective-permute-start | bytes 4718600 | tf_op jit(solution)/shard_map/ppermute | solution.py:1250
  90.0 33.6 %collective-permute-start.8 = (bf16[18,64,256]{2,1,0:T(8,128)(2,1)S(1)}, bf16[18,64,256]{2,1,0:T(8,128)(2,1)S(1)}, u32[]{:S(2)}, u32[]{:S(2)}) collective-permute-start(bf16[18,64,256]{2,1,0:T(8,128)(2,1)S(1)} %collective-permute-done.4), channel_id=1, source_target_pairs={{0,8},{4,12},{8,16},{12,20},{16,24},{20,28},{24,0},{28,4},{1,9},{5... | collective-permute-start | bytes 1769480 | tf_op jit(solution)/shard_map/ppermute | solution.py:1192
  92.7 30.9 %collective-permute-start.6 = (bf16[18,64,256]{2,1,0:T(8,128)(2,1)S(1)}, bf16[18,64,256]{2,1,0:T(8,128)(2,1)S(1)}, u32[]{:S(2)}, u32[]{:S(2)}) collective-permute-start(bf16[18,64,256]{2,1,0:T(8,128)(2,1)S(1)} %collective-permute-done.4), channel_id=1, source_target_pairs={{0,4},{4,0},{8,12},{12,8},{16,20},{20,16},{24,28},{28,24},{1,5},{5... | collective-permute-start | bytes 1769480 | tf_op jit(solution)/shard_map/ppermute | solution.py:1245
  92.8 10.4 %collective-permute-start.7 = (bf16[12,64,256]{2,1,0:T(8,128)(2,1)S(1)}, bf16[12,64,256]{2,1,0:T(8,128)(2,1)S(1)}, u32[]{:S(2)}, u32[]{:S(2)}) collective-permute-start(bf16[12,64,256]{2,1,0:T(8,128)(2,1)S(1)} %pad_maximum_fusion.32), channel_id=1, source_target_pairs={{0,2},{1,3},{2,0},{3,1},{4,6},{5,7},{6,4},{7,5},{8,10},{9,11},{10,... | collective-permute-start | bytes 1179656 | tf_op jit(solution)/shard_map/ppermute | solution.py:1248
  128.8 40.4 %collective-permute-start.9 = (bf16[48,64,256]{2,1,0:T(8,128)(2,1)}, bf16[48,64,256]{2,1,0:T(8,128)(2,1)}, u32[]{:S(2)}, u32[]{:S(2)}) collective-permute-start(bf16[48,64,256]{2,1,0:T(8,128)(2,1)} %get-tuple-element.586), channel_id=1, source_target_pairs={{0,1},{1,0},{2,3},{3,2},{4,5},{5,4},{6,7},{7,6},{8,9},{9,8},{10,11... | collective-permute-start | bytes 4718600 | tf_op jit(solution)/shard_map/ppermute | solution.py:1250
  140.0 19.5 %collective-permute-start.11 = (bf16[12,64,256]{2,1,0:T(8,128)(2,1)S(1)}, bf16[12,64,256]{2,1,0:T(8,128)(2,1)S(1)}, u32[]{:S(2)}, u32[]{:S(2)}) collective-permute-start(bf16[12,64,256]{2,1,0:T(8,128)(2,1)S(1)} %pad_maximum_fusion.33), channel_id=1, source_target_pairs={{0,2},{1,3},{2,0},{3,1},{4,6},{5,7},{6,4},{7,5},{8,10},{9,11},{10,... | collective-permute-start | bytes 1179656 | tf_op jit(solution)/shard_map/ppermute | solution.py:1248
  141.4 27.8 %collective-permute-start.10 = (bf16[18,64,256]{2,1,0:T(8,128)(2,1)S(1)}, bf16[18,64,256]{2,1,0:T(8,128)(2,1)S(1)}, u32[]{:S(2)}, u32[]{:S(2)}) collective-permute-start(bf16[18,64,256]{2,1,0:T(8,128)(2,1)S(1)} %collective-permute-done.8), channel_id=1, source_target_pairs={{0,4},{4,0},{8,12},{12,8},{16,20},{20,16},{24,28},{28,24},{1,5},{5... | collective-permute-start | bytes 1769480 | tf_op jit(solution)/shard_map/ppermute | solution.py:1245
  169.6 22.6 %collective-permute-start.12 = (bf16[48,64,256]{2,1,0:T(8,128)(2,1)S(1)}, bf16[48,64,256]{2,1,0:T(8,128)(2,1)S(1)}, u32[]{:S(2)}, u32[]{:S(2)}) collective-permute-start(bf16[48,64,256]{2,1,0:T(8,128)(2,1)S(1)} %get-tuple-element.582), channel_id=1, source_target_pairs={{0,1},{1,0},{2,3},{3,2},{4,5},{5,4},{6,7},{7,6},{8,9},{9,8},{10,11... | collective-permute-start | bytes 4718600 | tf_op jit(solution)/shard_map/ppermute | solution.py:1250
  172.7 19.5 %collective-permute-start.13 = (bf16[12,64,256]{2,1,0:T(8,128)(2,1)S(1)}, bf16[12,64,256]{2,1,0:T(8,128)(2,1)S(1)}, u32[]{:S(2)}, u32[]{:S(2)}) collective-permute-start(bf16[12,64,256]{2,1,0:T(8,128)(2,1)S(1)} %pad_maximum_fusion.34), channel_id=1, source_target_pairs={{0,2},{1,3},{2,0},{3,1},{4,6},{5,7},{6,4},{7,5},{8,10},{9,11},{10,... | collective-permute-start | bytes 1179656 | tf_op jit(solution)/shard_map/ppermute | solution.py:1248
  192.7 6.9 collective-permute-start.14
  315.2 202.0 %reduce-scatter.5.cloned.1.call-start = ((), (), s32[]{:S(2)}) async-start(), calls=%async_computation.4 | async-start | bytes 9175040 | tf_op jit(solution)/shard_map/reduce_scatter | solution.py:1310
  317.9 62.6 %collective-permute-start.15 = (bf16[2,24,64,256]{3,2,1,0:T(8,128)(2,1)S(1)}, bf16[2,24,64,256]{3,2,1,0:T(8,128)(2,1)}, u32[]{:S(2)}, u32[]{:S(2)}) collective-permute-start(bf16[2,24,64,256]{3,2,1,0:T(8,128)(2,1)S(1)} %pad_maximum_fusion.3), channel_id=1, source_target_pairs={{0,1},{1,0},{2,3},{3,2},{4,5},{5,4},{6,7},{7,6},{8,9},{9,8},{10,11... | collective-permute-start | bytes 4718600 | tf_op jit(solution)/shard_map/ppermute | solution.py:1328
  385.3 20.1 %collective-permute-start.16 = (bf16[26,64,256]{2,1,0:T(8,128)(2,1)}, bf16[26,64,256]{2,1,0:T(8,128)(2,1)}, u32[]{:S(2)}, u32[]{:S(2)}) collective-permute-start(bf16[26,64,256]{2,1,0:T(8,128)(2,1)} %pad_maximum_fusion.13), channel_id=1, source_target_pairs={{0,4},{4,0},{8,12},{12,8},{16,20},{20,16},{24,28},{28,24},{1,5},{5... | collective-permute-start | bytes 2555912 | tf_op jit(solution)/shard_map/ppermute | solution.py:1338
  424.1 26.3 %collective-permute-start.17 = (bf16[26,64,256]{2,1,0:T(8,128)(2,1)}, bf16[26,64,256]{2,1,0:T(8,128)(2,1)}, u32[]{:S(2)}, u32[]{:S(2)}) collective-permute-start(bf16[26,64,256]{2,1,0:T(8,128)(2,1)} %pad_maximum_fusion.14), channel_id=1, source_target_pairs={{0,4},{4,0},{8,12},{12,8},{16,20},{20,16},{24,28},{28,24},{1,5},{5... | collective-permute-start | bytes 2555912 | tf_op jit(solution)/shard_map/ppermute | solution.py:1338
  426.1 24.3 %collective-permute-start.18 = (bf16[26,64,256]{2,1,0:T(8,128)(2,1)S(1)}, bf16[26,64,256]{2,1,0:T(8,128)(2,1)S(1)}, u32[]{:S(2)}, u32[]{:S(2)}) collective-permute-start(bf16[26,64,256]{2,1,0:T(8,128)(2,1)S(1)} %add_convert_fusion.37), channel_id=1, source_target_pairs={{24,16},{28,20},{0,8},{4,12},{25,17},{29,21},{1,9},{5,13},{26,18},... | collective-permute-start | bytes 2555912 | tf_op jit(solution)/shard_map/ppermute | solution.py:1192
  451.6 20.6 %collective-permute-start.20 = (bf16[26,64,256]{2,1,0:T(8,128)(2,1)}, bf16[26,64,256]{2,1,0:T(8,128)(2,1)}, u32[]{:S(2)}, u32[]{:S(2)}) collective-permute-start(bf16[26,64,256]{2,1,0:T(8,128)(2,1)} %add_convert_fusion.35), channel_id=1, source_target_pairs={{16,8},{20,12},{17,9},{21,13},{18,10},{22,14},{19,11},{23,15}} | collective-permute-start | bytes 2555912 | tf_op jit(solution)/shard_map/ppermute | solution.py:1192
  455.3 22.8 %collective-permute-start.19 = (bf16[26,64,256]{2,1,0:T(8,128)(2,1)}, bf16[26,64,256]{2,1,0:T(8,128)(2,1)}, u32[]{:S(2)}, u32[]{:S(2)}) collective-permute-start(bf16[26,64,256]{2,1,0:T(8,128)(2,1)} %add_convert_fusion.36), channel_id=1, source_target_pairs={{24,16},{28,20},{0,8},{4,12},{25,17},{29,21},{1,9},{5,13},{26,18},... | collective-permute-start | bytes 2555912 | tf_op jit(solution)/shard_map/ppermute | solution.py:1192
  485.5 31.6 %collective-permute-start.24 = (bf16[80,64,256]{2,1,0:T(8,128)(2,1)}, bf16[80,64,256]{2,1,0:T(8,128)(2,1)}, u32[]{:S(2)}, u32[]{:S(2)}) collective-permute-start(bf16[80,64,256]{2,1,0:T(8,128)(2,1)} %fusion.1), channel_id=1, source_target_pairs={{0,1},{1,0},{2,3},{3,2},{4,5},{5,4},{6,7},{7,6},{8,9},{9,8},{10,11... | collective-permute-start | bytes 7864328 | tf_op jit(solution)/shard_map/ppermute | solution.py:1326
  487.8 29.4 %collective-permute-start.23 = (bf16[80,64,256]{2,1,0:T(8,128)(2,1)}, bf16[80,64,256]{2,1,0:T(8,128)(2,1)}, u32[]{:S(2)}, u32[]{:S(2)}) collective-permute-start(bf16[80,64,256]{2,1,0:T(8,128)(2,1)} %constant_dynamic-slice_fusion), channel_id=1, source_target_pairs={{0,1},{1,0},{2,3},{3,2},{4,5},{5,4},{6,7},{7,6},{8,9},{9,8},{10,11... | collective-permute-start | bytes 7864328 | tf_op jit(solution)/shard_map/ppermute | solution.py:1326
  492.2 15.2 %collective-permute-start.25 = (bf16[2,24,64,256]{3,2,1,0:T(8,128)(2,1)}, bf16[2,24,64,256]{3,2,1,0:T(8,128)(2,1)}, u32[]{:S(2)}, u32[]{:S(2)}) collective-permute-start(bf16[2,24,64,256]{3,2,1,0:T(8,128)(2,1)} %pad_maximum_fusion.4), channel_id=1, source_target_pairs={{0,1},{1,0},{2,3},{3,2},{4,5},{5,4},{6,7},{7,6},{8,9},{9,8},{10,11... | collective-permute-start | bytes 4718600 | tf_op jit(solution)/shard_map/ppermute | solution.py:1328
  494.6 22.6 %collective-permute-start.26 = (bf16[26,64,256]{2,1,0:T(8,128)(2,1)S(1)}, bf16[26,64,256]{2,1,0:T(8,128)(2,1)S(1)}, u32[]{:S(2)}, u32[]{:S(2)}) collective-permute-start(bf16[26,64,256]{2,1,0:T(8,128)(2,1)S(1)} %add_convert_fusion.34), channel_id=1, source_target_pairs={{16,8},{20,12},{17,9},{21,13},{18,10},{22,14},{19,11},{23,15}} | collective-permute-start | bytes 2555912 | tf_op jit(solution)/shard_map/ppermute | solution.py:1192
  499.8 8.1 collective-permute-start.27
  507.5 32.1 %collective-permute-start.22 = (bf16[80,64,256]{2,1,0:T(8,128)(2,1)}, bf16[80,64,256]{2,1,0:T(8,128)(2,1)}, u32[]{:S(2)}, u32[]{:S(2)}) collective-permute-start(bf16[80,64,256]{2,1,0:T(8,128)(2,1)} %constant_dynamic-slice_fusion.1), channel_id=1, source_target_pairs={{0,1},{1,0},{2,3},{3,2},{4,5},{5,4},{6,7},{7,6},{8,9},{9,8},{10,11... | collective-permute-start | bytes 7864328 | tf_op jit(solution)/shard_map/ppermute | solution.py:1326
  507.9 31.7 %collective-permute-start.21 = (bf16[80,64,256]{2,1,0:T(8,128)(2,1)}, bf16[80,64,256]{2,1,0:T(8,128)(2,1)}, u32[]{:S(2)}, u32[]{:S(2)}) collective-permute-start(bf16[80,64,256]{2,1,0:T(8,128)(2,1)} %constant_dynamic-slice_fusion.2), channel_id=1, source_target_pairs={{0,1},{1,0},{2,3},{3,2},{4,5},{5,4},{6,7},{7,6},{8,9},{9,8},{10,11... | collective-permute-start | bytes 7864328 | tf_op jit(solution)/shard_map/ppermute | solution.py:1326
  527.8 26.6 %collective-permute-start.28 = (bf16[2,14,64,256]{3,2,1,0:T(8,128)(2,1)}, bf16[2,14,64,256]{3,2,1,0:T(8,128)(2,1)}, u32[]{:S(2)}, u32[]{:S(2)}) collective-permute-start(bf16[2,14,64,256]{3,2,1,0:T(8,128)(2,1)} %pad_maximum_fusion.7), channel_id=1, source_target_pairs={{0,2},{1,3},{2,0},{3,1},{4,6},{5,7},{6,4},{7,5},{8,10},{9,11},{10,... | collective-permute-start | bytes 2752520 | tf_op jit(solution)/shard_map/ppermute | solution.py:1331
  534.0 20.4 %collective-permute-start.29 = (bf16[26,64,256]{2,1,0:T(8,128)(2,1)}, bf16[26,64,256]{2,1,0:T(8,128)(2,1)}, u32[]{:S(2)}, u32[]{:S(2)}) collective-permute-start(bf16[26,64,256]{2,1,0:T(8,128)(2,1)} %pad_maximum_fusion.15), channel_id=1, source_target_pairs={{0,4},{4,0},{8,12},{12,8},{16,20},{20,16},{24,28},{28,24},{1,5},{5... | collective-permute-start | bytes 2555912 | tf_op jit(solution)/shard_map/ppermute | solution.py:1338
  568.7 23.4 %collective-permute-start.31 = (bf16[26,64,256]{2,1,0:T(8,128)(2,1)}, bf16[26,64,256]{2,1,0:T(8,128)(2,1)}, u32[]{:S(2)}, u32[]{:S(2)}) collective-permute-start(bf16[26,64,256]{2,1,0:T(8,128)(2,1)} %pad_maximum_fusion.16), channel_id=1, source_target_pairs={{0,4},{4,0},{8,12},{12,8},{16,20},{20,16},{24,28},{28,24},{1,5},{5... | collective-permute-start | bytes 2555912 | tf_op jit(solution)/shard_map/ppermute | solution.py:1338
  570.9 24.2 %collective-permute-start.30 = (bf16[2,14,64,256]{3,2,1,0:T(8,128)(2,1)}, bf16[2,14,64,256]{3,2,1,0:T(8,128)(2,1)}, u32[]{:S(2)}, u32[]{:S(2)}) collective-permute-start(bf16[2,14,64,256]{3,2,1,0:T(8,128)(2,1)} %pad_maximum_fusion.8), channel_id=1, source_target_pairs={{0,2},{1,3},{2,0},{3,1},{4,6},{5,7},{6,4},{7,5},{8,10},{9,11},{10,... | collective-permute-start | bytes 2752520 | tf_op jit(solution)/shard_map/ppermute | solution.py:1331
  574.3 20.7 %collective-permute-start.32 = (bf16[26,64,256]{2,1,0:T(8,128)(2,1)}, bf16[26,64,256]{2,1,0:T(8,128)(2,1)}, u32[]{:S(2)}, u32[]{:S(2)}) collective-permute-start(bf16[26,64,256]{2,1,0:T(8,128)(2,1)} %add_convert_fusion.31), channel_id=1, source_target_pairs={{0,8},{4,12},{1,9},{5,13},{2,10},{6,14},{3,11},{7,15}} | collective-permute-start | bytes 2555912 | tf_op jit(solution)/shard_map/ppermute | solution.py:1192
  575.6 16.5 %collective-permute-start.33 = (f32[2,5376]{1,0:T(2,128)}, f32[2,5376]{1,0:T(2,128)S(1)}, u32[]{:S(2)}, u32[]{:S(2)}) collective-permute-start(f32[2,5376]{1,0:T(2,128)} %add.567), channel_id=1, source_target_pairs={{0,2},{1,3},{2,0},{3,1},{4,6},{5,7},{6,4},{7,5},{8,10},{9,11},{10,... | collective-permute-start | bytes 129032 | tf_op jit(solution)/shard_map/ppermute | solution.py:1350
  605.2 22.2 %collective-permute-start.36 = (bf16[26,64,256]{2,1,0:T(8,128)(2,1)}, bf16[26,64,256]{2,1,0:T(8,128)(2,1)}, u32[]{:S(2)}, u32[]{:S(2)}) collective-permute-start(bf16[26,64,256]{2,1,0:T(8,128)(2,1)} %add_convert_fusion.30), channel_id=1, source_target_pairs={{8,16},{12,20},{9,17},{13,21},{10,18},{14,22},{11,19},{15,23}} | collective-permute-start | bytes 2555912 | tf_op jit(solution)/shard_map/ppermute | solution.py:1192
  608.6 18.8 %collective-permute-start.35 = (bf16[26,64,256]{2,1,0:T(8,128)(2,1)}, bf16[26,64,256]{2,1,0:T(8,128)(2,1)}, u32[]{:S(2)}, u32[]{:S(2)}) collective-permute-start(bf16[26,64,256]{2,1,0:T(8,128)(2,1)} %pad_maximum_fusion.17), channel_id=1, source_target_pairs={{0,4},{4,0},{8,12},{12,8},{16,20},{20,16},{24,28},{28,24},{1,5},{5... | collective-permute-start | bytes 2555912 | tf_op jit(solution)/shard_map/ppermute | solution.py:1338
  609.6 18.8 %collective-permute-start.34 = (bf16[2,14,64,256]{3,2,1,0:T(8,128)(2,1)}, bf16[2,14,64,256]{3,2,1,0:T(8,128)(2,1)}, u32[]{:S(2)}, u32[]{:S(2)}) collective-permute-start(bf16[2,14,64,256]{3,2,1,0:T(8,128)(2,1)} %pad_maximum_fusion.9), channel_id=1, source_target_pairs={{0,2},{1,3},{2,0},{3,1},{4,6},{5,7},{6,4},{7,5},{8,10},{9,11},{10,... | collective-permute-start | bytes 2752520 | tf_op jit(solution)/shard_map/ppermute | solution.py:1331
  612.8 14.6 %collective-permute-start.37 = (bf16[26,64,256]{2,1,0:T(8,128)(2,1)}, bf16[26,64,256]{2,1,0:T(8,128)(2,1)}, u32[]{:S(2)}, u32[]{:S(2)}) collective-permute-start(bf16[26,64,256]{2,1,0:T(8,128)(2,1)} %add_convert_fusion.29), channel_id=1, source_target_pairs={{24,16},{28,20},{25,17},{29,21},{26,18},{30,22},{27,19},{31,23}} | collective-permute-start | bytes 2555912 | tf_op jit(solution)/shard_map/ppermute | solution.py:1192
  615.6 11.9 %collective-permute-start.38 = (f32[2,5376]{1,0:T(2,128)S(1)}, f32[2,5376]{1,0:T(2,128)S(1)}, u32[]{:S(2)}, u32[]{:S(2)}) collective-permute-start(f32[2,5376]{1,0:T(2,128)S(1)} %add.581), channel_id=1, source_target_pairs={{0,4},{4,0},{8,12},{12,8},{16,20},{20,16},{24,28},{28,24},{1,5},{5... | collective-permute-start | bytes 129032 | tf_op jit(solution)/shard_map/ppermute | solution.py:1350
  633.5 18.0 %collective-permute-start.42 = (bf16[26,64,256]{2,1,0:T(8,128)(2,1)S(1)}, bf16[26,64,256]{2,1,0:T(8,128)(2,1)S(1)}, u32[]{:S(2)}, u32[]{:S(2)}) collective-permute-start(bf16[26,64,256]{2,1,0:T(8,128)(2,1)S(1)} %add_convert_fusion.27), channel_id=1, source_target_pairs={{16,8},{20,12},{17,9},{21,13},{18,10},{22,14},{19,11},{23,15}} | collective-permute-start | bytes 2555912 | tf_op jit(solution)/shard_map/ppermute | solution.py:1192
  634.8 16.7 %collective-permute-start.40 = (bf16[26,64,256]{2,1,0:T(8,128)(2,1)S(1)}, bf16[26,64,256]{2,1,0:T(8,128)(2,1)S(1)}, u32[]{:S(2)}, u32[]{:S(2)}) collective-permute-start(bf16[26,64,256]{2,1,0:T(8,128)(2,1)S(1)} %pad_maximum_fusion.18), channel_id=1, source_target_pairs={{0,4},{4,0},{8,12},{12,8},{16,20},{20,16},{24,28},{28,24},{1,5},{5... | collective-permute-start | bytes 2555912 | tf_op jit(solution)/shard_map/ppermute | solution.py:1338
  638.1 18.0 %collective-permute-start.43 = (bf16[26,64,256]{2,1,0:T(8,128)(2,1)S(1)}, bf16[26,64,256]{2,1,0:T(8,128)(2,1)S(1)}, u32[]{:S(2)}, u32[]{:S(2)}) collective-permute-start(bf16[26,64,256]{2,1,0:T(8,128)(2,1)S(1)} %add_convert_fusion.26), channel_id=1, source_target_pairs={{0,8},{4,12},{24,16},{28,20},{1,9},{5,13},{25,17},{29,21},{2,10},{... | collective-permute-start | bytes 2555912 | tf_op jit(solution)/shard_map/ppermute | solution.py:1192
  639.5 17.6 %collective-permute-start.39 = (bf16[2,14,64,256]{3,2,1,0:T(8,128)(2,1)S(1)}, bf16[2,14,64,256]{3,2,1,0:T(8,128)(2,1)S(1)}, u32[]{:S(2)}, u32[]{:S(2)}) collective-permute-start(bf16[2,14,64,256]{3,2,1,0:T(8,128)(2,1)S(1)} %pad_maximum_fusion.10), channel_id=1, source_target_pairs={{0,2},{1,3},{2,0},{3,1},{4,6},{5,7},{6,4},{7,5},{8,10},{9,11},{10,... | collective-permute-start | bytes 2752520 | tf_op jit(solution)/shard_map/ppermute | solution.py:1331
  641.2 14.8 %collective-permute-start.41 = (bf16[26,64,256]{2,1,0:T(8,128)(2,1)S(1)}, bf16[26,64,256]{2,1,0:T(8,128)(2,1)S(1)}, u32[]{:S(2)}, u32[]{:S(2)}) collective-permute-start(bf16[26,64,256]{2,1,0:T(8,128)(2,1)S(1)} %add_convert_fusion.28), channel_id=1, source_target_pairs={{16,24},{20,28},{17,25},{21,29},{18,26},{22,30},{19,27},{23,31}} | collective-permute-start | bytes 2555912 | tf_op jit(solution)/shard_map/ppermute | solution.py:1192
  657.1 15.3 %collective-permute-start.48 = (f32[2,5376]{1,0:T(2,128)S(1)}, f32[2,5376]{1,0:T(2,128)S(1)}, u32[]{:S(2)}, u32[]{:S(2)}) collective-permute-start(f32[2,5376]{1,0:T(2,128)S(1)} %add.588), channel_id=1, source_target_pairs={{0,8},{4,12},{8,0},{12,4},{16,24},{20,28},{24,16},{28,20},{1,9},{5... | collective-permute-start | bytes 129032 | tf_op jit(solution)/shard_map/ppermute | solution.py:1350
  660.5 16.7 %collective-permute-start.47 = (bf16[26,64,256]{2,1,0:T(8,128)(2,1)S(1)}, bf16[26,64,256]{2,1,0:T(8,128)(2,1)S(1)}, u32[]{:S(2)}, u32[]{:S(2)}) collective-permute-start(bf16[26,64,256]{2,1,0:T(8,128)(2,1)S(1)} %add_convert_fusion.23), channel_id=1, source_target_pairs={{8,16},{12,20},{9,17},{13,21},{10,18},{14,22},{11,19},{15,23}} | collective-permute-start | bytes 2555912 | tf_op jit(solution)/shard_map/ppermute | solution.py:1192
  666.3 12.5 %collective-permute-start.46 = (bf16[26,64,256]{2,1,0:T(8,128)(2,1)S(1)}, bf16[26,64,256]{2,1,0:T(8,128)(2,1)S(1)}, u32[]{:S(2)}, u32[]{:S(2)}) collective-permute-start(bf16[26,64,256]{2,1,0:T(8,128)(2,1)S(1)} %add_convert_fusion.24), channel_id=1, source_target_pairs={{8,0},{12,4},{9,1},{13,5},{10,2},{14,6},{11,3},{15,7}} | collective-permute-start | bytes 2555912 | tf_op jit(solution)/shard_map/ppermute | solution.py:1192
  667.8 13.2 %collective-permute-start.44 = (bf16[26,64,256]{2,1,0:T(8,128)(2,1)S(1)}, bf16[26,64,256]{2,1,0:T(8,128)(2,1)S(1)}, u32[]{:S(2)}, u32[]{:S(2)}) collective-permute-start(bf16[26,64,256]{2,1,0:T(8,128)(2,1)S(1)} %pad_maximum_fusion.19), channel_id=1, source_target_pairs={{0,4},{4,0},{8,12},{12,8},{16,20},{20,16},{24,28},{28,24},{1,5},{5... | collective-permute-start | bytes 2555912 | tf_op jit(solution)/shard_map/ppermute | solution.py:1338
  669.2 15.0 %collective-permute-start.45 = (bf16[26,64,256]{2,1,0:T(8,128)(2,1)S(1)}, bf16[26,64,256]{2,1,0:T(8,128)(2,1)S(1)}, u32[]{:S(2)}, u32[]{:S(2)}) collective-permute-start(bf16[26,64,256]{2,1,0:T(8,128)(2,1)S(1)} %add_convert_fusion.25), channel_id=1, source_target_pairs={{0,8},{4,12},{1,9},{5,13},{2,10},{6,14},{3,11},{7,15}} | collective-permute-start | bytes 2555912 | tf_op jit(solution)/shard_map/ppermute | solution.py:1192
  684.7 13.1 %collective-permute-start.51 = (bf16[26,64,256]{2,1,0:T(8,128)(2,1)S(1)}, bf16[26,64,256]{2,1,0:T(8,128)(2,1)S(1)}, u32[]{:S(2)}, u32[]{:S(2)}) collective-permute-start(bf16[26,64,256]{2,1,0:T(8,128)(2,1)S(1)} %add_convert_fusion.19), channel_id=1, source_target_pairs={{8,16},{12,20},{9,17},{13,21},{10,18},{14,22},{11,19},{15,23}} | collective-permute-start | bytes 2555912 | tf_op jit(solution)/shard_map/ppermute | solution.py:1192
  686.5 11.3 %collective-permute-start.52 = (bf16[26,64,256]{2,1,0:T(8,128)(2,1)S(1)}, bf16[26,64,256]{2,1,0:T(8,128)(2,1)S(1)}, u32[]{:S(2)}, u32[]{:S(2)}) collective-permute-start(bf16[26,64,256]{2,1,0:T(8,128)(2,1)S(1)} %add_convert_fusion.18), channel_id=1, source_target_pairs={{24,16},{28,20},{25,17},{29,21},{26,18},{30,22},{27,19},{31,23}} | collective-permute-start | bytes 2555912 | tf_op jit(solution)/shard_map/ppermute | solution.py:1192
  687.3 11.6 %collective-permute-start.50 = (bf16[26,64,256]{2,1,0:T(8,128)(2,1)S(1)}, bf16[26,64,256]{2,1,0:T(8,128)(2,1)S(1)}, u32[]{:S(2)}, u32[]{:S(2)}) collective-permute-start(bf16[26,64,256]{2,1,0:T(8,128)(2,1)S(1)} %pad_maximum_fusion.20), channel_id=1, source_target_pairs={{0,4},{4,0},{8,12},{12,8},{16,20},{20,16},{24,28},{28,24},{1,5},{5... | collective-permute-start | bytes 2555912 | tf_op jit(solution)/shard_map/ppermute | solution.py:1338
  688.5 12.2 %collective-permute-start.49 = (bf16[26,64,256]{2,1,0:T(8,128)(2,1)S(1)}, bf16[26,64,256]{2,1,0:T(8,128)(2,1)S(1)}, u32[]{:S(2)}, u32[]{:S(2)}) collective-permute-start(bf16[26,64,256]{2,1,0:T(8,128)(2,1)S(1)} %select_select_fusion.1), channel_id=1, source_target_pairs={{0,2},{1,3},{2,0},{3,1},{4,6},{5,7},{6,4},{7,5},{8,10},{9,11},{10,... | collective-permute-start | bytes 2555912 | tf_op jit(solution)/shard_map/ppermute | solution.py:1345
  690.3 7.5 collective-permute-start.53
  701.3 13.9 %collective-permute-start.56 = (bf16[26,64,256]{2,1,0:T(8,128)(2,1)S(1)}, bf16[26,64,256]{2,1,0:T(8,128)(2,1)S(1)}, u32[]{:S(2)}, u32[]{:S(2)}) collective-permute-start(bf16[26,64,256]{2,1,0:T(8,128)(2,1)S(1)} %add_convert_fusion.16), channel_id=1, source_target_pairs={{16,8},{20,12},{17,9},{21,13},{18,10},{22,14},{19,11},{23,15}} | collective-permute-start | bytes 2555912 | tf_op jit(solution)/shard_map/ppermute | solution.py:1192
  702.7 33.5 %collective-permute-start.54 = (bf16[40,64,256]{2,1,0:T(8,128)(2,1)S(1)}, bf16[40,64,256]{2,1,0:T(8,128)(2,1)S(1)}, u32[]{:S(2)}, u32[]{:S(2)}) collective-permute-start(bf16[40,64,256]{2,1,0:T(8,128)(2,1)S(1)} %pad_maximum_fusion.5), channel_id=1, source_target_pairs={{0,1},{1,0},{2,3},{3,2},{4,5},{5,4},{6,7},{7,6},{8,9},{9,8},{10,11... | collective-permute-start | bytes 3932168 | tf_op jit(solution)/shard_map/ppermute | solution.py:1347
  712.8 22.5 %collective-permute-start.57 = (bf16[26,64,256]{2,1,0:T(8,128)(2,1)S(1)}, bf16[26,64,256]{2,1,0:T(8,128)(2,1)S(1)}, u32[]{:S(2)}, u32[]{:S(2)}) collective-permute-start(bf16[26,64,256]{2,1,0:T(8,128)(2,1)S(1)} %add_convert_fusion.15), channel_id=1, source_target_pairs={{0,8},{4,12},{24,16},{28,20},{1,9},{5,13},{25,17},{29,21},{2,10},{... | collective-permute-start | bytes 2555912 | tf_op jit(solution)/shard_map/ppermute | solution.py:1192
  714.4 20.9 %collective-permute-start.55 = (bf16[26,64,256]{2,1,0:T(8,128)(2,1)S(1)}, bf16[26,64,256]{2,1,0:T(8,128)(2,1)S(1)}, u32[]{:S(2)}, u32[]{:S(2)}) collective-permute-start(bf16[26,64,256]{2,1,0:T(8,128)(2,1)S(1)} %add_convert_fusion.17), channel_id=1, source_target_pairs={{16,24},{20,28},{17,25},{21,29},{18,26},{22,30},{19,27},{23,31}} | collective-permute-start | bytes 2555912 | tf_op jit(solution)/shard_map/ppermute | solution.py:1192
  737.6 34.6 %collective-permute-start.59 = (bf16[26,64,256]{2,1,0:T(8,128)(2,1)}, bf16[26,64,256]{2,1,0:T(8,128)(2,1)}, u32[]{:S(2)}, u32[]{:S(2)}) collective-permute-start(bf16[26,64,256]{2,1,0:T(8,128)(2,1)} %add_convert_fusion.13), channel_id=1, source_target_pairs={{8,16},{12,20},{9,17},{13,21},{10,18},{14,22},{11,19},{15,23}} | collective-permute-start | bytes 2555912 | tf_op jit(solution)/shard_map/ppermute | solution.py:1192
  745.2 26.9 %collective-permute-start.58 = (bf16[26,64,256]{2,1,0:T(8,128)(2,1)}, bf16[26,64,256]{2,1,0:T(8,128)(2,1)}, u32[]{:S(2)}, u32[]{:S(2)}) collective-permute-start(bf16[26,64,256]{2,1,0:T(8,128)(2,1)} %add_convert_fusion.14), channel_id=1, source_target_pairs={{8,0},{12,4},{9,1},{13,5},{10,2},{14,6},{11,3},{15,7}} | collective-permute-start | bytes 2555912 | tf_op jit(solution)/shard_map/ppermute | solution.py:1192
  775.8 23.2 %collective-permute-start.60 = (bf16[26,64,256]{2,1,0:T(8,128)(2,1)S(1)}, bf16[26,64,256]{2,1,0:T(8,128)(2,1)S(1)}, u32[]{:S(2)}, u32[]{:S(2)}) collective-permute-start(bf16[26,64,256]{2,1,0:T(8,128)(2,1)S(1)} %select_select_fusion), channel_id=1, source_target_pairs={{0,2},{1,3},{2,0},{3,1},{4,6},{5,7},{6,4},{7,5},{8,10},{9,11},{10,... | collective-permute-start | bytes 2555912 | tf_op jit(solution)/shard_map/ppermute | solution.py:1345
  (64 other events, 731.5 us)
Sparse Core Ops, SparseCore 0:
  18.0 219.1 all-gather.1
  315.4 65.1 reduce-scatter.2
  423.1 66.2 reduce-scatter.4

commit v3 on v2

--- a/solution.py
+++ b/solution.py
@@ -521,9 +521,9 @@
 FAR = 46
 G_HALF = 24
 G_LONE = 6
-R_HALF = 80
-R_STEP = 78
 R_LONE = 28
+R_BOTH = 24
+R_HALF = 2 * R_LONE + R_BOTH
 CHUNKS = 2
 SWAP_CORE = [(i, i ^ 1) for i in range(4)]
 SWAP_Y = [(i, i ^ 2) for i in range(4)]
@@ -572,41 +572,54 @@
     return jnp.where(row == 2 * (column % 32) + column // 32, 1.0, 0.0).astype(BF16)
 
 
-def prep_rows(pairs_ref, x_ref, o_ref):
+def prep_rows(number, pairs_ref, x_any, o_ref, rows_in, sems):
+    def fetch(i):
+        rows = pl.ds(pl.multiple_of(pairs_ref[i] * 256, 256), 256)
+        return pltpu.make_async_copy(x_any.at[rows], rows_in.at[i], sems.at[i])
+
+    for i in range(number):
+        fetch(i).start()
     low = lanes_low(32)
     order = natural_order()
-    for k in range(2):
-        for m in range(2):
-            one = spread_of(x_ref, 4 * k + 2 * m)
-            two = spread_of(x_ref, 4 * k + 2 * m + 1)
-            rows = jnp.concatenate(
+
+    def step(i, carry):
+        fetch(i).wait()
+        x_ref = rows_in.at[i]
+        spots = range(4)
+        one = [spread_of(x_ref, 2 * m) for m in spots]
+        two = [spread_of(x_ref, 2 * m + 1) for m in spots]
+        rows = [
+            jnp.concatenate(
                 [
-                    jnp.where(low, one, pltpu.roll(two, SUB, 1)),
-                    jnp.where(low, pltpu.roll(one, SUB, 1), two),
+                    jnp.where(low, one[m], pltpu.roll(two[m], SUB, 1)),
+                    jnp.where(low, pltpu.roll(one[m], SUB, 1), two[m]),
                 ],
                 0,
-            )
-            o_ref[k, :, m * 128 : (m + 1) * 128] = dot(order, rows.astype(BF16)).astype(BF16)
+            ).astype(BF16)
+            for m in spots
+        ]
+        made = [dot(order, rows[m]).astype(BF16) for m in spots]
+        for m in spots:
+            o_ref[2 * i + m // 2, :, (m % 2) * 128 : (m % 2 + 1) * 128] = made[m]
+        return carry
+
+    lax.fori_loop(0, number, step, 0, unroll=2 if number % 2 == 0 else 3)
 
 
 def prep(master_blocks, pairs):
     number = pairs.shape[0]
     return pl.pallas_call(
-        prep_rows,
-        grid_spec=pltpu.PrefetchScalarGridSpec(
-            num_scalar_prefetch=1,
-            grid=(number,),
-            in_specs=[pl.BlockSpec((256, 128), lambda i, which: (which[i], 0))],
-            out_specs=pl.BlockSpec((2, SUB, WIDE), lambda i, which: (i, 0, 0)),
-        ),
+        functools.partial(prep_rows, number),
+        in_specs=[pl.BlockSpec(memory_space=pltpu.SMEM), pl.BlockSpec(memory_space=pl.ANY)],
+        out_specs=pl.BlockSpec(memory_space=pltpu.VMEM),
         out_shape=jax.ShapeDtypeStruct((number * 2, SUB, WIDE), BF16),
+        scratch_shapes=[pltpu.VMEM((number, 256, 128), F32), pltpu.SemaphoreType.DMA((number,))],
         compiler_params=params(),
         cost_estimate=cost(0.4 * number),
     )(pairs, linear(master_blocks))
 
 
-def renew_body(which_ref, g_ref, m_ref, sl_ref, sr_ref, rl_ref, rr_ref, *refs):
-    go_ref, lo_ref, ro_ref, mo_ref, place = refs[-5:]
+def renew_eight(g_ref, m_ref, sl_ref, sr_ref, rl_ref, rr_ref, go_ref, lo_ref, ro_ref, mo_ref, place):
     low = lanes_low(SUB)
     low_half = lanes_low(32)
     nothing = jnp.zeros((SUB, 128), F32)
@@ -654,22 +667,84 @@
             mo_ref[at, :] = m_ref[at, :] - WEIGHT_RATE * made[3][i]
 
 
+SLOTS = 4
+
+
+def renew_body(steps, which_ref, g_any, *refs):
+    ins = refs[:5]
+    outs = refs[-9:-5]
+    gbuf, inbuf, outbuf, place, sems = refs[-5:]
+
+    def rows(i):
+        return pl.ds(pl.multiple_of(which_ref[i] * 256, 256), 256)
+
+    def fetch(i):
+        slot = lax.rem(i, SLOTS)
+        copies = [pltpu.make_async_copy(g_any.at[pl.ds(2 * i, 2)], gbuf.at[slot], sems.at[slot, 0])]
+        for k, ref in enumerate(ins):
+            copies.append(
+                pltpu.make_async_copy(ref.at[rows(i)], inbuf.at[slot, k], sems.at[slot, 1 + k])
+            )
+        return copies
+
+    def put(i):
+        slot = lax.rem(i, SLOTS)
+        return [
+            pltpu.make_async_copy(outbuf.at[slot, k], ref.at[rows(i)], sems.at[slot, 6 + k])
+            for k, ref in enumerate(outs)
+        ]
+
+    def start(copies):
+        for copy in copies:
+            copy.start()
+
+    def wait(copies):
+        for copy in copies:
+            copy.wait()
+
+    for i in range(min(SLOTS, steps)):
+        start(fetch(i))
+
+    def step(i, carry):
+        slot = lax.rem(i, SLOTS)
+        wait(fetch(i))
+
+        @pl.when(i >= SLOTS)
+        def _():
+            wait(put(i - SLOTS))
+
+        renew_eight(
+            gbuf.at[slot], *(inbuf.at[slot, k] for k in range(5)), *(outbuf.at[slot, k] for k in range(4)), place
+        )
+        start(put(i))
+
+        @pl.when(i + SLOTS < steps)
+        def _():
+            start(fetch(i + SLOTS))
+
+        return carry
+
+    lax.fori_loop(0, steps, step, 0)
+    for i in range(max(0, steps - SLOTS), steps):
+        wait(put(i))
+
+
 def renew(which, owned, master_blocks, stat_left, stat_right, root_left, root_right, before):
     steps = which.shape[0]
-    flat = pl.BlockSpec((256, 128), lambda i, which: (which[i], 0))
     shape = jax.ShapeDtypeStruct((master_blocks.shape[0] * 32, 128), F32)
+    anywhere = pl.BlockSpec(memory_space=pl.ANY)
     made = pl.pallas_call(
-        renew_body,
-        grid_spec=pltpu.PrefetchScalarGridSpec(
-            num_scalar_prefetch=1,
-            grid=(steps,),
-            in_specs=[pl.BlockSpec((2, SUB, WIDE), lambda i, which: (i, 0, 0))]
-            + [flat] * 5
-            + [pl.BlockSpec(memory_space=pl.ANY)] * len(before),
-            out_specs=[flat] * 4,
-            scratch_shapes=[pltpu.VMEM((4, 6, SUB, 128), F32)],
-        ),
+        functools.partial(renew_body, steps),
+        in_specs=[pl.BlockSpec(memory_space=pltpu.SMEM)] + [anywhere] * (6 + len(before)),
+        out_specs=[anywhere] * 4,
         out_shape=[shape] * 4,
+        scratch_shapes=[
+            pltpu.VMEM((SLOTS, 2, SUB, WIDE), BF16),
+            pltpu.VMEM((SLOTS, 5, 256, 128), F32),
+            pltpu.VMEM((SLOTS, 4, 256, 128), F32),
+            pltpu.VMEM((4, 6, SUB, 128), F32),
+            pltpu.SemaphoreType.DMA((SLOTS, 10)),
+        ],
         input_output_aliases={7 + i: i for i in range(len(before))},
         compiler_params=params(),
         cost_estimate=cost(0.7 * steps),
@@ -707,16 +782,21 @@
     return pl.ds(pl.multiple_of(i * WIDE, WIDE), WIDE)
 
 
-def softmax_of(query, keys, scale, limit):
-    scores = dot(query, keys, NT) * scale
-    column = lax.broadcasted_iota(jnp.int32, scores.shape, 1)
-    scores = jnp.where(column < limit, scores, MASK_FILL)
-    raised = jnp.exp(scores - jnp.max(scores, 1, keepdims=True))
-    return raised / jnp.sum(raised, 1, keepdims=True)
-
-
-def score_grad(probs, dprobs):
-    return (probs * (dprobs - jnp.sum(probs * dprobs, 1, keepdims=True))).astype(BF16)
+def softmax_all(products, scale, limits):
+    scores = []
+    for product, limit in zip(products, limits):
+        column = lax.broadcasted_iota(jnp.int32, product.shape, 1)
+        scores.append(jnp.where(column < limit, product * scale, MASK_FILL))
+    tops = [jnp.max(score, 1, keepdims=True) for score in scores]
+    raised = [jnp.exp(score - top) for score, top in zip(scores, tops)]
+    shares = [1.0 / jnp.sum(value, 1, keepdims=True) for value in raised]
+    return [value * share for value, share in zip(raised, shares)]
+
+
+def score_grads(probs, dprobs):
+    weighted = [p * d for p, d in zip(probs, dprobs)]
+    totals = [jnp.sum(value, 1, keepdims=True) for value in weighted]
+    return [(value - p * total).astype(BF16) for value, p, total in zip(weighted, probs, totals)]
 
 
 def at128(i):
@@ -780,15 +860,18 @@
     scale = HEAD ** (-0.5)
     reg = len_ref[2]
     heads = BI // HEAD
+    vis = [slice(pair * VIS_PAD, (pair + 1) * VIS_PAD) for pair in range(2)]
+    text = [slice(pair * 128, (pair + 1) * 128) for pair in range(2)]
+    limits = [len_ref[0], len_ref[1], reg, reg]
+
     def head(j, carry):
+        qv, kv, vv = ([cv_ref[rows, at128(j + heads * s)] for rows in vis] for s in range(3))
+        qt, kt, vt = ([ct_ref[rows, at128(j + heads * s)] for rows in text] for s in range(3))
+        probs = softmax_all([dot(q, k, NT) for q, k in zip(qv + qt, kt + kv)], scale, limits)
+        found = [dot(p.astype(BF16), v).astype(BF16) for p, v in zip(probs, vt + vv)]
         for pair in range(2):
-            vis = slice(pair * VIS_PAD, (pair + 1) * VIS_PAD)
-            text = slice(pair * 128, (pair + 1) * 128)
-            live = len_ref[pair]
-            qv, kv, vv = (cv_ref[vis, at128(j + heads * s)] for s in range(3))
-            qt, kt, vt = (ct_ref[text, at128(j + heads * s)] for s in range(3))
-            fv_ref[vis, at128(j)] = dot(softmax_of(qv, kt, scale, live).astype(BF16), vt).astype(BF16)
-            ft_ref[text, at128(j)] = dot(softmax_of(qt, kv, scale, reg).astype(BF16), vv).astype(BF16)
+            fv_ref[vis[pair], at128(j)] = found[pair]
+            ft_ref[text[pair], at128(j)] = found[2 + pair]
         return carry
 
     lax.fori_loop(0, heads, head, 0, unroll=2)
@@ -823,28 +906,32 @@
     scale = HEAD ** (-0.5)
     reg = len_ref[2]
     heads = BI // HEAD
+    vis = [slice(pair * VIS_PAD, (pair + 1) * VIS_PAD) for pair in range(2)]
+    text = [slice(pair * 128, (pair + 1) * 128) for pair in range(2)]
+    limits = [len_ref[0], len_ref[1], reg, reg]
+
     def head(j, carry):
+        qv, kv, vv = ([cv_ref[rows, at128(j + heads * s)] for rows in vis] for s in range(3))
+        qt, kt, vt = ([ct_ref[rows, at128(j + heads * s)] for rows in text] for s in range(3))
+        up = [dv_ref[rows, at128(j)] for rows in vis] + [dt_ref[rows, at128(j)] for rows in text]
+        queries, keys, values = qv + qt, kt + kv, vt + vv
+        products = [dot(q, k, NT) for q, k in zip(queries, keys)]
+        dprobs = [dot(u, v, NT) for u, v in zip(up, values)]
+        probs = softmax_all(products, scale, limits)
+        ds = score_grads(probs, dprobs)
+        dvalues = [dot(p.astype(BF16), u, TN).astype(BF16) for p, u in zip(probs, up)]
+        dqueries = [(dot(d, k) * scale).astype(BF16) for d, k in zip(ds, keys)]
+        dkeys = [(dot(d, q, TN) * scale).astype(BF16) for d, q in zip(ds, queries)]
         for pair in range(2):
-            vis = slice(pair * VIS_PAD, (pair + 1) * VIS_PAD)
-            text = slice(pair * 128, (pair + 1) * 128)
-            live = len_ref[pair]
-            qv, kv, vv = (cv_ref[vis, at128(j + heads * s)] for s in range(3))
-            qt, kt, vt = (ct_ref[text, at128(j + heads * s)] for s in range(3))
-            dv = dv_ref[vis, at128(j)]
-            dt = dt_ref[text, at128(j)]
-            probs = softmax_of(qv, kt, scale, live)
-            ds = score_grad(probs, dot(dv, vt, NT))
-            gv_ref[vis, at128(j)] = (dot(ds, kt) * scale).astype(BF16)
-            gt_ref[text, at128(j + heads)] = (dot(ds, qv, TN) * scale).astype(BF16)
-            gt_ref[text, at128(j + 2 * heads)] = dot(probs.astype(BF16), dv, TN).astype(BF16)
-            probs = softmax_of(qt, kv, scale, reg)
-            ds = score_grad(probs, dot(dt, vv, NT))
-            gt_ref[text, at128(j)] = (dot(ds, kv) * scale).astype(BF16)
-            gv_ref[vis, at128(j + heads)] = (dot(ds, qt, TN) * scale).astype(BF16)
-            gv_ref[vis, at128(j + 2 * heads)] = dot(probs.astype(BF16), dt, TN).astype(BF16)
+            gv_ref[vis[pair], at128(j)] = dqueries[pair]
+            gt_ref[text[pair], at128(j + heads)] = dkeys[pair]
+            gt_ref[text[pair], at128(j + 2 * heads)] = dvalues[pair]
+            gt_ref[text[pair], at128(j)] = dqueries[2 + pair]
+            gv_ref[vis[pair], at128(j + heads)] = dkeys[2 + pair]
+            gv_ref[vis[pair], at128(j + 2 * heads)] = dvalues[2 + pair]
         return carry
 
-    lax.fori_loop(0, heads, head, 0)
+    lax.fori_loop(0, heads, head, 0, unroll=2)
     for which, at, g_ref, r_ref, o_ref, copy in (
         (0, base[0], gv_ref, rv_ref, ov_ref, copies[0]),
         (6, base[1], gt_ref, rt_ref, ot_ref, copies[1]),
@@ -938,7 +1025,7 @@
     def co_out(i):
         wide[:, at256(i)] = times(ctx_ref[...], w, base[0], r, g, 0, i)
 
-    loop(g, co_out)
+    loop(g, co_out, g)
 
     def norm_one(i):
         value = norm(wide[at_chunk(i), :] + x_ref[at_chunk(i), :].astype(F32), 0, i, n1, s1)
@@ -969,7 +1056,7 @@
         act_ref[:, at256(i)] = act
         acc[...] += dot(act, down_rows(i))
 
-    loop(g_up, feed, 2)
+    loop(g_up, feed, 4)
 
     def norm_two(i):
         value = norm(wide[at_chunk(i), :] + acc[at_chunk(i), :], 1, i, n2, s2)
@@ -983,7 +1070,7 @@
     def self_in(i):
         selfs[:, at256(i)] = times(second_ref[...], w, base[3], r_s, g_s, i // g_s, i % g_s).astype(BF16)
 
-    loop(count_s * g_s, self_in, 3)
+    loop(count_s * g_s, self_in, g_s)
     scale = head ** (-0.5)
     groups = width // 128
     per = 128 // head
@@ -1002,26 +1089,27 @@
         keep = low if h == 0 else jnp.logical_not(low)
         return jnp.where(keep, value, jnp.zeros_like(value))
 
+    own = [slice(pair * span, (pair + 1) * span) for pair in range(pairs)]
+    each = [(pair, h) for pair in range(pairs) for h in range(per)]
+
     def attend(j):
+        q, k, v = ([selfs[rows_of, at128(j + groups * s)] for rows_of in own] for s in range(3))
+        products = [dot(only(q[pair], h), k[pair], NT) for pair, h in each]
+        p = softmax_all(products, scale, [len_ref[pair] for pair, _ in each])
+        found = [dot(value.astype(BF16), v[pair]) for value, (pair, _) in zip(p, each)]
+        for i, value in enumerate(p):
+            probs[j * len(each) + i] = value
         for pair in range(pairs):
-            own = slice(pair * span, (pair + 1) * span)
-            live = len_ref[pair]
-            q, k, v = (selfs[own, at128(j + groups * s)] for s in range(3))
-            found = []
-            for h in range(per):
-                p = softmax_of(only(q, h), k, scale, live)
-                probs[(pair * groups + j) * per + h] = p
-                found.append(dot(p.astype(BF16), v))
-            sctx_ref[own, at128(j)] = halves(found).astype(BF16)
-
-    loop(groups, attend)
+            sctx_ref[own[pair], at128(j)] = halves(found[pair * per : (pair + 1) * per]).astype(BF16)
+
+    loop(groups, attend, 2)
     _, r_o, g_o = shapes[4]
     arrive(copies[4])
 
     def self_out(i):
         acc[:, at256(i)] = times(sctx_ref[...], w, base[4], r_o, g_o, 0, i)
 
-    loop(g_o, self_out)
+    loop(g_o, self_out, g_o)
 
     def norm_three(i):
         value = norm(wide[at_chunk(i), :] + acc[at_chunk(i), :], 2, i, n3, s3)
@@ -1035,29 +1123,28 @@
     def self_out_back(i):
         dctx_ref[:, at256(i)] = times_back(tback_ref, w, base[4], r_o, g_o, 1, i).astype(BF16)
 
-    loop(r_o // 4, self_out_back)
+    loop(r_o // 4, self_out_back, r_o // 4)
     def attend_back(j):
+        q, k, v = ([selfs[rows_of, at128(j + groups * s)] for rows_of in own] for s in range(3))
+        up = [dctx_ref[rows_of, at128(j)] for rows_of in own]
+        p = [probs[j * len(each) + i] for i in range(len(each))]
+        dprobs = [dot(only(up[pair], h), v[pair], NT) for pair, h in each]
+        dv = [dot(value.astype(BF16), up[pair], TN) for value, (pair, _) in zip(p, each)]
+        ds = score_grads(p, dprobs)
+        dq = [dot(value, k[pair]) for value, (pair, _) in zip(ds, each)]
+        dk = [dot(value, q[pair], TN) for value, (pair, _) in zip(ds, each)]
         for pair in range(pairs):
-            own = slice(pair * span, (pair + 1) * span)
-            q, k, v = (selfs[own, at128(j + groups * s)] for s in range(3))
-            up = dctx_ref[own, at128(j)]
-            dq, dk, dv = [], [], []
-            for h in range(per):
-                p = probs[(pair * groups + j) * per + h]
-                ds = score_grad(p, dot(only(up, h), v, NT))
-                dq.append(dot(ds, k))
-                dk.append(dot(ds, q, TN))
-                dv.append(dot(p.astype(BF16), up, TN))
-            dself_ref[own, at128(j)] = (halves(dq) * scale).astype(BF16)
-            dself_ref[own, at128(j + groups)] = (halves(dk) * scale).astype(BF16)
-            dself_ref[own, at128(j + 2 * groups)] = halves(dv).astype(BF16)
-
-    loop(groups, attend_back)
+            mine = slice(pair * per, (pair + 1) * per)
+            dself_ref[own[pair], at128(j)] = (halves(dq[mine]) * scale).astype(BF16)
+            dself_ref[own[pair], at128(j + groups)] = (halves(dk[mine]) * scale).astype(BF16)
+            dself_ref[own[pair], at128(j + 2 * groups)] = halves(dv[mine]).astype(BF16)
+
+    loop(groups, attend_back, 2)
 
     def self_in_back(i):
         acc[:, at256(i)] = times_back(dself_ref, w, base[3], r_s, g_s, count_s, i)
 
-    loop(r_s // 4, self_in_back)
+    loop(r_s // 4, self_in_back, r_s // 4)
 
     def norm_two_back(i):
         value = norm_back(wide[at_chunk(i), :] + acc[at_chunk(i), :], 1, i, n2, s2)
@@ -1070,12 +1157,12 @@
         act_grad = dot(bback_ref[...], down_rows(i), NT)
         pback_ref[:, at256(i)] = (act_grad * pre[i]).astype(BF16)
 
-    loop(g_up, feed_back, 2)
+    loop(g_up, feed_back, 4)
 
     def up_back(i):
         acc[:, at256(i)] = times_back(pback_ref, w, base[1], r_up, g_up, 1, i)
 
-    loop(r_up // 4, up_back)
+    loop(r_up // 4, up_back, r_up // 4)
 
     def norm_one_back(i):
         value = norm_back(wide[at_chunk(i), :] + acc[at_chunk(i), :], 0, i, n1, s1)
@@ -1087,7 +1174,7 @@
     def co_out_back(i):
         dctx_ref[:, at256(i)] = times_back(fback_ref, w, base[0], r, g, 1, i).astype(BF16)
 
-    loop(r // 4, co_out_back)
+    loop(r // 4, co_out_back, r // 4)
     sums_ref[...] = jnp.sum(stat[...], 1)
 
 
@@ -1151,14 +1238,16 @@
             r4 = lax.rem(i, r // 4)
             across[...] = jnp.transpose(a_ref[:, at256(r4)])
             left = across[...]
-            for col in range(g):
-                made = dot(left, b_ref[:, at256(part * g + col)]).astype(BF16)
-                for a in range(4):
-                    stage[slot, a * g + col] = made[a * SUB : (a + 1) * SUB]
+            for first in range(0, g, 4 if g % 4 == 0 else 3):
+                columns = range(first, first + (4 if g % 4 == 0 else 3))
+                made = [dot(left, b_ref[:, at256(part * g + col)]).astype(BF16) for col in columns]
+                for col, value in zip(columns, made):
+                    for a in range(4):
+                        stage[slot, a * g + col] = value[a * SUB : (a + 1) * SUB]
             copy(i, slot).start()
             return carry
 
-        lax.fori_loop(0, total, step, 0)
+        lax.fori_loop(0, total, step, 0, unroll=2 if total % 2 == 0 else 3)
         for i in range(max(0, total - 4), total):
             copy(i, i % 4).wait()
         offset += count * r * g
@@ -1278,17 +1367,47 @@
     (((0, 1),), ((1, 2),), ((2, 3),)),
 )
 LONE = R_LONE // CHUNKS
-BOTH = (R_HALF - 2 * R_LONE) // CHUNKS
+BOTH = R_BOTH // CHUNKS
+GROUP_ORDER = [[0, 2, 1, 3]]
+
+
+def lone_at(core):
+    return 2 * R_LONE * core
+
+
+def both_at(core):
+    return 4 * R_LONE + (SHARD - 4 * R_LONE - R_BOTH) * core
 
 
 def chunk_pairs(k):
     table = []
     for core in range(2):
-        begin = R_STEP * core // 2
         for y in range(2):
-            table += [begin + (R_LONE * y + LONE * k) // 2 + i for i in range(LONE // 2)]
-        table += [begin + R_LONE + BOTH * k // 2 + i for i in range(BOTH // 2)]
+            table += [(lone_at(core) + R_LONE * y + LONE * k) // 2 + i for i in range(LONE // 2)]
+        table += [(both_at(core) + BOTH * k) // 2 + i for i in range(BOTH // 2)]
     return jnp.asarray(table, jnp.int32)
+
+
+def half_of(source, core):
+    array, offset = source
+    return join([cut(array, offset + lone_at(core), 2 * R_LONE), cut(array, offset + both_at(core), R_BOTH)])
+
+
+def group_lone(array, offset):
+    return lax.psum_scatter(
+        array[offset : offset + 4 * R_LONE], "seq", scatter_dimension=0, tiled=True,
+        axis_index_groups=GROUP_ORDER,
+    )
+
+
+def both_parts(array, offset, core):
+    return jnp.stack([cut(array, offset + SHARD * i + both_at(core), R_BOTH) for i in range(2)])
+
+
+def chunks_of(lone, both):
+    return [
+        (lone[:, LONE * k : LONE * (k + 1)], both[:, BOTH * k : BOTH * (k + 1)]) for k in range(CHUNKS)
+    ]
 
 
 class Sums:
@@ -1296,55 +1415,24 @@
         self.at = spot()
         self.state = {}
 
-    def group(self, zi, place):
-        pair = (2 * zi, 2 * zi + 1)
-
-        def part(o, core, begin, size):
-            array, offset = place[o]
-            begin += offset + R_STEP * core
-            return array[begin : begin + size]
-
-        lone = jnp.concatenate(
-            [part(o, core, R_LONE * y, R_LONE) for y in range(2) for core in range(2) for o in pair]
-        )
-        lone = lax.psum_scatter(lone, "seq", scatter_dimension=0, tiled=True)
-        self.state["lone", zi] = lone.reshape(2, R_LONE, SUB, WIDE)
-        self.state["both", zi] = tuple(place[o] for o in pair)
-
-    def both_of(self, zi, core):
-        size = R_HALF - 2 * R_LONE
-        return jnp.stack(
-            [cut(array, offset + R_STEP * core + 2 * R_LONE, size) for array, offset in self.state["both", zi]]
-        )
-
     def send(self, task):
         z, x, y, core = self.at
         state = self.state
         kind, who = task[0], task[1]
-        if kind == "C":
-            array, offset = state["place", who]
-            return lax.ppermute(cut(array, offset + R_STEP * (1 - core), R_HALF), "seq", SWAP_CORE)
-        if kind == "B":
-            return lax.ppermute(self.both_of(who, 1 - core), "seq", SWAP_CORE)
         if kind == "Y":
-            k = task[2]
-            return lax.ppermute(
-                jnp.stack([cut(state["half", o], R_LONE * (1 - y) + LONE * k, LONE) for o in (2 * who, 2 * who + 1)]),
-                "seq",
-                SWAP_Y,
-            )
+            return lax.ppermute(cut(state["lone", who], 1 - y, 1)[0], "seq", SWAP_Y)
         if kind == "X":
-            lone, both = state["kept", who, task[2]]
+            lone, both = state["kept", who]
             return lax.ppermute(join([cut(lone, 1 - x, 1)[0], cut(both, 1 - x, 1)[0]]), "dp", SWAP_X)
         if kind == "Z":
-            return along_z(state["value", who, task[2]], ROUTES[who][task[3]])
+            return along_z(state["value", who], ROUTES[who][task[2]])
         if kind == "F":
-            values = [state["value", zi, who] for zi in range(4)]
+            values = [state["value", zi] for zi in range(4)]
             mine = jnp.where(z == 0, values[0], jnp.where(z == 1, values[1], jnp.where(z == 2, values[2], values[3])))
-            state["mine", who] = mine
+            state["mine", 0] = mine
             return lax.ppermute(mine, "seq", SWAP_Y)
         if kind == "G":
-            return lax.ppermute(state["whole", who], "seq", SWAP_CORE)
+            return lax.ppermute(state["whole", 0], "seq", SWAP_CORE)
         axis, step = (("seq", 1), ("seq", 2), ("dp", 1), ("dp", 2), ("dp", 4))[who]
         size = lax.axis_size(axis)
         return lax.ppermute(state["norms", 0], axis, [(i, i ^ step) for i in range(size)])
@@ -1353,48 +1441,51 @@
         z, x, y, core = self.at
         state = self.state
         kind, who = task[0], task[1]
-        if kind == "C":
-            array, offset = state["place", who]
-            state["half", who] = add(cut(array, offset + R_STEP * core, R_HALF), got)
-        elif kind == "B":
-            both = add(self.both_of(who, core), got)
-            lone = state.pop(("lone", who))
-            state.pop(("both", who))
-            for k in range(CHUNKS):
-                state["kept", who, k] = (
-                    lone[:, LONE * k : LONE * (k + 1)],
-                    both[:, BOTH * k : BOTH * (k + 1)],
-                )
-        elif kind == "Y":
-            k = task[2]
-            halves = [state["half", o] for o in (2 * who, 2 * who + 1)]
-            lone = add(jnp.stack([cut(h, R_LONE * y + LONE * k, LONE) for h in halves]), got)
-            both = jnp.stack([h[2 * R_LONE + BOTH * k : 2 * R_LONE + BOTH * (k + 1)] for h in halves])
-            state["kept", who, k] = (lone, both)
+        if kind == "Y":
+            state["kept", who] = (add(cut(state.pop(("lone", who)), y, 1)[0], got), state.pop(("both", who)))
         elif kind == "X":
-            lone, both = state.pop(("kept", who, task[2]))
-            state["value", who, task[2]] = add(join([cut(lone, x, 1)[0], cut(both, x, 1)[0]]), got)
+            lone, both = state.pop(("kept", who))
+            state["value", who] = add(join([cut(lone, x, 1)[0], cut(both, x, 1)[0]]), got)
         elif kind == "Z":
-            state["value", who, task[2]] = add(state["value", who, task[2]], got)
+            state["value", who] = add(state["value", who], got)
         elif kind == "F":
-            mine = state.pop(("mine", who))
-            state["whole", who] = join(by_y(y, mine[:LONE], got[:LONE]) + [add(mine[LONE:], got[LONE:])])
+            mine = state.pop(("mine", 0))
+            state["whole", 0] = join(by_y(y, mine[:LONE], got[:LONE]) + [add(mine[LONE:], got[LONE:])])
         elif kind == "G":
-            half = state.pop(("whole", who))
-            state["owned", who] = join([jnp.where(core == 0, half, got), jnp.where(core == 0, got, half)])
+            half = state.pop(("whole", 0))
+            state["owned", 0] = join([jnp.where(core == 0, half, got), jnp.where(core == 0, got, half)])
         else:
             state["norms", 0] = state["norms", 0] + got
 
-    def step(self, tasks, beside=None):
+    def step(self, tasks):
         out = [self.send(task) for task in tasks]
-        work = beside() if beside is not None else ()
-        fixed = {key: value for key, value in self.state.items() if key[0] in ("place", "both")}
-        moving = {key: value for key, value in self.state.items() if key not in fixed}
-        out, work, moving = lax.optimization_barrier((out, work, moving))
-        self.state = {**moving, **fixed}
+        out, self.state = lax.optimization_barrier((out, self.state))
         for task, got in zip(tasks, out):
             self.take(task, got)
-        return work
+
+
+def beside(chunks, tasks, work):
+    out = [chunks[k].send(task) for k, task in tasks]
+    made = work()
+    out, made, states = lax.optimization_barrier((out, made, [chunk.state for chunk in chunks]))
+    for chunk, state in zip(chunks, states):
+        chunk.state = state
+    for (k, task), got in zip(tasks, out):
+        chunks[k].take(task, got)
+    return made
+
+
+def pair_up(halves, chunks, zi):
+    for k, chunk in enumerate(chunks):
+        chunk.state["lone", zi] = jnp.stack(
+            [
+                jnp.stack([half[R_LONE * y + LONE * k : R_LONE * y + LONE * (k + 1)] for half in halves])
+                for y in range(2)
+            ]
+        )
+        chunk.state["both", zi] = jnp.stack(
+            [half[2 * R_LONE + BOTH * k : 2 * R_LONE + BOTH * (k + 1)] for half in halves]
+        )
 
 
 def pad_regions(value, pairs):
@@ -1427,71 +1518,78 @@
         (1, 2, 3, 4, 5), (vis_ctx, v_first, v_act, v_second, v_sctx),
         (v_fback, v_pback, v_bback, v_dself, v_tback),
     )
-    sums = Sums()
-    vis_at = TILES[1][0]
-    text_at = TILES[7][0]
-    sums.group(1, {o: (vis_mid, SHARD * o - vis_at) for o in (2, 3)})
+    _, _, _, core = spot()
+    chunks = [Sums() for _ in range(CHUNKS)]
+    vis_at, text_at = TILES[1][0], TILES[7][0]
+    vis_pair, text_pair = (vis_mid, 2 * SHARD - vis_at), 6 * SHARD - text_at
+    lone = [group_lone(vis_mid, vis_pair[1] + SHARD * i) for i in range(2)]
+    far_both = lax.ppermute(both_parts(*vis_pair, 1 - core), "seq", SWAP_CORE)
     (out_text, t_first, t_act, t_second, t_sctx, t_fback, t_pback, t_bback, t_dself, t_tback,
      t_resid, t_dctx, t_sums) = middle(
         7, lengths, text_ctx, x_text, cot_text, text_norms, near, far, x_text.shape[0] // pairs, HEAD_T, 32
     )
-    sums.state["norms", 0] = jnp.concatenate([v_sums.reshape(2, -1), t_sums.reshape(2, -1)], 1)
+    chunks[0].state["norms", 0] = jnp.concatenate([v_sums.reshape(2, -1), t_sums.reshape(2, -1)], 1)
     lefts = (text_ctx, t_first, t_act, t_second, t_sctx)
     rights = (t_fback, t_pback, t_bback, t_dself, t_tback)
-    later = sums.state.pop(("lone", 1))
-    lefts, rights, later = sums.step([], lambda: (lefts, rights, later))
-    sums.state["lone", 1] = later
-    sums.step([("B", 1)])
-    text_mid, back = sums.step(
-        [("X", 1, 0)],
-        lambda: (
-            weight_grads((7, 8, 9, 10, 11), lefts, rights),
-            (co_vis, co_text, v_dctx, t_dctx, v_resid, t_resid),
-        ),
-    )
-    sums.group(3, {o: (text_mid, SHARD * o - text_at) for o in (6, 7)})
-    later = sums.state.pop(("lone", 3))
-    dco_vis, dco_text, grad_vis, grad_text = sums.step(
-        [("X", 1, 1), ("Z", 1, 0, 0)], lambda: co_backward(lengths, *back, near, far)
-    )
-    vis_co, text_co = sums.step(
-        [("Z", 1, 1, 0), ("Z", 1, 0, 1)],
+    lefts, rights, far_both = lax.optimization_barrier((lefts, rights, far_both))
+    text_mid = weight_grads((7, 8, 9, 10, 11), lefts, rights)
+    both = add(both_parts(*vis_pair, core), far_both)
+    far_both = lax.ppermute(both_parts(text_mid, text_pair, 1 - core), "seq", SWAP_CORE)
+    back = (co_vis, co_text, v_dctx, t_dctx, v_resid, t_resid)
+    back, lone, both, text_mid = lax.optimization_barrier((back, lone, both, text_mid))
+    for k, kept in enumerate(chunks_of(jnp.stack(lone), both)):
+        chunks[k].state["kept", 1] = kept
+    lone = [group_lone(text_mid, text_pair + SHARD * i) for i in range(2)]
+    dco_vis, dco_text, grad_vis, grad_text, far_both = beside(
+        chunks,
+        [(0, ("X", 1)), (0, ("N", 0))],
+        lambda: (*co_backward(lengths, *back, near, far), far_both),
+    )
+    vis_co, text_co = beside(
+        chunks,
+        [(1, ("X", 1)), (0, ("Z", 1, 0)), (0, ("N", 1))],
         lambda: (weight_grads((0,), (xv,), (dco_vis,)), weight_grads((6,), (x_text,), (dco_text,))),
     )
-    sums.state["lone", 3] = later
-    sums.state["place", 0] = (vis_co, 0)
-    sums.state["place", 1] = (jnp.concatenate([vis_co[SHARD:], vis_mid[: 2 * SHARD - vis_at]]), 0)
-    sums.state["place", 4] = (
-        jnp.concatenate([vis_mid[4 * SHARD - vis_at :], text_co, text_mid[: 5 * SHARD - text_at]]), 0
-    )
-    sums.state["place", 5] = (text_mid, 5 * SHARD - text_at)
-    for tasks in (
-        [("C", 0), ("C", 1), ("B", 3), ("Z", 1, 1, 1), ("N", 0)],
-        [("C", 4), ("C", 5), ("Y", 0, 0), ("X", 3, 0)],
-        [("Y", 2, 0), ("X", 0, 0), ("Z", 3, 0, 0), ("N", 1)],
-        [("Y", 0, 1), ("X", 2, 0), ("Z", 3, 0, 1), ("Z", 0, 0, 0), ("N", 2)],
-        [("Y", 2, 1), ("X", 3, 1), ("Z", 3, 0, 2), ("Z", 0, 0, 1), ("Z", 2, 0, 0)],
-        [("X", 0, 1), ("Z", 3, 1, 0), ("Z", 0, 0, 2), ("Z", 2, 0, 1), ("N", 3)],
-        [("F", 0), ("X", 2, 1), ("Z", 3, 1, 1), ("Z", 0, 1, 0), ("N", 4)],
-        [("G", 0), ("Z", 3, 1, 2), ("Z", 0, 1, 1), ("Z", 2, 1, 0)],
-    ):
-        sums.step(tasks)
+    both = add(both_parts(text_mid, text_pair, core), far_both)
+    place = {
+        0: (vis_co, 0),
+        1: (jnp.concatenate([vis_co[SHARD:], vis_mid[: 2 * SHARD - vis_at]]), 0),
+        4: (jnp.concatenate([vis_mid[4 * SHARD - vis_at :], text_co, text_mid[: 5 * SHARD - text_at]]), 0),
+        5: (text_mid, 5 * SHARD - text_at),
+    }
+
+    def swap_halves(tasks, owners):
+        got = beside(
+            chunks, tasks, lambda: [lax.ppermute(half_of(place[o], 1 - core), "seq", SWAP_CORE) for o in owners]
+        )
+        pair_up([add(half_of(place[o], core), part) for o, part in zip(owners, got)], chunks, owners[0] // 2)
+
+    swap_halves([(0, ("Z", 1, 1)), (1, ("Z", 1, 0)), (0, ("N", 2))], (0, 1))
+    for k, kept in enumerate(chunks_of(jnp.stack(lone), both)):
+        chunks[k].state["kept", 3] = kept
+    swap_halves([(0, ("Y", 0)), (0, ("X", 3)), (1, ("Z", 1, 1))], (4, 5))
+    beside(chunks, [(0, ("Y", 2)), (0, ("X", 0)), (0, ("Z", 3, 0)), (1, ("X", 3)), (0, ("N", 3))], lambda: ())
+    chunks[1].step([("Y", 0), ("Z", 3, 0)])
+    chunks[0].step([("X", 2), ("Z", 0, 0), ("Z", 3, 1), ("N", 4)])
+    chunks[1].step([("Y", 2), ("X", 0), ("Z", 3, 1)])
+    chunks[0].step([("Z", 0, 1), ("Z", 2, 0), ("Z", 3, 2)])
+    chunks[1].step([("X", 2), ("Z", 0, 0), ("Z", 3, 2)])
+    chunks[0].step([("Z", 0, 2), ("Z", 2, 1)])
+    chunks[1].step([("Z", 0, 1), ("Z", 2, 0)])
+    chunks[0].step([("F", 0)])
+    beside(chunks, [(0, ("G", 0)), (1, ("Z", 0, 2)), (1, ("Z", 2, 1))], lambda: ())
     statistics = (master_blocks, stat_left, stat_right, root_left, root_right)
     early = chunk_pairs(0)
-    count = early.shape[0] // 2
-    renewed = sums.step(
-        [("Z", 0, 1, 2), ("Z", 2, 1, 1)],
-        lambda: renew(early[:count], sums.state["owned", 0][: 2 * count], *statistics, ()),
-    )
-    renewed = sums.step(
-        [("F", 1)],
-        lambda: renew(early[count:], sums.state["owned", 0][2 * count :], *statistics, renewed),
-    )
-    sums.step([("G", 1)])
+    count = 3 * early.shape[0] // 4
+    owned = chunks[0].state["owned", 0]
+    renewed = beside(chunks, [(1, ("F", 0))], lambda: renew(early[:count], owned[: 2 * count], *statistics, ()))
+    renewed = beside(
+        chunks, [(1, ("G", 0))], lambda: renew(early[count:], owned[2 * count :], *statistics, renewed)
+    )
     grad_blocks, left_new, right_new, master_new = renew(
-        chunk_pairs(1), sums.state["owned", 1], *statistics, renewed
-    )
-    norm_grads = sums.state["norms", 0]
+        chunk_pairs(1), chunks[1].state["owned", 0], *statistics, renewed
+    )
+    norm_grads = chunks[0].state["norms", 0]
     second_new = STAT_DECAY * norm_second + (1.0 - STAT_DECAY) * norm_grads * norm_grads
     norm_new = norm_params - NORM_RATE * norm_grads / (jnp.sqrt(second_new) + MOMENT_EPSILON)
     return (

time: 865 us -> 753 us (0.87)
  Pallas kernels: 257 us -> 187 us
  local copies, waits for them, and re-layouts: 116 us -> 81.2 us
  other arithmetic: 92.7 us -> 79.9 us
  starting transfers between devices: 99.2 us -> 110 us
    ppermute x23, waiting for transfers between devices: 112 us -> 78.4 us  [along_z(): lax.ppermute(value, 'dp', [(2 * a + x, 2 * b + x) for a, b in moves for x...]
    unnamed x132 -> x123, local copies, waits for them, and re-layouts: 41.3 us -> 8.16 us
    pallas_call x5, Pallas kernels: 95.6 us -> 64.8 us  [the longest x3 54.7 us: renew(): pl.pallas_call(functools.partial(renew_body, steps), in_specs=[pl.BlockSp...]
    pallas_call x2, Pallas kernels: 76.9 us -> 51.5 us  [middle(): pl.pallas_call(functools.partial(middle_body, (begin, rows, span, head, c...]
    ppermute x5, waiting for transfers between devices: 32 us -> 10.8 us  [send(): lax.ppermute(state['norms', 0], axis, [(i, i ^ step) for i in range(size)])]
    reduce_scatter x2 -> x4, waiting for transfers between devices: 12.5 us -> 31.1 us  [group_lone(): lax.psum_scatter(array[offset:offset + 4 * R_LONE], 'seq', scatter_dimens...]
    ppermute x12, starting transfers between devices: 16.8 us -> 34.7 us  [the longest x2 20.2 us: send(): return lax.ppermute(state['whole', 0], 'seq', SWAP_CORE)]
    ppermute x12, waiting for transfers between devices: 3.11 us -> 20.7 us  [the longest x4 20.7 us: send(): return lax.ppermute(cut(state['lone', who], 1 - y, 1)[0], 'seq', SWAP_Y)]
  transfers between devices with their start and end apart: 65 -> 67, of which waited for: 31 -> 29; matrix products, arithmetic and copies ran while one was open for 14% -> 16% of each run, Pallas kernels for 18% -> 15%
where the time goes in v3:
time: 753 us; the launch traced here: 743 us
  waiting for transfers between devices  269 us (36%)
  Pallas kernels  187 us (25%)
  starting transfers between devices  110 us (15%)
  local copies, waits for them, and re-layouts  81.2 us (11%)
  other arithmetic  79.9 us (11%)
  between operations  16.2 us (2%)
    ppermute x23, waiting for transfers between devices, along_z(): lax.ppermute(value, 'dp', [(2 * a + x, 2 * b + x) for a, b in moves for x...  78.4 us
    pallas_call x3, Pallas kernels, renew(): pl.pallas_call(functools.partial(renew_body, steps), in_specs=[pl.BlockSp...  54.7 us
    pallas_call x2, Pallas kernels, middle(): pl.pallas_call(functools.partial(middle_body, (begin, rows, span, head, c...  51.5 us
    pallas_call x4, Pallas kernels, weight_grads(): pl.pallas_call(functools.partial(weight_body, kinds), in_specs=whole(2 *...  44.2 us
    ppermute x23, starting transfers between devices, along_z(): lax.ppermute(value, 'dp', [(2 * a + x, 2 * b + x) for a, b in moves for x...  43.9 us
    all_gather x1, waiting for transfers between devices, gather_tiles(): far = lax.all_gather(last, ('dp', 'seq'), axis=0, tiled=True)  43.7 us
    convert_element_type x36, other arithmetic, add(): return (left.astype(F32) + right.astype(F32)).astype(BF16)  40.6 us
    ppermute x4, waiting for transfers between devices, gather_tiles(): lax.ppermute(join([part[:G_LONE] for part in here]), 'seq', SWAP_Y)  39.3 us
  transfers between devices with their start and end apart: 67, of which 29 were waited for; matrix products, arithmetic and copies ran while one was open for 16% of the time, Pallas kernels for 15%

profile of v3, /device:TPU:11, one launch (start us, length us, event | category | flops | bytes accessed | tf_op | source)
XLA Modules:
  0.0 742.7 jit_solution(13053406145917171058)
XLA Ops:
  7.7 5.7 shard_map.223
  14.1 4.4 shard_map.222
  20.2 23.1 %collective-permute-done.1 = bf16[18,64,256]{2,1,0:T(8,128)(2,1)S(1)} collective-permute-done((bf16[18,64,256]{2,1,0:T(8,128)(2,1)}, bf16[18,64,256]{2,1,0:T(8,128)(2,1)S(1)}, u32[]{:S(2)}, u32[]{:S(2)}) %collective-permute-start.1) | collective-permute-done | bytes 589856 | tf_op jit(solution)/shard_map/ppermute | solution.py:1281
  43.3 3.5 collective-permute-start.4
  50.1 6.0 collective-permute-done.3
  56.0 7.9 %collective-permute-done.4 = bf16[18,64,256]{2,1,0:T(8,128)(2,1)S(1)} collective-permute-done((bf16[18,64,256]{2,1,0:T(8,128)(2,1)S(1)}, bf16[18,64,256]{2,1,0:T(8,128)(2,1)S(1)}, u32[]{:S(2)}, u32[]{:S(2)}) %collective-permute-start.4) | collective-permute-done | bytes 589856 | tf_op jit(solution)/shard_map/ppermute | solution.py:1281
  65.6 7.9 %collective-permute-start.5 = (bf16[48,64,256]{2,1,0:T(8,128)(2,1)S(1)}, bf16[48,64,256]{2,1,0:T(8,128)(2,1)S(1)}, u32[]{:S(2)}, u32[]{:S(2)}) collective-permute-start(bf16[48,64,256]{2,1,0:T(8,128)(2,1)S(1)} %get-tuple-element.612), channel_id=1, source_target_pairs={{0,1},{1,0},{2,3},{3,2},{4,5},{5,4},{6,7},{7,6},{8,9},{9,8},{10,11... | collective-permute-start | bytes 4718600 | tf_op jit(solution)/shard_map/ppermute | solution.py:1339
  73.5 2.2 collective-permute-start.8
  77.6 9.3 %collective-permute-done.7 = bf16[12,64,256]{2,1,0:T(8,128)(2,1)S(1)} collective-permute-done((bf16[12,64,256]{2,1,0:T(8,128)(2,1)S(1)}, bf16[12,64,256]{2,1,0:T(8,128)(2,1)S(1)}, u32[]{:S(2)}, u32[]{:S(2)}) %collective-permute-start.7) | collective-permute-done | bytes 393248 | tf_op jit(solution)/shard_map/ppermute | solution.py:1337
  86.9 17.5 %collective-permute-done.8 = bf16[18,64,256]{2,1,0:T(8,128)(2,1)S(1)} collective-permute-done((bf16[18,64,256]{2,1,0:T(8,128)(2,1)S(1)}, bf16[18,64,256]{2,1,0:T(8,128)(2,1)S(1)}, u32[]{:S(2)}, u32[]{:S(2)}) %collective-permute-start.8) | collective-permute-done | bytes 589856 | tf_op jit(solution)/shard_map/ppermute | solution.py:1281
  124.8 8.8 %collective-permute-done.11 = bf16[12,64,256]{2,1,0:T(8,128)(2,1)S(1)} collective-permute-done((bf16[12,64,256]{2,1,0:T(8,128)(2,1)S(1)}, bf16[12,64,256]{2,1,0:T(8,128)(2,1)S(1)}, u32[]{:S(2)}, u32[]{:S(2)}) %collective-permute-start.11) | collective-permute-done | bytes 393248 | tf_op jit(solution)/shard_map/ppermute | solution.py:1337
  133.6 11.2 %collective-permute-done.10 = bf16[18,64,256]{2,1,0:T(8,128)(2,1)S(1)} collective-permute-done((bf16[18,64,256]{2,1,0:T(8,128)(2,1)S(1)}, bf16[18,64,256]{2,1,0:T(8,128)(2,1)S(1)}, u32[]{:S(2)}, u32[]{:S(2)}) %collective-permute-start.10) | collective-permute-done | bytes 589856 | tf_op jit(solution)/shard_map/ppermute | solution.py:1334
  145.3 2.6 collective-permute-start.12
  151.0 2.1 bitcast_dynamic-update-slice_fusion.10
  154.2 15.2 %collective-permute-done.13 = bf16[12,64,256]{2,1,0:T(8,128)(2,1)S(1)} collective-permute-done((bf16[12,64,256]{2,1,0:T(8,128)(2,1)S(1)}, bf16[12,64,256]{2,1,0:T(8,128)(2,1)S(1)}, u32[]{:S(2)}, u32[]{:S(2)}) %collective-permute-start.13) | collective-permute-done | bytes 393248 | tf_op jit(solution)/shard_map/ppermute | solution.py:1337
  170.6 2.1 bitcast_dynamic-update-slice_fusion.8
  180.5 43.7 %all-gather.2.cloned.1.call-done.far = bf16[896,64,256]{2,1,0:T(8,128)(2,1)} async-done(((bf16[28,64,256]{2,1,0:T(8,128)(2,1)}), bf16[896,64,256]{2,1,0:T(8,128)(2,1)}) %all-gather.2.cloned.1.call-update) | async-done | bytes 29360144 | tf_op jit(solution)/shard_map/all_gather | solution.py:1323
  224.2 12.8 %shard_map.224 = (bf16[96,3072]{1,0:T(8,128)(2,1)}, bf16[256,3072]{1,0:T(8,128)(2,1)}, bf16[96,1024]{1,0:T(8,128)(2,1)}, bf16[256,1024]{1,0:T(8,128)(2,1)}) custom-call(s32[4]{0:T(128)} %concatenate.151.len_ref, bf16[96,1024]{1,0:T(8,128)(2,1)} %bitcast.359, bf16[256,768]{1,0:T(8,128)(2,1)} %refs_0_.1, bf16[384,64,256]{2,1,0:T(8,128)(2,1)} %bitcast.330, ...), custom_call_target="tpu_custom_call" | custom-call | bytes 74800000 | tf_op jit(solution)/shard_map/pallas_call | solution.py:881
  237.5 19.5 %shard_map.226 = (bf16[96,1024]{1,0:T(8,128)(2,1)}, bf16[96,1024]{1,0:T(8,128)(2,1)}, bf16[96,1024]{1,0:T(8,128)(2,1)}, bf16[96,1024]{1,0:T(8,128)(2,1)}, bf16[9...) custom-call(s32[2]{0:T(128)} %broadcast_1_len_ref.2.len_ref, ...), custom_call_target="tpu_custom_call" | custom-call | bytes 136000000 | tf_op jit(solution)/shard_map/pallas_call | solution.py:1186
  257.0 15.1 %shard_map.227 = bf16[448,64,256]{2,1,0:T(8,128)(2,1)} custom-call(bf16[96,1024]{1,0:T(8,128)(2,1)} %get-tuple-element.280.ctx_ref.refs_0_, bf16[96,1024]{1,0:T(8,128)(2,1)} %get-tuple-element.288.refs_1_, bf16[96,1024]{1,0:T(8,128)(2,1)} %get-tuple-element.289.refs_2_, bf16[96,1024]{1,0:T(8,128)(2,1)} %get-tuple-element.290.refs_3_, ...), custom_call_target="tpu_custom_call" | custom-call | bytes 60928000 | tf_op jit(solution)/shard_map/pallas_call | solution.py:1259
  272.2 7.6 %fusion.18 = (bf16[112,64,256]{2,1,0:T(8,128)(2,1)}, bf16[112,64,256]{2,1,0:T(8,128)(2,1)}) fusion(bf16[448,64,256]{2,1,0:T(8,128)(2,1)} %shard_map.227), kind=kLoop, calls=%fused_computation.276 | loop fusion | bytes 14680064 | tf_op jit(solution)/shard_map/slice | solution.py:1398
  284.1 31.9 %shard_map.225 = (bf16[256,768]{1,0:T(8,128)(2,1)}, bf16[256,768]{1,0:T(8,128)(2,1)}, bf16[256,3072]{1,0:T(8,128)(2,1)}, bf16[256,768]{1,0:T(8,128)(2,1)}, bf16[...) custom-call(s32[4]{0:T(128)} %concatenate.151.len_ref, ...), custom_call_target="tpu_custom_call" | custom-call | bytes 136000000 | tf_op jit(solution)/shard_map/pallas_call | solution.py:1186
  316.0 17.8 %shard_map.228 = bf16[480,64,256]{2,1,0:T(8,128)(2,1)} custom-call(bf16[256,1024]{1,0:T(8,128)(2,1)} %get-tuple-element.307.ctx_ref.refs_0_, bf16[256,768]{1,0:T(8,128)(2,1)} %get-tuple-element.308.refs_1_, bf16[256,3072]{1,0:T(8,128)(2,1)} %get-tuple-element.309.refs_2_, bf16[256,768]{1,0:T(8,128)(2,1)} %get-tuple-element.310.refs_3_, ...), custom_call_target="tpu_custom_call" | custom-call | bytes 65280000 | tf_op jit(solution)/shard_map/pallas_call | solution.py:1259
  333.8 2.3 add_convert_fusion.5
  336.1 31.0 %reduce-scatter.5.cloned.1.call-done = bf16[28,64,256]{2,1,0:T(8,128)(2,1)} async-done(((bf16[112,64,256]{2,1,0:T(8,128)(2,1)}), bf16[28,64,256]{2,1,0:T(8,128)(2,1)}) %reduce-scatter.5.cloned.1.call-update) | async-done | bytes 917520 | tf_op jit(solution)/shard_map/reduce_scatter | solution.py:1397
  367.2 7.6 %fusion.17 = (bf16[112,64,256]{2,1,0:T(8,128)(2,1)}, bf16[112,64,256]{2,1,0:T(8,128)(2,1)}) fusion(bf16[480,64,256]{2,1,0:T(8,128)(2,1)} %shard_map.228), kind=kLoop, calls=%fused_computation.275 | loop fusion | bytes 14680064 | tf_op jit(solution)/shard_map/slice | solution.py:1398
  382.3 14.1 %shard_map.229 = (bf16[96,3072]{1,0:T(8,128)(2,1)}, bf16[256,3072]{1,0:T(8,128)(2,1)}, f32[96,1024]{1,0:T(8,128)}, f32[256,768]{1,0:T(8,128)}) custom-call(s32[4]{0:T(128)} %concatenate.151.len_ref, bf16[96,3072]{1,0:T(8,128)(2,1)} %get-tuple-element.322.cv_ref, bf16[256,3072]{1,0:T(8,128)(2,1)} %get-tuple-element.323.ct_ref, ...), custom_call_target="tpu_custom_call" | custom-call | bytes 78200000 | tf_op jit(solution)/shard_map/pallas_call | solution.py:950
  396.4 4.0 collective-permute-done.16
  401.8 2.4 add_convert_fusion.33
  405.6 2.8 slice.367
  408.8 4.4 constant_dynamic-slice_fusion.1
  413.2 5.3 shard_map.231
  418.5 6.0 shard_map.230
  428.1 3.2 collective-permute-start.26
  438.6 2.3 add_convert_fusion.4
  456.9 2.6 collective-permute-start.31
  459.5 6.3 collective-permute-done.22
  465.8 3.6 collective-permute-start.30
  473.9 2.8 add_convert_fusion.3
  490.3 8.0 %collective-permute-done.27 = bf16[2,14,64,256]{3,2,1,0:T(8,128)(2,1)} collective-permute-done((bf16[2,14,64,256]{3,2,1,0:T(8,128)(2,1)}, bf16[2,14,64,256]{3,2,1,0:T(8,128)(2,1)}, u32[]{:S(2)}, u32[]{:S(2)}) %collective-permute-start.27) | collective-permute-done | bytes 917536 | tf_op jit(solution)/shard_map/ppermute | solution.py:1423
  498.3 3.5 collective-permute-done.28
  501.8 2.9 add_convert_fusion
  506.5 2.9 add_convert_fusion.1
  517.9 2.6 add_convert_fusion.27
  520.6 6.8 collective-permute-done.35
  527.4 4.5 collective-permute-done.34
  531.9 13.7 %collective-permute-done.33 = bf16[26,64,256]{2,1,0:T(8,128)(2,1)S(1)} collective-permute-done((bf16[26,64,256]{2,1,0:T(8,128)(2,1)S(1)}, bf16[26,64,256]{2,1,0:T(8,128)(2,1)S(1)}, u32[]{:S(2)}, u32[]{:S(2)}) %collective-permute-start.33) | collective-permute-done | bytes 852000 | tf_op jit(solution)/shard_map/ppermute | solution.py:1426
  546.5 4.6 collective-permute-start.39
  557.4 10.8 %collective-permute-done.40 = f32[2,5376]{1,0:T(2,128)S(1)} collective-permute-done((f32[2,5376]{1,0:T(2,128)S(1)}, f32[2,5376]{1,0:T(2,128)S(1)}, u32[]{:S(2)}, u32[]{:S(2)}) %collective-permute-start.40) | collective-permute-done | bytes 43040 | tf_op jit(solution)/shard_map/ppermute | solution.py:1438
  573.4 10.1 %collective-permute-done.48 = bf16[2,14,64,256]{3,2,1,0:T(8,128)(2,1)S(1)} collective-permute-done((bf16[2,14,64,256]{3,2,1,0:T(8,128)(2,1)S(1)}, bf16[2,14,64,256]{3,2,1,0:T(8,128)(2,1)S(1)}, u32[]{:S(2)}, u32[]{:S(2)}) %collective-permute-start.48) | collective-permute-done | bytes 917536 | tf_op jit(solution)/shard_map/ppermute | solution.py:1423
  588.9 3.9 collective-permute-done.42
  594.0 2.2 collective-permute-start.45
  597.6 2.3 collective-permute-start.44
  599.8 2.5 collective-permute-done.50
  611.1 3.2 collective-permute-done.45
  614.3 2.8 select_select_fusion.1
  617.4 2.7 collective-permute-done.53
  629.5 10.4 %collective-permute-start.47 = (bf16[40,64,256]{2,1,0:T(8,128)(2,1)S(1)}, bf16[40,64,256]{2,1,0:T(8,128)(2,1)}, u32[]{:S(2)}, u32[]{:S(2)}) collective-permute-start(bf16[40,64,256]{2,1,0:T(8,128)(2,1)S(1)} %pad_maximum_fusion.13), channel_id=1, source_target_pairs={{0,1},{1,0},{2,3},{3,2},{4,5},{5,4},{6,7},{7,6},{8,9},{9,8},{10,11... | collective-permute-start | bytes 3932168 | tf_op jit(solution)/shard_map/ppermute | solution.py:1435
  640.1 6.8 collective-permute-start.59
  648.6 7.9 %collective-permute-done.59 = bf16[26,64,256]{2,1,0:T(8,128)(2,1)S(1)} collective-permute-done((bf16[26,64,256]{2,1,0:T(8,128)(2,1)S(1)}, bf16[26,64,256]{2,1,0:T(8,128)(2,1)S(1)}, u32[]{:S(2)}, u32[]{:S(2)}) %collective-permute-start.59) | collective-permute-done | bytes 852000 | tf_op jit(solution)/shard_map/ppermute | solution.py:1281
  662.6 20.1 %shard_map.232 = (f32[20224,128]{1,0:T(8,128)}, f32[20224,128]{1,0:T(8,128)}, f32[20224,128]{1,0:T(8,128)}, f32[20224,128]{1,0:T(8,128)}) custom-call(s32[30]{0:T(128)} %constant.225.which_ref, bf16[60,64,256]{2,1,0:T(8,128)(2,1)} %fusion.g_any, f32[20224,128]{1,0:T(8,128)} %bitcast.336, f32[20224,128]{1,0:T(8,128)} %bitcast.339, f32[20224,128]{1,0:T(8,128)} %bitcast.342, ...), custom_call_target="tpu_custom_call" | custom-call | bytes 71400000 | tf_op jit(solution)/shard_map/pallas_call | solution.py:736
  685.2 9.9 %collective-permute-start.61 = (bf16[40,64,256]{2,1,0:T(8,128)(2,1)S(1)}, bf16[40,64,256]{2,1,0:T(8,128)(2,1)}, u32[]{:S(2)}, u32[]{:S(2)}) collective-permute-start(bf16[40,64,256]{2,1,0:T(8,128)(2,1)S(1)} %pad_maximum_fusion.14), channel_id=1, source_target_pairs={{0,1},{1,0},{2,3},{3,2},{4,5},{5,4},{6,7},{7,6},{8,9},{9,8},{10,11... | collective-permute-start | bytes 3932168 | tf_op jit(solution)/shard_map/ppermute | solution.py:1435
  697.4 8.7 %shard_map.233 = (f32[20224,128]{1,0:T(8,128)}, f32[20224,128]{1,0:T(8,128)}, f32[20224,128]{1,0:T(8,128)}, f32[20224,128]{1,0:T(8,128)}) custom-call(s32[10]{0:T(128)} %constant.226.which_ref, bf16[20,64,256]{2,1,0:T(8,128)(2,1)} %slice.398.g_any, f32[20224,128]{1,0:T(8,128)} %bitcast.337, ...), custom_call_target="tpu_custom_call", output_to_operand_aliasing={{0}: (7, {}), {1}: (8, {}), {2}: (9, {}), {3}: (10, {})} | custom-call | bytes 23800000 | tf_op jit(solution)/shard_map/pallas_call | solution.py:736
  710.1 25.9 %shard_map.234 = (f32[20224,128]{1,0:T(8,128)}, f32[20224,128]{1,0:T(8,128)}, f32[20224,128]{1,0:T(8,128)}, f32[20224,128]{1,0:T(8,128)}) custom-call(s32[40]{0:T(128)} %constant.215.clone.which_ref, bf16[80,64,256]{2,1,0:T(8,128)(2,1)} %pad_maximum_fusion.6.g_any, ...), custom_call_target="tpu_custom_call", output_to_operand_aliasing={{0}: (7, {}), {1}: (8, {}), {2}: (9, {}), {3}: (10, {})} | custom-call | bytes 95200000 | tf_op jit(solution)/shard_map/pallas_call | solution.py:736
  (446 shorter events, 168.1 us)
Async XLA Ops:
  7.2 217.0 %all-gather.2.cloned.1.call-start = ((), (), s32[]{:S(2)}) async-start(), calls=%async_computation.4 | async-start | bytes 30277632 | tf_op jit(solution)/shard_map/all_gather | solution.py:1323
  13.5 322.7 %reduce-scatter.7.cloned.1.call-start = ((), (), s32[]{:S(2)}) async-start(), calls=%async_computation.6 | async-start | bytes 4587520 | tf_op jit(solution)/shard_map/reduce_scatter | solution.py:1397
  18.6 24.7 %collective-permute-start.1 = (bf16[18,64,256]{2,1,0:T(8,128)(2,1)}, bf16[18,64,256]{2,1,0:T(8,128)(2,1)S(1)}, u32[]{:S(2)}, u32[]{:S(2)}) collective-permute-start(bf16[18,64,256]{2,1,0:T(8,128)(2,1)} %shard_map.222), channel_id=1, source_target_pairs={{0,8},{4,12},{8,16},{12,20},{16,24},{20,28},{24,0},{28,4},{1,9},{5... | collective-permute-start | bytes 1769480 | tf_op jit(solution)/shard_map/ppermute | solution.py:1281
  19.9 23.4 %collective-permute-start = (bf16[18,64,256]{2,1,0:T(8,128)(2,1)}, bf16[18,64,256]{2,1,0:T(8,128)(2,1)S(1)}, u32[]{:S(2)}, u32[]{:S(2)}) collective-permute-start(bf16[18,64,256]{2,1,0:T(8,128)(2,1)} %shard_map.222), channel_id=1, source_target_pairs={{0,4},{4,0},{8,12},{12,8},{16,20},{20,16},{24,28},{28,24},{1,5},{5... | collective-permute-start | bytes 1769480 | tf_op jit(solution)/shard_map/ppermute | solution.py:1334
  43.3 20.6 %collective-permute-start.4 = (bf16[18,64,256]{2,1,0:T(8,128)(2,1)S(1)}, bf16[18,64,256]{2,1,0:T(8,128)(2,1)S(1)}, u32[]{:S(2)}, u32[]{:S(2)}) collective-permute-start(bf16[18,64,256]{2,1,0:T(8,128)(2,1)S(1)} %collective-permute-done.1), channel_id=1, source_target_pairs={{0,8},{4,12},{8,16},{12,20},{16,24},{20,28},{24,0},{28,4},{1,9},{5... | collective-permute-start | bytes 1769480 | tf_op jit(solution)/shard_map/ppermute | solution.py:1281
  46.8 17.1 %collective-permute-start.2 = (bf16[18,64,256]{2,1,0:T(8,128)(2,1)S(1)}, bf16[18,64,256]{2,1,0:T(8,128)(2,1)S(1)}, u32[]{:S(2)}, u32[]{:S(2)}) collective-permute-start(bf16[18,64,256]{2,1,0:T(8,128)(2,1)S(1)} %collective-permute-done.1), channel_id=1, source_target_pairs={{0,4},{4,0},{8,12},{12,8},{16,20},{20,16},{24,28},{28,24},{1,5},{5... | collective-permute-start | bytes 1769480 | tf_op jit(solution)/shard_map/ppermute | solution.py:1334
  65.6 38.8 %collective-permute-start.5 = (bf16[48,64,256]{2,1,0:T(8,128)(2,1)S(1)}, bf16[48,64,256]{2,1,0:T(8,128)(2,1)S(1)}, u32[]{:S(2)}, u32[]{:S(2)}) collective-permute-start(bf16[48,64,256]{2,1,0:T(8,128)(2,1)S(1)} %get-tuple-element.612), channel_id=1, source_target_pairs={{0,1},{1,0},{2,3},{3,2},{4,5},{5,4},{6,7},{7,6},{8,9},{9,8},{10,11... | collective-permute-start | bytes 4718600 | tf_op jit(solution)/shard_map/ppermute | solution.py:1339
  73.5 30.9 %collective-permute-start.8 = (bf16[18,64,256]{2,1,0:T(8,128)(2,1)S(1)}, bf16[18,64,256]{2,1,0:T(8,128)(2,1)S(1)}, u32[]{:S(2)}, u32[]{:S(2)}) collective-permute-start(bf16[18,64,256]{2,1,0:T(8,128)(2,1)S(1)} %collective-permute-done.4), channel_id=1, source_target_pairs={{0,8},{4,12},{8,16},{12,20},{16,24},{20,28},{24,0},{28,4},{1,9},{5... | collective-permute-start | bytes 1769480 | tf_op jit(solution)/shard_map/ppermute | solution.py:1281
  75.7 28.7 %collective-permute-start.6 = (bf16[18,64,256]{2,1,0:T(8,128)(2,1)S(1)}, bf16[18,64,256]{2,1,0:T(8,128)(2,1)S(1)}, u32[]{:S(2)}, u32[]{:S(2)}) collective-permute-start(bf16[18,64,256]{2,1,0:T(8,128)(2,1)S(1)} %collective-permute-done.4), channel_id=1, source_target_pairs={{0,4},{4,0},{8,12},{12,8},{16,20},{20,16},{24,28},{28,24},{1,5},{5... | collective-permute-start | bytes 1769480 | tf_op jit(solution)/shard_map/ppermute | solution.py:1334
  76.2 10.7 %collective-permute-start.7 = (bf16[12,64,256]{2,1,0:T(8,128)(2,1)S(1)}, bf16[12,64,256]{2,1,0:T(8,128)(2,1)S(1)}, u32[]{:S(2)}, u32[]{:S(2)}) collective-permute-start(bf16[12,64,256]{2,1,0:T(8,128)(2,1)S(1)} %pad_maximum_fusion.38), channel_id=1, source_target_pairs={{0,2},{1,3},{2,0},{3,1},{4,6},{5,7},{6,4},{7,5},{8,10},{9,11},{10,... | collective-permute-start | bytes 1179656 | tf_op jit(solution)/shard_map/ppermute | solution.py:1337
  109.7 35.2 %collective-permute-start.9 = (bf16[48,64,256]{2,1,0:T(8,128)(2,1)}, bf16[48,64,256]{2,1,0:T(8,128)(2,1)}, u32[]{:S(2)}, u32[]{:S(2)}) collective-permute-start(bf16[48,64,256]{2,1,0:T(8,128)(2,1)} %get-tuple-element.608), channel_id=1, source_target_pairs={{0,1},{1,0},{2,3},{3,2},{4,5},{5,4},{6,7},{7,6},{8,9},{9,8},{10,11... | collective-permute-start | bytes 4718600 | tf_op jit(solution)/shard_map/ppermute | solution.py:1339
  120.0 13.6 %collective-permute-start.11 = (bf16[12,64,256]{2,1,0:T(8,128)(2,1)S(1)}, bf16[12,64,256]{2,1,0:T(8,128)(2,1)S(1)}, u32[]{:S(2)}, u32[]{:S(2)}) collective-permute-start(bf16[12,64,256]{2,1,0:T(8,128)(2,1)S(1)} %pad_maximum_fusion.39), channel_id=1, source_target_pairs={{0,2},{1,3},{2,0},{3,1},{4,6},{5,7},{6,4},{7,5},{8,10},{9,11},{10,... | collective-permute-start | bytes 1179656 | tf_op jit(solution)/shard_map/ppermute | solution.py:1337
  121.3 23.6 %collective-permute-start.10 = (bf16[18,64,256]{2,1,0:T(8,128)(2,1)S(1)}, bf16[18,64,256]{2,1,0:T(8,128)(2,1)S(1)}, u32[]{:S(2)}, u32[]{:S(2)}) collective-permute-start(bf16[18,64,256]{2,1,0:T(8,128)(2,1)S(1)} %collective-permute-done.8), channel_id=1, source_target_pairs={{0,4},{4,0},{8,12},{12,8},{16,20},{20,16},{24,28},{28,24},{1,5},{5... | collective-permute-start | bytes 1769480 | tf_op jit(solution)/shard_map/ppermute | solution.py:1334
  145.3 24.1 %collective-permute-start.12 = (bf16[48,64,256]{2,1,0:T(8,128)(2,1)S(1)}, bf16[48,64,256]{2,1,0:T(8,128)(2,1)S(1)}, u32[]{:S(2)}, u32[]{:S(2)}) collective-permute-start(bf16[48,64,256]{2,1,0:T(8,128)(2,1)S(1)} %get-tuple-element.604), channel_id=1, source_target_pairs={{0,1},{1,0},{2,3},{3,2},{4,5},{5,4},{6,7},{7,6},{8,9},{9,8},{10,11... | collective-permute-start | bytes 4718600 | tf_op jit(solution)/shard_map/ppermute | solution.py:1339
  149.8 19.5 %collective-permute-start.13 = (bf16[12,64,256]{2,1,0:T(8,128)(2,1)S(1)}, bf16[12,64,256]{2,1,0:T(8,128)(2,1)S(1)}, u32[]{:S(2)}, u32[]{:S(2)}) collective-permute-start(bf16[12,64,256]{2,1,0:T(8,128)(2,1)S(1)} %pad_maximum_fusion.40), channel_id=1, source_target_pairs={{0,2},{1,3},{2,0},{3,1},{4,6},{5,7},{6,4},{7,5},{8,10},{9,11},{10,... | collective-permute-start | bytes 1179656 | tf_op jit(solution)/shard_map/ppermute | solution.py:1337
  279.8 87.4 %reduce-scatter.5.cloned.1.call-start = ((), (), s32[]{:S(2)}) async-start(), calls=%async_computation.5 | async-start | bytes 4587520 | tf_op jit(solution)/shard_map/reduce_scatter | solution.py:1397
  280.5 202.2 %reduce-scatter.11.cloned.1.call-start = ((), (), s32[]{:S(2)}) async-start(), calls=%async_computation.8 | async-start | bytes 4587520 | tf_op jit(solution)/shard_map/reduce_scatter | solution.py:1397
  282.9 33.1 %collective-permute-start.15 = (bf16[2,24,64,256]{3,2,1,0:T(8,128)(2,1)S(1)}, bf16[2,24,64,256]{3,2,1,0:T(8,128)(2,1)}, u32[]{:S(2)}, u32[]{:S(2)}) collective-permute-start(bf16[2,24,64,256]{3,2,1,0:T(8,128)(2,1)S(1)} %pad_maximum_fusion.11), channel_id=1, source_target_pairs={{0,1},{1,0},{2,3},{3,2},{4,5},{5,4},{6,7},{7,6},{8,9},{9,8},{10,11... | collective-permute-start | bytes 4718600 | tf_op jit(solution)/shard_map/ppermute | solution.py:1526
  374.8 107.9 %reduce-scatter.9.cloned.1.call-start = ((), (), s32[]{:S(2)}) async-start(), calls=%async_computation.7 | async-start | bytes 4587520 | tf_op jit(solution)/shard_map/reduce_scatter | solution.py:1397
  377.8 18.6 %collective-permute-start.18 = (bf16[2,24,64,256]{3,2,1,0:T(8,128)(2,1)}, bf16[2,24,64,256]{3,2,1,0:T(8,128)(2,1)}, u32[]{:S(2)}, u32[]{:S(2)}) collective-permute-start(bf16[2,24,64,256]{3,2,1,0:T(8,128)(2,1)} %pad_maximum_fusion.12), channel_id=1, source_target_pairs={{0,1},{1,0},{2,3},{3,2},{4,5},{5,4},{6,7},{7,6},{8,9},{9,8},{10,11... | collective-permute-start | bytes 4718600 | tf_op jit(solution)/shard_map/ppermute | solution.py:1537
  380.6 19.8 %collective-permute-start.16 = (bf16[26,64,256]{2,1,0:T(8,128)(2,1)}, bf16[26,64,256]{2,1,0:T(8,128)(2,1)}, u32[]{:S(2)}, u32[]{:S(2)}) collective-permute-start(bf16[26,64,256]{2,1,0:T(8,128)(2,1)} %pad_maximum_fusion.17), channel_id=1, source_target_pairs={{0,4},{4,0},{8,12},{12,8},{16,20},{20,16},{24,28},{28,24},{1,5},{5... | collective-permute-start | bytes 2555912 | tf_op jit(solution)/shard_map/ppermute | solution.py:1426
  381.0 15.4 %collective-permute-start.17 = (f32[2,5376]{1,0:T(2,128)S(1)}, f32[2,5376]{1,0:T(2,128)S(1)}, u32[]{:S(2)}, u32[]{:S(2)}) collective-permute-start(f32[2,5376]{1,0:T(2,128)S(1)} %constant_dynamic-update-slice_fusion.24), channel_id=1, source_target_pairs={{0,1},{1,0},{2,3},{3,2},{4,5},{5,4},{6,7},{7,6},{8,9},{9,8},{10,11... | collective-permute-start | bytes 129032 | tf_op jit(solution)/shard_map/ppermute | solution.py:1438
  401.5 23.0 %collective-permute-start.19 = (bf16[26,64,256]{2,1,0:T(8,128)(2,1)}, bf16[26,64,256]{2,1,0:T(8,128)(2,1)}, u32[]{:S(2)}, u32[]{:S(2)}) collective-permute-start(bf16[26,64,256]{2,1,0:T(8,128)(2,1)} %pad_maximum_fusion.18), channel_id=1, source_target_pairs={{0,4},{4,0},{8,12},{12,8},{16,20},{20,16},{24,28},{28,24},{1,5},{5... | collective-permute-start | bytes 2555912 | tf_op jit(solution)/shard_map/ppermute | solution.py:1426
  404.2 20.5 %collective-permute-start.20 = (bf16[26,64,256]{2,1,0:T(8,128)(2,1)}, bf16[26,64,256]{2,1,0:T(8,128)(2,1)}, u32[]{:S(2)}, u32[]{:S(2)}) collective-permute-start(bf16[26,64,256]{2,1,0:T(8,128)(2,1)} %add_convert_fusion.33), channel_id=1, source_target_pairs={{24,16},{28,20},{0,8},{4,12},{25,17},{29,21},{1,9},{5,13},{26,18},... | collective-permute-start | bytes 2555912 | tf_op jit(solution)/shard_map/ppermute | solution.py:1281
  408.5 16.0 %collective-permute-start.21 = (f32[2,5376]{1,0:T(2,128)S(1)}, f32[2,5376]{1,0:T(2,128)}, u32[]{:S(2)}, u32[]{:S(2)}) collective-permute-start(f32[2,5376]{1,0:T(2,128)S(1)} %add.583), channel_id=1, source_target_pairs={{0,2},{1,3},{2,0},{3,1},{4,6},{5,7},{6,4},{7,5},{8,10},{9,11},{10,... | collective-permute-start | bytes 129032 | tf_op jit(solution)/shard_map/ppermute | solution.py:1438
  428.1 41.3 %collective-permute-start.26 = (bf16[80,64,256]{2,1,0:T(8,128)(2,1)S(1)}, bf16[80,64,256]{2,1,0:T(8,128)(2,1)S(1)}, u32[]{:S(2)}, u32[]{:S(2)}) collective-permute-start(bf16[80,64,256]{2,1,0:T(8,128)(2,1)S(1)} %pad_maximum_fusion.3), channel_id=1, source_target_pairs={{0,1},{1,0},{2,3},{3,2},{4,5},{5,4},{6,7},{7,6},{8,9},{9,8},{10,11... | collective-permute-start | bytes 7864328 | tf_op jit(solution)/shard_map/ppermute | solution.py:1563
  432.3 37.1 %collective-permute-start.25 = (bf16[80,64,256]{2,1,0:T(8,128)(2,1)S(1)}, bf16[80,64,256]{2,1,0:T(8,128)(2,1)}, u32[]{:S(2)}, u32[]{:S(2)}) collective-permute-start(bf16[80,64,256]{2,1,0:T(8,128)(2,1)S(1)} %pad_maximum_fusion.2), channel_id=1, source_target_pairs={{0,1},{1,0},{2,3},{3,2},{4,5},{5,4},{6,7},{7,6},{8,9},{9,8},{10,11... | collective-permute-start | bytes 7864328 | tf_op jit(solution)/shard_map/ppermute | solution.py:1563
  443.6 13.3 %collective-permute-start.24 = (f32[2,5376]{1,0:T(2,128)S(1)}, f32[2,5376]{1,0:T(2,128)S(1)}, u32[]{:S(2)}, u32[]{:S(2)}) collective-permute-start(f32[2,5376]{1,0:T(2,128)S(1)} %add.591), channel_id=1, source_target_pairs={{0,4},{4,0},{8,12},{12,8},{16,20},{20,16},{24,28},{28,24},{1,5},{5... | collective-permute-start | bytes 129032 | tf_op jit(solution)/shard_map/ppermute | solution.py:1438
  446.1 19.7 %collective-permute-start.22 = (bf16[26,64,256]{2,1,0:T(8,128)(2,1)S(1)}, bf16[26,64,256]{2,1,0:T(8,128)(2,1)S(1)}, u32[]{:S(2)}, u32[]{:S(2)}) collective-permute-start(bf16[26,64,256]{2,1,0:T(8,128)(2,1)S(1)} %add_convert_fusion.32), channel_id=1, source_target_pairs={{16,8},{20,12},{17,9},{21,13},{18,10},{22,14},{19,11},{23,15}} | collective-permute-start | bytes 2555912 | tf_op jit(solution)/shard_map/ppermute | solution.py:1281
  449.1 20.3 %collective-permute-start.23 = (bf16[26,64,256]{2,1,0:T(8,128)(2,1)S(1)}, bf16[26,64,256]{2,1,0:T(8,128)(2,1)S(1)}, u32[]{:S(2)}, u32[]{:S(2)}) collective-permute-start(bf16[26,64,256]{2,1,0:T(8,128)(2,1)S(1)} %add_convert_fusion.31), channel_id=1, source_target_pairs={{24,16},{28,20},{0,8},{4,12},{25,17},{29,21},{1,9},{5,13},{26,18},... | collective-permute-start | bytes 2555912 | tf_op jit(solution)/shard_map/ppermute | solution.py:1281
  456.9 31.8 %collective-permute-start.31 = (bf16[80,64,256]{2,1,0:T(8,128)(2,1)}, bf16[80,64,256]{2,1,0:T(8,128)(2,1)}, u32[]{:S(2)}, u32[]{:S(2)}) collective-permute-start(bf16[80,64,256]{2,1,0:T(8,128)(2,1)} %pad_maximum_fusion.5), channel_id=1, source_target_pairs={{0,1},{1,0},{2,3},{3,2},{4,5},{5,4},{6,7},{7,6},{8,9},{9,8},{10,11... | collective-permute-start | bytes 7864328 | tf_op jit(solution)/shard_map/ppermute | solution.py:1563
  465.8 22.9 %collective-permute-start.30 = (bf16[80,64,256]{2,1,0:T(8,128)(2,1)}, bf16[80,64,256]{2,1,0:T(8,128)(2,1)}, u32[]{:S(2)}, u32[]{:S(2)}) collective-permute-start(bf16[80,64,256]{2,1,0:T(8,128)(2,1)} %pad_maximum_fusion.4), channel_id=1, source_target_pairs={{0,1},{1,0},{2,3},{3,2},{4,5},{5,4},{6,7},{7,6},{8,9},{9,8},{10,11... | collective-permute-start | bytes 7864328 | tf_op jit(solution)/shard_map/ppermute | solution.py:1563
  470.6 19.7 %collective-permute-start.29 = (bf16[26,64,256]{2,1,0:T(8,128)(2,1)}, bf16[26,64,256]{2,1,0:T(8,128)(2,1)}, u32[]{:S(2)}, u32[]{:S(2)}) collective-permute-start(bf16[26,64,256]{2,1,0:T(8,128)(2,1)} %add_convert_fusion.30), channel_id=1, source_target_pairs={{16,8},{20,12},{17,9},{21,13},{18,10},{22,14},{19,11},{23,15}} | collective-permute-start | bytes 2555912 | tf_op jit(solution)/shard_map/ppermute | solution.py:1281
  479.1 19.2 %collective-permute-start.27 = (bf16[2,14,64,256]{3,2,1,0:T(8,128)(2,1)}, bf16[2,14,64,256]{3,2,1,0:T(8,128)(2,1)}, u32[]{:S(2)}, u32[]{:S(2)}) collective-permute-start(bf16[2,14,64,256]{3,2,1,0:T(8,128)(2,1)} %fusion.12), channel_id=1, source_target_pairs={{0,2},{1,3},{2,0},{3,1},{4,6},{5,7},{6,4},{7,5},{8,10},{9,11},{10,... | collective-permute-start | bytes 2752520 | tf_op jit(solution)/shard_map/ppermute | solution.py:1423
  484.6 17.3 %collective-permute-start.28 = (bf16[26,64,256]{2,1,0:T(8,128)(2,1)S(1)}, bf16[26,64,256]{2,1,0:T(8,128)(2,1)S(1)}, u32[]{:S(2)}, u32[]{:S(2)}) collective-permute-start(bf16[26,64,256]{2,1,0:T(8,128)(2,1)S(1)} %pad_maximum_fusion.19), channel_id=1, source_target_pairs={{0,4},{4,0},{8,12},{12,8},{16,20},{20,16},{24,28},{28,24},{1,5},{5... | collective-permute-start | bytes 2555912 | tf_op jit(solution)/shard_map/ppermute | solution.py:1426
  511.1 16.3 %collective-permute-start.35 = (bf16[26,64,256]{2,1,0:T(8,128)(2,1)S(1)}, bf16[26,64,256]{2,1,0:T(8,128)(2,1)S(1)}, u32[]{:S(2)}, u32[]{:S(2)}) collective-permute-start(bf16[26,64,256]{2,1,0:T(8,128)(2,1)S(1)} %pad_maximum_fusion.21), channel_id=1, source_target_pairs={{0,4},{4,0},{8,12},{12,8},{16,20},{20,16},{24,28},{28,24},{1,5},{5... | collective-permute-start | bytes 2555912 | tf_op jit(solution)/shard_map/ppermute | solution.py:1426
  512.7 19.2 %collective-permute-start.34 = (bf16[26,64,256]{2,1,0:T(8,128)(2,1)S(1)}, bf16[26,64,256]{2,1,0:T(8,128)(2,1)S(1)}, u32[]{:S(2)}, u32[]{:S(2)}) collective-permute-start(bf16[26,64,256]{2,1,0:T(8,128)(2,1)S(1)} %add_convert_fusion.28), channel_id=1, source_target_pairs={{0,8},{4,12},{1,9},{5,13},{2,10},{6,14},{3,11},{7,15}} | collective-permute-start | bytes 2555912 | tf_op jit(solution)/shard_map/ppermute | solution.py:1281
  516.1 29.6 %collective-permute-start.33 = (bf16[26,64,256]{2,1,0:T(8,128)(2,1)S(1)}, bf16[26,64,256]{2,1,0:T(8,128)(2,1)S(1)}, u32[]{:S(2)}, u32[]{:S(2)}) collective-permute-start(bf16[26,64,256]{2,1,0:T(8,128)(2,1)S(1)} %pad_maximum_fusion.20), channel_id=1, source_target_pairs={{0,4},{4,0},{8,12},{12,8},{16,20},{20,16},{24,28},{28,24},{1,5},{5... | collective-permute-start | bytes 2555912 | tf_op jit(solution)/shard_map/ppermute | solution.py:1426
  516.8 28.8 %collective-permute-start.32 = (bf16[2,14,64,256]{3,2,1,0:T(8,128)(2,1)S(1)}, bf16[2,14,64,256]{3,2,1,0:T(8,128)(2,1)S(1)}, u32[]{:S(2)}, u32[]{:S(2)}) collective-permute-start(bf16[2,14,64,256]{3,2,1,0:T(8,128)(2,1)S(1)} %fusion.10), channel_id=1, source_target_pairs={{0,2},{1,3},{2,0},{3,1},{4,6},{5,7},{6,4},{7,5},{8,10},{9,11},{10,... | collective-permute-start | bytes 2752520 | tf_op jit(solution)/shard_map/ppermute | solution.py:1423
  546.5 21.9 %collective-permute-start.39 = (bf16[26,64,256]{2,1,0:T(8,128)(2,1)S(1)}, bf16[26,64,256]{2,1,0:T(8,128)(2,1)S(1)}, u32[]{:S(2)}, u32[]{:S(2)}) collective-permute-start(bf16[26,64,256]{2,1,0:T(8,128)(2,1)S(1)} %add_convert_fusion.25), channel_id=1, source_target_pairs={{8,16},{12,20},{9,17},{13,21},{10,18},{14,22},{11,19},{15,23}} | collective-permute-start | bytes 2555912 | tf_op jit(solution)/shard_map/ppermute | solution.py:1281
  551.4 17.0 %collective-permute-start.38 = (bf16[26,64,256]{2,1,0:T(8,128)(2,1)S(1)}, bf16[26,64,256]{2,1,0:T(8,128)(2,1)S(1)}, u32[]{:S(2)}, u32[]{:S(2)}) collective-permute-start(bf16[26,64,256]{2,1,0:T(8,128)(2,1)S(1)} %add_convert_fusion.26), channel_id=1, source_target_pairs={{24,16},{28,20},{25,17},{29,21},{26,18},{30,22},{27,19},{31,23}} | collective-permute-start | bytes 2555912 | tf_op jit(solution)/shard_map/ppermute | solution.py:1281
  552.2 16.2 %collective-permute-start.37 = (bf16[26,64,256]{2,1,0:T(8,128)(2,1)S(1)}, bf16[26,64,256]{2,1,0:T(8,128)(2,1)S(1)}, u32[]{:S(2)}, u32[]{:S(2)}) collective-permute-start(bf16[26,64,256]{2,1,0:T(8,128)(2,1)S(1)} %pad_maximum_fusion.22), channel_id=1, source_target_pairs={{0,4},{4,0},{8,12},{12,8},{16,20},{20,16},{24,28},{28,24},{1,5},{5... | collective-permute-start | bytes 2555912 | tf_op jit(solution)/shard_map/ppermute | solution.py:1426
  553.8 14.4 %collective-permute-start.40 = (f32[2,5376]{1,0:T(2,128)S(1)}, f32[2,5376]{1,0:T(2,128)S(1)}, u32[]{:S(2)}, u32[]{:S(2)}) collective-permute-start(f32[2,5376]{1,0:T(2,128)S(1)} %add.625), channel_id=1, source_target_pairs={{0,16},{4,20},{8,24},{12,28},{16,0},{20,4},{24,8},{28,12},{1,17},{... | collective-permute-start | bytes 129032 | tf_op jit(solution)/shard_map/ppermute | solution.py:1438
  556.0 17.4 %collective-permute-start.49 = (bf16[26,64,256]{2,1,0:T(8,128)(2,1)S(1)}, bf16[26,64,256]{2,1,0:T(8,128)(2,1)S(1)}, u32[]{:S(2)}, u32[]{:S(2)}) collective-permute-start(bf16[26,64,256]{2,1,0:T(8,128)(2,1)S(1)} %add_convert_fusion.16), channel_id=1, source_target_pairs={{0,8},{4,12},{1,9},{5,13},{2,10},{6,14},{3,11},{7,15}} | collective-permute-start | bytes 2555912 | tf_op jit(solution)/shard_map/ppermute | solution.py:1281
  568.2 15.4 %collective-permute-start.48 = (bf16[2,14,64,256]{3,2,1,0:T(8,128)(2,1)S(1)}, bf16[2,14,64,256]{3,2,1,0:T(8,128)(2,1)S(1)}, u32[]{:S(2)}, u32[]{:S(2)}) collective-permute-start(bf16[2,14,64,256]{3,2,1,0:T(8,128)(2,1)S(1)} %dynamic-slice_bitcast_fusion.1), channel_id=1, source_target_pairs={{0,2},{1,3},{2,0},{3,1},{4,6},{5,7},{6,4},{7,5},{8,10},{9,11},{10,... | collective-permute-start | bytes 2752520 | tf_op jit(solution)/shard_map/ppermute | solution.py:1423
  568.8 17.4 %collective-permute-start.43 = (bf16[26,64,256]{2,1,0:T(8,128)(2,1)S(1)}, bf16[26,64,256]{2,1,0:T(8,128)(2,1)S(1)}, u32[]{:S(2)}, u32[]{:S(2)}) collective-permute-start(bf16[26,64,256]{2,1,0:T(8,128)(2,1)S(1)} %add_convert_fusion.22), channel_id=1, source_target_pairs={{16,24},{20,28},{17,25},{21,29},{18,26},{22,30},{19,27},{23,31}} | collective-permute-start | bytes 2555912 | tf_op jit(solution)/shard_map/ppermute | solution.py:1281
  569.9 22.9 %collective-permute-start.42 = (bf16[26,64,256]{2,1,0:T(8,128)(2,1)S(1)}, bf16[26,64,256]{2,1,0:T(8,128)(2,1)S(1)}, u32[]{:S(2)}, u32[]{:S(2)}) collective-permute-start(bf16[26,64,256]{2,1,0:T(8,128)(2,1)S(1)} %add_convert_fusion.23), channel_id=1, source_target_pairs={{0,8},{4,12},{24,16},{28,20},{1,9},{5,13},{25,17},{29,21},{2,10},{... | collective-permute-start | bytes 2555912 | tf_op jit(solution)/shard_map/ppermute | solution.py:1281
  571.5 21.3 %collective-permute-start.41 = (bf16[26,64,256]{2,1,0:T(8,128)(2,1)S(1)}, bf16[26,64,256]{2,1,0:T(8,128)(2,1)S(1)}, u32[]{:S(2)}, u32[]{:S(2)}) collective-permute-start(bf16[26,64,256]{2,1,0:T(8,128)(2,1)S(1)} %add_convert_fusion.24), channel_id=1, source_target_pairs={{16,8},{20,12},{17,9},{21,13},{18,10},{22,14},{19,11},{23,15}} | collective-permute-start | bytes 2555912 | tf_op jit(solution)/shard_map/ppermute | solution.py:1281
  583.9 16.0 %collective-permute-start.52 = (bf16[26,64,256]{2,1,0:T(8,128)(2,1)S(1)}, bf16[26,64,256]{2,1,0:T(8,128)(2,1)S(1)}, u32[]{:S(2)}, u32[]{:S(2)}) collective-permute-start(bf16[26,64,256]{2,1,0:T(8,128)(2,1)S(1)} %add_convert_fusion.15), channel_id=1, source_target_pairs={{8,16},{12,20},{9,17},{13,21},{10,18},{14,22},{11,19},{15,23}} | collective-permute-start | bytes 2555912 | tf_op jit(solution)/shard_map/ppermute | solution.py:1281
  585.3 17.0 %collective-permute-start.50 = (bf16[2,14,64,256]{3,2,1,0:T(8,128)(2,1)S(1)}, bf16[2,14,64,256]{3,2,1,0:T(8,128)(2,1)S(1)}, u32[]{:S(2)}, u32[]{:S(2)}) collective-permute-start(bf16[2,14,64,256]{3,2,1,0:T(8,128)(2,1)S(1)} %dynamic-slice_bitcast_fusion), channel_id=1, source_target_pairs={{0,2},{1,3},{2,0},{3,1},{4,6},{5,7},{6,4},{7,5},{8,10},{9,11},{10,... | collective-permute-start | bytes 2752520 | tf_op jit(solution)/shard_map/ppermute | solution.py:1423
  586.2 13.6 %collective-permute-start.51 = (bf16[26,64,256]{2,1,0:T(8,128)(2,1)S(1)}, bf16[26,64,256]{2,1,0:T(8,128)(2,1)S(1)}, u32[]{:S(2)}, u32[]{:S(2)}) collective-permute-start(bf16[26,64,256]{2,1,0:T(8,128)(2,1)S(1)} %pad_maximum_fusion.23), channel_id=1, source_target_pairs={{0,4},{4,0},{8,12},{12,8},{16,20},{20,16},{24,28},{28,24},{1,5},{5... | collective-permute-start | bytes 2555912 | tf_op jit(solution)/shard_map/ppermute | solution.py:1426
  594.0 20.3 %collective-permute-start.45 = (bf16[26,64,256]{2,1,0:T(8,128)(2,1)}, bf16[26,64,256]{2,1,0:T(8,128)(2,1)}, u32[]{:S(2)}, u32[]{:S(2)}) collective-permute-start(bf16[26,64,256]{2,1,0:T(8,128)(2,1)} %add_convert_fusion.20), channel_id=1, source_target_pairs={{8,16},{12,20},{9,17},{13,21},{10,18},{14,22},{11,19},{15,23}} | collective-permute-start | bytes 2555912 | tf_op jit(solution)/shard_map/ppermute | solution.py:1281
  597.6 16.8 %collective-permute-start.44 = (bf16[26,64,256]{2,1,0:T(8,128)(2,1)}, bf16[26,64,256]{2,1,0:T(8,128)(2,1)}, u32[]{:S(2)}, u32[]{:S(2)}) collective-permute-start(bf16[26,64,256]{2,1,0:T(8,128)(2,1)} %add_convert_fusion.21), channel_id=1, source_target_pairs={{8,0},{12,4},{9,1},{13,5},{10,2},{14,6},{11,3},{15,7}} | collective-permute-start | bytes 2555912 | tf_op jit(solution)/shard_map/ppermute | solution.py:1281
  602.7 14.6 %collective-permute-start.55 = (bf16[26,64,256]{2,1,0:T(8,128)(2,1)S(1)}, bf16[26,64,256]{2,1,0:T(8,128)(2,1)}, u32[]{:S(2)}, u32[]{:S(2)}) collective-permute-start(bf16[26,64,256]{2,1,0:T(8,128)(2,1)S(1)} %add_convert_fusion.13), channel_id=1, source_target_pairs={{16,24},{20,28},{17,25},{21,29},{18,26},{22,30},{19,27},{23,31}} | collective-permute-start | bytes 2555912 | tf_op jit(solution)/shard_map/ppermute | solution.py:1281
  604.6 12.7 %collective-permute-start.54 = (bf16[26,64,256]{2,1,0:T(8,128)(2,1)S(1)}, bf16[26,64,256]{2,1,0:T(8,128)(2,1)}, u32[]{:S(2)}, u32[]{:S(2)}) collective-permute-start(bf16[26,64,256]{2,1,0:T(8,128)(2,1)S(1)} %add_convert_fusion.14), channel_id=1, source_target_pairs={{24,16},{28,20},{25,17},{29,21},{26,18},{30,22},{27,19},{31,23}} | collective-permute-start | bytes 2555912 | tf_op jit(solution)/shard_map/ppermute | solution.py:1281
  607.7 12.4 %collective-permute-start.53 = (bf16[26,64,256]{2,1,0:T(8,128)(2,1)}, bf16[26,64,256]{2,1,0:T(8,128)(2,1)}, u32[]{:S(2)}, u32[]{:S(2)}) collective-permute-start(bf16[26,64,256]{2,1,0:T(8,128)(2,1)} %pad_maximum_fusion.24), channel_id=1, source_target_pairs={{0,4},{4,0},{8,12},{12,8},{16,20},{20,16},{24,28},{28,24},{1,5},{5... | collective-permute-start | bytes 2555912 | tf_op jit(solution)/shard_map/ppermute | solution.py:1426
  617.1 12.0 %collective-permute-start.46 = (bf16[26,64,256]{2,1,0:T(8,128)(2,1)S(1)}, bf16[26,64,256]{2,1,0:T(8,128)(2,1)S(1)}, u32[]{:S(2)}, u32[]{:S(2)}) collective-permute-start(bf16[26,64,256]{2,1,0:T(8,128)(2,1)S(1)} %select_select_fusion.1), channel_id=1, source_target_pairs={{0,2},{1,3},{2,0},{3,1},{4,6},{5,7},{6,4},{7,5},{8,10},{9,11},{10,... | collective-permute-start | bytes 2555912 | tf_op jit(solution)/shard_map/ppermute | solution.py:1433
  621.5 18.3 %collective-permute-start.57 = (bf16[26,64,256]{2,1,0:T(8,128)(2,1)S(1)}, bf16[26,64,256]{2,1,0:T(8,128)(2,1)S(1)}, u32[]{:S(2)}, u32[]{:S(2)}) collective-permute-start(bf16[26,64,256]{2,1,0:T(8,128)(2,1)S(1)} %add_convert_fusion.11), channel_id=1, source_target_pairs={{0,8},{4,12},{24,16},{28,20},{1,9},{5,13},{25,17},{29,21},{2,10},{... | collective-permute-start | bytes 2555912 | tf_op jit(solution)/shard_map/ppermute | solution.py:1281
  624.3 15.5 %collective-permute-start.56 = (bf16[26,64,256]{2,1,0:T(8,128)(2,1)S(1)}, bf16[26,64,256]{2,1,0:T(8,128)(2,1)S(1)}, u32[]{:S(2)}, u32[]{:S(2)}) collective-permute-start(bf16[26,64,256]{2,1,0:T(8,128)(2,1)S(1)} %add_convert_fusion.12), channel_id=1, source_target_pairs={{16,8},{20,12},{17,9},{21,13},{18,10},{22,14},{19,11},{23,15}} | collective-permute-start | bytes 2555912 | tf_op jit(solution)/shard_map/ppermute | solution.py:1281
  629.5 28.7 %collective-permute-start.47 = (bf16[40,64,256]{2,1,0:T(8,128)(2,1)S(1)}, bf16[40,64,256]{2,1,0:T(8,128)(2,1)}, u32[]{:S(2)}, u32[]{:S(2)}) collective-permute-start(bf16[40,64,256]{2,1,0:T(8,128)(2,1)S(1)} %pad_maximum_fusion.13), channel_id=1, source_target_pairs={{0,1},{1,0},{2,3},{3,2},{4,5},{5,4},{6,7},{7,6},{8,9},{9,8},{10,11... | collective-permute-start | bytes 3932168 | tf_op jit(solution)/shard_map/ppermute | solution.py:1435
  640.1 16.4 %collective-permute-start.59 = (bf16[26,64,256]{2,1,0:T(8,128)(2,1)S(1)}, bf16[26,64,256]{2,1,0:T(8,128)(2,1)S(1)}, u32[]{:S(2)}, u32[]{:S(2)}) collective-permute-start(bf16[26,64,256]{2,1,0:T(8,128)(2,1)S(1)} %add_convert_fusion.8), channel_id=1, source_target_pairs={{8,16},{12,20},{9,17},{13,21},{10,18},{14,22},{11,19},{15,23}} | collective-permute-start | bytes 2555912 | tf_op jit(solution)/shard_map/ppermute | solution.py:1281
  647.2 10.9 %collective-permute-start.58 = (bf16[26,64,256]{2,1,0:T(8,128)(2,1)S(1)}, bf16[26,64,256]{2,1,0:T(8,128)(2,1)S(1)}, u32[]{:S(2)}, u32[]{:S(2)}) collective-permute-start(bf16[26,64,256]{2,1,0:T(8,128)(2,1)S(1)} %add_convert_fusion.9), channel_id=1, source_target_pairs={{8,0},{12,4},{9,1},{13,5},{10,2},{14,6},{11,3},{15,7}} | collective-permute-start | bytes 2555912 | tf_op jit(solution)/shard_map/ppermute | solution.py:1281
  659.1 23.7 %collective-permute-start.60 = (bf16[26,64,256]{2,1,0:T(8,128)(2,1)S(1)}, bf16[26,64,256]{2,1,0:T(8,128)(2,1)}, u32[]{:S(2)}, u32[]{:S(2)}) collective-permute-start(bf16[26,64,256]{2,1,0:T(8,128)(2,1)S(1)} %select_select_fusion), channel_id=1, source_target_pairs={{0,2},{1,3},{2,0},{3,1},{4,6},{5,7},{6,4},{7,5},{8,10},{9,11},{10,... | collective-permute-start | bytes 2555912 | tf_op jit(solution)/shard_map/ppermute | solution.py:1433
  685.2 20.9 %collective-permute-start.61 = (bf16[40,64,256]{2,1,0:T(8,128)(2,1)S(1)}, bf16[40,64,256]{2,1,0:T(8,128)(2,1)}, u32[]{:S(2)}, u32[]{:S(2)}) collective-permute-start(bf16[40,64,256]{2,1,0:T(8,128)(2,1)S(1)} %pad_maximum_fusion.14), channel_id=1, source_target_pairs={{0,1},{1,0},{2,3},{3,2},{4,5},{5,4},{6,7},{7,6},{8,9},{9,8},{10,11... | collective-permute-start | bytes 3932168 | tf_op jit(solution)/shard_map/ppermute | solution.py:1435
  (68 other events, 572.4 us)
Sparse Core Ops, SparseCore 0:
  13.6 210.5 all-gather.1
  279.9 42.6 reduce-scatter.6
  325.9 41.2 reduce-scatter.4
  374.9 42.1 reduce-scatter.10
  420.2 40.7 reduce-scatter.8

commit v4 on v3

--- a/solution.py
+++ b/solution.py
@@ -518,9 +518,9 @@
 
 TILES = tile_table()
 SHARD = 158
-FAR = 46
-G_HALF = 24
-G_LONE = 6
+FAR = 62
+G_HALF = 32
+G_LONE = 8
 R_LONE = 28
 R_BOTH = 24
 R_HALF = 2 * R_LONE + R_BOTH
@@ -1388,20 +1388,165 @@
     return jnp.asarray(table, jnp.int32)
 
 
-def half_of(source, core):
-    array, offset = source
-    return join([cut(array, offset + lone_at(core), 2 * R_LONE), cut(array, offset + both_at(core), R_BOTH)])
+def pieces_of(owner, ranges, begins):
+    pieces = []
+    at = 0
+    for begin, size in ranges:
+        first, last = SHARD * owner + begin, SHARD * owner + begin + size
+        for which, (lo, hi) in enumerate(begins):
+            start, end = max(first, lo), min(last, hi)
+            if start < end:
+                pieces.append((which, start - lo, end - start, at + start - first))
+        at += size
+    return pieces
+
+
+def half_plan(owner, begins, other):
+    return [
+        pieces_of(owner, ((lone_at(core ^ other), 2 * R_LONE), (both_at(core ^ other), R_BOTH)), begins)
+        for core in range(2)
+    ]
+
+
+def both_plan(owner, begins, other):
+    plan = []
+    for core in range(2):
+        pieces = []
+        for i in range(2):
+            for which, begin, size, at in pieces_of(owner + i, ((both_at(core ^ other), R_BOTH),), begins):
+                pieces.append((which, begin, size, at + R_BOTH * i))
+        plan.append(pieces)
+    return plan
+
+
+def follow(core_ref, plans, arrays, outs, sems):
+    for core in range(2):
+
+        @pl.when(core_ref[0] == core)
+        def _(core=core):
+            copies = []
+            for j, plan in enumerate(plans):
+                for i, (which, begin, size, at) in enumerate(plan[core]):
+                    copies.append(
+                        pltpu.make_async_copy(
+                            arrays[which].at[pl.ds(begin, size)], outs[j].at[pl.ds(at, size)], sems.at[j, i]
+                        )
+                    )
+            for copy in copies:
+                copy.start()
+            for copy in copies:
+                copy.wait()
+
+
+def pick_body(plans, number, core_ref, *refs):
+    follow(core_ref, plans, refs[:number], refs[number:-1], refs[-1])
+
+
+def pick(core, sources, plans, sizes):
+    arrays = [array for _, array in sources]
+    return pl.pallas_call(
+        functools.partial(pick_body, plans, len(arrays)),
+        in_specs=[pl.BlockSpec(memory_space=pltpu.SMEM)] + [pl.BlockSpec(memory_space=pl.ANY)] * len(arrays),
+        out_specs=whole(len(plans)),
+        out_shape=[jax.ShapeDtypeStruct((size, SUB, WIDE), BF16) for size in sizes],
+        scratch_shapes=[pltpu.SemaphoreType.DMA((len(plans), 6))],
+        compiler_params=params(),
+        cost_estimate=cost(2 * len(plans)),
+    )(core.reshape(1), *arrays)
+
+
+def begins_of(sources):
+    return [(begin, begin + array.shape[0]) for begin, array in sources]
+
+
+def merge_body(plans, number, core_ref, *refs):
+    arrays, got = refs[:number], refs[number : number + 2]
+    outs = refs[number + 2 : -2]
+    own, sems = refs[-2:]
+    follow(core_ref, plans, arrays, [own.at[0], own.at[1]], sems)
+
+    def total(out, size, i, begin):
+        def tile(t, carry):
+            out[t] = add(own[i, begin + t], got[i][begin + t])
+            return carry
+
+        lax.fori_loop(0, size, tile, 0, unroll=2)
+
+    for k in range(CHUNKS):
+        for i in range(2):
+            for y in range(2):
+                total(outs[2 * k].at[y, i], LONE, i, R_LONE * y + LONE * k)
+            total(outs[2 * k + 1].at[i], BOTH, i, 2 * R_LONE + BOTH * k)
+
+
+def merge(core, sources, zi, got, chunks):
+    arrays = [array for _, array in sources]
+    plans = [half_plan(2 * zi + i, begins_of(sources), 0) for i in range(2)]
+    shapes = []
+    for _ in range(CHUNKS):
+        shapes += [(2, 2, LONE, SUB, WIDE), (2, BOTH, SUB, WIDE)]
+    made = pl.pallas_call(
+        functools.partial(merge_body, plans, len(arrays)),
+        in_specs=[pl.BlockSpec(memory_space=pltpu.SMEM)]
+        + [pl.BlockSpec(memory_space=pl.ANY)] * len(arrays)
+        + whole(2),
+        out_specs=whole(len(shapes)),
+        out_shape=[jax.ShapeDtypeStruct(shape, BF16) for shape in shapes],
+        scratch_shapes=[
+            pltpu.VMEM((2, R_HALF, SUB, WIDE), BF16),
+            pltpu.SemaphoreType.DMA((2, 6)),
+        ],
+        compiler_params=params(),
+        cost_estimate=cost(8),
+    )(core.reshape(1), *arrays, *got)
+    for k, chunk in enumerate(chunks):
+        chunk.state["lone", zi], chunk.state["both", zi] = made[2 * k : 2 * k + 2]
+
+
+def arrange_body(pieces, x_any, o_any, held, sems):
+    arrivals = []
+    at = 0
+    for i, (begin, size) in enumerate(pieces):
+        spot_of = pl.ds(at, size)
+        arrivals.append(
+            (
+                pltpu.make_async_copy(x_any.at[pl.ds(begin, size)], held.at[spot_of], sems.at[0, i]),
+                pltpu.make_async_copy(held.at[spot_of], o_any.at[spot_of], sems.at[1, i]),
+            )
+        )
+        arrivals[-1][0].start()
+        at += size
+    for came, goes in arrivals:
+        came.wait()
+        goes.start()
+    for _, goes in arrivals:
+        goes.wait()
+
+
+def arrange(array, pieces):
+    number = sum(size for _, size in pieces)
+    return pl.pallas_call(
+        functools.partial(arrange_body, pieces),
+        in_specs=[pl.BlockSpec(memory_space=pl.ANY)],
+        out_specs=pl.BlockSpec(memory_space=pl.ANY),
+        out_shape=jax.ShapeDtypeStruct((number, SUB, WIDE), BF16),
+        scratch_shapes=[
+            pltpu.VMEM((number, SUB, WIDE), BF16),
+            pltpu.SemaphoreType.DMA((2, len(pieces))),
+        ],
+        compiler_params=params(),
+        cost_estimate=cost(6),
+    )(array)
 
 
 def group_lone(array, offset):
-    return lax.psum_scatter(
-        array[offset : offset + 4 * R_LONE], "seq", scatter_dimension=0, tiled=True,
-        axis_index_groups=GROUP_ORDER,
-    )
-
-
-def both_parts(array, offset, core):
-    return jnp.stack([cut(array, offset + SHARD * i + both_at(core), R_BOTH) for i in range(2)])
+    pieces = tuple(
+        (offset + SHARD * o + R_LONE * part, R_LONE) for part in range(4) for o in range(2)
+    )
+    made = lax.psum_scatter(
+        arrange(array, pieces), "seq", scatter_dimension=0, tiled=True, axis_index_groups=GROUP_ORDER
+    )
+    return made.reshape(2, R_LONE, SUB, WIDE)
 
 
 def chunks_of(lone, both):
@@ -1475,19 +1620,6 @@
     return made
 
 
-def pair_up(halves, chunks, zi):
-    for k, chunk in enumerate(chunks):
-        chunk.state["lone", zi] = jnp.stack(
-            [
-                jnp.stack([half[R_LONE * y + LONE * k : R_LONE * y + LONE * (k + 1)] for half in halves])
-                for y in range(2)
-            ]
-        )
-        chunk.state["both", zi] = jnp.stack(
-            [half[2 * R_LONE + BOTH * k : 2 * R_LONE + BOTH * (k + 1)] for half in halves]
-        )
-
-
 def pad_regions(value, pairs):
     reg = value.shape[0] // pairs
     cube = value.reshape(pairs, reg, value.shape[1])
@@ -1522,8 +1654,19 @@
     chunks = [Sums() for _ in range(CHUNKS)]
     vis_at, text_at = TILES[1][0], TILES[7][0]
     vis_pair, text_pair = (vis_mid, 2 * SHARD - vis_at), 6 * SHARD - text_at
-    lone = [group_lone(vis_mid, vis_pair[1] + SHARD * i) for i in range(2)]
-    far_both = lax.ppermute(both_parts(*vis_pair, 1 - core), "seq", SWAP_CORE)
+    lone = group_lone(*vis_pair)
+    vis_source = (vis_at, vis_mid)
+
+    def pick_both(source, owner):
+        begins = begins_of([source])
+        plans = [both_plan(owner, begins, 1), both_plan(owner, begins, 0)]
+        send, own = pick(core, [source], plans, [2 * R_BOTH] * 2)
+        return own, lax.ppermute(send, "seq", SWAP_CORE)
+
+    def both_sum(own, got):
+        return add(own, got).reshape(2, R_BOTH, SUB, WIDE)
+
+    own_both, far_both = pick_both(vis_source, 2)
     (out_text, t_first, t_act, t_second, t_sctx, t_fback, t_pback, t_bback, t_dself, t_tback,
      t_resid, t_dctx, t_sums) = middle(
         7, lengths, text_ctx, x_text, cot_text, text_norms, near, far, x_text.shape[0] // pairs, HEAD_T, 32
@@ -1533,59 +1676,73 @@
     rights = (t_fback, t_pback, t_bback, t_dself, t_tback)
     lefts, rights, far_both = lax.optimization_barrier((lefts, rights, far_both))
     text_mid = weight_grads((7, 8, 9, 10, 11), lefts, rights)
-    both = add(both_parts(*vis_pair, core), far_both)
-    far_both = lax.ppermute(both_parts(text_mid, text_pair, 1 - core), "seq", SWAP_CORE)
+    text_source = (text_at, text_mid)
+    both = both_sum(own_both, far_both)
+    own_both, far_both = pick_both(text_source, 6)
     back = (co_vis, co_text, v_dctx, t_dctx, v_resid, t_resid)
     back, lone, both, text_mid = lax.optimization_barrier((back, lone, both, text_mid))
-    for k, kept in enumerate(chunks_of(jnp.stack(lone), both)):
+    for k, kept in enumerate(chunks_of(lone, both)):
         chunks[k].state["kept", 1] = kept
-    lone = [group_lone(text_mid, text_pair + SHARD * i) for i in range(2)]
-    dco_vis, dco_text, grad_vis, grad_text, far_both = beside(
+    lone = group_lone(text_mid, text_pair)
+    def swap_halves(sources, owners):
+        plans = [half_plan(o, begins_of(sources), 1) for o in owners]
+        return [
+            lax.ppermute(part, "seq", SWAP_CORE) for part in pick(core, sources, plans, [R_HALF] * len(owners))
+        ]
+
+    dco_vis, dco_text, grad_vis, grad_text, far_both, far_half = beside(
         chunks,
         [(0, ("X", 1)), (0, ("N", 0))],
-        lambda: (*co_backward(lengths, *back, near, far), far_both),
-    )
-    vis_co, text_co = beside(
+        lambda: (*co_backward(lengths, *back, near, far), far_both, swap_halves([text_source], (5,))[0]),
+    )
+    late_sources = [vis_source, None, text_source]
+
+    def co_grads():
+        text_co = weight_grads((6,), (x_text,), (dco_text,))
+        late_sources[1] = (TILES[6][0], text_co)
+        return text_co, swap_halves(late_sources, (4,))[0], weight_grads((0,), (xv,), (dco_vis,))
+
+    text_co, far_four, vis_co = beside(
+        chunks, [(1, ("X", 1)), (0, ("Z", 1, 0)), (0, ("N", 1))], co_grads
+    )
+    early_sources = [(0, vis_co), vis_source]
+    late_sources[1] = (TILES[6][0], text_co)
+
+    def merge_late():
+        merge(core, late_sources, 2, [far_four, far_half], chunks)
+        return swap_halves(early_sources, (0, 1))
+
+    got = beside(chunks, [(0, ("Z", 1, 1)), (1, ("Z", 1, 0))], merge_late)
+    for k, kept in enumerate(chunks_of(lone, both_sum(own_both, far_both))):
+        chunks[k].state["kept", 3] = kept
+    beside(
         chunks,
-        [(1, ("X", 1)), (0, ("Z", 1, 0)), (0, ("N", 1))],
-        lambda: (weight_grads((0,), (xv,), (dco_vis,)), weight_grads((6,), (x_text,), (dco_text,))),
-    )
-    both = add(both_parts(text_mid, text_pair, core), far_both)
-    place = {
-        0: (vis_co, 0),
-        1: (jnp.concatenate([vis_co[SHARD:], vis_mid[: 2 * SHARD - vis_at]]), 0),
-        4: (jnp.concatenate([vis_mid[4 * SHARD - vis_at :], text_co, text_mid[: 5 * SHARD - text_at]]), 0),
-        5: (text_mid, 5 * SHARD - text_at),
-    }
-
-    def swap_halves(tasks, owners):
-        got = beside(
-            chunks, tasks, lambda: [lax.ppermute(half_of(place[o], 1 - core), "seq", SWAP_CORE) for o in owners]
-        )
-        pair_up([add(half_of(place[o], core), part) for o, part in zip(owners, got)], chunks, owners[0] // 2)
-
-    swap_halves([(0, ("Z", 1, 1)), (1, ("Z", 1, 0)), (0, ("N", 2))], (0, 1))
-    for k, kept in enumerate(chunks_of(jnp.stack(lone), both)):
-        chunks[k].state["kept", 3] = kept
-    swap_halves([(0, ("Y", 0)), (0, ("X", 3)), (1, ("Z", 1, 1))], (4, 5))
-    beside(chunks, [(0, ("Y", 2)), (0, ("X", 0)), (0, ("Z", 3, 0)), (1, ("X", 3)), (0, ("N", 3))], lambda: ())
-    chunks[1].step([("Y", 0), ("Z", 3, 0)])
-    chunks[0].step([("X", 2), ("Z", 0, 0), ("Z", 3, 1), ("N", 4)])
-    chunks[1].step([("Y", 2), ("X", 0), ("Z", 3, 1)])
-    chunks[0].step([("Z", 0, 1), ("Z", 2, 0), ("Z", 3, 2)])
-    chunks[1].step([("X", 2), ("Z", 0, 0), ("Z", 3, 2)])
-    chunks[0].step([("Z", 0, 2), ("Z", 2, 1)])
-    chunks[1].step([("Z", 0, 1), ("Z", 2, 0)])
+        [(0, ("Y", 2)), (0, ("X", 3)), (1, ("Z", 1, 1))],
+        lambda: merge(core, early_sources, 0, got, chunks),
+    )
+    beside(chunks, [(0, ("Y", 0)), (0, ("X", 2)), (0, ("Z", 3, 0)), (1, ("X", 3)), (0, ("N", 2))], lambda: ())
+    chunks[1].step([("Y", 2), ("Z", 3, 0)])
+    chunks[0].step([("X", 0), ("Z", 2, 0), ("Z", 3, 1), ("N", 3)])
+    chunks[1].step([("Y", 0), ("X", 2), ("Z", 3, 1)])
+    chunks[0].step([("Z", 0, 0), ("Z", 2, 1), ("Z", 3, 2), ("N", 4)])
+    chunks[1].step([("X", 0), ("Z", 2, 0), ("Z", 3, 2)])
+    chunks[0].step([("Z", 0, 1)])
+    chunks[1].step([("Z", 0, 0), ("Z", 2, 1)])
+    chunks[0].step([("Z", 0, 2)])
+    chunks[1].step([("Z", 0, 1)])
     chunks[0].step([("F", 0)])
-    beside(chunks, [(0, ("G", 0)), (1, ("Z", 0, 2)), (1, ("Z", 2, 1))], lambda: ())
+    chunks[0].step([("G", 0)])
     statistics = (master_blocks, stat_left, stat_right, root_left, root_right)
     early = chunk_pairs(0)
-    count = 3 * early.shape[0] // 4
+    count = early.shape[0] // 2
     owned = chunks[0].state["owned", 0]
-    renewed = beside(chunks, [(1, ("F", 0))], lambda: renew(early[:count], owned[: 2 * count], *statistics, ()))
     renewed = beside(
-        chunks, [(1, ("G", 0))], lambda: renew(early[count:], owned[2 * count :], *statistics, renewed)
-    )
+        chunks, [(1, ("Z", 0, 2))], lambda: renew(early[:count], owned[: 2 * count], *statistics, ())
+    )
+    renewed = beside(
+        chunks, [(1, ("F", 0))], lambda: renew(early[count:], owned[2 * count :], *statistics, renewed)
+    )
+    chunks[1].step([("G", 0)])
     grad_blocks, left_new, right_new, master_new = renew(
         chunk_pairs(1), chunks[1].state["owned", 0], *statistics, renewed
     )

time: 753 us -> 724 us (0.961)
  Pallas kernels: 187 us -> 237 us
  local copies, waits for them, and re-layouts: 81.2 us -> 47.7 us
  other arithmetic: 79.9 us -> 57.3 us
  waiting for transfers between devices: 269 us -> 251 us
    pallas_call x0 -> x9, Pallas kernels: none -> 49 us  [the longest x5 18.8 us: pick(): pl.pallas_call(functools.partial(pick_body, plans, len(arrays)), in_specs...]
    all_gather x1, waiting for transfers between devices: 43.7 us -> 0.01 us  [gather_tiles(): far = lax.all_gather(last, ('dp', 'seq'), axis=0, tiled=True)]
    ppermute x5, waiting for transfers between devices: 10.8 us -> 40.6 us  [send(): lax.ppermute(state['norms', 0], axis, [(i, i ^ step) for i in range(size)])]
    ppermute x4, waiting for transfers between devices: 11.2 us -> 37.9 us  [gather_tiles(): out['x'] = lax.ppermute(rows[phase], 'dp', SWAP_X)]
    ppermute x8, waiting for transfers between devices: 30.7 us -> 8.7 us  [send(): lax.ppermute(join([cut(lone, 1 - x, 1)[0], cut(both, 1 - x, 1)[0]]), 'dp'...]
    ppermute x4, waiting for transfers between devices: 39.3 us -> 59.4 us  [gather_tiles(): lax.ppermute(join([part[:G_LONE] for part in here]), 'seq', SWAP_Y)]
    ppermute x4, waiting for transfers between devices: 20.7 us -> 2.07 us  [send(): return lax.ppermute(cut(state['lone', who], 1 - y, 1)[0], 'seq', SWAP_Y)]
    slice x9 -> x2, local copies, waits for them, and re-layouts: 20.4 us -> 1.83 us  [chunks_of(): lone[:, LONE * k:LONE * (k + 1)]]
  transfers between devices with their start and end apart: 67 -> 65, of which waited for: 29 -> 30; matrix products, arithmetic and copies ran while one was open for 16% -> 13% of each run, Pallas kernels for 15% -> 20%
where the time goes in v4:
time: 724 us; the launch traced here: 717 us
  waiting for transfers between devices  251 us (35%)
  Pallas kernels  237 us (33%)
  starting transfers between devices  108 us (15%)
  other arithmetic  57.3 us (8%)
  local copies, waits for them, and re-layouts  47.7 us (7%)
  between operations  15.9 us (2%)
    ppermute x23, waiting for transfers between devices, along_z(): lax.ppermute(value, 'dp', [(2 * a + x, 2 * b + x) for a, b in moves for x...  81.1 us
    ppermute x4, waiting for transfers between devices, gather_tiles(): lax.ppermute(join([part[:G_LONE] for part in here]), 'seq', SWAP_Y)  59.4 us
    pallas_call x3, Pallas kernels, renew(): pl.pallas_call(functools.partial(renew_body, steps), in_specs=[pl.BlockSp...  54.8 us
    pallas_call x2, Pallas kernels, middle(): pl.pallas_call(functools.partial(middle_body, (begin, rows, span, head, c...  50.5 us
    ppermute x23, starting transfers between devices, along_z(): lax.ppermute(value, 'dp', [(2 * a + x, 2 * b + x) for a, b in moves for x...  47.9 us
    pallas_call x4, Pallas kernels, weight_grads(): pl.pallas_call(functools.partial(weight_body, kinds), in_specs=whole(2 *...  44.7 us
    ppermute x5, waiting for transfers between devices, send(): lax.ppermute(state['norms', 0], axis, [(i, i ^ step) for i in range(size)])  40.6 us
    ppermute x4, waiting for transfers between devices, gather_tiles(): out['x'] = lax.ppermute(rows[phase], 'dp', SWAP_X)  37.9 us
  transfers between devices with their start and end apart: 65, of which 30 were waited for; matrix products, arithmetic and copies ran while one was open for 13% of the time, Pallas kernels for 20%

profile of v4, /device:TPU:11, one launch (start us, length us, event | category | flops | bytes accessed | tf_op | source)
XLA Modules:
  0.0 716.9 jit_solution(7181412322335815317)
XLA Ops:
  7.7 5.2 shard_map.223
  13.7 5.2 shard_map.222
  20.5 22.8 %collective-permute-done = bf16[24,64,256]{2,1,0:T(8,128)(2,1)S(1)} collective-permute-done((bf16[24,64,256]{2,1,0:T(8,128)(2,1)}, bf16[24,64,256]{2,1,0:T(8,128)(2,1)S(1)}, u32[]{:S(2)}, u32[]{:S(2)}) %collective-permute-start) | collective-permute-done | bytes 786464 | tf_op jit(solution)/shard_map/ppermute | solution.py:1334
  43.3 8.7 %collective-permute-done.1 = bf16[24,64,256]{2,1,0:T(8,128)(2,1)} collective-permute-done((bf16[24,64,256]{2,1,0:T(8,128)(2,1)}, bf16[24,64,256]{2,1,0:T(8,128)(2,1)}, u32[]{:S(2)}, u32[]{:S(2)}) %collective-permute-start.1) | collective-permute-done | bytes 786464 | tf_op jit(solution)/shard_map/ppermute | solution.py:1281
  53.9 2.3 collective-permute-start.4
  58.6 14.3 %collective-permute-done.3 = bf16[16,64,256]{2,1,0:T(8,128)(2,1)S(1)} collective-permute-done((bf16[16,64,256]{2,1,0:T(8,128)(2,1)S(1)}, bf16[16,64,256]{2,1,0:T(8,128)(2,1)S(1)}, u32[]{:S(2)}, u32[]{:S(2)}) %collective-permute-start.3) | collective-permute-done | bytes 524320 | tf_op jit(solution)/shard_map/ppermute | solution.py:1337
  74.4 11.5 %collective-permute-done.4 = bf16[24,64,256]{2,1,0:T(8,128)(2,1)S(1)} collective-permute-done((bf16[24,64,256]{2,1,0:T(8,128)(2,1)}, bf16[24,64,256]{2,1,0:T(8,128)(2,1)S(1)}, u32[]{:S(2)}, u32[]{:S(2)}) %collective-permute-start.4) | collective-permute-done | bytes 786464 | tf_op jit(solution)/shard_map/ppermute | solution.py:1281
  87.7 15.6 %collective-permute-start.5 = (bf16[64,64,256]{2,1,0:T(8,128)(2,1)S(1)}, bf16[64,64,256]{2,1,0:T(8,128)(2,1)S(1)}, u32[]{:S(2)}, u32[]{:S(2)}) collective-permute-start(bf16[64,64,256]{2,1,0:T(8,128)(2,1)S(1)} %get-tuple-element.618), channel_id=1, source_target_pairs={{0,1},{1,0},{2,3},{3,2},{4,5},{5,4},{6,7},{7,6},{8,9},{9,8},{10,11... | collective-permute-start | bytes 6291464 | tf_op jit(solution)/shard_map/ppermute | solution.py:1339
  103.3 2.1 collective-permute-start.8
  108.9 10.6 %collective-permute-done.7 = bf16[16,64,256]{2,1,0:T(8,128)(2,1)S(1)} collective-permute-done((bf16[16,64,256]{2,1,0:T(8,128)(2,1)S(1)}, bf16[16,64,256]{2,1,0:T(8,128)(2,1)S(1)}, u32[]{:S(2)}, u32[]{:S(2)}) %collective-permute-start.7) | collective-permute-done | bytes 524320 | tf_op jit(solution)/shard_map/ppermute | solution.py:1337
  119.5 2.8 collective-permute-done.6
  131.1 23.5 %collective-permute-done.11 = bf16[16,64,256]{2,1,0:T(8,128)(2,1)S(1)} collective-permute-done((bf16[16,64,256]{2,1,0:T(8,128)(2,1)S(1)}, bf16[16,64,256]{2,1,0:T(8,128)(2,1)S(1)}, u32[]{:S(2)}, u32[]{:S(2)}) %collective-permute-start.11) | collective-permute-done | bytes 524320 | tf_op jit(solution)/shard_map/ppermute | solution.py:1337
  154.6 10.8 %collective-permute-done.10 = bf16[24,64,256]{2,1,0:T(8,128)(2,1)S(1)} collective-permute-done((bf16[24,64,256]{2,1,0:T(8,128)(2,1)S(1)}, bf16[24,64,256]{2,1,0:T(8,128)(2,1)S(1)}, u32[]{:S(2)}, u32[]{:S(2)}) %collective-permute-start.10) | collective-permute-done | bytes 786464 | tf_op jit(solution)/shard_map/ppermute | solution.py:1334
  179.6 2.4 bitcast_dynamic-update-slice_fusion.15
  188.0 11.1 %collective-permute-done.13 = bf16[16,64,256]{2,1,0:T(8,128)(2,1)S(1)} collective-permute-done((bf16[16,64,256]{2,1,0:T(8,128)(2,1)S(1)}, bf16[16,64,256]{2,1,0:T(8,128)(2,1)S(1)}, u32[]{:S(2)}, u32[]{:S(2)}) %collective-permute-start.13) | collective-permute-done | bytes 524320 | tf_op jit(solution)/shard_map/ppermute | solution.py:1337
  205.5 2.3 bitcast_dynamic-update-slice_fusion.6
  208.9 2.3 bitcast_dynamic-update-slice_fusion.4
  215.6 13.0 %shard_map.224 = (bf16[96,3072]{1,0:T(8,128)(2,1)}, bf16[256,3072]{1,0:T(8,128)(2,1)}, bf16[96,1024]{1,0:T(8,128)(2,1)}, bf16[256,1024]{1,0:T(8,128)(2,1)}) custom-call(s32[4]{0:T(128)} %concatenate.119.len_ref, bf16[96,1024]{1,0:T(8,128)(2,1)} %bitcast.278, bf16[256,768]{1,0:T(8,128)(2,1)} %refs_0_.1, bf16[512,64,256]{2,1,0:T(8,128)(2,1)} %bitcast.251, ...), custom_call_target="tpu_custom_call" | custom-call | bytes 74800000 | tf_op jit(solution)/shard_map/pallas_call | solution.py:881
  229.1 19.5 %shard_map.226 = (bf16[96,1024]{1,0:T(8,128)(2,1)}, bf16[96,1024]{1,0:T(8,128)(2,1)}, bf16[96,1024]{1,0:T(8,128)(2,1)}, bf16[96,1024]{1,0:T(8,128)(2,1)}, bf16[9...) custom-call(s32[2]{0:T(128)} %broadcast_1_len_ref.2.len_ref, ...), custom_call_target="tpu_custom_call" | custom-call | bytes 136000000 | tf_op jit(solution)/shard_map/pallas_call | solution.py:1186
  248.6 15.1 %shard_map.227.x_any.refs_0_.refs_1_ = bf16[448,64,256]{2,1,0:T(8,128)(2,1)} custom-call(bf16[96,1024]{1,0:T(8,128)(2,1)} %get-tuple-element.310.ctx_ref.refs_0_, bf16[96,1024]{1,0:T(8,128)(2,1)} %get-tuple-element.318.refs_1_, bf16[96,1024]{1,0:T(8,128)(2,1)} %get-tuple-element.319.refs_2_, bf16[96,1024]{1,0:T(8,128)(2,1)} %get-tuple-element.320.refs_3_, ...), custom_call_target="tpu_custom_call" | custom-call | bytes 60928000 | tf_op jit(solution)/shard_map/pallas_call | solution.py:1259
  263.8 6.1 shard_map.228
  270.0 3.7 shard_map.229
  275.1 31.0 %shard_map.225 = (bf16[256,768]{1,0:T(8,128)(2,1)}, bf16[256,768]{1,0:T(8,128)(2,1)}, bf16[256,3072]{1,0:T(8,128)(2,1)}, bf16[256,768]{1,0:T(8,128)(2,1)}, bf16[...) custom-call(s32[4]{0:T(128)} %concatenate.119.len_ref, ...), custom_call_target="tpu_custom_call" | custom-call | bytes 136000000 | tf_op jit(solution)/shard_map/pallas_call | solution.py:1186
  306.1 18.3 %shard_map.230.refs_0_.refs_2_.x_any = bf16[480,64,256]{2,1,0:T(8,128)(2,1)} custom-call(bf16[256,1024]{1,0:T(8,128)(2,1)} %get-tuple-element.339.ctx_ref.refs_0_, bf16[256,768]{1,0:T(8,128)(2,1)} %get-tuple-element.340.refs_1_, bf16[256,3072]{1,0:T(8,128)(2,1)} %get-tuple-element.341.refs_2_, bf16[256,768]{1,0:T(8,128)(2,1)} %get-tuple-element.342.refs_3_, ...), custom_call_target="tpu_custom_call" | custom-call | bytes 65280000 | tf_op jit(solution)/shard_map/pallas_call | solution.py:1259
  324.4 2.0 add_convert_fusion.1
  326.4 14.7 %reduce-scatter.3.cloned.1.call-done = bf16[56,64,256]{2,1,0:T(8,128)(2,1)} async-done(((bf16[224,64,256]{2,1,0:T(8,128)(2,1)}), bf16[56,64,256]{2,1,0:T(8,128)(2,1)}) %reduce-scatter.3.cloned.1.call-update) | async-done | bytes 1835024 | tf_op jit(solution)/shard_map/reduce_scatter | solution.py:1546
  341.1 6.1 shard_map.239
  347.3 3.2 shard_map.233
  351.2 3.7 shard_map.232
  358.7 14.2 %shard_map.231 = (bf16[96,3072]{1,0:T(8,128)(2,1)}, bf16[256,3072]{1,0:T(8,128)(2,1)}, f32[96,1024]{1,0:T(8,128)}, f32[256,768]{1,0:T(8,128)}) custom-call(s32[4]{0:T(128)} %concatenate.119.len_ref, bf16[96,3072]{1,0:T(8,128)(2,1)} %get-tuple-element.353.cv_ref, bf16[256,3072]{1,0:T(8,128)(2,1)} %get-tuple-element.354.ct_ref, ...), custom_call_target="tpu_custom_call" | custom-call | bytes 78200000 | tf_op jit(solution)/shard_map/pallas_call | solution.py:950
  372.9 5.2 collective-permute-done.16
  378.2 5.3 shard_map.234.refs_1_
  383.5 3.3 shard_map.235
  392.9 6.0 shard_map.236.refs_0_
  399.0 13.0 %collective-permute-done.21 = bf16[26,64,256]{2,1,0:T(8,128)(2,1)S(1)} collective-permute-done((bf16[26,64,256]{2,1,0:T(8,128)(2,1)S(1)}, bf16[26,64,256]{2,1,0:T(8,128)(2,1)S(1)}, u32[]{:S(2)}, u32[]{:S(2)}) %collective-permute-start.21) | collective-permute-done | bytes 852000 | tf_op jit(solution)/shard_map/ppermute | solution.py:1281
  412.7 5.0 shard_map.237
  423.2 2.5 add_convert_fusion
  428.2 8.9 %shard_map.238 = (bf16[2,2,14,64,256]{4,3,2,1,0:T(8,128)(2,1)}, bf16[2,12,64,256]{3,2,1,0:T(8,128)(2,1)}, bf16[2,2,14,64,256]{4,3,2,1,0:T(8,128)(2,1)}, bf16[2,12,64,256]{3,2,1,0:T(8,128)(2,1)}) custom-call(s32[1]{0:T(128)} %bitcast.26.core_ref, bf16[448,64,256]{2,1,0:T(8,128)(2,1)} %shard_map.227.x_any.refs_0_.refs_1_, ...), custom_call_target="tpu_custom_call" | custom-call | bytes 27200000 | tf_op jit(solution)/shard_map/pallas_call | solution.py:1488
  437.2 5.8 collective-permute-done.25
  452.4 9.0 %shard_map.240 = (bf16[2,2,14,64,256]{4,3,2,1,0:T(8,128)(2,1)}, bf16[2,12,64,256]{3,2,1,0:T(8,128)(2,1)}, bf16[2,2,14,64,256]{4,3,2,1,0:T(8,128)(2,1)}, bf16[2,12,64,256]{3,2,1,0:T(8,128)(2,1)}) custom-call(s32[1]{0:T(128)} %bitcast.26.core_ref, bf16[192,64,256]{2,1,0:T(8,128)(2,1)} %shard_map.236.refs_0_, ...), custom_call_target="tpu_custom_call" | custom-call | bytes 27200000 | tf_op jit(solution)/shard_map/pallas_call | solution.py:1488
  461.4 2.4 add_convert_fusion.25
  463.8 3.8 collective-permute-done.30
  467.6 2.1 collective-permute-done.28
  481.1 27.8 %collective-permute-done.35 = f32[2,5376]{1,0:T(2,128)S(1)} collective-permute-done((f32[2,5376]{1,0:T(2,128)S(1)}, f32[2,5376]{1,0:T(2,128)S(1)}, u32[]{:S(2)}, u32[]{:S(2)}) %collective-permute-start.35) | collective-permute-done | bytes 43040 | tf_op jit(solution)/shard_map/ppermute | solution.py:1583
  509.2 4.4 collective-permute-start.50
  516.4 2.2 collective-permute-start.51
  520.8 12.8 %collective-permute-done.51 = f32[2,5376]{1,0:T(2,128)S(1)} collective-permute-done((f32[2,5376]{1,0:T(2,128)S(1)}, f32[2,5376]{1,0:T(2,128)S(1)}, u32[]{:S(2)}, u32[]{:S(2)}) %collective-permute-start.51) | collective-permute-done | bytes 43040 | tf_op jit(solution)/shard_map/ppermute | solution.py:1583
  535.8 6.0 collective-permute-start.53
  542.2 9.7 %collective-permute-done.37 = bf16[26,64,256]{2,1,0:T(8,128)(2,1)S(1)} collective-permute-done((bf16[26,64,256]{2,1,0:T(8,128)(2,1)S(1)}, bf16[26,64,256]{2,1,0:T(8,128)(2,1)S(1)}, u32[]{:S(2)}, u32[]{:S(2)}) %collective-permute-start.37) | collective-permute-done | bytes 852000 | tf_op jit(solution)/shard_map/ppermute | solution.py:1281
  557.7 16.8 %collective-permute-done.40 = bf16[26,64,256]{2,1,0:T(8,128)(2,1)S(1)} collective-permute-done((bf16[26,64,256]{2,1,0:T(8,128)(2,1)S(1)}, bf16[26,64,256]{2,1,0:T(8,128)(2,1)S(1)}, u32[]{:S(2)}, u32[]{:S(2)}) %collective-permute-start.40) | collective-permute-done | bytes 852000 | tf_op jit(solution)/shard_map/ppermute | solution.py:1281
  583.5 5.8 collective-permute-start.57
  589.3 3.5 collective-permute-done.42
  595.4 4.9 collective-permute-start.45
  602.6 2.1 select_select_fusion.1
  607.0 4.1 collective-permute-done.45
  612.8 4.9 collective-permute-done.58
  618.0 8.6 %collective-permute-start.59 = (bf16[40,64,256]{2,1,0:T(8,128)(2,1)S(1)}, bf16[40,64,256]{2,1,0:T(8,128)(2,1)}, u32[]{:S(2)}, u32[]{:S(2)}) collective-permute-start(bf16[40,64,256]{2,1,0:T(8,128)(2,1)S(1)} %pad_maximum_fusion.1), channel_id=1, source_target_pairs={{0,1},{1,0},{2,3},{3,2},{4,5},{5,4},{6,7},{7,6},{8,9},{9,8},{10,11... | collective-permute-start | bytes 3932168 | tf_op jit(solution)/shard_map/ppermute | solution.py:1580
  630.2 2.4 collective-permute-start.47
  632.6 3.0 broadcast_select_fusion.2
  635.6 14.5 %shard_map.241 = (f32[20224,128]{1,0:T(8,128)}, f32[20224,128]{1,0:T(8,128)}, f32[20224,128]{1,0:T(8,128)}, f32[20224,128]{1,0:T(8,128)}) custom-call(s32[20]{0:T(128)} %constant.168.which_ref, bf16[40,64,256]{2,1,0:T(8,128)(2,1)} %get-tuple-element.592.g_any, f32[20224,128]{1,0:T(8,128)} %bitcast.257, f32[20224,128]{1,0:T(8,128)} %bitcast.260, ...), custom_call_target="tpu_custom_call" | custom-call | bytes 47600000 | tf_op jit(solution)/shard_map/pallas_call | solution.py:736
  650.2 2.1 select_select_fusion
  655.8 14.4 %shard_map.242 = (f32[20224,128]{1,0:T(8,128)}, f32[20224,128]{1,0:T(8,128)}, f32[20224,128]{1,0:T(8,128)}, f32[20224,128]{1,0:T(8,128)}) custom-call(s32[20]{0:T(128)} %constant.169.which_ref, bf16[40,64,256]{2,1,0:T(8,128)(2,1)} %get-tuple-element.591.g_any, ...), custom_call_target="tpu_custom_call", output_to_operand_aliasing={{0}: (7, {}), {1}: (8, {}), {2}: (9, {}), {3}: (10, {})} | custom-call | bytes 47600000 | tf_op jit(solution)/shard_map/pallas_call | solution.py:736
  670.5 9.1 %collective-permute-start.61 = (bf16[40,64,256]{2,1,0:T(8,128)(2,1)S(1)}, bf16[40,64,256]{2,1,0:T(8,128)(2,1)S(1)}, u32[]{:S(2)}, u32[]{:S(2)}) collective-permute-start(bf16[40,64,256]{2,1,0:T(8,128)(2,1)S(1)} %pad_maximum_fusion.2), channel_id=1, source_target_pairs={{0,1},{1,0},{2,3},{3,2},{4,5},{5,4},{6,7},{7,6},{8,9},{9,8},{10,11... | collective-permute-start | bytes 3932168 | tf_op jit(solution)/shard_map/ppermute | solution.py:1580
  684.3 25.9 %shard_map.243 = (f32[20224,128]{1,0:T(8,128)}, f32[20224,128]{1,0:T(8,128)}, f32[20224,128]{1,0:T(8,128)}, f32[20224,128]{1,0:T(8,128)}) custom-call(s32[40]{0:T(128)} %constant.158.clone.which_ref, bf16[80,64,256]{2,1,0:T(8,128)(2,1)} %pad_maximum_fusion.g_any, ...), custom_call_target="tpu_custom_call", output_to_operand_aliasing={{0}: (7, {}), {1}: (8, {}), {2}: (9, {}), {3}: (10, {})} | custom-call | bytes 95200000 | tf_op jit(solution)/shard_map/pallas_call | solution.py:736
  (389 shorter events, 139.5 us)
Async XLA Ops:
  7.2 208.4 %all-gather.2.cloned.1.call-start = ((), (), s32[]{:S(2)}) async-start(), calls=%async_computation.2 | async-start | bytes 25952256 | tf_op jit(solution)/shard_map/all_gather | solution.py:1323
  13.0 328.1 %reduce-scatter.3.cloned.1.call-start = ((), (), s32[]{:S(2)}) async-start(), calls=%async_computation.3 | async-start | bytes 9175040 | tf_op jit(solution)/shard_map/reduce_scatter | solution.py:1546
  18.9 24.4 %collective-permute-start = (bf16[24,64,256]{2,1,0:T(8,128)(2,1)}, bf16[24,64,256]{2,1,0:T(8,128)(2,1)S(1)}, u32[]{:S(2)}, u32[]{:S(2)}) collective-permute-start(bf16[24,64,256]{2,1,0:T(8,128)(2,1)} %shard_map.222), channel_id=1, source_target_pairs={{0,4},{4,0},{8,12},{12,8},{16,20},{20,16},{24,28},{28,24},{1,5},{5... | collective-permute-start | bytes 2359304 | tf_op jit(solution)/shard_map/ppermute | solution.py:1334
  19.2 32.8 %collective-permute-start.1 = (bf16[24,64,256]{2,1,0:T(8,128)(2,1)}, bf16[24,64,256]{2,1,0:T(8,128)(2,1)}, u32[]{:S(2)}, u32[]{:S(2)}) collective-permute-start(bf16[24,64,256]{2,1,0:T(8,128)(2,1)} %shard_map.222), channel_id=1, source_target_pairs={{0,8},{4,12},{8,16},{12,20},{16,24},{20,28},{24,0},{28,4},{1,9},{5... | collective-permute-start | bytes 2359304 | tf_op jit(solution)/shard_map/ppermute | solution.py:1281
  52.0 22.4 %collective-permute-start.2 = (bf16[24,64,256]{2,1,0:T(8,128)(2,1)}, bf16[24,64,256]{2,1,0:T(8,128)(2,1)S(1)}, u32[]{:S(2)}, u32[]{:S(2)}) collective-permute-start(bf16[24,64,256]{2,1,0:T(8,128)(2,1)} %collective-permute-done.1), channel_id=1, source_target_pairs={{0,4},{4,0},{8,12},{12,8},{16,20},{20,16},{24,28},{28,24},{1,5},{5... | collective-permute-start | bytes 2359304 | tf_op jit(solution)/shard_map/ppermute | solution.py:1334
  53.9 32.0 %collective-permute-start.4 = (bf16[24,64,256]{2,1,0:T(8,128)(2,1)}, bf16[24,64,256]{2,1,0:T(8,128)(2,1)S(1)}, u32[]{:S(2)}, u32[]{:S(2)}) collective-permute-start(bf16[24,64,256]{2,1,0:T(8,128)(2,1)} %collective-permute-done.1), channel_id=1, source_target_pairs={{0,8},{4,12},{8,16},{12,20},{16,24},{20,28},{24,0},{28,4},{1,9},{5... | collective-permute-start | bytes 2359304 | tf_op jit(solution)/shard_map/ppermute | solution.py:1281
  57.3 15.6 %collective-permute-start.3 = (bf16[16,64,256]{2,1,0:T(8,128)(2,1)S(1)}, bf16[16,64,256]{2,1,0:T(8,128)(2,1)S(1)}, u32[]{:S(2)}, u32[]{:S(2)}) collective-permute-start(bf16[16,64,256]{2,1,0:T(8,128)(2,1)S(1)} %pad_maximum_fusion.19), channel_id=1, source_target_pairs={{0,2},{1,3},{2,0},{3,1},{4,6},{5,7},{6,4},{7,5},{8,10},{9,11},{10,... | collective-permute-start | bytes 1572872 | tf_op jit(solution)/shard_map/ppermute | solution.py:1337
  87.7 36.6 %collective-permute-start.5 = (bf16[64,64,256]{2,1,0:T(8,128)(2,1)S(1)}, bf16[64,64,256]{2,1,0:T(8,128)(2,1)S(1)}, u32[]{:S(2)}, u32[]{:S(2)}) collective-permute-start(bf16[64,64,256]{2,1,0:T(8,128)(2,1)S(1)} %get-tuple-element.618), channel_id=1, source_target_pairs={{0,1},{1,0},{2,3},{3,2},{4,5},{5,4},{6,7},{7,6},{8,9},{9,8},{10,11... | collective-permute-start | bytes 6291464 | tf_op jit(solution)/shard_map/ppermute | solution.py:1339
  103.3 19.1 %collective-permute-start.6 = (bf16[24,64,256]{2,1,0:T(8,128)(2,1)S(1)}, bf16[24,64,256]{2,1,0:T(8,128)(2,1)S(1)}, u32[]{:S(2)}, u32[]{:S(2)}) collective-permute-start(bf16[24,64,256]{2,1,0:T(8,128)(2,1)S(1)} %collective-permute-done.4), channel_id=1, source_target_pairs={{0,4},{4,0},{8,12},{12,8},{16,20},{20,16},{24,28},{28,24},{1,5},{5... | collective-permute-start | bytes 2359304 | tf_op jit(solution)/shard_map/ppermute | solution.py:1334
  103.3 21.0 %collective-permute-start.8 = (bf16[24,64,256]{2,1,0:T(8,128)(2,1)S(1)}, bf16[24,64,256]{2,1,0:T(8,128)(2,1)S(1)}, u32[]{:S(2)}, u32[]{:S(2)}) collective-permute-start(bf16[24,64,256]{2,1,0:T(8,128)(2,1)S(1)} %collective-permute-done.4), channel_id=1, source_target_pairs={{0,8},{4,12},{8,16},{12,20},{16,24},{20,28},{24,0},{28,4},{1,9},{5... | collective-permute-start | bytes 2359304 | tf_op jit(solution)/shard_map/ppermute | solution.py:1281
  106.4 13.1 %collective-permute-start.7 = (bf16[16,64,256]{2,1,0:T(8,128)(2,1)S(1)}, bf16[16,64,256]{2,1,0:T(8,128)(2,1)S(1)}, u32[]{:S(2)}, u32[]{:S(2)}) collective-permute-start(bf16[16,64,256]{2,1,0:T(8,128)(2,1)S(1)} %pad_maximum_fusion.20), channel_id=1, source_target_pairs={{0,2},{1,3},{2,0},{3,1},{4,6},{5,7},{6,4},{7,5},{8,10},{9,11},{10,... | collective-permute-start | bytes 1572872 | tf_op jit(solution)/shard_map/ppermute | solution.py:1337
  128.3 37.0 %collective-permute-start.9 = (bf16[64,64,256]{2,1,0:T(8,128)(2,1)S(1)}, bf16[64,64,256]{2,1,0:T(8,128)(2,1)S(1)}, u32[]{:S(2)}, u32[]{:S(2)}) collective-permute-start(bf16[64,64,256]{2,1,0:T(8,128)(2,1)S(1)} %get-tuple-element.614), channel_id=1, source_target_pairs={{0,1},{1,0},{2,3},{3,2},{4,5},{5,4},{6,7},{7,6},{8,9},{9,8},{10,11... | collective-permute-start | bytes 6291464 | tf_op jit(solution)/shard_map/ppermute | solution.py:1339
  129.0 36.3 %collective-permute-start.10 = (bf16[24,64,256]{2,1,0:T(8,128)(2,1)S(1)}, bf16[24,64,256]{2,1,0:T(8,128)(2,1)S(1)}, u32[]{:S(2)}, u32[]{:S(2)}) collective-permute-start(bf16[24,64,256]{2,1,0:T(8,128)(2,1)S(1)} %collective-permute-done.8), channel_id=1, source_target_pairs={{0,4},{4,0},{8,12},{12,8},{16,20},{20,16},{24,28},{28,24},{1,5},{5... | collective-permute-start | bytes 2359304 | tf_op jit(solution)/shard_map/ppermute | solution.py:1334
  129.5 25.1 %collective-permute-start.11 = (bf16[16,64,256]{2,1,0:T(8,128)(2,1)S(1)}, bf16[16,64,256]{2,1,0:T(8,128)(2,1)S(1)}, u32[]{:S(2)}, u32[]{:S(2)}) collective-permute-start(bf16[16,64,256]{2,1,0:T(8,128)(2,1)S(1)} %pad_maximum_fusion.21), channel_id=1, source_target_pairs={{0,2},{1,3},{2,0},{3,1},{4,6},{5,7},{6,4},{7,5},{8,10},{9,11},{10,... | collective-permute-start | bytes 1572872 | tf_op jit(solution)/shard_map/ppermute | solution.py:1337
  171.1 27.9 %collective-permute-start.12 = (bf16[64,64,256]{2,1,0:T(8,128)(2,1)}, bf16[64,64,256]{2,1,0:T(8,128)(2,1)}, u32[]{:S(2)}, u32[]{:S(2)}) collective-permute-start(bf16[64,64,256]{2,1,0:T(8,128)(2,1)} %get-tuple-element.610), channel_id=1, source_target_pairs={{0,1},{1,0},{2,3},{3,2},{4,5},{5,4},{6,7},{7,6},{8,9},{9,8},{10,11... | collective-permute-start | bytes 6291464 | tf_op jit(solution)/shard_map/ppermute | solution.py:1339
  185.4 13.7 %collective-permute-start.13 = (bf16[16,64,256]{2,1,0:T(8,128)(2,1)S(1)}, bf16[16,64,256]{2,1,0:T(8,128)(2,1)S(1)}, u32[]{:S(2)}, u32[]{:S(2)}) collective-permute-start(bf16[16,64,256]{2,1,0:T(8,128)(2,1)S(1)} %pad_maximum_fusion.22), channel_id=1, source_target_pairs={{0,2},{1,3},{2,0},{3,1},{4,6},{5,7},{6,4},{7,5},{8,10},{9,11},{10,... | collective-permute-start | bytes 1572872 | tf_op jit(solution)/shard_map/ppermute | solution.py:1337
  199.6 11.5 %collective-permute-start.14 = (bf16[64,64,256]{2,1,0:T(8,128)(2,1)S(1)}, bf16[64,64,256]{2,1,0:T(8,128)(2,1)S(1)}, u32[]{:S(2)}, u32[]{:S(2)}) collective-permute-start(bf16[64,64,256]{2,1,0:T(8,128)(2,1)S(1)} %get-tuple-element.606), channel_id=1, source_target_pairs={{0,1},{1,0},{2,3},{3,2},{4,5},{5,4},{6,7},{7,6},{8,9},{9,8},{10,11... | collective-permute-start | bytes 6291464 | tf_op jit(solution)/shard_map/ppermute | solution.py:1339
  269.9 179.5 %reduce-scatter.5.cloned.1.call-start = ((), (), s32[]{:S(2)}) async-start(), calls=%async_computation.4 | async-start | bytes 9175040 | tf_op jit(solution)/shard_map/reduce_scatter | solution.py:1546
  273.6 32.4 %collective-permute-start.15 = (bf16[48,64,256]{2,1,0:T(8,128)(2,1)}, bf16[48,64,256]{2,1,0:T(8,128)(2,1)S(1)}, u32[]{:S(2)}, u32[]{:S(2)}) collective-permute-start(bf16[48,64,256]{2,1,0:T(8,128)(2,1)} %get-tuple-element.337), channel_id=1, source_target_pairs={{0,1},{1,0},{2,3},{3,2},{4,5},{5,4},{6,7},{7,6},{8,9},{9,8},{10,11... | collective-permute-start | bytes 4718600 | tf_op jit(solution)/shard_map/ppermute | solution.py:1664
  350.5 22.4 %collective-permute-start.19 = (bf16[80,64,256]{2,1,0:T(8,128)(2,1)}, bf16[80,64,256]{2,1,0:T(8,128)(2,1)}, u32[]{:S(2)}, u32[]{:S(2)}) collective-permute-start(bf16[80,64,256]{2,1,0:T(8,128)(2,1)} %shard_map.233), channel_id=1, source_target_pairs={{0,1},{1,0},{2,3},{3,2},{4,5},{5,4},{6,7},{7,6},{8,9},{9,8},{10,11... | collective-permute-start | bytes 7864328 | tf_op jit(solution)/shard_map/ppermute | solution.py:1690
  354.9 18.0 %collective-permute-start.18 = (bf16[48,64,256]{2,1,0:T(8,128)(2,1)}, bf16[48,64,256]{2,1,0:T(8,128)(2,1)}, u32[]{:S(2)}, u32[]{:S(2)}) collective-permute-start(bf16[48,64,256]{2,1,0:T(8,128)(2,1)} %get-tuple-element.363), channel_id=1, source_target_pairs={{0,1},{1,0},{2,3},{3,2},{4,5},{5,4},{6,7},{7,6},{8,9},{9,8},{10,11... | collective-permute-start | bytes 4718600 | tf_op jit(solution)/shard_map/ppermute | solution.py:1664
  357.6 20.5 %collective-permute-start.16 = (bf16[26,64,256]{2,1,0:T(8,128)(2,1)}, bf16[26,64,256]{2,1,0:T(8,128)(2,1)}, u32[]{:S(2)}, u32[]{:S(2)}) collective-permute-start(bf16[26,64,256]{2,1,0:T(8,128)(2,1)} %pad_maximum_fusion.11), channel_id=1, source_target_pairs={{0,4},{4,0},{8,12},{12,8},{16,20},{20,16},{24,28},{28,24},{1,5},{5... | collective-permute-start | bytes 2555912 | tf_op jit(solution)/shard_map/ppermute | solution.py:1571
  358.0 14.9 %collective-permute-start.17 = (f32[2,5376]{1,0:T(2,128)S(1)}, f32[2,5376]{1,0:T(2,128)S(1)}, u32[]{:S(2)}, u32[]{:S(2)}) collective-permute-start(f32[2,5376]{1,0:T(2,128)S(1)} %constant_dynamic-update-slice_fusion.24), channel_id=1, source_target_pairs={{0,1},{1,0},{2,3},{3,2},{4,5},{5,4},{6,7},{7,6},{8,9},{9,8},{10,11... | collective-permute-start | bytes 129032 | tf_op jit(solution)/shard_map/ppermute | solution.py:1583
  386.8 25.9 %collective-permute-start.23 = (bf16[80,64,256]{2,1,0:T(8,128)(2,1)}, bf16[80,64,256]{2,1,0:T(8,128)(2,1)}, u32[]{:S(2)}, u32[]{:S(2)}) collective-permute-start(bf16[80,64,256]{2,1,0:T(8,128)(2,1)} %shard_map.235), channel_id=1, source_target_pairs={{0,1},{1,0},{2,3},{3,2},{4,5},{5,4},{6,7},{7,6},{8,9},{9,8},{10,11... | collective-permute-start | bytes 7864328 | tf_op jit(solution)/shard_map/ppermute | solution.py:1690
  389.5 22.5 %collective-permute-start.21 = (bf16[26,64,256]{2,1,0:T(8,128)(2,1)S(1)}, bf16[26,64,256]{2,1,0:T(8,128)(2,1)S(1)}, u32[]{:S(2)}, u32[]{:S(2)}) collective-permute-start(bf16[26,64,256]{2,1,0:T(8,128)(2,1)S(1)} %add_convert_fusion.29), channel_id=1, source_target_pairs={{24,16},{28,20},{0,8},{4,12},{25,17},{29,21},{1,9},{5,13},{26,18},... | collective-permute-start | bytes 2555912 | tf_op jit(solution)/shard_map/ppermute | solution.py:1281
  391.8 20.9 %collective-permute-start.20 = (bf16[26,64,256]{2,1,0:T(8,128)(2,1)}, bf16[26,64,256]{2,1,0:T(8,128)(2,1)}, u32[]{:S(2)}, u32[]{:S(2)}) collective-permute-start(bf16[26,64,256]{2,1,0:T(8,128)(2,1)} %pad_maximum_fusion.12), channel_id=1, source_target_pairs={{0,4},{4,0},{8,12},{12,8},{16,20},{20,16},{24,28},{28,24},{1,5},{5... | collective-permute-start | bytes 2555912 | tf_op jit(solution)/shard_map/ppermute | solution.py:1571
  392.2 6.8 collective-permute-start.22
  417.7 26.3 %collective-permute-start.26 = (bf16[80,64,256]{2,1,0:T(8,128)(2,1)}, bf16[80,64,256]{2,1,0:T(8,128)(2,1)}, u32[]{:S(2)}, u32[]{:S(2)}) collective-permute-start(bf16[80,64,256]{2,1,0:T(8,128)(2,1)} %get-tuple-element.381), channel_id=1, source_target_pairs={{0,1},{1,0},{2,3},{3,2},{4,5},{5,4},{6,7},{7,6},{8,9},{9,8},{10,11... | collective-permute-start | bytes 7864328 | tf_op jit(solution)/shard_map/ppermute | solution.py:1690
  418.6 25.4 %collective-permute-start.27 = (bf16[80,64,256]{2,1,0:T(8,128)(2,1)}, bf16[80,64,256]{2,1,0:T(8,128)(2,1)}, u32[]{:S(2)}, u32[]{:S(2)}) collective-permute-start(bf16[80,64,256]{2,1,0:T(8,128)(2,1)} %get-tuple-element.382), channel_id=1, source_target_pairs={{0,1},{1,0},{2,3},{3,2},{4,5},{5,4},{6,7},{7,6},{8,9},{9,8},{10,11... | collective-permute-start | bytes 7864328 | tf_op jit(solution)/shard_map/ppermute | solution.py:1690
  420.3 22.7 %collective-permute-start.25 = (bf16[26,64,256]{2,1,0:T(8,128)(2,1)S(1)}, bf16[26,64,256]{2,1,0:T(8,128)(2,1)}, u32[]{:S(2)}, u32[]{:S(2)}) collective-permute-start(bf16[26,64,256]{2,1,0:T(8,128)(2,1)S(1)} %add_convert_fusion.27), channel_id=1, source_target_pairs={{24,16},{28,20},{0,8},{4,12},{25,17},{29,21},{1,9},{5,13},{26,18},... | collective-permute-start | bytes 2555912 | tf_op jit(solution)/shard_map/ppermute | solution.py:1281
  421.9 22.1 %collective-permute-start.24 = (bf16[26,64,256]{2,1,0:T(8,128)(2,1)S(1)}, bf16[26,64,256]{2,1,0:T(8,128)(2,1)S(1)}, u32[]{:S(2)}, u32[]{:S(2)}) collective-permute-start(bf16[26,64,256]{2,1,0:T(8,128)(2,1)S(1)} %add_convert_fusion.28), channel_id=1, source_target_pairs={{16,8},{20,12},{17,9},{21,13},{18,10},{22,14},{19,11},{23,15}} | collective-permute-start | bytes 2555912 | tf_op jit(solution)/shard_map/ppermute | solution.py:1281
  446.3 21.3 %collective-permute-start.30 = (bf16[26,64,256]{2,1,0:T(8,128)(2,1)S(1)}, bf16[26,64,256]{2,1,0:T(8,128)(2,1)}, u32[]{:S(2)}, u32[]{:S(2)}) collective-permute-start(bf16[26,64,256]{2,1,0:T(8,128)(2,1)S(1)} %add_convert_fusion.26), channel_id=1, source_target_pairs={{16,8},{20,12},{17,9},{21,13},{18,10},{22,14},{19,11},{23,15}} | collective-permute-start | bytes 2555912 | tf_op jit(solution)/shard_map/ppermute | solution.py:1281
  448.7 21.0 %collective-permute-start.28 = (bf16[2,14,64,256]{3,2,1,0:T(8,128)(2,1)}, bf16[2,14,64,256]{3,2,1,0:T(8,128)(2,1)}, u32[]{:S(2)}, u32[]{:S(2)}) collective-permute-start(bf16[2,14,64,256]{3,2,1,0:T(8,128)(2,1)} %dynamic-slice_bitcast_fusion.3), channel_id=1, source_target_pairs={{0,2},{1,3},{2,0},{3,1},{4,6},{5,7},{6,4},{7,5},{8,10},{9,11},{10,... | collective-permute-start | bytes 2752520 | tf_op jit(solution)/shard_map/ppermute | solution.py:1568
  452.1 19.3 %collective-permute-start.29 = (bf16[26,64,256]{2,1,0:T(8,128)(2,1)}, bf16[26,64,256]{2,1,0:T(8,128)(2,1)}, u32[]{:S(2)}, u32[]{:S(2)}) collective-permute-start(bf16[26,64,256]{2,1,0:T(8,128)(2,1)} %pad_maximum_fusion.13), channel_id=1, source_target_pairs={{0,4},{4,0},{8,12},{12,8},{16,20},{20,16},{24,28},{28,24},{1,5},{5... | collective-permute-start | bytes 2555912 | tf_op jit(solution)/shard_map/ppermute | solution.py:1571
  471.6 37.3 %collective-permute-start.34 = (bf16[26,64,256]{2,1,0:T(8,128)(2,1)S(1)}, bf16[26,64,256]{2,1,0:T(8,128)(2,1)S(1)}, u32[]{:S(2)}, u32[]{:S(2)}) collective-permute-start(bf16[26,64,256]{2,1,0:T(8,128)(2,1)S(1)} %pad_maximum_fusion.15), channel_id=1, source_target_pairs={{0,4},{4,0},{8,12},{12,8},{16,20},{20,16},{24,28},{28,24},{1,5},{5... | collective-permute-start | bytes 2555912 | tf_op jit(solution)/shard_map/ppermute | solution.py:1571
  474.0 34.9 %collective-permute-start.33 = (bf16[26,64,256]{2,1,0:T(8,128)(2,1)S(1)}, bf16[26,64,256]{2,1,0:T(8,128)(2,1)S(1)}, u32[]{:S(2)}, u32[]{:S(2)}) collective-permute-start(bf16[26,64,256]{2,1,0:T(8,128)(2,1)S(1)} %add_convert_fusion.24), channel_id=1, source_target_pairs={{0,8},{4,12},{1,9},{5,13},{2,10},{6,14},{3,11},{7,15}} | collective-permute-start | bytes 2555912 | tf_op jit(solution)/shard_map/ppermute | solution.py:1281
  477.2 31.7 %collective-permute-start.31 = (bf16[2,14,64,256]{3,2,1,0:T(8,128)(2,1)S(1)}, bf16[2,14,64,256]{3,2,1,0:T(8,128)(2,1)S(1)}, u32[]{:S(2)}, u32[]{:S(2)}) collective-permute-start(bf16[2,14,64,256]{3,2,1,0:T(8,128)(2,1)S(1)} %dynamic-slice_bitcast_fusion.2), channel_id=1, source_target_pairs={{0,2},{1,3},{2,0},{3,1},{4,6},{5,7},{6,4},{7,5},{8,10},{9,11},{10,... | collective-permute-start | bytes 2752520 | tf_op jit(solution)/shard_map/ppermute | solution.py:1568
  478.1 30.8 %collective-permute-start.32 = (bf16[26,64,256]{2,1,0:T(8,128)(2,1)S(1)}, bf16[26,64,256]{2,1,0:T(8,128)(2,1)S(1)}, u32[]{:S(2)}, u32[]{:S(2)}) collective-permute-start(bf16[26,64,256]{2,1,0:T(8,128)(2,1)S(1)} %pad_maximum_fusion.14), channel_id=1, source_target_pairs={{0,4},{4,0},{8,12},{12,8},{16,20},{20,16},{24,28},{28,24},{1,5},{5... | collective-permute-start | bytes 2555912 | tf_op jit(solution)/shard_map/ppermute | solution.py:1571
  478.8 30.1 %collective-permute-start.35 = (f32[2,5376]{1,0:T(2,128)S(1)}, f32[2,5376]{1,0:T(2,128)S(1)}, u32[]{:S(2)}, u32[]{:S(2)}) collective-permute-start(f32[2,5376]{1,0:T(2,128)S(1)} %copy-done.46), channel_id=1, source_target_pairs={{0,4},{4,0},{8,12},{12,8},{16,20},{20,16},{24,28},{28,24},{1,5},{5... | collective-permute-start | bytes 129032 | tf_op jit(solution)/shard_map/ppermute | solution.py:1583
  509.2 25.1 %collective-permute-start.50 = (bf16[26,64,256]{2,1,0:T(8,128)(2,1)S(1)}, bf16[26,64,256]{2,1,0:T(8,128)(2,1)S(1)}, u32[]{:S(2)}, u32[]{:S(2)}) collective-permute-start(bf16[26,64,256]{2,1,0:T(8,128)(2,1)S(1)} %add_convert_fusion.11), channel_id=1, source_target_pairs={{8,16},{12,20},{9,17},{13,21},{10,18},{14,22},{11,19},{15,23}} | collective-permute-start | bytes 2555912 | tf_op jit(solution)/shard_map/ppermute | solution.py:1281
  514.0 20.3 %collective-permute-start.49 = (bf16[26,64,256]{2,1,0:T(8,128)(2,1)S(1)}, bf16[26,64,256]{2,1,0:T(8,128)(2,1)S(1)}, u32[]{:S(2)}, u32[]{:S(2)}) collective-permute-start(bf16[26,64,256]{2,1,0:T(8,128)(2,1)S(1)} %add_convert_fusion.12), channel_id=1, source_target_pairs={{0,8},{4,12},{24,16},{28,20},{1,9},{5,13},{25,17},{29,21},{2,10},{... | collective-permute-start | bytes 2555912 | tf_op jit(solution)/shard_map/ppermute | solution.py:1281
  516.0 18.4 %collective-permute-start.48 = (bf16[26,64,256]{2,1,0:T(8,128)(2,1)S(1)}, bf16[26,64,256]{2,1,0:T(8,128)(2,1)S(1)}, u32[]{:S(2)}, u32[]{:S(2)}) collective-permute-start(bf16[26,64,256]{2,1,0:T(8,128)(2,1)S(1)} %pad_maximum_fusion.18), channel_id=1, source_target_pairs={{0,4},{4,0},{8,12},{12,8},{16,20},{20,16},{24,28},{28,24},{1,5},{5... | collective-permute-start | bytes 2555912 | tf_op jit(solution)/shard_map/ppermute | solution.py:1571
  516.4 17.2 %collective-permute-start.51 = (f32[2,5376]{1,0:T(2,128)S(1)}, f32[2,5376]{1,0:T(2,128)S(1)}, u32[]{:S(2)}, u32[]{:S(2)}) collective-permute-start(f32[2,5376]{1,0:T(2,128)S(1)} %add.410), channel_id=1, source_target_pairs={{0,8},{4,12},{8,0},{12,4},{16,24},{20,28},{24,16},{28,20},{1,9},{5... | collective-permute-start | bytes 129032 | tf_op jit(solution)/shard_map/ppermute | solution.py:1583
  519.0 32.9 %collective-permute-start.37 = (bf16[26,64,256]{2,1,0:T(8,128)(2,1)S(1)}, bf16[26,64,256]{2,1,0:T(8,128)(2,1)S(1)}, u32[]{:S(2)}, u32[]{:S(2)}) collective-permute-start(bf16[26,64,256]{2,1,0:T(8,128)(2,1)S(1)} %add_convert_fusion.22), channel_id=1, source_target_pairs={{0,8},{4,12},{1,9},{5,13},{2,10},{6,14},{3,11},{7,15}} | collective-permute-start | bytes 2555912 | tf_op jit(solution)/shard_map/ppermute | solution.py:1281
  533.6 19.0 %collective-permute-start.36 = (bf16[2,14,64,256]{3,2,1,0:T(8,128)(2,1)S(1)}, bf16[2,14,64,256]{3,2,1,0:T(8,128)(2,1)S(1)}, u32[]{:S(2)}, u32[]{:S(2)}) collective-permute-start(bf16[2,14,64,256]{3,2,1,0:T(8,128)(2,1)S(1)} %dynamic-slice_bitcast_fusion.1), channel_id=1, source_target_pairs={{0,2},{1,3},{2,0},{3,1},{4,6},{5,7},{6,4},{7,5},{8,10},{9,11},{10,... | collective-permute-start | bytes 2752520 | tf_op jit(solution)/shard_map/ppermute | solution.py:1568
  534.4 20.0 %collective-permute-start.55 = (f32[2,5376]{1,0:T(2,128)S(1)}, f32[2,5376]{1,0:T(2,128)S(1)}, u32[]{:S(2)}, u32[]{:S(2)}) collective-permute-start(f32[2,5376]{1,0:T(2,128)S(1)} %add.414), channel_id=1, source_target_pairs={{0,16},{4,20},{8,24},{12,28},{16,0},{20,4},{24,8},{28,12},{1,17},{... | collective-permute-start | bytes 129032 | tf_op jit(solution)/shard_map/ppermute | solution.py:1583
  534.8 20.9 %collective-permute-start.54 = (bf16[26,64,256]{2,1,0:T(8,128)(2,1)S(1)}, bf16[26,64,256]{2,1,0:T(8,128)(2,1)S(1)}, u32[]{:S(2)}, u32[]{:S(2)}) collective-permute-start(bf16[26,64,256]{2,1,0:T(8,128)(2,1)S(1)} %add_convert_fusion.8), channel_id=1, source_target_pairs={{16,24},{20,28},{17,25},{21,29},{18,26},{22,30},{19,27},{23,31}} | collective-permute-start | bytes 2555912 | tf_op jit(solution)/shard_map/ppermute | solution.py:1281
  535.8 20.2 %collective-permute-start.53 = (bf16[26,64,256]{2,1,0:T(8,128)(2,1)S(1)}, bf16[26,64,256]{2,1,0:T(8,128)(2,1)S(1)}, u32[]{:S(2)}, u32[]{:S(2)}) collective-permute-start(bf16[26,64,256]{2,1,0:T(8,128)(2,1)S(1)} %add_convert_fusion.9), channel_id=1, source_target_pairs={{8,16},{12,20},{9,17},{13,21},{10,18},{14,22},{11,19},{15,23}} | collective-permute-start | bytes 2555912 | tf_op jit(solution)/shard_map/ppermute | solution.py:1281
  552.7 21.9 %collective-permute-start.38 = (bf16[2,14,64,256]{3,2,1,0:T(8,128)(2,1)S(1)}, bf16[2,14,64,256]{3,2,1,0:T(8,128)(2,1)S(1)}, u32[]{:S(2)}, u32[]{:S(2)}) collective-permute-start(bf16[2,14,64,256]{3,2,1,0:T(8,128)(2,1)S(1)} %dynamic-slice_bitcast_fusion), channel_id=1, source_target_pairs={{0,2},{1,3},{2,0},{3,1},{4,6},{5,7},{6,4},{7,5},{8,10},{9,11},{10,... | collective-permute-start | bytes 2752520 | tf_op jit(solution)/shard_map/ppermute | solution.py:1568
  554.4 20.2 %collective-permute-start.40 = (bf16[26,64,256]{2,1,0:T(8,128)(2,1)S(1)}, bf16[26,64,256]{2,1,0:T(8,128)(2,1)S(1)}, u32[]{:S(2)}, u32[]{:S(2)}) collective-permute-start(bf16[26,64,256]{2,1,0:T(8,128)(2,1)S(1)} %add_convert_fusion.21), channel_id=1, source_target_pairs={{8,16},{12,20},{9,17},{13,21},{10,18},{14,22},{11,19},{15,23}} | collective-permute-start | bytes 2555912 | tf_op jit(solution)/shard_map/ppermute | solution.py:1281
  555.7 18.8 %collective-permute-start.39 = (bf16[26,64,256]{2,1,0:T(8,128)(2,1)S(1)}, bf16[26,64,256]{2,1,0:T(8,128)(2,1)S(1)}, u32[]{:S(2)}, u32[]{:S(2)}) collective-permute-start(bf16[26,64,256]{2,1,0:T(8,128)(2,1)S(1)} %pad_maximum_fusion.16), channel_id=1, source_target_pairs={{0,4},{4,0},{8,12},{12,8},{16,20},{20,16},{24,28},{28,24},{1,5},{5... | collective-permute-start | bytes 2555912 | tf_op jit(solution)/shard_map/ppermute | solution.py:1571
  556.4 25.9 %collective-permute-start.56 = (bf16[26,64,256]{2,1,0:T(8,128)(2,1)S(1)}, bf16[26,64,256]{2,1,0:T(8,128)(2,1)S(1)}, u32[]{:S(2)}, u32[]{:S(2)}) collective-permute-start(bf16[26,64,256]{2,1,0:T(8,128)(2,1)S(1)} %add_convert_fusion.7), channel_id=1, source_target_pairs={{16,8},{20,12},{17,9},{21,13},{18,10},{22,14},{19,11},{23,15}} | collective-permute-start | bytes 2555912 | tf_op jit(solution)/shard_map/ppermute | solution.py:1281
  574.8 14.5 %collective-permute-start.43 = (bf16[26,64,256]{2,1,0:T(8,128)(2,1)S(1)}, bf16[26,64,256]{2,1,0:T(8,128)(2,1)}, u32[]{:S(2)}, u32[]{:S(2)}) collective-permute-start(bf16[26,64,256]{2,1,0:T(8,128)(2,1)S(1)} %add_convert_fusion.19), channel_id=1, source_target_pairs={{16,24},{20,28},{17,25},{21,29},{18,26},{22,30},{19,27},{23,31}} | collective-permute-start | bytes 2555912 | tf_op jit(solution)/shard_map/ppermute | solution.py:1281
  576.8 16.1 %collective-permute-start.42 = (bf16[26,64,256]{2,1,0:T(8,128)(2,1)S(1)}, bf16[26,64,256]{2,1,0:T(8,128)(2,1)}, u32[]{:S(2)}, u32[]{:S(2)}) collective-permute-start(bf16[26,64,256]{2,1,0:T(8,128)(2,1)S(1)} %add_convert_fusion.20), channel_id=1, source_target_pairs={{0,8},{4,12},{24,16},{28,20},{1,9},{5,13},{25,17},{29,21},{2,10},{... | collective-permute-start | bytes 2555912 | tf_op jit(solution)/shard_map/ppermute | solution.py:1281
  579.5 14.4 %collective-permute-start.41 = (bf16[26,64,256]{2,1,0:T(8,128)(2,1)}, bf16[26,64,256]{2,1,0:T(8,128)(2,1)}, u32[]{:S(2)}, u32[]{:S(2)}) collective-permute-start(bf16[26,64,256]{2,1,0:T(8,128)(2,1)} %pad_maximum_fusion.17), channel_id=1, source_target_pairs={{0,4},{4,0},{8,12},{12,8},{16,20},{20,16},{24,28},{28,24},{1,5},{5... | collective-permute-start | bytes 2555912 | tf_op jit(solution)/shard_map/ppermute | solution.py:1571
  583.5 19.1 %collective-permute-start.57 = (bf16[26,64,256]{2,1,0:T(8,128)(2,1)}, bf16[26,64,256]{2,1,0:T(8,128)(2,1)}, u32[]{:S(2)}, u32[]{:S(2)}) collective-permute-start(bf16[26,64,256]{2,1,0:T(8,128)(2,1)} %add_convert_fusion.4), channel_id=1, source_target_pairs={{8,0},{12,4},{9,1},{13,5},{10,2},{14,6},{11,3},{15,7}} | collective-permute-start | bytes 2555912 | tf_op jit(solution)/shard_map/ppermute | solution.py:1281
  595.4 15.8 %collective-permute-start.45 = (bf16[26,64,256]{2,1,0:T(8,128)(2,1)S(1)}, bf16[26,64,256]{2,1,0:T(8,128)(2,1)S(1)}, u32[]{:S(2)}, u32[]{:S(2)}) collective-permute-start(bf16[26,64,256]{2,1,0:T(8,128)(2,1)S(1)} %add_convert_fusion.17), channel_id=1, source_target_pairs={{8,16},{12,20},{9,17},{13,21},{10,18},{14,22},{11,19},{15,23}} | collective-permute-start | bytes 2555912 | tf_op jit(solution)/shard_map/ppermute | solution.py:1281
  601.8 9.3 %collective-permute-start.44 = (bf16[26,64,256]{2,1,0:T(8,128)(2,1)S(1)}, bf16[26,64,256]{2,1,0:T(8,128)(2,1)S(1)}, u32[]{:S(2)}, u32[]{:S(2)}) collective-permute-start(bf16[26,64,256]{2,1,0:T(8,128)(2,1)S(1)} %add_convert_fusion.18), channel_id=1, source_target_pairs={{24,16},{28,20},{25,17},{29,21},{26,18},{30,22},{27,19},{31,23}} | collective-permute-start | bytes 2555912 | tf_op jit(solution)/shard_map/ppermute | solution.py:1281
  604.7 12.9 %collective-permute-start.58 = (bf16[26,64,256]{2,1,0:T(8,128)(2,1)S(1)}, bf16[26,64,256]{2,1,0:T(8,128)(2,1)S(1)}, u32[]{:S(2)}, u32[]{:S(2)}) collective-permute-start(bf16[26,64,256]{2,1,0:T(8,128)(2,1)S(1)} %select_select_fusion.1), channel_id=1, source_target_pairs={{0,2},{1,3},{2,0},{3,1},{4,6},{5,7},{6,4},{7,5},{8,10},{9,11},{10,... | collective-permute-start | bytes 2555912 | tf_op jit(solution)/shard_map/ppermute | solution.py:1578
  611.5 17.4 %collective-permute-start.46 = (bf16[26,64,256]{2,1,0:T(8,128)(2,1)S(1)}, bf16[26,64,256]{2,1,0:T(8,128)(2,1)S(1)}, u32[]{:S(2)}, u32[]{:S(2)}) collective-permute-start(bf16[26,64,256]{2,1,0:T(8,128)(2,1)S(1)} %add_convert_fusion.15), channel_id=1, source_target_pairs={{16,8},{20,12},{17,9},{21,13},{18,10},{22,14},{19,11},{23,15}} | collective-permute-start | bytes 2555912 | tf_op jit(solution)/shard_map/ppermute | solution.py:1281
  618.0 14.6 %collective-permute-start.59 = (bf16[40,64,256]{2,1,0:T(8,128)(2,1)S(1)}, bf16[40,64,256]{2,1,0:T(8,128)(2,1)}, u32[]{:S(2)}, u32[]{:S(2)}) collective-permute-start(bf16[40,64,256]{2,1,0:T(8,128)(2,1)S(1)} %pad_maximum_fusion.1), channel_id=1, source_target_pairs={{0,1},{1,0},{2,3},{3,2},{4,5},{5,4},{6,7},{7,6},{8,9},{9,8},{10,11... | collective-permute-start | bytes 3932168 | tf_op jit(solution)/shard_map/ppermute | solution.py:1580
  630.2 20.0 %collective-permute-start.47 = (bf16[26,64,256]{2,1,0:T(8,128)(2,1)}, bf16[26,64,256]{2,1,0:T(8,128)(2,1)}, u32[]{:S(2)}, u32[]{:S(2)}) collective-permute-start(bf16[26,64,256]{2,1,0:T(8,128)(2,1)} %add_convert_fusion.13), channel_id=1, source_target_pairs={{8,0},{12,4},{9,1},{13,5},{10,2},{14,6},{11,3},{15,7}} | collective-permute-start | bytes 2555912 | tf_op jit(solution)/shard_map/ppermute | solution.py:1281
  652.3 17.9 %collective-permute-start.60 = (bf16[26,64,256]{2,1,0:T(8,128)(2,1)S(1)}, bf16[26,64,256]{2,1,0:T(8,128)(2,1)S(1)}, u32[]{:S(2)}, u32[]{:S(2)}) collective-permute-start(bf16[26,64,256]{2,1,0:T(8,128)(2,1)S(1)} %select_select_fusion), channel_id=1, source_target_pairs={{0,2},{1,3},{2,0},{3,1},{4,6},{5,7},{6,4},{7,5},{8,10},{9,11},{10,... | collective-permute-start | bytes 2555912 | tf_op jit(solution)/shard_map/ppermute | solution.py:1578
  670.5 11.8 %collective-permute-start.61 = (bf16[40,64,256]{2,1,0:T(8,128)(2,1)S(1)}, bf16[40,64,256]{2,1,0:T(8,128)(2,1)S(1)}, u32[]{:S(2)}, u32[]{:S(2)}) collective-permute-start(bf16[40,64,256]{2,1,0:T(8,128)(2,1)S(1)} %pad_maximum_fusion.2), channel_id=1, source_target_pairs={{0,1},{1,0},{2,3},{3,2},{4,5},{5,4},{6,7},{7,6},{8,9},{9,8},{10,11... | collective-permute-start | bytes 3932168 | tf_op jit(solution)/shard_map/ppermute | solution.py:1580
  (62 other events, 636.1 us)
Sparse Core Ops, SparseCore 0:
  13.1 201.8 all-gather.1
  270.0 71.0 reduce-scatter.2
  347.4 68.8 reduce-scatter.4

commit v5 on v4

--- a/solution.py
+++ b/solution.py
@@ -521,8 +521,8 @@
 FAR = 62
 G_HALF = 32
 G_LONE = 8
-R_LONE = 28
-R_BOTH = 24
+R_LONE = 32
+R_BOTH = 16
 R_HALF = 2 * R_LONE + R_BOTH
 CHUNKS = 2
 SWAP_CORE = [(i, i ^ 1) for i in range(4)]
@@ -1306,7 +1306,7 @@
     )()
 
 
-def gather_tiles(master_blocks):
+def gather_tiles(master_blocks, others):
     z, x, y, core = spot()
     lone, both, half = G_LONE // 2, (G_HALF - 2 * G_LONE) // 2, G_HALF // 2
     fourth = (SHARD - FAR) // 4
@@ -1337,7 +1337,9 @@
             out["y"] = lax.ppermute(join([part[:G_LONE] for part in here]), "seq", SWAP_Y)
         if phase >= 2:
             out["core"] = lax.ppermute(join(halves[phase - 2]), "seq", SWAP_CORE)
-        out, rows, cross, halves = lax.optimization_barrier((out, rows, cross, halves))
+        out, rows, cross, halves, near, others = lax.optimization_barrier(
+            (out, rows, cross, halves, near, others)
+        )
         if "z" in out:
             rows = rows + [out["z"]]
         if "x" in out:
@@ -1357,7 +1359,7 @@
                 got = out["core"][None, G_HALF * side : G_HALF * (side + 1)]
                 near = lax.dynamic_update_slice(near, own, (owner, G_HALF * core, 0, 0))
                 near = lax.dynamic_update_slice(near, got, (owner, G_HALF * (1 - core), 0, 0))
-    return near.reshape(-1, SUB, WIDE), far
+    return near.reshape(-1, SUB, WIDE), far, others
 
 
 ROUTES = (
@@ -1636,11 +1638,11 @@
 ):
     pairs = caption_len.shape[0]
     reg = x_vis.shape[0] // pairs
-    near, far = gather_tiles(master_blocks)
+    xv = pad_regions(x_vis, pairs)
+    cv = pad_regions(cot_vis, pairs)
+    near, far, (xv, cv) = gather_tiles(master_blocks, (xv, cv))
     lengths = jnp.concatenate([caption_len, jnp.full((2,), reg, jnp.int32)])
     regions = jnp.full((2,), reg, jnp.int32)
-    xv = pad_regions(x_vis, pairs)
-    cv = pad_regions(cot_vis, pairs)
     vis_norms = norm_params[:, : 3 * VIS].reshape(2, 3, VIS)
     text_norms = norm_params[:, 3 * VIS :].reshape(2, 3, TXT)
     co_vis, co_text, vis_ctx, text_ctx = co_forward(lengths, xv, x_text, near, far)
@@ -1680,7 +1682,7 @@
     both = both_sum(own_both, far_both)
     own_both, far_both = pick_both(text_source, 6)
     back = (co_vis, co_text, v_dctx, t_dctx, v_resid, t_resid)
-    back, lone, both, text_mid = lax.optimization_barrier((back, lone, both, text_mid))
+    back, both, text_mid = lax.optimization_barrier((back, both, text_mid))
     for k, kept in enumerate(chunks_of(lone, both)):
         chunks[k].state["kept", 1] = kept
     lone = group_lone(text_mid, text_pair)

time: 724 us -> 707 us (0.977)
  waiting for transfers between devices: 251 us -> 217 us
  other arithmetic: 57.3 us -> 66.4 us
    ppermute x23, waiting for transfers between devices: 81.1 us -> 67.1 us  [along_z(): lax.ppermute(value, 'dp', [(2 * a + x, 2 * b + x) for a, b in moves for x...]
    ppermute x4, waiting for transfers between devices: 59.4 us -> 49 us  [gather_tiles(): lax.ppermute(join([part[:G_LONE] for part in here]), 'seq', SWAP_Y)]
    unnamed x16, other arithmetic: 7.99 us -> 16.2 us
  transfers between devices with their start and end apart: 65 -> 65, of which waited for: 30 -> 28; matrix products, arithmetic and copies ran while one was open for 13% -> 16% of each run, Pallas kernels for 20% -> 22%
where the time goes in v5:
time: 707 us; the launch traced here: 698 us
  Pallas kernels  236 us (33%)
  waiting for transfers between devices  217 us (31%)
  starting transfers between devices  109 us (15%)
  other arithmetic  66.4 us (9%)
  local copies, waits for them, and re-layouts  53.5 us (8%)
  between operations  16.1 us (2%)
    ppermute x23, waiting for transfers between devices, along_z(): lax.ppermute(value, 'dp', [(2 * a + x, 2 * b + x) for a, b in moves for x...  67.1 us
    pallas_call x3, Pallas kernels, renew(): pl.pallas_call(functools.partial(renew_body, steps), in_specs=[pl.BlockSp...  54.8 us
    ppermute x23, starting transfers between devices, along_z(): lax.ppermute(value, 'dp', [(2 * a + x, 2 * b + x) for a, b in moves for x...  52.2 us
    pallas_call x2, Pallas kernels, middle(): pl.pallas_call(functools.partial(middle_body, (begin, rows, span, head, c...  51.2 us
    ppermute x4, waiting for transfers between devices, gather_tiles(): lax.ppermute(join([part[:G_LONE] for part in here]), 'seq', SWAP_Y)  49 us
    pallas_call x4, Pallas kernels, weight_grads(): pl.pallas_call(functools.partial(weight_body, kinds), in_specs=whole(2 *...  44.3 us
    ppermute x4, waiting for transfers between devices, gather_tiles(): out['x'] = lax.ppermute(rows[phase], 'dp', SWAP_X)  37.9 us
    ppermute x5, waiting for transfers between devices, send(): lax.ppermute(state['norms', 0], axis, [(i, i ^ step) for i in range(size)])  35.9 us
  transfers between devices with their start and end apart: 65, of which 28 were waited for; matrix products, arithmetic and copies ran while one was open for 16% of the time, Pallas kernels for 22%

profile of v5, /device:TPU:11, one launch (start us, length us, event | category | flops | bytes accessed | tf_op | source)
XLA Modules:
  0.0 698.0 jit_solution(16477065469775347800)
XLA Ops:
  7.7 5.2 shard_map.223
  13.6 5.2 shard_map.221
  22.0 21.3 %collective-permute-done = bf16[24,64,256]{2,1,0:T(8,128)(2,1)S(1)} collective-permute-done((bf16[24,64,256]{2,1,0:T(8,128)(2,1)}, bf16[24,64,256]{2,1,0:T(8,128)(2,1)S(1)}, u32[]{:S(2)}, u32[]{:S(2)}) %collective-permute-start) | collective-permute-done | bytes 786464 | tf_op jit(solution)/shard_map/ppermute | solution.py:1334
  43.3 8.7 %collective-permute-done.1 = bf16[24,64,256]{2,1,0:T(8,128)(2,1)S(1)} collective-permute-done((bf16[24,64,256]{2,1,0:T(8,128)(2,1)}, bf16[24,64,256]{2,1,0:T(8,128)(2,1)S(1)}, u32[]{:S(2)}, u32[]{:S(2)}) %collective-permute-start.1) | collective-permute-done | bytes 786464 | tf_op jit(solution)/shard_map/ppermute | solution.py:1281
  58.5 14.0 %collective-permute-done.3 = bf16[16,64,256]{2,1,0:T(8,128)(2,1)S(1)} collective-permute-done((bf16[16,64,256]{2,1,0:T(8,128)(2,1)S(1)}, bf16[16,64,256]{2,1,0:T(8,128)(2,1)S(1)}, u32[]{:S(2)}, u32[]{:S(2)}) %collective-permute-start.3) | collective-permute-done | bytes 524320 | tf_op jit(solution)/shard_map/ppermute | solution.py:1337
  74.0 10.7 %collective-permute-done.4 = bf16[24,64,256]{2,1,0:T(8,128)(2,1)S(1)} collective-permute-done((bf16[24,64,256]{2,1,0:T(8,128)(2,1)S(1)}, bf16[24,64,256]{2,1,0:T(8,128)(2,1)S(1)}, u32[]{:S(2)}, u32[]{:S(2)}) %collective-permute-start.4) | collective-permute-done | bytes 786464 | tf_op jit(solution)/shard_map/ppermute | solution.py:1281
  86.4 15.8 %collective-permute-start.5 = (bf16[64,64,256]{2,1,0:T(8,128)(2,1)S(1)}, bf16[64,64,256]{2,1,0:T(8,128)(2,1)S(1)}, u32[]{:S(2)}, u32[]{:S(2)}) collective-permute-start(bf16[64,64,256]{2,1,0:T(8,128)(2,1)S(1)} %get-tuple-element.652), channel_id=1, source_target_pairs={{0,1},{1,0},{2,3},{3,2},{4,5},{5,4},{6,7},{7,6},{8,9},{9,8},{10,11... | collective-permute-start | bytes 6291464 | tf_op jit(solution)/shard_map/ppermute | solution.py:1339
  102.2 2.6 collective-permute-start.8
  107.4 11.5 %collective-permute-done.7 = bf16[16,64,256]{2,1,0:T(8,128)(2,1)S(1)} collective-permute-done((bf16[16,64,256]{2,1,0:T(8,128)(2,1)S(1)}, bf16[16,64,256]{2,1,0:T(8,128)(2,1)S(1)}, u32[]{:S(2)}, u32[]{:S(2)}) %collective-permute-start.7) | collective-permute-done | bytes 524320 | tf_op jit(solution)/shard_map/ppermute | solution.py:1337
  118.9 2.5 collective-permute-done.6
  121.4 2.7 collective-permute-done.8
  142.1 17.1 %collective-permute-done.11 = bf16[16,64,256]{2,1,0:T(8,128)(2,1)S(1)} collective-permute-done((bf16[16,64,256]{2,1,0:T(8,128)(2,1)S(1)}, bf16[16,64,256]{2,1,0:T(8,128)(2,1)S(1)}, u32[]{:S(2)}, u32[]{:S(2)}) %collective-permute-start.11) | collective-permute-done | bytes 524320 | tf_op jit(solution)/shard_map/ppermute | solution.py:1337
  159.2 12.6 %collective-permute-done.10 = bf16[24,64,256]{2,1,0:T(8,128)(2,1)S(1)} collective-permute-done((bf16[24,64,256]{2,1,0:T(8,128)(2,1)}, bf16[24,64,256]{2,1,0:T(8,128)(2,1)S(1)}, u32[]{:S(2)}, u32[]{:S(2)}) %collective-permute-start.10) | collective-permute-done | bytes 786464 | tf_op jit(solution)/shard_map/ppermute | solution.py:1334
  182.2 2.3 bitcast_dynamic-update-slice_fusion.10
  185.6 2.3 bitcast_dynamic-update-slice_fusion.8
  187.9 6.5 collective-permute-done.13
  206.6 2.6 bitcast_dynamic-update-slice_fusion.6
  213.7 2.3 bitcast_dynamic-update-slice_fusion.2
  217.1 2.3 bitcast_dynamic-update-slice_fusion
  219.4 13.0 %shard_map.224 = (bf16[96,3072]{1,0:T(8,128)(2,1)}, bf16[256,3072]{1,0:T(8,128)(2,1)}, bf16[96,1024]{1,0:T(8,128)(2,1)}, bf16[256,1024]{1,0:T(8,128)(2,1)}) custom-call(s32[4]{0:T(128)} %concatenate.119.len_ref, bf16[96,1024]{1,0:T(8,128)(2,1)} %bitcast.278, bf16[256,768]{1,0:T(8,128)(2,1)} %refs_0_.1, bf16[512,64,256]{2,1,0:T(8,128)(2,1)} %bitcast.251, ...), custom_call_target="tpu_custom_call" | custom-call | bytes 74800000 | tf_op jit(solution)/shard_map/pallas_call | solution.py:881
  233.0 19.5 %shard_map.226 = (bf16[96,1024]{1,0:T(8,128)(2,1)}, bf16[96,1024]{1,0:T(8,128)(2,1)}, bf16[96,1024]{1,0:T(8,128)(2,1)}, bf16[96,1024]{1,0:T(8,128)(2,1)}, bf16[9...) custom-call(s32[2]{0:T(128)} %broadcast_1_len_ref.2.len_ref, ...), custom_call_target="tpu_custom_call" | custom-call | bytes 136000000 | tf_op jit(solution)/shard_map/pallas_call | solution.py:1186
  252.5 15.1 %shard_map.227.x_any.refs_0_.refs_1_ = bf16[448,64,256]{2,1,0:T(8,128)(2,1)} custom-call(bf16[96,1024]{1,0:T(8,128)(2,1)} %get-tuple-element.344.ctx_ref.refs_0_, bf16[96,1024]{1,0:T(8,128)(2,1)} %get-tuple-element.347.refs_1_, bf16[96,1024]{1,0:T(8,128)(2,1)} %get-tuple-element.348.refs_2_, bf16[96,1024]{1,0:T(8,128)(2,1)} %get-tuple-element.349.refs_3_, ...), custom_call_target="tpu_custom_call" | custom-call | bytes 60928000 | tf_op jit(solution)/shard_map/pallas_call | solution.py:1259
  267.6 6.4 shard_map.228
  274.1 2.9 shard_map.229
  277.8 31.7 %shard_map.225 = (bf16[256,768]{1,0:T(8,128)(2,1)}, bf16[256,768]{1,0:T(8,128)(2,1)}, bf16[256,3072]{1,0:T(8,128)(2,1)}, bf16[256,768]{1,0:T(8,128)(2,1)}, bf16[...) custom-call(s32[4]{0:T(128)} %concatenate.119.len_ref, ...), custom_call_target="tpu_custom_call" | custom-call | bytes 136000000 | tf_op jit(solution)/shard_map/pallas_call | solution.py:1186
  309.4 17.8 %shard_map.230.refs_0_.refs_2_.x_any = bf16[480,64,256]{2,1,0:T(8,128)(2,1)} custom-call(bf16[256,1024]{1,0:T(8,128)(2,1)} %get-tuple-element.374.ctx_ref.refs_0_, bf16[256,768]{1,0:T(8,128)(2,1)} %get-tuple-element.375.refs_1_, bf16[256,3072]{1,0:T(8,128)(2,1)} %get-tuple-element.376.refs_2_, bf16[256,768]{1,0:T(8,128)(2,1)} %get-tuple-element.377.refs_3_, ...), custom_call_target="tpu_custom_call" | custom-call | bytes 65280000 | tf_op jit(solution)/shard_map/pallas_call | solution.py:1259
  327.7 6.4 shard_map.239
  334.2 3.2 shard_map.233
  338.0 2.9 shard_map.232
  341.2 7.0 %reduce-scatter.3.cloned.1.call-done = bf16[64,64,256]{2,1,0:T(8,128)(2,1)} async-done(((bf16[256,64,256]{2,1,0:T(8,128)(2,1)}), bf16[64,64,256]{2,1,0:T(8,128)(2,1)}) %reduce-scatter.3.cloned.1.call-update) | async-done | bytes 2097168 | tf_op jit(solution)/shard_map/reduce_scatter | solution.py:1548
  352.3 13.9 %shard_map.231 = (bf16[96,3072]{1,0:T(8,128)(2,1)}, bf16[256,3072]{1,0:T(8,128)(2,1)}, f32[96,1024]{1,0:T(8,128)}, f32[256,768]{1,0:T(8,128)}) custom-call(s32[4]{0:T(128)} %concatenate.119.len_ref, bf16[96,3072]{1,0:T(8,128)(2,1)} %get-tuple-element.387.cv_ref, bf16[256,3072]{1,0:T(8,128)(2,1)} %get-tuple-element.388.ct_ref, ...), custom_call_target="tpu_custom_call" | custom-call | bytes 78200000 | tf_op jit(solution)/shard_map/pallas_call | solution.py:950
  366.2 3.4 collective-permute-done.16
  369.7 5.3 shard_map.234.refs_1_
  375.0 3.7 shard_map.235
  383.8 6.0 shard_map.236.refs_0_
  389.8 12.6 %collective-permute-done.21 = bf16[24,64,256]{2,1,0:T(8,128)(2,1)} collective-permute-done((bf16[24,64,256]{2,1,0:T(8,128)(2,1)S(1)}, bf16[24,64,256]{2,1,0:T(8,128)(2,1)}, u32[]{:S(2)}, u32[]{:S(2)}) %collective-permute-start.21) | collective-permute-done | bytes 786464 | tf_op jit(solution)/shard_map/ppermute | solution.py:1281
  402.4 5.0 shard_map.237
  410.4 2.3 add_convert_fusion.27
  418.3 5.9 reduce-scatter.5.cloned.1.call-done
  427.2 9.0 %shard_map.238 = (bf16[2,2,16,64,256]{4,3,2,1,0:T(8,128)(2,1)}, bf16[2,8,64,256]{3,2,1,0:T(8,128)(2,1)}, bf16[2,2,16,64,256]{4,3,2,1,0:T(8,128)(2,1)}, bf16[2,8,64,256]{3,2,1,0:T(8,128)(2,1)}) custom-call(s32[1]{0:T(128)} %bitcast.27.core_ref, bf16[448,64,256]{2,1,0:T(8,128)(2,1)} %shard_map.227.x_any.refs_0_.refs_1_, ...), custom_call_target="tpu_custom_call" | custom-call | bytes 27200000 | tf_op jit(solution)/shard_map/pallas_call | solution.py:1490
  436.3 2.3 dynamic-slice_bitcast_fusion.3
  439.0 2.6 add_convert_fusion.26
  442.9 9.0 %shard_map.240 = (bf16[2,2,16,64,256]{4,3,2,1,0:T(8,128)(2,1)}, bf16[2,8,64,256]{3,2,1,0:T(8,128)(2,1)}, bf16[2,2,16,64,256]{4,3,2,1,0:T(8,128)(2,1)}, bf16[2,8,64,256]{3,2,1,0:T(8,128)(2,1)}) custom-call(s32[1]{0:T(128)} %bitcast.27.core_ref, bf16[192,64,256]{2,1,0:T(8,128)(2,1)} %shard_map.236.refs_0_, ...), custom_call_target="tpu_custom_call" | custom-call | bytes 27200000 | tf_op jit(solution)/shard_map/pallas_call | solution.py:1490
  454.2 7.1 %collective-permute-done.30 = bf16[24,64,256]{2,1,0:T(8,128)(2,1)} collective-permute-done((bf16[24,64,256]{2,1,0:T(8,128)(2,1)}, bf16[24,64,256]{2,1,0:T(8,128)(2,1)}, u32[]{:S(2)}, u32[]{:S(2)}) %collective-permute-start.30) | collective-permute-done | bytes 786464 | tf_op jit(solution)/shard_map/ppermute | solution.py:1281
  470.8 2.6 add_convert_fusion.23
  473.3 24.3 %collective-permute-done.35 = f32[2,5376]{1,0:T(2,128)S(1)} collective-permute-done((f32[2,5376]{1,0:T(2,128)S(1)}, f32[2,5376]{1,0:T(2,128)S(1)}, u32[]{:S(2)}, u32[]{:S(2)}) %collective-permute-start.35) | collective-permute-done | bytes 43040 | tf_op jit(solution)/shard_map/ppermute | solution.py:1585
  497.9 3.3 collective-permute-start.50
  508.9 11.6 %collective-permute-done.51 = f32[2,5376]{1,0:T(2,128)S(1)} collective-permute-done((f32[2,5376]{1,0:T(2,128)S(1)}, f32[2,5376]{1,0:T(2,128)S(1)}, u32[]{:S(2)}, u32[]{:S(2)}) %collective-permute-start.51) | collective-permute-done | bytes 43040 | tf_op jit(solution)/shard_map/ppermute | solution.py:1585
  522.3 7.0 %collective-permute-start.53 = (bf16[24,64,256]{2,1,0:T(8,128)(2,1)S(1)}, bf16[24,64,256]{2,1,0:T(8,128)(2,1)}, u32[]{:S(2)}, u32[]{:S(2)}) collective-permute-start(bf16[24,64,256]{2,1,0:T(8,128)(2,1)S(1)} %add_convert_fusion.9), channel_id=1, source_target_pairs={{8,16},{12,20},{9,17},{13,21},{10,18},{14,22},{11,19},{15,23}} | collective-permute-start | bytes 2359304 | tf_op jit(solution)/shard_map/ppermute | solution.py:1281
  529.7 7.7 %collective-permute-done.37 = bf16[24,64,256]{2,1,0:T(8,128)(2,1)S(1)} collective-permute-done((bf16[24,64,256]{2,1,0:T(8,128)(2,1)S(1)}, bf16[24,64,256]{2,1,0:T(8,128)(2,1)S(1)}, u32[]{:S(2)}, u32[]{:S(2)}) %collective-permute-start.37) | collective-permute-done | bytes 786464 | tf_op jit(solution)/shard_map/ppermute | solution.py:1281
  542.9 5.0 collective-permute-start.40
  553.5 3.6 collective-permute-done.40
  557.1 3.7 collective-permute-done.39
  571.4 4.1 collective-permute-start.57
  579.6 7.0 %collective-permute-start.45 = (bf16[24,64,256]{2,1,0:T(8,128)(2,1)S(1)}, bf16[24,64,256]{2,1,0:T(8,128)(2,1)S(1)}, u32[]{:S(2)}, u32[]{:S(2)}) collective-permute-start(bf16[24,64,256]{2,1,0:T(8,128)(2,1)S(1)} %add_convert_fusion.17), channel_id=1, source_target_pairs={{8,16},{12,20},{9,17},{13,21},{10,18},{14,22},{11,19},{15,23}} | collective-permute-start | bytes 2359304 | tf_op jit(solution)/shard_map/ppermute | solution.py:1281
  588.9 8.1 %collective-permute-done.45 = bf16[24,64,256]{2,1,0:T(8,128)(2,1)S(1)} collective-permute-done((bf16[24,64,256]{2,1,0:T(8,128)(2,1)S(1)}, bf16[24,64,256]{2,1,0:T(8,128)(2,1)S(1)}, u32[]{:S(2)}, u32[]{:S(2)}) %collective-permute-start.45) | collective-permute-done | bytes 786464 | tf_op jit(solution)/shard_map/ppermute | solution.py:1281
  601.1 7.8 %collective-permute-start.59 = (bf16[40,64,256]{2,1,0:T(8,128)(2,1)S(1)}, bf16[40,64,256]{2,1,0:T(8,128)(2,1)}, u32[]{:S(2)}, u32[]{:S(2)}) collective-permute-start(bf16[40,64,256]{2,1,0:T(8,128)(2,1)S(1)} %pad_maximum_fusion.1), channel_id=1, source_target_pairs={{0,1},{1,0},{2,3},{3,2},{4,5},{5,4},{6,7},{7,6},{8,9},{9,8},{10,11... | collective-permute-start | bytes 3932168 | tf_op jit(solution)/shard_map/ppermute | solution.py:1582
  609.2 3.6 collective-permute-done.46
  614.0 2.4 collective-permute-start.47
  616.4 3.0 broadcast_select_fusion.2
  619.4 14.5 %shard_map.241 = (f32[20224,128]{1,0:T(8,128)}, f32[20224,128]{1,0:T(8,128)}, f32[20224,128]{1,0:T(8,128)}, f32[20224,128]{1,0:T(8,128)}) custom-call(s32[20]{0:T(128)} %constant.168.which_ref, bf16[40,64,256]{2,1,0:T(8,128)(2,1)} %get-tuple-element.626.g_any, f32[20224,128]{1,0:T(8,128)} %bitcast.257, f32[20224,128]{1,0:T(8,128)} %bitcast.260, ...), custom_call_target="tpu_custom_call" | custom-call | bytes 47600000 | tf_op jit(solution)/shard_map/pallas_call | solution.py:736
  637.7 14.4 %shard_map.242 = (f32[20224,128]{1,0:T(8,128)}, f32[20224,128]{1,0:T(8,128)}, f32[20224,128]{1,0:T(8,128)}, f32[20224,128]{1,0:T(8,128)}) custom-call(s32[20]{0:T(128)} %constant.169.which_ref, bf16[40,64,256]{2,1,0:T(8,128)(2,1)} %get-tuple-element.625.g_any, ...), custom_call_target="tpu_custom_call", output_to_operand_aliasing={{0}: (7, {}), {1}: (8, {}), {2}: (9, {}), {3}: (10, {})} | custom-call | bytes 47600000 | tf_op jit(solution)/shard_map/pallas_call | solution.py:736
  652.4 8.1 %collective-permute-start.61 = (bf16[40,64,256]{2,1,0:T(8,128)(2,1)S(1)}, bf16[40,64,256]{2,1,0:T(8,128)(2,1)S(1)}, u32[]{:S(2)}, u32[]{:S(2)}) collective-permute-start(bf16[40,64,256]{2,1,0:T(8,128)(2,1)S(1)} %pad_maximum_fusion.2), channel_id=1, source_target_pairs={{0,1},{1,0},{2,3},{3,2},{4,5},{5,4},{6,7},{7,6},{8,9},{9,8},{10,11... | collective-permute-start | bytes 3932168 | tf_op jit(solution)/shard_map/ppermute | solution.py:1582
  665.1 25.9 %shard_map.243 = (f32[20224,128]{1,0:T(8,128)}, f32[20224,128]{1,0:T(8,128)}, f32[20224,128]{1,0:T(8,128)}, f32[20224,128]{1,0:T(8,128)}) custom-call(s32[40]{0:T(128)} %constant.158.clone.which_ref, bf16[80,64,256]{2,1,0:T(8,128)(2,1)} %pad_maximum_fusion.g_any, ...), custom_call_target="tpu_custom_call", output_to_operand_aliasing={{0}: (7, {}), {1}: (8, {}), {2}: (9, {}), {3}: (10, {})} | custom-call | bytes 95200000 | tf_op jit(solution)/shard_map/pallas_call | solution.py:736
  (378 shorter events, 151.8 us)
Async XLA Ops:
  7.2 212.2 %all-gather.2.cloned.1.call-start = ((), (), s32[]{:S(2)}) async-start(), calls=%async_computation.2 | async-start | bytes 25952256 | tf_op jit(solution)/shard_map/all_gather | solution.py:1323
  13.0 335.2 %reduce-scatter.3.cloned.1.call-start = ((), (), s32[]{:S(2)}) async-start(), calls=%async_computation.3 | async-start | bytes 10485760 | tf_op jit(solution)/shard_map/reduce_scatter | solution.py:1548
  18.9 24.4 %collective-permute-start = (bf16[24,64,256]{2,1,0:T(8,128)(2,1)}, bf16[24,64,256]{2,1,0:T(8,128)(2,1)S(1)}, u32[]{:S(2)}, u32[]{:S(2)}) collective-permute-start(bf16[24,64,256]{2,1,0:T(8,128)(2,1)} %shard_map.221), channel_id=1, source_target_pairs={{0,4},{4,0},{8,12},{12,8},{16,20},{20,16},{24,28},{28,24},{1,5},{5... | collective-permute-start | bytes 2359304 | tf_op jit(solution)/shard_map/ppermute | solution.py:1334
  19.2 32.8 %collective-permute-start.1 = (bf16[24,64,256]{2,1,0:T(8,128)(2,1)}, bf16[24,64,256]{2,1,0:T(8,128)(2,1)S(1)}, u32[]{:S(2)}, u32[]{:S(2)}) collective-permute-start(bf16[24,64,256]{2,1,0:T(8,128)(2,1)} %shard_map.221), channel_id=1, source_target_pairs={{0,8},{4,12},{8,16},{12,20},{16,24},{20,28},{24,0},{28,4},{1,9},{5... | collective-permute-start | bytes 2359304 | tf_op jit(solution)/shard_map/ppermute | solution.py:1281
  52.0 22.0 %collective-permute-start.2 = (bf16[24,64,256]{2,1,0:T(8,128)(2,1)S(1)}, bf16[24,64,256]{2,1,0:T(8,128)(2,1)}, u32[]{:S(2)}, u32[]{:S(2)}) collective-permute-start(bf16[24,64,256]{2,1,0:T(8,128)(2,1)S(1)} %collective-permute-done.1), channel_id=1, source_target_pairs={{0,4},{4,0},{8,12},{12,8},{16,20},{20,16},{24,28},{28,24},{1,5},{5... | collective-permute-start | bytes 2359304 | tf_op jit(solution)/shard_map/ppermute | solution.py:1334
  53.9 30.8 %collective-permute-start.4 = (bf16[24,64,256]{2,1,0:T(8,128)(2,1)S(1)}, bf16[24,64,256]{2,1,0:T(8,128)(2,1)S(1)}, u32[]{:S(2)}, u32[]{:S(2)}) collective-permute-start(bf16[24,64,256]{2,1,0:T(8,128)(2,1)S(1)} %collective-permute-done.1), channel_id=1, source_target_pairs={{0,8},{4,12},{8,16},{12,20},{16,24},{20,28},{24,0},{28,4},{1,9},{5... | collective-permute-start | bytes 2359304 | tf_op jit(solution)/shard_map/ppermute | solution.py:1281
  57.2 15.3 %collective-permute-start.3 = (bf16[16,64,256]{2,1,0:T(8,128)(2,1)S(1)}, bf16[16,64,256]{2,1,0:T(8,128)(2,1)S(1)}, u32[]{:S(2)}, u32[]{:S(2)}) collective-permute-start(bf16[16,64,256]{2,1,0:T(8,128)(2,1)S(1)} %pad_maximum_fusion.19), channel_id=1, source_target_pairs={{0,2},{1,3},{2,0},{3,1},{4,6},{5,7},{6,4},{7,5},{8,10},{9,11},{10,... | collective-permute-start | bytes 1572872 | tf_op jit(solution)/shard_map/ppermute | solution.py:1337
  86.4 37.7 %collective-permute-start.5 = (bf16[64,64,256]{2,1,0:T(8,128)(2,1)S(1)}, bf16[64,64,256]{2,1,0:T(8,128)(2,1)S(1)}, u32[]{:S(2)}, u32[]{:S(2)}) collective-permute-start(bf16[64,64,256]{2,1,0:T(8,128)(2,1)S(1)} %get-tuple-element.652), channel_id=1, source_target_pairs={{0,1},{1,0},{2,3},{3,2},{4,5},{5,4},{6,7},{7,6},{8,9},{9,8},{10,11... | collective-permute-start | bytes 6291464 | tf_op jit(solution)/shard_map/ppermute | solution.py:1339
  102.2 19.2 %collective-permute-start.6 = (bf16[24,64,256]{2,1,0:T(8,128)(2,1)S(1)}, bf16[24,64,256]{2,1,0:T(8,128)(2,1)S(1)}, u32[]{:S(2)}, u32[]{:S(2)}) collective-permute-start(bf16[24,64,256]{2,1,0:T(8,128)(2,1)S(1)} %collective-permute-done.4), channel_id=1, source_target_pairs={{0,4},{4,0},{8,12},{12,8},{16,20},{20,16},{24,28},{28,24},{1,5},{5... | collective-permute-start | bytes 2359304 | tf_op jit(solution)/shard_map/ppermute | solution.py:1334
  102.2 21.9 %collective-permute-start.8 = (bf16[24,64,256]{2,1,0:T(8,128)(2,1)S(1)}, bf16[24,64,256]{2,1,0:T(8,128)(2,1)}, u32[]{:S(2)}, u32[]{:S(2)}) collective-permute-start(bf16[24,64,256]{2,1,0:T(8,128)(2,1)S(1)} %collective-permute-done.4), channel_id=1, source_target_pairs={{0,8},{4,12},{8,16},{12,20},{16,24},{20,28},{24,0},{28,4},{1,9},{5... | collective-permute-start | bytes 2359304 | tf_op jit(solution)/shard_map/ppermute | solution.py:1281
  105.9 13.0 %collective-permute-start.7 = (bf16[16,64,256]{2,1,0:T(8,128)(2,1)S(1)}, bf16[16,64,256]{2,1,0:T(8,128)(2,1)S(1)}, u32[]{:S(2)}, u32[]{:S(2)}) collective-permute-start(bf16[16,64,256]{2,1,0:T(8,128)(2,1)S(1)} %pad_maximum_fusion.20), channel_id=1, source_target_pairs={{0,2},{1,3},{2,0},{3,1},{4,6},{5,7},{6,4},{7,5},{8,10},{9,11},{10,... | collective-permute-start | bytes 1572872 | tf_op jit(solution)/shard_map/ppermute | solution.py:1337
  133.2 38.5 %collective-permute-start.9 = (bf16[64,64,256]{2,1,0:T(8,128)(2,1)}, bf16[64,64,256]{2,1,0:T(8,128)(2,1)}, u32[]{:S(2)}, u32[]{:S(2)}) collective-permute-start(bf16[64,64,256]{2,1,0:T(8,128)(2,1)} %get-tuple-element.648), channel_id=1, source_target_pairs={{0,1},{1,0},{2,3},{3,2},{4,5},{5,4},{6,7},{7,6},{8,9},{9,8},{10,11... | collective-permute-start | bytes 6291464 | tf_op jit(solution)/shard_map/ppermute | solution.py:1339
  134.0 25.2 %collective-permute-start.11 = (bf16[16,64,256]{2,1,0:T(8,128)(2,1)S(1)}, bf16[16,64,256]{2,1,0:T(8,128)(2,1)S(1)}, u32[]{:S(2)}, u32[]{:S(2)}) collective-permute-start(bf16[16,64,256]{2,1,0:T(8,128)(2,1)S(1)} %pad_maximum_fusion.21), channel_id=1, source_target_pairs={{0,2},{1,3},{2,0},{3,1},{4,6},{5,7},{6,4},{7,5},{8,10},{9,11},{10,... | collective-permute-start | bytes 1572872 | tf_op jit(solution)/shard_map/ppermute | solution.py:1337
  135.3 36.5 %collective-permute-start.10 = (bf16[24,64,256]{2,1,0:T(8,128)(2,1)}, bf16[24,64,256]{2,1,0:T(8,128)(2,1)S(1)}, u32[]{:S(2)}, u32[]{:S(2)}) collective-permute-start(bf16[24,64,256]{2,1,0:T(8,128)(2,1)} %collective-permute-done.8), channel_id=1, source_target_pairs={{0,4},{4,0},{8,12},{12,8},{16,20},{20,16},{24,28},{28,24},{1,5},{5... | collective-permute-start | bytes 2359304 | tf_op jit(solution)/shard_map/ppermute | solution.py:1334
  177.4 17.0 %collective-permute-start.12 = (bf16[64,64,256]{2,1,0:T(8,128)(2,1)}, bf16[64,64,256]{2,1,0:T(8,128)(2,1)}, u32[]{:S(2)}, u32[]{:S(2)}) collective-permute-start(bf16[64,64,256]{2,1,0:T(8,128)(2,1)} %get-tuple-element.644), channel_id=1, source_target_pairs={{0,1},{1,0},{2,3},{3,2},{4,5},{5,4},{6,7},{7,6},{8,9},{9,8},{10,11... | collective-permute-start | bytes 6291464 | tf_op jit(solution)/shard_map/ppermute | solution.py:1339
  179.6 14.8 %collective-permute-start.13 = (bf16[16,64,256]{2,1,0:T(8,128)(2,1)S(1)}, bf16[16,64,256]{2,1,0:T(8,128)(2,1)S(1)}, u32[]{:S(2)}, u32[]{:S(2)}) collective-permute-start(bf16[16,64,256]{2,1,0:T(8,128)(2,1)S(1)} %pad_maximum_fusion.22), channel_id=1, source_target_pairs={{0,2},{1,3},{2,0},{3,1},{4,6},{5,7},{6,4},{7,5},{8,10},{9,11},{10,... | collective-permute-start | bytes 1572872 | tf_op jit(solution)/shard_map/ppermute | solution.py:1337
  202.5 10.0 %collective-permute-start.14 = (bf16[64,64,256]{2,1,0:T(8,128)(2,1)}, bf16[64,64,256]{2,1,0:T(8,128)(2,1)}, u32[]{:S(2)}, u32[]{:S(2)}) collective-permute-start(bf16[64,64,256]{2,1,0:T(8,128)(2,1)} %get-tuple-element.640), channel_id=1, source_target_pairs={{0,1},{1,0},{2,3},{3,2},{4,5},{5,4},{6,7},{7,6},{8,9},{9,8},{10,11... | collective-permute-start | bytes 6291464 | tf_op jit(solution)/shard_map/ppermute | solution.py:1339
  274.0 150.1 %reduce-scatter.5.cloned.1.call-start = ((), (), s32[]{:S(2)}) async-start(), calls=%async_computation.4 | async-start | bytes 10485760 | tf_op jit(solution)/shard_map/reduce_scatter | solution.py:1548
  277.0 32.4 %collective-permute-start.15 = (bf16[32,64,256]{2,1,0:T(8,128)(2,1)}, bf16[32,64,256]{2,1,0:T(8,128)(2,1)S(1)}, u32[]{:S(2)}, u32[]{:S(2)}) collective-permute-start(bf16[32,64,256]{2,1,0:T(8,128)(2,1)} %get-tuple-element.372), channel_id=1, source_target_pairs={{0,1},{1,0},{2,3},{3,2},{4,5},{5,4},{6,7},{7,6},{8,9},{9,8},{10,11... | collective-permute-start | bytes 3145736 | tf_op jit(solution)/shard_map/ppermute | solution.py:1666
  337.4 28.8 %collective-permute-start.19 = (bf16[80,64,256]{2,1,0:T(8,128)(2,1)}, bf16[80,64,256]{2,1,0:T(8,128)(2,1)}, u32[]{:S(2)}, u32[]{:S(2)}) collective-permute-start(bf16[80,64,256]{2,1,0:T(8,128)(2,1)} %shard_map.233), channel_id=1, source_target_pairs={{0,1},{1,0},{2,3},{3,2},{4,5},{5,4},{6,7},{7,6},{8,9},{9,8},{10,11... | collective-permute-start | bytes 7864328 | tf_op jit(solution)/shard_map/ppermute | solution.py:1692
  340.9 25.3 %collective-permute-start.18 = (bf16[32,64,256]{2,1,0:T(8,128)(2,1)}, bf16[32,64,256]{2,1,0:T(8,128)(2,1)}, u32[]{:S(2)}, u32[]{:S(2)}) collective-permute-start(bf16[32,64,256]{2,1,0:T(8,128)(2,1)} %get-tuple-element.397), channel_id=1, source_target_pairs={{0,1},{1,0},{2,3},{3,2},{4,5},{5,4},{6,7},{7,6},{8,9},{9,8},{10,11... | collective-permute-start | bytes 3145736 | tf_op jit(solution)/shard_map/ppermute | solution.py:1666
  350.9 18.7 %collective-permute-start.16 = (bf16[24,64,256]{2,1,0:T(8,128)(2,1)}, bf16[24,64,256]{2,1,0:T(8,128)(2,1)}, u32[]{:S(2)}, u32[]{:S(2)}) collective-permute-start(bf16[24,64,256]{2,1,0:T(8,128)(2,1)} %pad_maximum_fusion.11), channel_id=1, source_target_pairs={{0,4},{4,0},{8,12},{12,8},{16,20},{20,16},{24,28},{28,24},{1,5},{5... | collective-permute-start | bytes 2359304 | tf_op jit(solution)/shard_map/ppermute | solution.py:1573
  351.3 14.9 %collective-permute-start.17 = (f32[2,5376]{1,0:T(2,128)S(1)}, f32[2,5376]{1,0:T(2,128)S(1)}, u32[]{:S(2)}, u32[]{:S(2)}) collective-permute-start(f32[2,5376]{1,0:T(2,128)S(1)} %constant_dynamic-update-slice_fusion.24), channel_id=1, source_target_pairs={{0,1},{1,0},{2,3},{3,2},{4,5},{5,4},{6,7},{7,6},{8,9},{9,8},{10,11... | collective-permute-start | bytes 129032 | tf_op jit(solution)/shard_map/ppermute | solution.py:1585
  378.7 23.7 %collective-permute-start.23 = (bf16[80,64,256]{2,1,0:T(8,128)(2,1)}, bf16[80,64,256]{2,1,0:T(8,128)(2,1)}, u32[]{:S(2)}, u32[]{:S(2)}) collective-permute-start(bf16[80,64,256]{2,1,0:T(8,128)(2,1)} %shard_map.235), channel_id=1, source_target_pairs={{0,1},{1,0},{2,3},{3,2},{4,5},{5,4},{6,7},{7,6},{8,9},{9,8},{10,11... | collective-permute-start | bytes 7864328 | tf_op jit(solution)/shard_map/ppermute | solution.py:1692
  381.3 21.1 %collective-permute-start.21 = (bf16[24,64,256]{2,1,0:T(8,128)(2,1)S(1)}, bf16[24,64,256]{2,1,0:T(8,128)(2,1)}, u32[]{:S(2)}, u32[]{:S(2)}) collective-permute-start(bf16[24,64,256]{2,1,0:T(8,128)(2,1)S(1)} %add_convert_fusion.29), channel_id=1, source_target_pairs={{24,16},{28,20},{0,8},{4,12},{25,17},{29,21},{1,9},{5,13},{26,18},... | collective-permute-start | bytes 2359304 | tf_op jit(solution)/shard_map/ppermute | solution.py:1281
  382.8 19.7 %collective-permute-start.20 = (bf16[24,64,256]{2,1,0:T(8,128)(2,1)S(1)}, bf16[24,64,256]{2,1,0:T(8,128)(2,1)}, u32[]{:S(2)}, u32[]{:S(2)}) collective-permute-start(bf16[24,64,256]{2,1,0:T(8,128)(2,1)S(1)} %pad_maximum_fusion.12), channel_id=1, source_target_pairs={{0,4},{4,0},{8,12},{12,8},{16,20},{20,16},{24,28},{28,24},{1,5},{5... | collective-permute-start | bytes 2359304 | tf_op jit(solution)/shard_map/ppermute | solution.py:1573
  407.4 28.9 %collective-permute-start.26 = (bf16[80,64,256]{2,1,0:T(8,128)(2,1)}, bf16[80,64,256]{2,1,0:T(8,128)(2,1)}, u32[]{:S(2)}, u32[]{:S(2)}) collective-permute-start(bf16[80,64,256]{2,1,0:T(8,128)(2,1)} %get-tuple-element.415), channel_id=1, source_target_pairs={{0,1},{1,0},{2,3},{3,2},{4,5},{5,4},{6,7},{7,6},{8,9},{9,8},{10,11... | collective-permute-start | bytes 7864328 | tf_op jit(solution)/shard_map/ppermute | solution.py:1692
  408.3 28.0 %collective-permute-start.27 = (bf16[80,64,256]{2,1,0:T(8,128)(2,1)}, bf16[80,64,256]{2,1,0:T(8,128)(2,1)}, u32[]{:S(2)}, u32[]{:S(2)}) collective-permute-start(bf16[80,64,256]{2,1,0:T(8,128)(2,1)} %get-tuple-element.416), channel_id=1, source_target_pairs={{0,1},{1,0},{2,3},{3,2},{4,5},{5,4},{6,7},{7,6},{8,9},{9,8},{10,11... | collective-permute-start | bytes 7864328 | tf_op jit(solution)/shard_map/ppermute | solution.py:1692
  412.7 23.6 %collective-permute-start.25 = (bf16[24,64,256]{2,1,0:T(8,128)(2,1)}, bf16[24,64,256]{2,1,0:T(8,128)(2,1)}, u32[]{:S(2)}, u32[]{:S(2)}) collective-permute-start(bf16[24,64,256]{2,1,0:T(8,128)(2,1)} %add_convert_fusion.27), channel_id=1, source_target_pairs={{24,16},{28,20},{0,8},{4,12},{25,17},{29,21},{1,9},{5,13},{26,18},... | collective-permute-start | bytes 2359304 | tf_op jit(solution)/shard_map/ppermute | solution.py:1281
  415.4 20.9 %collective-permute-start.24 = (bf16[24,64,256]{2,1,0:T(8,128)(2,1)S(1)}, bf16[24,64,256]{2,1,0:T(8,128)(2,1)}, u32[]{:S(2)}, u32[]{:S(2)}) collective-permute-start(bf16[24,64,256]{2,1,0:T(8,128)(2,1)S(1)} %add_convert_fusion.28), channel_id=1, source_target_pairs={{16,8},{20,12},{17,9},{21,13},{18,10},{22,14},{19,11},{23,15}} | collective-permute-start | bytes 2359304 | tf_op jit(solution)/shard_map/ppermute | solution.py:1281
  426.9 27.2 %collective-permute-start.29 = (bf16[24,64,256]{2,1,0:T(8,128)(2,1)}, bf16[24,64,256]{2,1,0:T(8,128)(2,1)}, u32[]{:S(2)}, u32[]{:S(2)}) collective-permute-start(bf16[24,64,256]{2,1,0:T(8,128)(2,1)} %pad_maximum_fusion.13), channel_id=1, source_target_pairs={{0,4},{4,0},{8,12},{12,8},{16,20},{20,16},{24,28},{28,24},{1,5},{5... | collective-permute-start | bytes 2359304 | tf_op jit(solution)/shard_map/ppermute | solution.py:1573
  438.6 23.9 %collective-permute-start.28 = (bf16[2,16,64,256]{3,2,1,0:T(8,128)(2,1)}, bf16[2,16,64,256]{3,2,1,0:T(8,128)(2,1)}, u32[]{:S(2)}, u32[]{:S(2)}) collective-permute-start(bf16[2,16,64,256]{3,2,1,0:T(8,128)(2,1)} %dynamic-slice_bitcast_fusion.3), channel_id=1, source_target_pairs={{0,2},{1,3},{2,0},{3,1},{4,6},{5,7},{6,4},{7,5},{8,10},{9,11},{10,... | collective-permute-start | bytes 3145736 | tf_op jit(solution)/shard_map/ppermute | solution.py:1570
  441.6 19.7 %collective-permute-start.30 = (bf16[24,64,256]{2,1,0:T(8,128)(2,1)}, bf16[24,64,256]{2,1,0:T(8,128)(2,1)}, u32[]{:S(2)}, u32[]{:S(2)}) collective-permute-start(bf16[24,64,256]{2,1,0:T(8,128)(2,1)} %add_convert_fusion.26), channel_id=1, source_target_pairs={{16,8},{20,12},{17,9},{21,13},{18,10},{22,14},{19,11},{23,15}} | collective-permute-start | bytes 2359304 | tf_op jit(solution)/shard_map/ppermute | solution.py:1281
  462.7 34.9 %collective-permute-start.34 = (bf16[24,64,256]{2,1,0:T(8,128)(2,1)S(1)}, bf16[24,64,256]{2,1,0:T(8,128)(2,1)S(1)}, u32[]{:S(2)}, u32[]{:S(2)}) collective-permute-start(bf16[24,64,256]{2,1,0:T(8,128)(2,1)S(1)} %pad_maximum_fusion.15), channel_id=1, source_target_pairs={{0,4},{4,0},{8,12},{12,8},{16,20},{20,16},{24,28},{28,24},{1,5},{5... | collective-permute-start | bytes 2359304 | tf_op jit(solution)/shard_map/ppermute | solution.py:1573
  465.7 31.9 %collective-permute-start.33 = (bf16[24,64,256]{2,1,0:T(8,128)(2,1)S(1)}, bf16[24,64,256]{2,1,0:T(8,128)(2,1)S(1)}, u32[]{:S(2)}, u32[]{:S(2)}) collective-permute-start(bf16[24,64,256]{2,1,0:T(8,128)(2,1)S(1)} %add_convert_fusion.24), channel_id=1, source_target_pairs={{0,8},{4,12},{1,9},{5,13},{2,10},{6,14},{3,11},{7,15}} | collective-permute-start | bytes 2359304 | tf_op jit(solution)/shard_map/ppermute | solution.py:1281
  467.1 30.5 %collective-permute-start.31 = (bf16[2,16,64,256]{3,2,1,0:T(8,128)(2,1)S(1)}, bf16[2,16,64,256]{3,2,1,0:T(8,128)(2,1)S(1)}, u32[]{:S(2)}, u32[]{:S(2)}) collective-permute-start(bf16[2,16,64,256]{3,2,1,0:T(8,128)(2,1)S(1)} %dynamic-slice_bitcast_fusion.2), channel_id=1, source_target_pairs={{0,2},{1,3},{2,0},{3,1},{4,6},{5,7},{6,4},{7,5},{8,10},{9,11},{10,... | collective-permute-start | bytes 3145736 | tf_op jit(solution)/shard_map/ppermute | solution.py:1570
  469.2 28.4 %collective-permute-start.32 = (bf16[24,64,256]{2,1,0:T(8,128)(2,1)S(1)}, bf16[24,64,256]{2,1,0:T(8,128)(2,1)S(1)}, u32[]{:S(2)}, u32[]{:S(2)}) collective-permute-start(bf16[24,64,256]{2,1,0:T(8,128)(2,1)S(1)} %pad_maximum_fusion.14), channel_id=1, source_target_pairs={{0,4},{4,0},{8,12},{12,8},{16,20},{20,16},{24,28},{28,24},{1,5},{5... | collective-permute-start | bytes 2359304 | tf_op jit(solution)/shard_map/ppermute | solution.py:1573
  470.0 27.6 %collective-permute-start.35 = (f32[2,5376]{1,0:T(2,128)S(1)}, f32[2,5376]{1,0:T(2,128)S(1)}, u32[]{:S(2)}, u32[]{:S(2)}) collective-permute-start(f32[2,5376]{1,0:T(2,128)S(1)} %add.386), channel_id=1, source_target_pairs={{0,4},{4,0},{8,12},{12,8},{16,20},{20,16},{24,28},{28,24},{1,5},{5... | collective-permute-start | bytes 129032 | tf_op jit(solution)/shard_map/ppermute | solution.py:1585
  497.9 22.9 %collective-permute-start.50 = (bf16[24,64,256]{2,1,0:T(8,128)(2,1)S(1)}, bf16[24,64,256]{2,1,0:T(8,128)(2,1)S(1)}, u32[]{:S(2)}, u32[]{:S(2)}) collective-permute-start(bf16[24,64,256]{2,1,0:T(8,128)(2,1)S(1)} %add_convert_fusion.11), channel_id=1, source_target_pairs={{8,16},{12,20},{9,17},{13,21},{10,18},{14,22},{11,19},{15,23}} | collective-permute-start | bytes 2359304 | tf_op jit(solution)/shard_map/ppermute | solution.py:1281
  501.6 19.2 %collective-permute-start.49 = (bf16[24,64,256]{2,1,0:T(8,128)(2,1)S(1)}, bf16[24,64,256]{2,1,0:T(8,128)(2,1)S(1)}, u32[]{:S(2)}, u32[]{:S(2)}) collective-permute-start(bf16[24,64,256]{2,1,0:T(8,128)(2,1)S(1)} %add_convert_fusion.12), channel_id=1, source_target_pairs={{0,8},{4,12},{24,16},{28,20},{1,9},{5,13},{25,17},{29,21},{2,10},{... | collective-permute-start | bytes 2359304 | tf_op jit(solution)/shard_map/ppermute | solution.py:1281
  503.6 17.2 %collective-permute-start.48 = (bf16[24,64,256]{2,1,0:T(8,128)(2,1)S(1)}, bf16[24,64,256]{2,1,0:T(8,128)(2,1)S(1)}, u32[]{:S(2)}, u32[]{:S(2)}) collective-permute-start(bf16[24,64,256]{2,1,0:T(8,128)(2,1)S(1)} %pad_maximum_fusion.18), channel_id=1, source_target_pairs={{0,4},{4,0},{8,12},{12,8},{16,20},{20,16},{24,28},{28,24},{1,5},{5... | collective-permute-start | bytes 2359304 | tf_op jit(solution)/shard_map/ppermute | solution.py:1573
  505.0 15.5 %collective-permute-start.51 = (f32[2,5376]{1,0:T(2,128)S(1)}, f32[2,5376]{1,0:T(2,128)S(1)}, u32[]{:S(2)}, u32[]{:S(2)}) collective-permute-start(f32[2,5376]{1,0:T(2,128)S(1)} %add.410), channel_id=1, source_target_pairs={{0,8},{4,12},{8,0},{12,4},{16,24},{20,28},{24,16},{28,20},{1,9},{5... | collective-permute-start | bytes 129032 | tf_op jit(solution)/shard_map/ppermute | solution.py:1585
  507.5 29.8 %collective-permute-start.37 = (bf16[24,64,256]{2,1,0:T(8,128)(2,1)S(1)}, bf16[24,64,256]{2,1,0:T(8,128)(2,1)S(1)}, u32[]{:S(2)}, u32[]{:S(2)}) collective-permute-start(bf16[24,64,256]{2,1,0:T(8,128)(2,1)S(1)} %add_convert_fusion.22), channel_id=1, source_target_pairs={{0,8},{4,12},{1,9},{5,13},{2,10},{6,14},{3,11},{7,15}} | collective-permute-start | bytes 2359304 | tf_op jit(solution)/shard_map/ppermute | solution.py:1281
  520.5 18.4 %collective-permute-start.36 = (bf16[2,16,64,256]{3,2,1,0:T(8,128)(2,1)S(1)}, bf16[2,16,64,256]{3,2,1,0:T(8,128)(2,1)S(1)}, u32[]{:S(2)}, u32[]{:S(2)}) collective-permute-start(bf16[2,16,64,256]{3,2,1,0:T(8,128)(2,1)S(1)} %dynamic-slice_bitcast_fusion.1), channel_id=1, source_target_pairs={{0,2},{1,3},{2,0},{3,1},{4,6},{5,7},{6,4},{7,5},{8,10},{9,11},{10,... | collective-permute-start | bytes 3145736 | tf_op jit(solution)/shard_map/ppermute | solution.py:1570
  520.8 22.1 %collective-permute-start.55 = (f32[2,5376]{1,0:T(2,128)S(1)}, f32[2,5376]{1,0:T(2,128)S(1)}, u32[]{:S(2)}, u32[]{:S(2)}) collective-permute-start(f32[2,5376]{1,0:T(2,128)S(1)} %add.414), channel_id=1, source_target_pairs={{0,16},{4,20},{8,24},{12,28},{16,0},{20,4},{24,8},{28,12},{1,17},{... | collective-permute-start | bytes 129032 | tf_op jit(solution)/shard_map/ppermute | solution.py:1585
  521.2 26.7 %collective-permute-start.54 = (bf16[24,64,256]{2,1,0:T(8,128)(2,1)S(1)}, bf16[24,64,256]{2,1,0:T(8,128)(2,1)S(1)}, u32[]{:S(2)}, u32[]{:S(2)}) collective-permute-start(bf16[24,64,256]{2,1,0:T(8,128)(2,1)S(1)} %add_convert_fusion.8), channel_id=1, source_target_pairs={{16,24},{20,28},{17,25},{21,29},{18,26},{22,30},{19,27},{23,31}} | collective-permute-start | bytes 2359304 | tf_op jit(solution)/shard_map/ppermute | solution.py:1281
  522.3 27.8 %collective-permute-start.53 = (bf16[24,64,256]{2,1,0:T(8,128)(2,1)S(1)}, bf16[24,64,256]{2,1,0:T(8,128)(2,1)}, u32[]{:S(2)}, u32[]{:S(2)}) collective-permute-start(bf16[24,64,256]{2,1,0:T(8,128)(2,1)S(1)} %add_convert_fusion.9), channel_id=1, source_target_pairs={{8,16},{12,20},{9,17},{13,21},{10,18},{14,22},{11,19},{15,23}} | collective-permute-start | bytes 2359304 | tf_op jit(solution)/shard_map/ppermute | solution.py:1281
  537.3 12.7 %collective-permute-start.52 = (bf16[24,64,256]{2,1,0:T(8,128)(2,1)S(1)}, bf16[24,64,256]{2,1,0:T(8,128)(2,1)}, u32[]{:S(2)}, u32[]{:S(2)}) collective-permute-start(bf16[24,64,256]{2,1,0:T(8,128)(2,1)S(1)} %add_convert_fusion.10), channel_id=1, source_target_pairs={{24,16},{28,20},{25,17},{29,21},{26,18},{30,22},{27,19},{31,23}} | collective-permute-start | bytes 2359304 | tf_op jit(solution)/shard_map/ppermute | solution.py:1281
  540.0 20.9 %collective-permute-start.38 = (bf16[2,16,64,256]{3,2,1,0:T(8,128)(2,1)}, bf16[2,16,64,256]{3,2,1,0:T(8,128)(2,1)}, u32[]{:S(2)}, u32[]{:S(2)}) collective-permute-start(bf16[2,16,64,256]{3,2,1,0:T(8,128)(2,1)} %dynamic-slice_bitcast_fusion), channel_id=1, source_target_pairs={{0,2},{1,3},{2,0},{3,1},{4,6},{5,7},{6,4},{7,5},{8,10},{9,11},{10,... | collective-permute-start | bytes 3145736 | tf_op jit(solution)/shard_map/ppermute | solution.py:1570
  542.9 14.2 %collective-permute-start.40 = (bf16[24,64,256]{2,1,0:T(8,128)(2,1)}, bf16[24,64,256]{2,1,0:T(8,128)(2,1)}, u32[]{:S(2)}, u32[]{:S(2)}) collective-permute-start(bf16[24,64,256]{2,1,0:T(8,128)(2,1)} %add_convert_fusion.21), channel_id=1, source_target_pairs={{8,16},{12,20},{9,17},{13,21},{10,18},{14,22},{11,19},{15,23}} | collective-permute-start | bytes 2359304 | tf_op jit(solution)/shard_map/ppermute | solution.py:1281
  548.8 12.1 %collective-permute-start.39 = (bf16[24,64,256]{2,1,0:T(8,128)(2,1)}, bf16[24,64,256]{2,1,0:T(8,128)(2,1)}, u32[]{:S(2)}, u32[]{:S(2)}) collective-permute-start(bf16[24,64,256]{2,1,0:T(8,128)(2,1)} %pad_maximum_fusion.16), channel_id=1, source_target_pairs={{0,4},{4,0},{8,12},{12,8},{16,20},{20,16},{24,28},{28,24},{1,5},{5... | collective-permute-start | bytes 2359304 | tf_op jit(solution)/shard_map/ppermute | solution.py:1573
  551.4 19.7 %collective-permute-start.56 = (bf16[24,64,256]{2,1,0:T(8,128)(2,1)S(1)}, bf16[24,64,256]{2,1,0:T(8,128)(2,1)S(1)}, u32[]{:S(2)}, u32[]{:S(2)}) collective-permute-start(bf16[24,64,256]{2,1,0:T(8,128)(2,1)S(1)} %add_convert_fusion.7), channel_id=1, source_target_pairs={{16,8},{20,12},{17,9},{21,13},{18,10},{22,14},{19,11},{23,15}} | collective-permute-start | bytes 2359304 | tf_op jit(solution)/shard_map/ppermute | solution.py:1281
  562.5 12.9 %collective-permute-start.43 = (bf16[24,64,256]{2,1,0:T(8,128)(2,1)S(1)}, bf16[24,64,256]{2,1,0:T(8,128)(2,1)S(1)}, u32[]{:S(2)}, u32[]{:S(2)}) collective-permute-start(bf16[24,64,256]{2,1,0:T(8,128)(2,1)S(1)} %add_convert_fusion.19), channel_id=1, source_target_pairs={{16,24},{20,28},{17,25},{21,29},{18,26},{22,30},{19,27},{23,31}} | collective-permute-start | bytes 2359304 | tf_op jit(solution)/shard_map/ppermute | solution.py:1281
  564.9 12.9 %collective-permute-start.42 = (bf16[24,64,256]{2,1,0:T(8,128)(2,1)S(1)}, bf16[24,64,256]{2,1,0:T(8,128)(2,1)S(1)}, u32[]{:S(2)}, u32[]{:S(2)}) collective-permute-start(bf16[24,64,256]{2,1,0:T(8,128)(2,1)S(1)} %add_convert_fusion.20), channel_id=1, source_target_pairs={{0,8},{4,12},{24,16},{28,20},{1,9},{5,13},{25,17},{29,21},{2,10},{... | collective-permute-start | bytes 2359304 | tf_op jit(solution)/shard_map/ppermute | solution.py:1281
  568.1 11.2 %collective-permute-start.41 = (bf16[24,64,256]{2,1,0:T(8,128)(2,1)S(1)}, bf16[24,64,256]{2,1,0:T(8,128)(2,1)S(1)}, u32[]{:S(2)}, u32[]{:S(2)}) collective-permute-start(bf16[24,64,256]{2,1,0:T(8,128)(2,1)S(1)} %pad_maximum_fusion.17), channel_id=1, source_target_pairs={{0,4},{4,0},{8,12},{12,8},{16,20},{20,16},{24,28},{28,24},{1,5},{5... | collective-permute-start | bytes 2359304 | tf_op jit(solution)/shard_map/ppermute | solution.py:1573
  571.4 16.4 %collective-permute-start.57 = (bf16[24,64,256]{2,1,0:T(8,128)(2,1)S(1)}, bf16[24,64,256]{2,1,0:T(8,128)(2,1)S(1)}, u32[]{:S(2)}, u32[]{:S(2)}) collective-permute-start(bf16[24,64,256]{2,1,0:T(8,128)(2,1)S(1)} %add_convert_fusion.4), channel_id=1, source_target_pairs={{8,0},{12,4},{9,1},{13,5},{10,2},{14,6},{11,3},{15,7}} | collective-permute-start | bytes 2359304 | tf_op jit(solution)/shard_map/ppermute | solution.py:1281
  579.6 17.3 %collective-permute-start.45 = (bf16[24,64,256]{2,1,0:T(8,128)(2,1)S(1)}, bf16[24,64,256]{2,1,0:T(8,128)(2,1)S(1)}, u32[]{:S(2)}, u32[]{:S(2)}) collective-permute-start(bf16[24,64,256]{2,1,0:T(8,128)(2,1)S(1)} %add_convert_fusion.17), channel_id=1, source_target_pairs={{8,16},{12,20},{9,17},{13,21},{10,18},{14,22},{11,19},{15,23}} | collective-permute-start | bytes 2359304 | tf_op jit(solution)/shard_map/ppermute | solution.py:1281
  587.0 9.9 %collective-permute-start.44 = (bf16[24,64,256]{2,1,0:T(8,128)(2,1)S(1)}, bf16[24,64,256]{2,1,0:T(8,128)(2,1)S(1)}, u32[]{:S(2)}, u32[]{:S(2)}) collective-permute-start(bf16[24,64,256]{2,1,0:T(8,128)(2,1)S(1)} %add_convert_fusion.18), channel_id=1, source_target_pairs={{24,16},{28,20},{25,17},{29,21},{26,18},{30,22},{27,19},{31,23}} | collective-permute-start | bytes 2359304 | tf_op jit(solution)/shard_map/ppermute | solution.py:1281
  588.5 12.3 %collective-permute-start.58 = (bf16[24,64,256]{2,1,0:T(8,128)(2,1)S(1)}, bf16[24,64,256]{2,1,0:T(8,128)(2,1)S(1)}, u32[]{:S(2)}, u32[]{:S(2)}) collective-permute-start(bf16[24,64,256]{2,1,0:T(8,128)(2,1)S(1)} %select_select_fusion.1), channel_id=1, source_target_pairs={{0,2},{1,3},{2,0},{3,1},{4,6},{5,7},{6,4},{7,5},{8,10},{9,11},{10,... | collective-permute-start | bytes 2359304 | tf_op jit(solution)/shard_map/ppermute | solution.py:1580
  597.2 15.6 %collective-permute-start.46 = (bf16[24,64,256]{2,1,0:T(8,128)(2,1)S(1)}, bf16[24,64,256]{2,1,0:T(8,128)(2,1)S(1)}, u32[]{:S(2)}, u32[]{:S(2)}) collective-permute-start(bf16[24,64,256]{2,1,0:T(8,128)(2,1)S(1)} %add_convert_fusion.15), channel_id=1, source_target_pairs={{16,8},{20,12},{17,9},{21,13},{18,10},{22,14},{19,11},{23,15}} | collective-permute-start | bytes 2359304 | tf_op jit(solution)/shard_map/ppermute | solution.py:1281
  601.1 15.3 %collective-permute-start.59 = (bf16[40,64,256]{2,1,0:T(8,128)(2,1)S(1)}, bf16[40,64,256]{2,1,0:T(8,128)(2,1)}, u32[]{:S(2)}, u32[]{:S(2)}) collective-permute-start(bf16[40,64,256]{2,1,0:T(8,128)(2,1)S(1)} %pad_maximum_fusion.1), channel_id=1, source_target_pairs={{0,1},{1,0},{2,3},{3,2},{4,5},{5,4},{6,7},{7,6},{8,9},{9,8},{10,11... | collective-permute-start | bytes 3932168 | tf_op jit(solution)/shard_map/ppermute | solution.py:1582
  614.0 20.0 %collective-permute-start.47 = (bf16[24,64,256]{2,1,0:T(8,128)(2,1)}, bf16[24,64,256]{2,1,0:T(8,128)(2,1)}, u32[]{:S(2)}, u32[]{:S(2)}) collective-permute-start(bf16[24,64,256]{2,1,0:T(8,128)(2,1)} %add_convert_fusion.13), channel_id=1, source_target_pairs={{8,0},{12,4},{9,1},{13,5},{10,2},{14,6},{11,3},{15,7}} | collective-permute-start | bytes 2359304 | tf_op jit(solution)/shard_map/ppermute | solution.py:1281
  636.1 16.0 %collective-permute-start.60 = (bf16[24,64,256]{2,1,0:T(8,128)(2,1)S(1)}, bf16[24,64,256]{2,1,0:T(8,128)(2,1)S(1)}, u32[]{:S(2)}, u32[]{:S(2)}) collective-permute-start(bf16[24,64,256]{2,1,0:T(8,128)(2,1)S(1)} %select_select_fusion), channel_id=1, source_target_pairs={{0,2},{1,3},{2,0},{3,1},{4,6},{5,7},{6,4},{7,5},{8,10},{9,11},{10,... | collective-permute-start | bytes 2359304 | tf_op jit(solution)/shard_map/ppermute | solution.py:1580
  652.4 10.8 %collective-permute-start.61 = (bf16[40,64,256]{2,1,0:T(8,128)(2,1)S(1)}, bf16[40,64,256]{2,1,0:T(8,128)(2,1)S(1)}, u32[]{:S(2)}, u32[]{:S(2)}) collective-permute-start(bf16[40,64,256]{2,1,0:T(8,128)(2,1)S(1)} %pad_maximum_fusion.2), channel_id=1, source_target_pairs={{0,1},{1,0},{2,3},{3,2},{4,5},{5,4},{6,7},{7,6},{8,9},{9,8},{10,11... | collective-permute-start | bytes 3932168 | tf_op jit(solution)/shard_map/ppermute | solution.py:1582
  (57 other events, 445.6 us)
Sparse Core Ops, SparseCore 0:
  13.1 202.3 all-gather.1
  274.1 74.0 reduce-scatter.2
  351.5 72.5 reduce-scatter.4

commit v6 on v5

--- a/solution.py
+++ b/solution.py
@@ -1472,7 +1472,7 @@
             out[t] = add(own[i, begin + t], got[i][begin + t])
             return carry
 
-        lax.fori_loop(0, size, tile, 0, unroll=2)
+        lax.fori_loop(0, size, tile, 0, unroll=4)
 
     for k in range(CHUNKS):
         for i in range(2):
@@ -1697,17 +1697,19 @@
         [(0, ("X", 1)), (0, ("N", 0))],
         lambda: (*co_backward(lengths, *back, near, far), far_both, swap_halves([text_source], (5,))[0]),
     )
+    early_sources = [None, vis_source]
     late_sources = [vis_source, None, text_source]
 
     def co_grads():
         text_co = weight_grads((6,), (x_text,), (dco_text,))
         late_sources[1] = (TILES[6][0], text_co)
-        return text_co, swap_halves(late_sources, (4,))[0], weight_grads((0,), (xv,), (dco_vis,))
-
-    text_co, far_four, vis_co = beside(
+        far_four = swap_halves(late_sources, (4,))[0]
+        early_sources[0] = (0, weight_grads((0,), (xv,), (dco_vis,)))
+        return text_co, far_four
+
+    text_co, far_four = beside(
         chunks, [(1, ("X", 1)), (0, ("Z", 1, 0)), (0, ("N", 1))], co_grads
     )
-    early_sources = [(0, vis_co), vis_source]
     late_sources[1] = (TILES[6][0], text_co)
 
     def merge_late():
@@ -1722,14 +1724,14 @@
         [(0, ("Y", 2)), (0, ("X", 3)), (1, ("Z", 1, 1))],
         lambda: merge(core, early_sources, 0, got, chunks),
     )
-    beside(chunks, [(0, ("Y", 0)), (0, ("X", 2)), (0, ("Z", 3, 0)), (1, ("X", 3)), (0, ("N", 2))], lambda: ())
-    chunks[1].step([("Y", 2), ("Z", 3, 0)])
+    beside(chunks, [(0, ("Y", 0)), (0, ("X", 2)), (0, ("Z", 3, 0)), (0, ("N", 2))], lambda: ())
+    chunks[1].step([("Y", 2), ("X", 3)])
     chunks[0].step([("X", 0), ("Z", 2, 0), ("Z", 3, 1), ("N", 3)])
-    chunks[1].step([("Y", 0), ("X", 2), ("Z", 3, 1)])
+    chunks[1].step([("Y", 0), ("X", 2), ("Z", 3, 0)])
     chunks[0].step([("Z", 0, 0), ("Z", 2, 1), ("Z", 3, 2), ("N", 4)])
-    chunks[1].step([("X", 0), ("Z", 2, 0), ("Z", 3, 2)])
+    chunks[1].step([("X", 0), ("Z", 2, 0), ("Z", 3, 1)])
     chunks[0].step([("Z", 0, 1)])
-    chunks[1].step([("Z", 0, 0), ("Z", 2, 1)])
+    chunks[1].step([("Z", 0, 0), ("Z", 2, 1), ("Z", 3, 2)])
     chunks[0].step([("Z", 0, 2)])
     chunks[1].step([("Z", 0, 1)])
     chunks[0].step([("F", 0)])

time: 707 us -> 696 us (0.984)
    ppermute x8, waiting for transfers between devices: 8.76 us -> 24 us  [send(): lax.ppermute(join([cut(lone, 1 - x, 1)[0], cut(both, 1 - x, 1)[0]]), 'dp'...]
    ppermute x23, waiting for transfers between devices: 67.1 us -> 55.2 us  [along_z(): lax.ppermute(value, 'dp', [(2 * a + x, 2 * b + x) for a, b in moves for x...]
    ppermute x5, waiting for transfers between devices: 35.9 us -> 24.8 us  [send(): lax.ppermute(state['norms', 0], axis, [(i, i ^ step) for i in range(size)])]
    ppermute x4, waiting for transfers between devices: 1.27 us -> 10.3 us  [send(): return lax.ppermute(cut(state['lone', who], 1 - y, 1)[0], 'seq', SWAP_Y)]
    ppermute x23, starting transfers between devices: 52.2 us -> 44.1 us  [along_z(): lax.ppermute(value, 'dp', [(2 * a + x, 2 * b + x) for a, b in moves for x...]
  transfers between devices with their start and end apart: 65 -> 65, of which waited for: 28 -> 34; matrix products, arithmetic and copies ran while one was open for 16% -> 16% of each run, Pallas kernels for 22% -> 22%
where the time goes in v6:
time: 696 us; the launch traced here: 689 us
  Pallas kernels  236 us (34%)
  waiting for transfers between devices  214 us (31%)
  starting transfers between devices  102 us (15%)
  other arithmetic  66.6 us (10%)
  local copies, waits for them, and re-layouts  54.7 us (8%)
  between operations  15.8 us (2%)
    ppermute x23, waiting for transfers between devices, along_z(): lax.ppermute(value, 'dp', [(2 * a + x, 2 * b + x) for a, b in moves for x...  55.2 us
    pallas_call x3, Pallas kernels, renew(): pl.pallas_call(functools.partial(renew_body, steps), in_specs=[pl.BlockSp...  54.8 us
    pallas_call x2, Pallas kernels, middle(): pl.pallas_call(functools.partial(middle_body, (begin, rows, span, head, c...  51.1 us
    ppermute x4, waiting for transfers between devices, gather_tiles(): lax.ppermute(join([part[:G_LONE] for part in here]), 'seq', SWAP_Y)  49 us
    pallas_call x4, Pallas kernels, weight_grads(): pl.pallas_call(functools.partial(weight_body, kinds), in_specs=whole(2 *...  44.4 us
    ppermute x23, starting transfers between devices, along_z(): lax.ppermute(value, 'dp', [(2 * a + x, 2 * b + x) for a, b in moves for x...  44.1 us
    ppermute x4, waiting for transfers between devices, gather_tiles(): out['x'] = lax.ppermute(rows[phase], 'dp', SWAP_X)  37.9 us
    convert_element_type x34, other arithmetic, add(): return (left.astype(F32) + right.astype(F32)).astype(BF16)  32.5 us
  transfers between devices with their start and end apart: 65, of which 34 were waited for; matrix products, arithmetic and copies ran while one was open for 16% of the time, Pallas kernels for 22%

profile of v6, /device:TPU:11, one launch (start us, length us, event | category | flops | bytes accessed | tf_op | source)
XLA Modules:
  0.0 688.8 jit_solution(9463793827998496763)
XLA Ops:
  7.7 5.2 shard_map.223
  13.7 5.2 shard_map.221
  22.0 21.3 %collective-permute-done = bf16[24,64,256]{2,1,0:T(8,128)(2,1)S(1)} collective-permute-done((bf16[24,64,256]{2,1,0:T(8,128)(2,1)}, bf16[24,64,256]{2,1,0:T(8,128)(2,1)S(1)}, u32[]{:S(2)}, u32[]{:S(2)}) %collective-permute-start) | collective-permute-done | bytes 786464 | tf_op jit(solution)/shard_map/ppermute | solution.py:1334
  43.3 8.7 %collective-permute-done.1 = bf16[24,64,256]{2,1,0:T(8,128)(2,1)S(1)} collective-permute-done((bf16[24,64,256]{2,1,0:T(8,128)(2,1)}, bf16[24,64,256]{2,1,0:T(8,128)(2,1)S(1)}, u32[]{:S(2)}, u32[]{:S(2)}) %collective-permute-start.1) | collective-permute-done | bytes 786464 | tf_op jit(solution)/shard_map/ppermute | solution.py:1281
  58.5 14.0 %collective-permute-done.3 = bf16[16,64,256]{2,1,0:T(8,128)(2,1)S(1)} collective-permute-done((bf16[16,64,256]{2,1,0:T(8,128)(2,1)S(1)}, bf16[16,64,256]{2,1,0:T(8,128)(2,1)S(1)}, u32[]{:S(2)}, u32[]{:S(2)}) %collective-permute-start.3) | collective-permute-done | bytes 524320 | tf_op jit(solution)/shard_map/ppermute | solution.py:1337
  74.0 10.7 %collective-permute-done.4 = bf16[24,64,256]{2,1,0:T(8,128)(2,1)S(1)} collective-permute-done((bf16[24,64,256]{2,1,0:T(8,128)(2,1)S(1)}, bf16[24,64,256]{2,1,0:T(8,128)(2,1)S(1)}, u32[]{:S(2)}, u32[]{:S(2)}) %collective-permute-start.4) | collective-permute-done | bytes 786464 | tf_op jit(solution)/shard_map/ppermute | solution.py:1281
  86.5 15.8 %collective-permute-start.5 = (bf16[64,64,256]{2,1,0:T(8,128)(2,1)S(1)}, bf16[64,64,256]{2,1,0:T(8,128)(2,1)S(1)}, u32[]{:S(2)}, u32[]{:S(2)}) collective-permute-start(bf16[64,64,256]{2,1,0:T(8,128)(2,1)S(1)} %get-tuple-element.652), channel_id=1, source_target_pairs={{0,1},{1,0},{2,3},{3,2},{4,5},{5,4},{6,7},{7,6},{8,9},{9,8},{10,11... | collective-permute-start | bytes 6291464 | tf_op jit(solution)/shard_map/ppermute | solution.py:1339
  102.2 2.6 collective-permute-start.8
  107.4 11.5 %collective-permute-done.7 = bf16[16,64,256]{2,1,0:T(8,128)(2,1)S(1)} collective-permute-done((bf16[16,64,256]{2,1,0:T(8,128)(2,1)S(1)}, bf16[16,64,256]{2,1,0:T(8,128)(2,1)S(1)}, u32[]{:S(2)}, u32[]{:S(2)}) %collective-permute-start.7) | collective-permute-done | bytes 524320 | tf_op jit(solution)/shard_map/ppermute | solution.py:1337
  118.9 2.5 collective-permute-done.6
  121.5 2.7 collective-permute-done.8
  142.1 17.1 %collective-permute-done.11 = bf16[16,64,256]{2,1,0:T(8,128)(2,1)S(1)} collective-permute-done((bf16[16,64,256]{2,1,0:T(8,128)(2,1)S(1)}, bf16[16,64,256]{2,1,0:T(8,128)(2,1)S(1)}, u32[]{:S(2)}, u32[]{:S(2)}) %collective-permute-start.11) | collective-permute-done | bytes 524320 | tf_op jit(solution)/shard_map/ppermute | solution.py:1337
  159.2 12.6 %collective-permute-done.10 = bf16[24,64,256]{2,1,0:T(8,128)(2,1)S(1)} collective-permute-done((bf16[24,64,256]{2,1,0:T(8,128)(2,1)}, bf16[24,64,256]{2,1,0:T(8,128)(2,1)S(1)}, u32[]{:S(2)}, u32[]{:S(2)}) %collective-permute-start.10) | collective-permute-done | bytes 786464 | tf_op jit(solution)/shard_map/ppermute | solution.py:1334
  182.2 2.3 bitcast_dynamic-update-slice_fusion.10
  185.6 2.3 bitcast_dynamic-update-slice_fusion.8
  187.9 6.4 collective-permute-done.13
  206.5 2.7 bitcast_dynamic-update-slice_fusion.6
  210.3 2.3 bitcast_dynamic-update-slice_fusion.4
  213.7 2.3 bitcast_dynamic-update-slice_fusion.2
  217.1 2.3 bitcast_dynamic-update-slice_fusion
  219.4 13.0 %shard_map.224 = (bf16[96,3072]{1,0:T(8,128)(2,1)}, bf16[256,3072]{1,0:T(8,128)(2,1)}, bf16[96,1024]{1,0:T(8,128)(2,1)}, bf16[256,1024]{1,0:T(8,128)(2,1)}) custom-call(s32[4]{0:T(128)} %concatenate.119.len_ref, bf16[96,1024]{1,0:T(8,128)(2,1)} %bitcast.278, bf16[256,768]{1,0:T(8,128)(2,1)} %refs_0_.1, bf16[512,64,256]{2,1,0:T(8,128)(2,1)} %bitcast.251, ...), custom_call_target="tpu_custom_call" | custom-call | bytes 74800000 | tf_op jit(solution)/shard_map/pallas_call | solution.py:881
  233.0 19.5 %shard_map.226 = (bf16[96,1024]{1,0:T(8,128)(2,1)}, bf16[96,1024]{1,0:T(8,128)(2,1)}, bf16[96,1024]{1,0:T(8,128)(2,1)}, bf16[96,1024]{1,0:T(8,128)(2,1)}, bf16[9...) custom-call(s32[2]{0:T(128)} %broadcast_1_len_ref.2.len_ref, ...), custom_call_target="tpu_custom_call" | custom-call | bytes 136000000 | tf_op jit(solution)/shard_map/pallas_call | solution.py:1186
  252.5 15.1 %shard_map.227.x_any.refs_0_.refs_1_ = bf16[448,64,256]{2,1,0:T(8,128)(2,1)} custom-call(bf16[96,1024]{1,0:T(8,128)(2,1)} %get-tuple-element.344.ctx_ref.refs_0_, bf16[96,1024]{1,0:T(8,128)(2,1)} %get-tuple-element.347.refs_1_, bf16[96,1024]{1,0:T(8,128)(2,1)} %get-tuple-element.348.refs_2_, bf16[96,1024]{1,0:T(8,128)(2,1)} %get-tuple-element.349.refs_3_, ...), custom_call_target="tpu_custom_call" | custom-call | bytes 60928000 | tf_op jit(solution)/shard_map/pallas_call | solution.py:1259
  267.6 6.4 shard_map.228
  274.1 2.9 shard_map.229
  277.8 31.7 %shard_map.225 = (bf16[256,768]{1,0:T(8,128)(2,1)}, bf16[256,768]{1,0:T(8,128)(2,1)}, bf16[256,3072]{1,0:T(8,128)(2,1)}, bf16[256,768]{1,0:T(8,128)(2,1)}, bf16[...) custom-call(s32[4]{0:T(128)} %concatenate.119.len_ref, ...), custom_call_target="tpu_custom_call" | custom-call | bytes 136000000 | tf_op jit(solution)/shard_map/pallas_call | solution.py:1186
  309.5 17.8 %shard_map.230.refs_0_.refs_2_.x_any = bf16[480,64,256]{2,1,0:T(8,128)(2,1)} custom-call(bf16[256,1024]{1,0:T(8,128)(2,1)} %get-tuple-element.374.ctx_ref.refs_0_, bf16[256,768]{1,0:T(8,128)(2,1)} %get-tuple-element.375.refs_1_, bf16[256,3072]{1,0:T(8,128)(2,1)} %get-tuple-element.376.refs_2_, bf16[256,768]{1,0:T(8,128)(2,1)} %get-tuple-element.377.refs_3_, ...), custom_call_target="tpu_custom_call" | custom-call | bytes 65280000 | tf_op jit(solution)/shard_map/pallas_call | solution.py:1259
  327.7 6.4 shard_map.239
  334.2 3.2 shard_map.233
  338.0 2.9 shard_map.232
  341.2 7.0 %reduce-scatter.3.cloned.1.call-done = bf16[64,64,256]{2,1,0:T(8,128)(2,1)} async-done(((bf16[256,64,256]{2,1,0:T(8,128)(2,1)}), bf16[64,64,256]{2,1,0:T(8,128)(2,1)}) %reduce-scatter.3.cloned.1.call-update) | async-done | bytes 2097168 | tf_op jit(solution)/shard_map/reduce_scatter | solution.py:1548
  352.2 13.9 %shard_map.231 = (bf16[96,3072]{1,0:T(8,128)(2,1)}, bf16[256,3072]{1,0:T(8,128)(2,1)}, f32[96,1024]{1,0:T(8,128)}, f32[256,768]{1,0:T(8,128)}) custom-call(s32[4]{0:T(128)} %concatenate.119.len_ref, bf16[96,3072]{1,0:T(8,128)(2,1)} %get-tuple-element.387.cv_ref, bf16[256,3072]{1,0:T(8,128)(2,1)} %get-tuple-element.388.ct_ref, ...), custom_call_target="tpu_custom_call" | custom-call | bytes 78200000 | tf_op jit(solution)/shard_map/pallas_call | solution.py:950
  366.2 3.5 collective-permute-done.16
  369.6 5.3 shard_map.234.refs_1_
  375.0 3.8 shard_map.235
  383.3 6.1 shard_map.236.refs_0_
  389.4 5.2 shard_map.237
  397.7 5.1 collective-permute-done.21
  402.8 11.7 %collective-permute-done.20 = bf16[24,64,256]{2,1,0:T(8,128)(2,1)} collective-permute-done((bf16[24,64,256]{2,1,0:T(8,128)(2,1)S(1)}, bf16[24,64,256]{2,1,0:T(8,128)(2,1)}, u32[]{:S(2)}, u32[]{:S(2)}) %collective-permute-start.20) | collective-permute-done | bytes 786464 | tf_op jit(solution)/shard_map/ppermute | solution.py:1573
  427.2 8.8 %shard_map.238 = (bf16[2,2,16,64,256]{4,3,2,1,0:T(8,128)(2,1)}, bf16[2,8,64,256]{3,2,1,0:T(8,128)(2,1)}, bf16[2,2,16,64,256]{4,3,2,1,0:T(8,128)(2,1)}, bf16[2,8,64,256]{3,2,1,0:T(8,128)(2,1)}) custom-call(s32[1]{0:T(128)} %bitcast.27.core_ref, bf16[448,64,256]{2,1,0:T(8,128)(2,1)} %shard_map.227.x_any.refs_0_.refs_1_, ...), custom_call_target="tpu_custom_call" | custom-call | bytes 27200000 | tf_op jit(solution)/shard_map/pallas_call | solution.py:1490
  439.6 2.3 dynamic-slice_bitcast_fusion.3
  442.0 2.5 add_convert_fusion.26
  445.9 8.8 %shard_map.240 = (bf16[2,2,16,64,256]{4,3,2,1,0:T(8,128)(2,1)}, bf16[2,8,64,256]{3,2,1,0:T(8,128)(2,1)}, bf16[2,2,16,64,256]{4,3,2,1,0:T(8,128)(2,1)}, bf16[2,8,64,256]{3,2,1,0:T(8,128)(2,1)}) custom-call(s32[1]{0:T(128)} %bitcast.27.core_ref, bf16[192,64,256]{2,1,0:T(8,128)(2,1)} %shard_map.236.refs_0_, ...), custom_call_target="tpu_custom_call" | custom-call | bytes 27200000 | tf_op jit(solution)/shard_map/pallas_call | solution.py:1490
  454.7 2.4 add_convert_fusion.25
  457.1 6.3 collective-permute-done.30
  471.6 2.5 add_convert_fusion.23
  474.1 12.7 %collective-permute-done.34 = f32[2,5376]{1,0:T(2,128)S(1)} collective-permute-done((f32[2,5376]{1,0:T(2,128)S(1)}, f32[2,5376]{1,0:T(2,128)S(1)}, u32[]{:S(2)}, u32[]{:S(2)}) %collective-permute-start.34) | collective-permute-done | bytes 43040 | tf_op jit(solution)/shard_map/ppermute | solution.py:1585
  486.8 3.2 collective-permute-done.31
  498.1 12.1 %collective-permute-done.51 = f32[2,5376]{1,0:T(2,128)S(1)} collective-permute-done((f32[2,5376]{1,0:T(2,128)S(1)}, f32[2,5376]{1,0:T(2,128)S(1)}, u32[]{:S(2)}, u32[]{:S(2)}) %collective-permute-start.51) | collective-permute-done | bytes 43040 | tf_op jit(solution)/shard_map/ppermute | solution.py:1585
  511.7 6.9 %collective-permute-start.53 = (bf16[24,64,256]{2,1,0:T(8,128)(2,1)S(1)}, bf16[24,64,256]{2,1,0:T(8,128)(2,1)}, u32[]{:S(2)}, u32[]{:S(2)}) collective-permute-start(bf16[24,64,256]{2,1,0:T(8,128)(2,1)S(1)} %add_convert_fusion.9), channel_id=1, source_target_pairs={{8,16},{12,20},{9,17},{13,21},{10,18},{14,22},{11,19},{15,23}} | collective-permute-start | bytes 2359304 | tf_op jit(solution)/shard_map/ppermute | solution.py:1281
  519.0 7.2 %collective-permute-done.36 = bf16[24,64,256]{2,1,0:T(8,128)(2,1)S(1)} collective-permute-done((bf16[24,64,256]{2,1,0:T(8,128)(2,1)S(1)}, bf16[24,64,256]{2,1,0:T(8,128)(2,1)S(1)}, u32[]{:S(2)}, u32[]{:S(2)}) %collective-permute-start.36) | collective-permute-done | bytes 786464 | tf_op jit(solution)/shard_map/ppermute | solution.py:1573
  540.4 7.4 %collective-permute-done.39 = bf16[24,64,256]{2,1,0:T(8,128)(2,1)} collective-permute-done((bf16[24,64,256]{2,1,0:T(8,128)(2,1)}, bf16[24,64,256]{2,1,0:T(8,128)(2,1)}, u32[]{:S(2)}, u32[]{:S(2)}) %collective-permute-start.39) | collective-permute-done | bytes 786464 | tf_op jit(solution)/shard_map/ppermute | solution.py:1281
  548.1 3.4 collective-permute-done.37
  562.3 4.1 collective-permute-start.57
  566.4 3.9 collective-permute-done.41
  572.9 4.5 collective-permute-start.44
  580.1 6.2 collective-permute-done.44
  590.4 9.4 %collective-permute-start.59 = (bf16[40,64,256]{2,1,0:T(8,128)(2,1)S(1)}, bf16[40,64,256]{2,1,0:T(8,128)(2,1)}, u32[]{:S(2)}, u32[]{:S(2)}) collective-permute-start(bf16[40,64,256]{2,1,0:T(8,128)(2,1)S(1)} %pad_maximum_fusion.1), channel_id=1, source_target_pairs={{0,1},{1,0},{2,3},{3,2},{4,5},{5,4},{6,7},{7,6},{8,9},{9,8},{10,11... | collective-permute-start | bytes 3932168 | tf_op jit(solution)/shard_map/ppermute | solution.py:1582
  602.2 2.6 collective-permute-start.47
  604.9 3.0 broadcast_select_fusion.2
  607.9 14.5 %shard_map.241 = (f32[20224,128]{1,0:T(8,128)}, f32[20224,128]{1,0:T(8,128)}, f32[20224,128]{1,0:T(8,128)}, f32[20224,128]{1,0:T(8,128)}) custom-call(s32[20]{0:T(128)} %constant.168.which_ref, bf16[40,64,256]{2,1,0:T(8,128)(2,1)} %get-tuple-element.626.g_any, f32[20224,128]{1,0:T(8,128)} %bitcast.257, f32[20224,128]{1,0:T(8,128)} %bitcast.260, ...), custom_call_target="tpu_custom_call" | custom-call | bytes 47600000 | tf_op jit(solution)/shard_map/pallas_call | solution.py:736
  626.9 14.4 %shard_map.242 = (f32[20224,128]{1,0:T(8,128)}, f32[20224,128]{1,0:T(8,128)}, f32[20224,128]{1,0:T(8,128)}, f32[20224,128]{1,0:T(8,128)}) custom-call(s32[20]{0:T(128)} %constant.169.which_ref, bf16[40,64,256]{2,1,0:T(8,128)(2,1)} %get-tuple-element.625.g_any, ...), custom_call_target="tpu_custom_call", output_to_operand_aliasing={{0}: (7, {}), {1}: (8, {}), {2}: (9, {}), {3}: (10, {})} | custom-call | bytes 47600000 | tf_op jit(solution)/shard_map/pallas_call | solution.py:736
  641.6 10.0 %collective-permute-start.61 = (bf16[40,64,256]{2,1,0:T(8,128)(2,1)S(1)}, bf16[40,64,256]{2,1,0:T(8,128)(2,1)S(1)}, u32[]{:S(2)}, u32[]{:S(2)}) collective-permute-start(bf16[40,64,256]{2,1,0:T(8,128)(2,1)S(1)} %pad_maximum_fusion.2), channel_id=1, source_target_pairs={{0,1},{1,0},{2,3},{3,2},{4,5},{5,4},{6,7},{7,6},{8,9},{9,8},{10,11... | collective-permute-start | bytes 3932168 | tf_op jit(solution)/shard_map/ppermute | solution.py:1582
  656.3 25.9 %shard_map.243 = (f32[20224,128]{1,0:T(8,128)}, f32[20224,128]{1,0:T(8,128)}, f32[20224,128]{1,0:T(8,128)}, f32[20224,128]{1,0:T(8,128)}) custom-call(s32[40]{0:T(128)} %constant.158.clone.which_ref, bf16[80,64,256]{2,1,0:T(8,128)(2,1)} %pad_maximum_fusion.g_any, ...), custom_call_target="tpu_custom_call", output_to_operand_aliasing={{0}: (7, {}), {1}: (8, {}), {2}: (9, {}), {3}: (10, {})} | custom-call | bytes 95200000 | tf_op jit(solution)/shard_map/pallas_call | solution.py:736
  (382 shorter events, 156.8 us)
Async XLA Ops:
  7.2 212.3 %all-gather.2.cloned.1.call-start = ((), (), s32[]{:S(2)}) async-start(), calls=%async_computation.2 | async-start | bytes 25952256 | tf_op jit(solution)/shard_map/all_gather | solution.py:1323
  13.0 335.2 %reduce-scatter.3.cloned.1.call-start = ((), (), s32[]{:S(2)}) async-start(), calls=%async_computation.3 | async-start | bytes 10485760 | tf_op jit(solution)/shard_map/reduce_scatter | solution.py:1548
  18.9 24.4 %collective-permute-start = (bf16[24,64,256]{2,1,0:T(8,128)(2,1)}, bf16[24,64,256]{2,1,0:T(8,128)(2,1)S(1)}, u32[]{:S(2)}, u32[]{:S(2)}) collective-permute-start(bf16[24,64,256]{2,1,0:T(8,128)(2,1)} %shard_map.221), channel_id=1, source_target_pairs={{0,4},{4,0},{8,12},{12,8},{16,20},{20,16},{24,28},{28,24},{1,5},{5... | collective-permute-start | bytes 2359304 | tf_op jit(solution)/shard_map/ppermute | solution.py:1334
  19.2 32.8 %collective-permute-start.1 = (bf16[24,64,256]{2,1,0:T(8,128)(2,1)}, bf16[24,64,256]{2,1,0:T(8,128)(2,1)S(1)}, u32[]{:S(2)}, u32[]{:S(2)}) collective-permute-start(bf16[24,64,256]{2,1,0:T(8,128)(2,1)} %shard_map.221), channel_id=1, source_target_pairs={{0,8},{4,12},{8,16},{12,20},{16,24},{20,28},{24,0},{28,4},{1,9},{5... | collective-permute-start | bytes 2359304 | tf_op jit(solution)/shard_map/ppermute | solution.py:1281
  52.0 22.0 %collective-permute-start.2 = (bf16[24,64,256]{2,1,0:T(8,128)(2,1)S(1)}, bf16[24,64,256]{2,1,0:T(8,128)(2,1)}, u32[]{:S(2)}, u32[]{:S(2)}) collective-permute-start(bf16[24,64,256]{2,1,0:T(8,128)(2,1)S(1)} %collective-permute-done.1), channel_id=1, source_target_pairs={{0,4},{4,0},{8,12},{12,8},{16,20},{20,16},{24,28},{28,24},{1,5},{5... | collective-permute-start | bytes 2359304 | tf_op jit(solution)/shard_map/ppermute | solution.py:1334
  53.9 30.8 %collective-permute-start.4 = (bf16[24,64,256]{2,1,0:T(8,128)(2,1)S(1)}, bf16[24,64,256]{2,1,0:T(8,128)(2,1)S(1)}, u32[]{:S(2)}, u32[]{:S(2)}) collective-permute-start(bf16[24,64,256]{2,1,0:T(8,128)(2,1)S(1)} %collective-permute-done.1), channel_id=1, source_target_pairs={{0,8},{4,12},{8,16},{12,20},{16,24},{20,28},{24,0},{28,4},{1,9},{5... | collective-permute-start | bytes 2359304 | tf_op jit(solution)/shard_map/ppermute | solution.py:1281
  57.2 15.3 %collective-permute-start.3 = (bf16[16,64,256]{2,1,0:T(8,128)(2,1)S(1)}, bf16[16,64,256]{2,1,0:T(8,128)(2,1)S(1)}, u32[]{:S(2)}, u32[]{:S(2)}) collective-permute-start(bf16[16,64,256]{2,1,0:T(8,128)(2,1)S(1)} %pad_maximum_fusion.19), channel_id=1, source_target_pairs={{0,2},{1,3},{2,0},{3,1},{4,6},{5,7},{6,4},{7,5},{8,10},{9,11},{10,... | collective-permute-start | bytes 1572872 | tf_op jit(solution)/shard_map/ppermute | solution.py:1337
  86.5 37.7 %collective-permute-start.5 = (bf16[64,64,256]{2,1,0:T(8,128)(2,1)S(1)}, bf16[64,64,256]{2,1,0:T(8,128)(2,1)S(1)}, u32[]{:S(2)}, u32[]{:S(2)}) collective-permute-start(bf16[64,64,256]{2,1,0:T(8,128)(2,1)S(1)} %get-tuple-element.652), channel_id=1, source_target_pairs={{0,1},{1,0},{2,3},{3,2},{4,5},{5,4},{6,7},{7,6},{8,9},{9,8},{10,11... | collective-permute-start | bytes 6291464 | tf_op jit(solution)/shard_map/ppermute | solution.py:1339
  102.2 19.2 %collective-permute-start.6 = (bf16[24,64,256]{2,1,0:T(8,128)(2,1)S(1)}, bf16[24,64,256]{2,1,0:T(8,128)(2,1)S(1)}, u32[]{:S(2)}, u32[]{:S(2)}) collective-permute-start(bf16[24,64,256]{2,1,0:T(8,128)(2,1)S(1)} %collective-permute-done.4), channel_id=1, source_target_pairs={{0,4},{4,0},{8,12},{12,8},{16,20},{20,16},{24,28},{28,24},{1,5},{5... | collective-permute-start | bytes 2359304 | tf_op jit(solution)/shard_map/ppermute | solution.py:1334
  102.2 21.9 %collective-permute-start.8 = (bf16[24,64,256]{2,1,0:T(8,128)(2,1)S(1)}, bf16[24,64,256]{2,1,0:T(8,128)(2,1)}, u32[]{:S(2)}, u32[]{:S(2)}) collective-permute-start(bf16[24,64,256]{2,1,0:T(8,128)(2,1)S(1)} %collective-permute-done.4), channel_id=1, source_target_pairs={{0,8},{4,12},{8,16},{12,20},{16,24},{20,28},{24,0},{28,4},{1,9},{5... | collective-permute-start | bytes 2359304 | tf_op jit(solution)/shard_map/ppermute | solution.py:1281
  105.9 13.0 %collective-permute-start.7 = (bf16[16,64,256]{2,1,0:T(8,128)(2,1)S(1)}, bf16[16,64,256]{2,1,0:T(8,128)(2,1)S(1)}, u32[]{:S(2)}, u32[]{:S(2)}) collective-permute-start(bf16[16,64,256]{2,1,0:T(8,128)(2,1)S(1)} %pad_maximum_fusion.20), channel_id=1, source_target_pairs={{0,2},{1,3},{2,0},{3,1},{4,6},{5,7},{6,4},{7,5},{8,10},{9,11},{10,... | collective-permute-start | bytes 1572872 | tf_op jit(solution)/shard_map/ppermute | solution.py:1337
  133.2 38.5 %collective-permute-start.9 = (bf16[64,64,256]{2,1,0:T(8,128)(2,1)}, bf16[64,64,256]{2,1,0:T(8,128)(2,1)}, u32[]{:S(2)}, u32[]{:S(2)}) collective-permute-start(bf16[64,64,256]{2,1,0:T(8,128)(2,1)} %get-tuple-element.648), channel_id=1, source_target_pairs={{0,1},{1,0},{2,3},{3,2},{4,5},{5,4},{6,7},{7,6},{8,9},{9,8},{10,11... | collective-permute-start | bytes 6291464 | tf_op jit(solution)/shard_map/ppermute | solution.py:1339
  134.0 25.2 %collective-permute-start.11 = (bf16[16,64,256]{2,1,0:T(8,128)(2,1)S(1)}, bf16[16,64,256]{2,1,0:T(8,128)(2,1)S(1)}, u32[]{:S(2)}, u32[]{:S(2)}) collective-permute-start(bf16[16,64,256]{2,1,0:T(8,128)(2,1)S(1)} %pad_maximum_fusion.21), channel_id=1, source_target_pairs={{0,2},{1,3},{2,0},{3,1},{4,6},{5,7},{6,4},{7,5},{8,10},{9,11},{10,... | collective-permute-start | bytes 1572872 | tf_op jit(solution)/shard_map/ppermute | solution.py:1337
  135.3 36.5 %collective-permute-start.10 = (bf16[24,64,256]{2,1,0:T(8,128)(2,1)}, bf16[24,64,256]{2,1,0:T(8,128)(2,1)S(1)}, u32[]{:S(2)}, u32[]{:S(2)}) collective-permute-start(bf16[24,64,256]{2,1,0:T(8,128)(2,1)} %collective-permute-done.8), channel_id=1, source_target_pairs={{0,4},{4,0},{8,12},{12,8},{16,20},{20,16},{24,28},{28,24},{1,5},{5... | collective-permute-start | bytes 2359304 | tf_op jit(solution)/shard_map/ppermute | solution.py:1334
  177.4 17.0 %collective-permute-start.12 = (bf16[64,64,256]{2,1,0:T(8,128)(2,1)}, bf16[64,64,256]{2,1,0:T(8,128)(2,1)}, u32[]{:S(2)}, u32[]{:S(2)}) collective-permute-start(bf16[64,64,256]{2,1,0:T(8,128)(2,1)} %get-tuple-element.644), channel_id=1, source_target_pairs={{0,1},{1,0},{2,3},{3,2},{4,5},{5,4},{6,7},{7,6},{8,9},{9,8},{10,11... | collective-permute-start | bytes 6291464 | tf_op jit(solution)/shard_map/ppermute | solution.py:1339
  179.6 14.8 %collective-permute-start.13 = (bf16[16,64,256]{2,1,0:T(8,128)(2,1)S(1)}, bf16[16,64,256]{2,1,0:T(8,128)(2,1)S(1)}, u32[]{:S(2)}, u32[]{:S(2)}) collective-permute-start(bf16[16,64,256]{2,1,0:T(8,128)(2,1)S(1)} %pad_maximum_fusion.22), channel_id=1, source_target_pairs={{0,2},{1,3},{2,0},{3,1},{4,6},{5,7},{6,4},{7,5},{8,10},{9,11},{10,... | collective-permute-start | bytes 1572872 | tf_op jit(solution)/shard_map/ppermute | solution.py:1337
  202.6 10.0 %collective-permute-start.14 = (bf16[64,64,256]{2,1,0:T(8,128)(2,1)}, bf16[64,64,256]{2,1,0:T(8,128)(2,1)}, u32[]{:S(2)}, u32[]{:S(2)}) collective-permute-start(bf16[64,64,256]{2,1,0:T(8,128)(2,1)} %get-tuple-element.640), channel_id=1, source_target_pairs={{0,1},{1,0},{2,3},{3,2},{4,5},{5,4},{6,7},{7,6},{8,9},{9,8},{10,11... | collective-permute-start | bytes 6291464 | tf_op jit(solution)/shard_map/ppermute | solution.py:1339
  274.1 150.1 %reduce-scatter.5.cloned.1.call-start = ((), (), s32[]{:S(2)}) async-start(), calls=%async_computation.4 | async-start | bytes 10485760 | tf_op jit(solution)/shard_map/reduce_scatter | solution.py:1548
  277.1 32.4 %collective-permute-start.15 = (bf16[32,64,256]{2,1,0:T(8,128)(2,1)}, bf16[32,64,256]{2,1,0:T(8,128)(2,1)S(1)}, u32[]{:S(2)}, u32[]{:S(2)}) collective-permute-start(bf16[32,64,256]{2,1,0:T(8,128)(2,1)} %get-tuple-element.372), channel_id=1, source_target_pairs={{0,1},{1,0},{2,3},{3,2},{4,5},{5,4},{6,7},{7,6},{8,9},{9,8},{10,11... | collective-permute-start | bytes 3145736 | tf_op jit(solution)/shard_map/ppermute | solution.py:1666
  337.4 28.7 %collective-permute-start.19 = (bf16[80,64,256]{2,1,0:T(8,128)(2,1)}, bf16[80,64,256]{2,1,0:T(8,128)(2,1)}, u32[]{:S(2)}, u32[]{:S(2)}) collective-permute-start(bf16[80,64,256]{2,1,0:T(8,128)(2,1)} %shard_map.233), channel_id=1, source_target_pairs={{0,1},{1,0},{2,3},{3,2},{4,5},{5,4},{6,7},{7,6},{8,9},{9,8},{10,11... | collective-permute-start | bytes 7864328 | tf_op jit(solution)/shard_map/ppermute | solution.py:1692
  341.0 25.2 %collective-permute-start.18 = (bf16[32,64,256]{2,1,0:T(8,128)(2,1)}, bf16[32,64,256]{2,1,0:T(8,128)(2,1)}, u32[]{:S(2)}, u32[]{:S(2)}) collective-permute-start(bf16[32,64,256]{2,1,0:T(8,128)(2,1)} %get-tuple-element.397), channel_id=1, source_target_pairs={{0,1},{1,0},{2,3},{3,2},{4,5},{5,4},{6,7},{7,6},{8,9},{9,8},{10,11... | collective-permute-start | bytes 3145736 | tf_op jit(solution)/shard_map/ppermute | solution.py:1666
  350.9 18.7 %collective-permute-start.16 = (bf16[24,64,256]{2,1,0:T(8,128)(2,1)}, bf16[24,64,256]{2,1,0:T(8,128)(2,1)}, u32[]{:S(2)}, u32[]{:S(2)}) collective-permute-start(bf16[24,64,256]{2,1,0:T(8,128)(2,1)} %pad_maximum_fusion.11), channel_id=1, source_target_pairs={{0,4},{4,0},{8,12},{12,8},{16,20},{20,16},{24,28},{28,24},{1,5},{5... | collective-permute-start | bytes 2359304 | tf_op jit(solution)/shard_map/ppermute | solution.py:1573
  351.2 14.9 %collective-permute-start.17 = (f32[2,5376]{1,0:T(2,128)S(1)}, f32[2,5376]{1,0:T(2,128)S(1)}, u32[]{:S(2)}, u32[]{:S(2)}) collective-permute-start(f32[2,5376]{1,0:T(2,128)S(1)} %constant_dynamic-update-slice_fusion.24), channel_id=1, source_target_pairs={{0,1},{1,0},{2,3},{3,2},{4,5},{5,4},{6,7},{7,6},{8,9},{9,8},{10,11... | collective-permute-start | bytes 129032 | tf_op jit(solution)/shard_map/ppermute | solution.py:1585
  378.7 35.8 %collective-permute-start.23 = (bf16[80,64,256]{2,1,0:T(8,128)(2,1)}, bf16[80,64,256]{2,1,0:T(8,128)(2,1)}, u32[]{:S(2)}, u32[]{:S(2)}) collective-permute-start(bf16[80,64,256]{2,1,0:T(8,128)(2,1)} %shard_map.235), channel_id=1, source_target_pairs={{0,1},{1,0},{2,3},{3,2},{4,5},{5,4},{6,7},{7,6},{8,9},{9,8},{10,11... | collective-permute-start | bytes 7864328 | tf_op jit(solution)/shard_map/ppermute | solution.py:1692
  379.8 15.5 %collective-permute-start.22 = (f32[2,5376]{1,0:T(2,128)S(1)}, f32[2,5376]{1,0:T(2,128)S(1)}, u32[]{:S(2)}, u32[]{:S(2)}) collective-permute-start(f32[2,5376]{1,0:T(2,128)S(1)} %add.383), channel_id=1, source_target_pairs={{0,2},{1,3},{2,0},{3,1},{4,6},{5,7},{6,4},{7,5},{8,10},{9,11},{10,... | collective-permute-start | bytes 129032 | tf_op jit(solution)/shard_map/ppermute | solution.py:1585
  382.0 20.8 %collective-permute-start.21 = (bf16[24,64,256]{2,1,0:T(8,128)(2,1)S(1)}, bf16[24,64,256]{2,1,0:T(8,128)(2,1)}, u32[]{:S(2)}, u32[]{:S(2)}) collective-permute-start(bf16[24,64,256]{2,1,0:T(8,128)(2,1)S(1)} %add_convert_fusion.29), channel_id=1, source_target_pairs={{24,16},{28,20},{0,8},{4,12},{25,17},{29,21},{1,9},{5,13},{26,18},... | collective-permute-start | bytes 2359304 | tf_op jit(solution)/shard_map/ppermute | solution.py:1281
  394.6 41.5 %collective-permute-start.26 = (bf16[80,64,256]{2,1,0:T(8,128)(2,1)}, bf16[80,64,256]{2,1,0:T(8,128)(2,1)}, u32[]{:S(2)}, u32[]{:S(2)}) collective-permute-start(bf16[80,64,256]{2,1,0:T(8,128)(2,1)} %get-tuple-element.414), channel_id=1, source_target_pairs={{0,1},{1,0},{2,3},{3,2},{4,5},{5,4},{6,7},{7,6},{8,9},{9,8},{10,11... | collective-permute-start | bytes 7864328 | tf_op jit(solution)/shard_map/ppermute | solution.py:1692
  394.8 41.2 %collective-permute-start.27 = (bf16[80,64,256]{2,1,0:T(8,128)(2,1)}, bf16[80,64,256]{2,1,0:T(8,128)(2,1)}, u32[]{:S(2)}, u32[]{:S(2)}) collective-permute-start(bf16[80,64,256]{2,1,0:T(8,128)(2,1)} %get-tuple-element.415), channel_id=1, source_target_pairs={{0,1},{1,0},{2,3},{3,2},{4,5},{5,4},{6,7},{7,6},{8,9},{9,8},{10,11... | collective-permute-start | bytes 7864328 | tf_op jit(solution)/shard_map/ppermute | solution.py:1692
  395.3 19.1 %collective-permute-start.20 = (bf16[24,64,256]{2,1,0:T(8,128)(2,1)S(1)}, bf16[24,64,256]{2,1,0:T(8,128)(2,1)}, u32[]{:S(2)}, u32[]{:S(2)}) collective-permute-start(bf16[24,64,256]{2,1,0:T(8,128)(2,1)S(1)} %pad_maximum_fusion.12), channel_id=1, source_target_pairs={{0,4},{4,0},{8,12},{12,8},{16,20},{20,16},{24,28},{28,24},{1,5},{5... | collective-permute-start | bytes 2359304 | tf_op jit(solution)/shard_map/ppermute | solution.py:1573
  416.9 20.7 %collective-permute-start.25 = (bf16[24,64,256]{2,1,0:T(8,128)(2,1)}, bf16[24,64,256]{2,1,0:T(8,128)(2,1)}, u32[]{:S(2)}, u32[]{:S(2)}) collective-permute-start(bf16[24,64,256]{2,1,0:T(8,128)(2,1)} %add_convert_fusion.27), channel_id=1, source_target_pairs={{24,16},{28,20},{0,8},{4,12},{25,17},{29,21},{1,9},{5,13},{26,18},... | collective-permute-start | bytes 2359304 | tf_op jit(solution)/shard_map/ppermute | solution.py:1281
  419.6 20.1 %collective-permute-start.24 = (bf16[24,64,256]{2,1,0:T(8,128)(2,1)S(1)}, bf16[24,64,256]{2,1,0:T(8,128)(2,1)}, u32[]{:S(2)}, u32[]{:S(2)}) collective-permute-start(bf16[24,64,256]{2,1,0:T(8,128)(2,1)S(1)} %add_convert_fusion.28), channel_id=1, source_target_pairs={{16,8},{20,12},{17,9},{21,13},{18,10},{22,14},{19,11},{23,15}} | collective-permute-start | bytes 2359304 | tf_op jit(solution)/shard_map/ppermute | solution.py:1281
  426.9 30.1 %collective-permute-start.29 = (bf16[24,64,256]{2,1,0:T(8,128)(2,1)}, bf16[24,64,256]{2,1,0:T(8,128)(2,1)}, u32[]{:S(2)}, u32[]{:S(2)}) collective-permute-start(bf16[24,64,256]{2,1,0:T(8,128)(2,1)} %pad_maximum_fusion.13), channel_id=1, source_target_pairs={{0,4},{4,0},{8,12},{12,8},{16,20},{20,16},{24,28},{28,24},{1,5},{5... | collective-permute-start | bytes 2359304 | tf_op jit(solution)/shard_map/ppermute | solution.py:1573
  441.9 23.1 %collective-permute-start.28 = (bf16[2,16,64,256]{3,2,1,0:T(8,128)(2,1)}, bf16[2,16,64,256]{3,2,1,0:T(8,128)(2,1)}, u32[]{:S(2)}, u32[]{:S(2)}) collective-permute-start(bf16[2,16,64,256]{3,2,1,0:T(8,128)(2,1)} %dynamic-slice_bitcast_fusion.3), channel_id=1, source_target_pairs={{0,2},{1,3},{2,0},{3,1},{4,6},{5,7},{6,4},{7,5},{8,10},{9,11},{10,... | collective-permute-start | bytes 3145736 | tf_op jit(solution)/shard_map/ppermute | solution.py:1570
  444.6 18.8 %collective-permute-start.30 = (bf16[24,64,256]{2,1,0:T(8,128)(2,1)}, bf16[24,64,256]{2,1,0:T(8,128)(2,1)}, u32[]{:S(2)}, u32[]{:S(2)}) collective-permute-start(bf16[24,64,256]{2,1,0:T(8,128)(2,1)} %add_convert_fusion.26), channel_id=1, source_target_pairs={{16,8},{20,12},{17,9},{21,13},{18,10},{22,14},{19,11},{23,15}} | collective-permute-start | bytes 2359304 | tf_op jit(solution)/shard_map/ppermute | solution.py:1281
  466.7 20.1 %collective-permute-start.33 = (bf16[24,64,256]{2,1,0:T(8,128)(2,1)S(1)}, bf16[24,64,256]{2,1,0:T(8,128)(2,1)S(1)}, u32[]{:S(2)}, u32[]{:S(2)}) collective-permute-start(bf16[24,64,256]{2,1,0:T(8,128)(2,1)S(1)} %add_convert_fusion.24), channel_id=1, source_target_pairs={{0,8},{4,12},{1,9},{5,13},{2,10},{6,14},{3,11},{7,15}} | collective-permute-start | bytes 2359304 | tf_op jit(solution)/shard_map/ppermute | solution.py:1281
  468.1 21.9 %collective-permute-start.31 = (bf16[2,16,64,256]{3,2,1,0:T(8,128)(2,1)S(1)}, bf16[2,16,64,256]{3,2,1,0:T(8,128)(2,1)S(1)}, u32[]{:S(2)}, u32[]{:S(2)}) collective-permute-start(bf16[2,16,64,256]{3,2,1,0:T(8,128)(2,1)S(1)} %dynamic-slice_bitcast_fusion.2), channel_id=1, source_target_pairs={{0,2},{1,3},{2,0},{3,1},{4,6},{5,7},{6,4},{7,5},{8,10},{9,11},{10,... | collective-permute-start | bytes 3145736 | tf_op jit(solution)/shard_map/ppermute | solution.py:1570
  470.0 16.7 %collective-permute-start.32 = (bf16[24,64,256]{2,1,0:T(8,128)(2,1)S(1)}, bf16[24,64,256]{2,1,0:T(8,128)(2,1)S(1)}, u32[]{:S(2)}, u32[]{:S(2)}) collective-permute-start(bf16[24,64,256]{2,1,0:T(8,128)(2,1)S(1)} %pad_maximum_fusion.14), channel_id=1, source_target_pairs={{0,4},{4,0},{8,12},{12,8},{16,20},{20,16},{24,28},{28,24},{1,5},{5... | collective-permute-start | bytes 2359304 | tf_op jit(solution)/shard_map/ppermute | solution.py:1573
  470.4 16.3 %collective-permute-start.34 = (f32[2,5376]{1,0:T(2,128)S(1)}, f32[2,5376]{1,0:T(2,128)S(1)}, u32[]{:S(2)}, u32[]{:S(2)}) collective-permute-start(f32[2,5376]{1,0:T(2,128)S(1)} %add.386), channel_id=1, source_target_pairs={{0,4},{4,0},{8,12},{12,8},{16,20},{20,16},{24,28},{28,24},{1,5},{5... | collective-permute-start | bytes 129032 | tf_op jit(solution)/shard_map/ppermute | solution.py:1585
  490.3 20.0 %collective-permute-start.50 = (bf16[24,64,256]{2,1,0:T(8,128)(2,1)S(1)}, bf16[24,64,256]{2,1,0:T(8,128)(2,1)S(1)}, u32[]{:S(2)}, u32[]{:S(2)}) collective-permute-start(bf16[24,64,256]{2,1,0:T(8,128)(2,1)S(1)} %add_convert_fusion.11), channel_id=1, source_target_pairs={{8,16},{12,20},{9,17},{13,21},{10,18},{14,22},{11,19},{15,23}} | collective-permute-start | bytes 2359304 | tf_op jit(solution)/shard_map/ppermute | solution.py:1281
  492.0 18.3 %collective-permute-start.49 = (bf16[24,64,256]{2,1,0:T(8,128)(2,1)S(1)}, bf16[24,64,256]{2,1,0:T(8,128)(2,1)S(1)}, u32[]{:S(2)}, u32[]{:S(2)}) collective-permute-start(bf16[24,64,256]{2,1,0:T(8,128)(2,1)S(1)} %add_convert_fusion.12), channel_id=1, source_target_pairs={{0,8},{4,12},{24,16},{28,20},{1,9},{5,13},{25,17},{29,21},{2,10},{... | collective-permute-start | bytes 2359304 | tf_op jit(solution)/shard_map/ppermute | solution.py:1281
  494.1 16.2 %collective-permute-start.48 = (bf16[24,64,256]{2,1,0:T(8,128)(2,1)S(1)}, bf16[24,64,256]{2,1,0:T(8,128)(2,1)S(1)}, u32[]{:S(2)}, u32[]{:S(2)}) collective-permute-start(bf16[24,64,256]{2,1,0:T(8,128)(2,1)S(1)} %pad_maximum_fusion.18), channel_id=1, source_target_pairs={{0,4},{4,0},{8,12},{12,8},{16,20},{20,16},{24,28},{28,24},{1,5},{5... | collective-permute-start | bytes 2359304 | tf_op jit(solution)/shard_map/ppermute | solution.py:1573
  494.5 15.7 %collective-permute-start.51 = (f32[2,5376]{1,0:T(2,128)S(1)}, f32[2,5376]{1,0:T(2,128)S(1)}, u32[]{:S(2)}, u32[]{:S(2)}) collective-permute-start(f32[2,5376]{1,0:T(2,128)S(1)} %add.410), channel_id=1, source_target_pairs={{0,8},{4,12},{8,0},{12,4},{16,24},{20,28},{24,16},{28,20},{1,9},{5... | collective-permute-start | bytes 129032 | tf_op jit(solution)/shard_map/ppermute | solution.py:1585
  496.9 29.4 %collective-permute-start.36 = (bf16[24,64,256]{2,1,0:T(8,128)(2,1)S(1)}, bf16[24,64,256]{2,1,0:T(8,128)(2,1)S(1)}, u32[]{:S(2)}, u32[]{:S(2)}) collective-permute-start(bf16[24,64,256]{2,1,0:T(8,128)(2,1)S(1)} %pad_maximum_fusion.15), channel_id=1, source_target_pairs={{0,4},{4,0},{8,12},{12,8},{16,20},{20,16},{24,28},{28,24},{1,5},{5... | collective-permute-start | bytes 2359304 | tf_op jit(solution)/shard_map/ppermute | solution.py:1573
  510.2 19.5 %collective-permute-start.35 = (bf16[2,16,64,256]{3,2,1,0:T(8,128)(2,1)S(1)}, bf16[2,16,64,256]{3,2,1,0:T(8,128)(2,1)S(1)}, u32[]{:S(2)}, u32[]{:S(2)}) collective-permute-start(bf16[2,16,64,256]{3,2,1,0:T(8,128)(2,1)S(1)} %dynamic-slice_bitcast_fusion.1), channel_id=1, source_target_pairs={{0,2},{1,3},{2,0},{3,1},{4,6},{5,7},{6,4},{7,5},{8,10},{9,11},{10,... | collective-permute-start | bytes 3145736 | tf_op jit(solution)/shard_map/ppermute | solution.py:1570
  510.3 23.9 %collective-permute-start.55 = (f32[2,5376]{1,0:T(2,128)S(1)}, f32[2,5376]{1,0:T(2,128)S(1)}, u32[]{:S(2)}, u32[]{:S(2)}) collective-permute-start(f32[2,5376]{1,0:T(2,128)S(1)} %add.414), channel_id=1, source_target_pairs={{0,16},{4,20},{8,24},{12,28},{16,0},{20,4},{24,8},{28,12},{1,17},{... | collective-permute-start | bytes 129032 | tf_op jit(solution)/shard_map/ppermute | solution.py:1585
  510.7 24.9 %collective-permute-start.54 = (bf16[24,64,256]{2,1,0:T(8,128)(2,1)S(1)}, bf16[24,64,256]{2,1,0:T(8,128)(2,1)S(1)}, u32[]{:S(2)}, u32[]{:S(2)}) collective-permute-start(bf16[24,64,256]{2,1,0:T(8,128)(2,1)S(1)} %add_convert_fusion.8), channel_id=1, source_target_pairs={{16,24},{20,28},{17,25},{21,29},{18,26},{22,30},{19,27},{23,31}} | collective-permute-start | bytes 2359304 | tf_op jit(solution)/shard_map/ppermute | solution.py:1281
  511.7 25.2 %collective-permute-start.53 = (bf16[24,64,256]{2,1,0:T(8,128)(2,1)S(1)}, bf16[24,64,256]{2,1,0:T(8,128)(2,1)}, u32[]{:S(2)}, u32[]{:S(2)}) collective-permute-start(bf16[24,64,256]{2,1,0:T(8,128)(2,1)S(1)} %add_convert_fusion.9), channel_id=1, source_target_pairs={{8,16},{12,20},{9,17},{13,21},{10,18},{14,22},{11,19},{15,23}} | collective-permute-start | bytes 2359304 | tf_op jit(solution)/shard_map/ppermute | solution.py:1281
  526.3 10.6 %collective-permute-start.52 = (bf16[24,64,256]{2,1,0:T(8,128)(2,1)S(1)}, bf16[24,64,256]{2,1,0:T(8,128)(2,1)}, u32[]{:S(2)}, u32[]{:S(2)}) collective-permute-start(bf16[24,64,256]{2,1,0:T(8,128)(2,1)S(1)} %add_convert_fusion.10), channel_id=1, source_target_pairs={{24,16},{28,20},{25,17},{29,21},{26,18},{30,22},{27,19},{31,23}} | collective-permute-start | bytes 2359304 | tf_op jit(solution)/shard_map/ppermute | solution.py:1281
  531.0 20.5 %collective-permute-start.37 = (bf16[2,16,64,256]{3,2,1,0:T(8,128)(2,1)}, bf16[2,16,64,256]{3,2,1,0:T(8,128)(2,1)}, u32[]{:S(2)}, u32[]{:S(2)}) collective-permute-start(bf16[2,16,64,256]{3,2,1,0:T(8,128)(2,1)} %dynamic-slice_bitcast_fusion), channel_id=1, source_target_pairs={{0,2},{1,3},{2,0},{3,1},{4,6},{5,7},{6,4},{7,5},{8,10},{9,11},{10,... | collective-permute-start | bytes 3145736 | tf_op jit(solution)/shard_map/ppermute | solution.py:1570
  534.3 13.5 %collective-permute-start.39 = (bf16[24,64,256]{2,1,0:T(8,128)(2,1)}, bf16[24,64,256]{2,1,0:T(8,128)(2,1)}, u32[]{:S(2)}, u32[]{:S(2)}) collective-permute-start(bf16[24,64,256]{2,1,0:T(8,128)(2,1)} %add_convert_fusion.22), channel_id=1, source_target_pairs={{0,8},{4,12},{1,9},{5,13},{2,10},{6,14},{3,11},{7,15}} | collective-permute-start | bytes 2359304 | tf_op jit(solution)/shard_map/ppermute | solution.py:1281
  536.4 11.7 %collective-permute-start.38 = (bf16[24,64,256]{2,1,0:T(8,128)(2,1)}, bf16[24,64,256]{2,1,0:T(8,128)(2,1)}, u32[]{:S(2)}, u32[]{:S(2)}) collective-permute-start(bf16[24,64,256]{2,1,0:T(8,128)(2,1)} %pad_maximum_fusion.16), channel_id=1, source_target_pairs={{0,4},{4,0},{8,12},{12,8},{16,20},{20,16},{24,28},{28,24},{1,5},{5... | collective-permute-start | bytes 2359304 | tf_op jit(solution)/shard_map/ppermute | solution.py:1573
  538.3 23.7 %collective-permute-start.56 = (bf16[24,64,256]{2,1,0:T(8,128)(2,1)S(1)}, bf16[24,64,256]{2,1,0:T(8,128)(2,1)S(1)}, u32[]{:S(2)}, u32[]{:S(2)}) collective-permute-start(bf16[24,64,256]{2,1,0:T(8,128)(2,1)S(1)} %add_convert_fusion.7), channel_id=1, source_target_pairs={{16,8},{20,12},{17,9},{21,13},{18,10},{22,14},{19,11},{23,15}} | collective-permute-start | bytes 2359304 | tf_op jit(solution)/shard_map/ppermute | solution.py:1281
  553.1 13.2 %collective-permute-start.42 = (bf16[24,64,256]{2,1,0:T(8,128)(2,1)S(1)}, bf16[24,64,256]{2,1,0:T(8,128)(2,1)S(1)}, u32[]{:S(2)}, u32[]{:S(2)}) collective-permute-start(bf16[24,64,256]{2,1,0:T(8,128)(2,1)S(1)} %add_convert_fusion.20), channel_id=1, source_target_pairs={{8,16},{12,20},{9,17},{13,21},{10,18},{14,22},{11,19},{15,23}} | collective-permute-start | bytes 2359304 | tf_op jit(solution)/shard_map/ppermute | solution.py:1281
  556.1 14.2 %collective-permute-start.41 = (bf16[24,64,256]{2,1,0:T(8,128)(2,1)S(1)}, bf16[24,64,256]{2,1,0:T(8,128)(2,1)S(1)}, u32[]{:S(2)}, u32[]{:S(2)}) collective-permute-start(bf16[24,64,256]{2,1,0:T(8,128)(2,1)S(1)} %add_convert_fusion.21), channel_id=1, source_target_pairs={{0,8},{4,12},{24,16},{28,20},{1,9},{5,13},{25,17},{29,21},{2,10},{... | collective-permute-start | bytes 2359304 | tf_op jit(solution)/shard_map/ppermute | solution.py:1281
  559.4 12.2 %collective-permute-start.40 = (bf16[24,64,256]{2,1,0:T(8,128)(2,1)S(1)}, bf16[24,64,256]{2,1,0:T(8,128)(2,1)S(1)}, u32[]{:S(2)}, u32[]{:S(2)}) collective-permute-start(bf16[24,64,256]{2,1,0:T(8,128)(2,1)S(1)} %pad_maximum_fusion.17), channel_id=1, source_target_pairs={{0,4},{4,0},{8,12},{12,8},{16,20},{20,16},{24,28},{28,24},{1,5},{5... | collective-permute-start | bytes 2359304 | tf_op jit(solution)/shard_map/ppermute | solution.py:1573
  562.3 16.2 %collective-permute-start.57 = (bf16[24,64,256]{2,1,0:T(8,128)(2,1)S(1)}, bf16[24,64,256]{2,1,0:T(8,128)(2,1)S(1)}, u32[]{:S(2)}, u32[]{:S(2)}) collective-permute-start(bf16[24,64,256]{2,1,0:T(8,128)(2,1)S(1)} %add_convert_fusion.4), channel_id=1, source_target_pairs={{8,0},{12,4},{9,1},{13,5},{10,2},{14,6},{11,3},{15,7}} | collective-permute-start | bytes 2359304 | tf_op jit(solution)/shard_map/ppermute | solution.py:1281
  572.9 13.4 %collective-permute-start.44 = (bf16[24,64,256]{2,1,0:T(8,128)(2,1)S(1)}, bf16[24,64,256]{2,1,0:T(8,128)(2,1)S(1)}, u32[]{:S(2)}, u32[]{:S(2)}) collective-permute-start(bf16[24,64,256]{2,1,0:T(8,128)(2,1)S(1)} %add_convert_fusion.18), channel_id=1, source_target_pairs={{8,16},{12,20},{9,17},{13,21},{10,18},{14,22},{11,19},{15,23}} | collective-permute-start | bytes 2359304 | tf_op jit(solution)/shard_map/ppermute | solution.py:1281
  577.8 8.5 %collective-permute-start.43 = (bf16[24,64,256]{2,1,0:T(8,128)(2,1)S(1)}, bf16[24,64,256]{2,1,0:T(8,128)(2,1)S(1)}, u32[]{:S(2)}, u32[]{:S(2)}) collective-permute-start(bf16[24,64,256]{2,1,0:T(8,128)(2,1)S(1)} %add_convert_fusion.19), channel_id=1, source_target_pairs={{24,16},{28,20},{25,17},{29,21},{26,18},{30,22},{27,19},{31,23}} | collective-permute-start | bytes 2359304 | tf_op jit(solution)/shard_map/ppermute | solution.py:1281
  579.2 10.9 %collective-permute-start.58 = (bf16[24,64,256]{2,1,0:T(8,128)(2,1)S(1)}, bf16[24,64,256]{2,1,0:T(8,128)(2,1)S(1)}, u32[]{:S(2)}, u32[]{:S(2)}) collective-permute-start(bf16[24,64,256]{2,1,0:T(8,128)(2,1)S(1)} %select_select_fusion.1), channel_id=1, source_target_pairs={{0,2},{1,3},{2,0},{3,1},{4,6},{5,7},{6,4},{7,5},{8,10},{9,11},{10,... | collective-permute-start | bytes 2359304 | tf_op jit(solution)/shard_map/ppermute | solution.py:1580
  586.5 14.5 %collective-permute-start.46 = (bf16[24,64,256]{2,1,0:T(8,128)(2,1)S(1)}, bf16[24,64,256]{2,1,0:T(8,128)(2,1)S(1)}, u32[]{:S(2)}, u32[]{:S(2)}) collective-permute-start(bf16[24,64,256]{2,1,0:T(8,128)(2,1)S(1)} %add_convert_fusion.16), channel_id=1, source_target_pairs={{16,8},{20,12},{17,9},{21,13},{18,10},{22,14},{19,11},{23,15}} | collective-permute-start | bytes 2359304 | tf_op jit(solution)/shard_map/ppermute | solution.py:1281
  590.4 14.4 %collective-permute-start.59 = (bf16[40,64,256]{2,1,0:T(8,128)(2,1)S(1)}, bf16[40,64,256]{2,1,0:T(8,128)(2,1)}, u32[]{:S(2)}, u32[]{:S(2)}) collective-permute-start(bf16[40,64,256]{2,1,0:T(8,128)(2,1)S(1)} %pad_maximum_fusion.1), channel_id=1, source_target_pairs={{0,1},{1,0},{2,3},{3,2},{4,5},{5,4},{6,7},{7,6},{8,9},{9,8},{10,11... | collective-permute-start | bytes 3932168 | tf_op jit(solution)/shard_map/ppermute | solution.py:1582
  602.2 20.2 %collective-permute-start.47 = (bf16[24,64,256]{2,1,0:T(8,128)(2,1)}, bf16[24,64,256]{2,1,0:T(8,128)(2,1)}, u32[]{:S(2)}, u32[]{:S(2)}) collective-permute-start(bf16[24,64,256]{2,1,0:T(8,128)(2,1)} %add_convert_fusion.13), channel_id=1, source_target_pairs={{8,0},{12,4},{9,1},{13,5},{10,2},{14,6},{11,3},{15,7}} | collective-permute-start | bytes 2359304 | tf_op jit(solution)/shard_map/ppermute | solution.py:1281
  624.5 16.7 %collective-permute-start.60 = (bf16[24,64,256]{2,1,0:T(8,128)(2,1)S(1)}, bf16[24,64,256]{2,1,0:T(8,128)(2,1)S(1)}, u32[]{:S(2)}, u32[]{:S(2)}) collective-permute-start(bf16[24,64,256]{2,1,0:T(8,128)(2,1)S(1)} %select_select_fusion), channel_id=1, source_target_pairs={{0,2},{1,3},{2,0},{3,1},{4,6},{5,7},{6,4},{7,5},{8,10},{9,11},{10,... | collective-permute-start | bytes 2359304 | tf_op jit(solution)/shard_map/ppermute | solution.py:1580
  641.6 12.7 %collective-permute-start.61 = (bf16[40,64,256]{2,1,0:T(8,128)(2,1)S(1)}, bf16[40,64,256]{2,1,0:T(8,128)(2,1)S(1)}, u32[]{:S(2)}, u32[]{:S(2)}) collective-permute-start(bf16[40,64,256]{2,1,0:T(8,128)(2,1)S(1)} %pad_maximum_fusion.2), channel_id=1, source_target_pairs={{0,1},{1,0},{2,3},{3,2},{4,5},{5,4},{6,7},{7,6},{8,9},{9,8},{10,11... | collective-permute-start | bytes 3932168 | tf_op jit(solution)/shard_map/ppermute | solution.py:1582
  (59 other events, 550.7 us)
Sparse Core Ops, SparseCore 0:
  13.1 202.3 all-gather.1
  274.2 73.9 reduce-scatter.2
  351.5 72.6 reduce-scatter.4

commit v7 on v6

--- a/solution.py
+++ b/solution.py
@@ -1703,17 +1703,16 @@
     def co_grads():
         text_co = weight_grads((6,), (x_text,), (dco_text,))
         late_sources[1] = (TILES[6][0], text_co)
-        far_four = swap_halves(late_sources, (4,))[0]
+        far_parts.append(swap_halves(late_sources, (4,))[0])
         early_sources[0] = (0, weight_grads((0,), (xv,), (dco_vis,)))
-        return text_co, far_four
-
-    text_co, far_four = beside(
+        return text_co
+
+    far_parts = []
+    beside(
         chunks, [(1, ("X", 1)), (0, ("Z", 1, 0)), (0, ("N", 1))], co_grads
     )
-    late_sources[1] = (TILES[6][0], text_co)
-
     def merge_late():
-        merge(core, late_sources, 2, [far_four, far_half], chunks)
+        merge(core, late_sources, 2, [far_parts[0], far_half], chunks)
         return swap_halves(early_sources, (0, 1))
 
     got = beside(chunks, [(0, ("Z", 1, 1)), (1, ("Z", 1, 0))], merge_late)

time: 696 us -> 700 us (level)
  starting transfers between devices: 102 us -> 111 us
  transfers between devices with their start and end apart: 65 -> 65, of which waited for: 34 -> 32; matrix products, arithmetic and copies ran while one was open for 16% -> 16% of each run, Pallas kernels for 22% -> 22%
where the time goes in v7:
time: 700 us; the launch traced here: 693 us
  Pallas kernels  235 us (34%)
  waiting for transfers between devices  209 us (30%)
  starting transfers between devices  111 us (16%)
  other arithmetic  66.5 us (10%)
  local copies, waits for them, and re-layouts  54.8 us (8%)
  between operations  15.7 us (2%)
    pallas_call x3, Pallas kernels, renew(): pl.pallas_call(functools.partial(renew_body, steps), in_specs=[pl.BlockSp...  54.8 us
    pallas_call x2, Pallas kernels, middle(): pl.pallas_call(functools.partial(middle_body, (begin, rows, span, head, c...  51.1 us
    ppermute x23, waiting for transfers between devices, along_z(): lax.ppermute(value, 'dp', [(2 * a + x, 2 * b + x) for a, b in moves for x...  50.6 us
    ppermute x4, waiting for transfers between devices, gather_tiles(): lax.ppermute(join([part[:G_LONE] for part in here]), 'seq', SWAP_Y)  49 us
    ppermute x23, starting transfers between devices, along_z(): lax.ppermute(value, 'dp', [(2 * a + x, 2 * b + x) for a, b in moves for x...  46.7 us
    pallas_call x4, Pallas kernels, weight_grads(): pl.pallas_call(functools.partial(weight_body, kinds), in_specs=whole(2 *...  44.3 us
    ppermute x4, waiting for transfers between devices, gather_tiles(): out['x'] = lax.ppermute(rows[phase], 'dp', SWAP_X)  37.9 us
    convert_element_type x34, other arithmetic, add(): return (left.astype(F32) + right.astype(F32)).astype(BF16)  32.3 us
  transfers between devices with their start and end apart: 65, of which 32 were waited for; matrix products, arithmetic and copies ran while one was open for 16% of the time, Pallas kernels for 22%

profile of v7, /device:TPU:11, one launch (start us, length us, event | category | flops | bytes accessed | tf_op | source)
XLA Modules:
  0.0 692.8 jit_solution(6582370996424398213)
XLA Ops:
  7.7 5.2 shard_map.223
  13.7 5.2 shard_map.221
  22.0 21.3 %collective-permute-done = bf16[24,64,256]{2,1,0:T(8,128)(2,1)S(1)} collective-permute-done((bf16[24,64,256]{2,1,0:T(8,128)(2,1)}, bf16[24,64,256]{2,1,0:T(8,128)(2,1)S(1)}, u32[]{:S(2)}, u32[]{:S(2)}) %collective-permute-start) | collective-permute-done | bytes 786464 | tf_op jit(solution)/shard_map/ppermute | solution.py:1334
  43.3 8.7 %collective-permute-done.1 = bf16[24,64,256]{2,1,0:T(8,128)(2,1)S(1)} collective-permute-done((bf16[24,64,256]{2,1,0:T(8,128)(2,1)}, bf16[24,64,256]{2,1,0:T(8,128)(2,1)S(1)}, u32[]{:S(2)}, u32[]{:S(2)}) %collective-permute-start.1) | collective-permute-done | bytes 786464 | tf_op jit(solution)/shard_map/ppermute | solution.py:1281
  58.5 14.0 %collective-permute-done.3 = bf16[16,64,256]{2,1,0:T(8,128)(2,1)S(1)} collective-permute-done((bf16[16,64,256]{2,1,0:T(8,128)(2,1)S(1)}, bf16[16,64,256]{2,1,0:T(8,128)(2,1)S(1)}, u32[]{:S(2)}, u32[]{:S(2)}) %collective-permute-start.3) | collective-permute-done | bytes 524320 | tf_op jit(solution)/shard_map/ppermute | solution.py:1337
  74.0 10.7 %collective-permute-done.4 = bf16[24,64,256]{2,1,0:T(8,128)(2,1)S(1)} collective-permute-done((bf16[24,64,256]{2,1,0:T(8,128)(2,1)S(1)}, bf16[24,64,256]{2,1,0:T(8,128)(2,1)S(1)}, u32[]{:S(2)}, u32[]{:S(2)}) %collective-permute-start.4) | collective-permute-done | bytes 786464 | tf_op jit(solution)/shard_map/ppermute | solution.py:1281
  86.5 15.8 %collective-permute-start.5 = (bf16[64,64,256]{2,1,0:T(8,128)(2,1)S(1)}, bf16[64,64,256]{2,1,0:T(8,128)(2,1)S(1)}, u32[]{:S(2)}, u32[]{:S(2)}) collective-permute-start(bf16[64,64,256]{2,1,0:T(8,128)(2,1)S(1)} %get-tuple-element.648), channel_id=1, source_target_pairs={{0,1},{1,0},{2,3},{3,2},{4,5},{5,4},{6,7},{7,6},{8,9},{9,8},{10,11... | collective-permute-start | bytes 6291464 | tf_op jit(solution)/shard_map/ppermute | solution.py:1339
  102.2 2.6 collective-permute-start.8
  107.4 11.5 %collective-permute-done.7 = bf16[16,64,256]{2,1,0:T(8,128)(2,1)S(1)} collective-permute-done((bf16[16,64,256]{2,1,0:T(8,128)(2,1)S(1)}, bf16[16,64,256]{2,1,0:T(8,128)(2,1)S(1)}, u32[]{:S(2)}, u32[]{:S(2)}) %collective-permute-start.7) | collective-permute-done | bytes 524320 | tf_op jit(solution)/shard_map/ppermute | solution.py:1337
  118.9 2.5 collective-permute-done.6
  121.5 2.7 collective-permute-done.8
  142.1 17.1 %collective-permute-done.11 = bf16[16,64,256]{2,1,0:T(8,128)(2,1)S(1)} collective-permute-done((bf16[16,64,256]{2,1,0:T(8,128)(2,1)S(1)}, bf16[16,64,256]{2,1,0:T(8,128)(2,1)S(1)}, u32[]{:S(2)}, u32[]{:S(2)}) %collective-permute-start.11) | collective-permute-done | bytes 524320 | tf_op jit(solution)/shard_map/ppermute | solution.py:1337
  159.2 12.6 %collective-permute-done.10 = bf16[24,64,256]{2,1,0:T(8,128)(2,1)S(1)} collective-permute-done((bf16[24,64,256]{2,1,0:T(8,128)(2,1)}, bf16[24,64,256]{2,1,0:T(8,128)(2,1)S(1)}, u32[]{:S(2)}, u32[]{:S(2)}) %collective-permute-start.10) | collective-permute-done | bytes 786464 | tf_op jit(solution)/shard_map/ppermute | solution.py:1334
  182.2 2.3 bitcast_dynamic-update-slice_fusion.10
  187.9 6.4 collective-permute-done.13
  206.5 2.7 bitcast_dynamic-update-slice_fusion.6
  213.7 2.3 bitcast_dynamic-update-slice_fusion.2
  217.1 2.3 bitcast_dynamic-update-slice_fusion
  219.4 13.0 %shard_map.224 = (bf16[96,3072]{1,0:T(8,128)(2,1)}, bf16[256,3072]{1,0:T(8,128)(2,1)}, bf16[96,1024]{1,0:T(8,128)(2,1)}, bf16[256,1024]{1,0:T(8,128)(2,1)}) custom-call(s32[4]{0:T(128)} %concatenate.119.len_ref, bf16[96,1024]{1,0:T(8,128)(2,1)} %bitcast.278, bf16[256,768]{1,0:T(8,128)(2,1)} %refs_0_.1, bf16[512,64,256]{2,1,0:T(8,128)(2,1)} %bitcast.251, ...), custom_call_target="tpu_custom_call" | custom-call | bytes 74800000 | tf_op jit(solution)/shard_map/pallas_call | solution.py:881
  233.0 19.5 %shard_map.226 = (bf16[96,1024]{1,0:T(8,128)(2,1)}, bf16[96,1024]{1,0:T(8,128)(2,1)}, bf16[96,1024]{1,0:T(8,128)(2,1)}, bf16[96,1024]{1,0:T(8,128)(2,1)}, bf16[9...) custom-call(s32[2]{0:T(128)} %broadcast_1_len_ref.2.len_ref, ...), custom_call_target="tpu_custom_call" | custom-call | bytes 136000000 | tf_op jit(solution)/shard_map/pallas_call | solution.py:1186
  252.5 15.1 %shard_map.227.x_any.refs_0_.refs_1_ = bf16[448,64,256]{2,1,0:T(8,128)(2,1)} custom-call(bf16[96,1024]{1,0:T(8,128)(2,1)} %get-tuple-element.342.ctx_ref.refs_0_, bf16[96,1024]{1,0:T(8,128)(2,1)} %get-tuple-element.345.refs_1_, bf16[96,1024]{1,0:T(8,128)(2,1)} %get-tuple-element.346.refs_2_, bf16[96,1024]{1,0:T(8,128)(2,1)} %get-tuple-element.347.refs_3_, ...), custom_call_target="tpu_custom_call" | custom-call | bytes 60928000 | tf_op jit(solution)/shard_map/pallas_call | solution.py:1259
  267.6 6.4 shard_map.228
  274.1 2.9 shard_map.229
  277.8 31.7 %shard_map.225 = (bf16[256,768]{1,0:T(8,128)(2,1)}, bf16[256,768]{1,0:T(8,128)(2,1)}, bf16[256,3072]{1,0:T(8,128)(2,1)}, bf16[256,768]{1,0:T(8,128)(2,1)}, bf16[...) custom-call(s32[4]{0:T(128)} %concatenate.119.len_ref, ...), custom_call_target="tpu_custom_call" | custom-call | bytes 136000000 | tf_op jit(solution)/shard_map/pallas_call | solution.py:1186
  309.5 17.8 %shard_map.230.refs_0_.refs_2_.x_any = bf16[480,64,256]{2,1,0:T(8,128)(2,1)} custom-call(bf16[256,1024]{1,0:T(8,128)(2,1)} %get-tuple-element.372.ctx_ref.refs_0_, bf16[256,768]{1,0:T(8,128)(2,1)} %get-tuple-element.373.refs_1_, bf16[256,3072]{1,0:T(8,128)(2,1)} %get-tuple-element.374.refs_2_, bf16[256,768]{1,0:T(8,128)(2,1)} %get-tuple-element.375.refs_3_, ...), custom_call_target="tpu_custom_call" | custom-call | bytes 65280000 | tf_op jit(solution)/shard_map/pallas_call | solution.py:1259
  327.7 6.4 shard_map.239
  334.2 3.2 shard_map.233
  338.0 2.9 shard_map.232
  341.2 7.0 %reduce-scatter.3.cloned.1.call-done = bf16[64,64,256]{2,1,0:T(8,128)(2,1)} async-done(((bf16[256,64,256]{2,1,0:T(8,128)(2,1)}), bf16[64,64,256]{2,1,0:T(8,128)(2,1)}) %reduce-scatter.3.cloned.1.call-update) | async-done | bytes 2097168 | tf_op jit(solution)/shard_map/reduce_scatter | solution.py:1548
  352.3 13.9 %shard_map.231 = (bf16[96,3072]{1,0:T(8,128)(2,1)}, bf16[256,3072]{1,0:T(8,128)(2,1)}, f32[96,1024]{1,0:T(8,128)}, f32[256,768]{1,0:T(8,128)}) custom-call(s32[4]{0:T(128)} %concatenate.119.len_ref, bf16[96,3072]{1,0:T(8,128)(2,1)} %get-tuple-element.385.cv_ref, bf16[256,3072]{1,0:T(8,128)(2,1)} %get-tuple-element.386.ct_ref, ...), custom_call_target="tpu_custom_call" | custom-call | bytes 78200000 | tf_op jit(solution)/shard_map/pallas_call | solution.py:950
  366.3 3.4 collective-permute-done.16
  372.8 5.3 shard_map.234.refs_1_
  378.2 3.2 shard_map.237
  383.5 6.1 shard_map.235.refs_0_
  389.6 5.0 shard_map.236
  397.6 16.9 %collective-permute-done.20 = bf16[24,64,256]{2,1,0:T(8,128)(2,1)} collective-permute-done((bf16[24,64,256]{2,1,0:T(8,128)(2,1)S(1)}, bf16[24,64,256]{2,1,0:T(8,128)(2,1)}, u32[]{:S(2)}, u32[]{:S(2)}) %collective-permute-start.20) | collective-permute-done | bytes 786464 | tf_op jit(solution)/shard_map/ppermute | solution.py:1573
  426.4 8.8 %shard_map.238 = (bf16[2,2,16,64,256]{4,3,2,1,0:T(8,128)(2,1)}, bf16[2,8,64,256]{3,2,1,0:T(8,128)(2,1)}, bf16[2,2,16,64,256]{4,3,2,1,0:T(8,128)(2,1)}, bf16[2,8,64,256]{3,2,1,0:T(8,128)(2,1)}) custom-call(s32[1]{0:T(128)} %bitcast.27.core_ref, bf16[448,64,256]{2,1,0:T(8,128)(2,1)} %shard_map.227.x_any.refs_0_.refs_1_, ...), custom_call_target="tpu_custom_call" | custom-call | bytes 27200000 | tf_op jit(solution)/shard_map/pallas_call | solution.py:1490
  435.2 3.4 collective-permute-done.24
  439.6 2.3 dynamic-slice_bitcast_fusion.3
  443.2 2.5 add_convert_fusion.26
  447.1 8.8 %shard_map.240 = (bf16[2,2,16,64,256]{4,3,2,1,0:T(8,128)(2,1)}, bf16[2,8,64,256]{3,2,1,0:T(8,128)(2,1)}, bf16[2,2,16,64,256]{4,3,2,1,0:T(8,128)(2,1)}, bf16[2,8,64,256]{3,2,1,0:T(8,128)(2,1)}) custom-call(s32[1]{0:T(128)} %bitcast.27.core_ref, bf16[192,64,256]{2,1,0:T(8,128)(2,1)} %shard_map.235.refs_0_, ...), custom_call_target="tpu_custom_call" | custom-call | bytes 27200000 | tf_op jit(solution)/shard_map/pallas_call | solution.py:1490
  455.9 2.4 add_convert_fusion.25
  458.3 6.7 collective-permute-done.30
  472.9 2.5 add_convert_fusion.23
  475.4 13.0 %collective-permute-done.34 = f32[2,5376]{1,0:T(2,128)S(1)} collective-permute-done((f32[2,5376]{1,0:T(2,128)S(1)}, f32[2,5376]{1,0:T(2,128)S(1)}, u32[]{:S(2)}, u32[]{:S(2)}) %collective-permute-start.34) | collective-permute-done | bytes 43040 | tf_op jit(solution)/shard_map/ppermute | solution.py:1585
  490.2 2.6 collective-permute-start.50
  499.3 12.3 %collective-permute-done.51 = f32[2,5376]{1,0:T(2,128)S(1)} collective-permute-done((f32[2,5376]{1,0:T(2,128)S(1)}, f32[2,5376]{1,0:T(2,128)S(1)}, u32[]{:S(2)}, u32[]{:S(2)}) %collective-permute-start.51) | collective-permute-done | bytes 43040 | tf_op jit(solution)/shard_map/ppermute | solution.py:1585
  514.2 6.9 collective-permute-start.53
  521.5 6.1 collective-permute-done.36
  542.9 7.8 %collective-permute-done.39 = bf16[24,64,256]{2,1,0:T(8,128)(2,1)} collective-permute-done((bf16[24,64,256]{2,1,0:T(8,128)(2,1)}, bf16[24,64,256]{2,1,0:T(8,128)(2,1)}, u32[]{:S(2)}, u32[]{:S(2)}) %collective-permute-start.39) | collective-permute-done | bytes 786464 | tf_op jit(solution)/shard_map/ppermute | solution.py:1281
  554.7 2.5 collective-permute-start.42
  564.9 4.1 collective-permute-start.57
  569.0 4.0 collective-permute-done.41
  575.5 4.8 collective-permute-start.44
  584.1 5.1 collective-permute-done.44
  590.8 2.7 collective-permute-done.58
  593.7 9.2 %collective-permute-start.59 = (bf16[40,64,256]{2,1,0:T(8,128)(2,1)S(1)}, bf16[40,64,256]{2,1,0:T(8,128)(2,1)}, u32[]{:S(2)}, u32[]{:S(2)}) collective-permute-start(bf16[40,64,256]{2,1,0:T(8,128)(2,1)S(1)} %pad_maximum_fusion.1), channel_id=1, source_target_pairs={{0,1},{1,0},{2,3},{3,2},{4,5},{5,4},{6,7},{7,6},{8,9},{9,8},{10,11... | collective-permute-start | bytes 3932168 | tf_op jit(solution)/shard_map/ppermute | solution.py:1582
  605.2 2.6 collective-permute-start.47
  607.8 3.0 broadcast_select_fusion.2
  610.8 14.5 %shard_map.241 = (f32[20224,128]{1,0:T(8,128)}, f32[20224,128]{1,0:T(8,128)}, f32[20224,128]{1,0:T(8,128)}, f32[20224,128]{1,0:T(8,128)}) custom-call(s32[20]{0:T(128)} %constant.168.which_ref, bf16[40,64,256]{2,1,0:T(8,128)(2,1)} %get-tuple-element.622.g_any, f32[20224,128]{1,0:T(8,128)} %bitcast.257, f32[20224,128]{1,0:T(8,128)} %bitcast.260, ...), custom_call_target="tpu_custom_call" | custom-call | bytes 47600000 | tf_op jit(solution)/shard_map/pallas_call | solution.py:736
  627.5 2.4 collective-permute-start.60
  631.4 14.4 %shard_map.242 = (f32[20224,128]{1,0:T(8,128)}, f32[20224,128]{1,0:T(8,128)}, f32[20224,128]{1,0:T(8,128)}, f32[20224,128]{1,0:T(8,128)}) custom-call(s32[20]{0:T(128)} %constant.169.which_ref, bf16[40,64,256]{2,1,0:T(8,128)(2,1)} %get-tuple-element.621.g_any, ...), custom_call_target="tpu_custom_call", output_to_operand_aliasing={{0}: (7, {}), {1}: (8, {}), {2}: (9, {}), {3}: (10, {})} | custom-call | bytes 47600000 | tf_op jit(solution)/shard_map/pallas_call | solution.py:736
  646.2 9.5 %collective-permute-start.61 = (bf16[40,64,256]{2,1,0:T(8,128)(2,1)S(1)}, bf16[40,64,256]{2,1,0:T(8,128)(2,1)S(1)}, u32[]{:S(2)}, u32[]{:S(2)}) collective-permute-start(bf16[40,64,256]{2,1,0:T(8,128)(2,1)S(1)} %pad_maximum_fusion.2), channel_id=1, source_target_pairs={{0,1},{1,0},{2,3},{3,2},{4,5},{5,4},{6,7},{7,6},{8,9},{9,8},{10,11... | collective-permute-start | bytes 3932168 | tf_op jit(solution)/shard_map/ppermute | solution.py:1582
  660.3 25.9 %shard_map.243 = (f32[20224,128]{1,0:T(8,128)}, f32[20224,128]{1,0:T(8,128)}, f32[20224,128]{1,0:T(8,128)}, f32[20224,128]{1,0:T(8,128)}) custom-call(s32[40]{0:T(128)} %constant.158.clone.which_ref, bf16[80,64,256]{2,1,0:T(8,128)(2,1)} %pad_maximum_fusion.g_any, ...), custom_call_target="tpu_custom_call", output_to_operand_aliasing={{0}: (7, {}), {1}: (8, {}), {2}: (9, {}), {3}: (10, {})} | custom-call | bytes 95200000 | tf_op jit(solution)/shard_map/pallas_call | solution.py:736
  (382 shorter events, 160.5 us)
Async XLA Ops:
  7.2 212.3 %all-gather.2.cloned.1.call-start = ((), (), s32[]{:S(2)}) async-start(), calls=%async_computation.2 | async-start | bytes 25952256 | tf_op jit(solution)/shard_map/all_gather | solution.py:1323
  13.0 335.2 %reduce-scatter.3.cloned.1.call-start = ((), (), s32[]{:S(2)}) async-start(), calls=%async_computation.3 | async-start | bytes 10485760 | tf_op jit(solution)/shard_map/reduce_scatter | solution.py:1548
  18.9 24.4 %collective-permute-start = (bf16[24,64,256]{2,1,0:T(8,128)(2,1)}, bf16[24,64,256]{2,1,0:T(8,128)(2,1)S(1)}, u32[]{:S(2)}, u32[]{:S(2)}) collective-permute-start(bf16[24,64,256]{2,1,0:T(8,128)(2,1)} %shard_map.221), channel_id=1, source_target_pairs={{0,4},{4,0},{8,12},{12,8},{16,20},{20,16},{24,28},{28,24},{1,5},{5... | collective-permute-start | bytes 2359304 | tf_op jit(solution)/shard_map/ppermute | solution.py:1334
  19.2 32.8 %collective-permute-start.1 = (bf16[24,64,256]{2,1,0:T(8,128)(2,1)}, bf16[24,64,256]{2,1,0:T(8,128)(2,1)S(1)}, u32[]{:S(2)}, u32[]{:S(2)}) collective-permute-start(bf16[24,64,256]{2,1,0:T(8,128)(2,1)} %shard_map.221), channel_id=1, source_target_pairs={{0,8},{4,12},{8,16},{12,20},{16,24},{20,28},{24,0},{28,4},{1,9},{5... | collective-permute-start | bytes 2359304 | tf_op jit(solution)/shard_map/ppermute | solution.py:1281
  52.0 22.0 %collective-permute-start.2 = (bf16[24,64,256]{2,1,0:T(8,128)(2,1)S(1)}, bf16[24,64,256]{2,1,0:T(8,128)(2,1)}, u32[]{:S(2)}, u32[]{:S(2)}) collective-permute-start(bf16[24,64,256]{2,1,0:T(8,128)(2,1)S(1)} %collective-permute-done.1), channel_id=1, source_target_pairs={{0,4},{4,0},{8,12},{12,8},{16,20},{20,16},{24,28},{28,24},{1,5},{5... | collective-permute-start | bytes 2359304 | tf_op jit(solution)/shard_map/ppermute | solution.py:1334
  53.9 30.8 %collective-permute-start.4 = (bf16[24,64,256]{2,1,0:T(8,128)(2,1)S(1)}, bf16[24,64,256]{2,1,0:T(8,128)(2,1)S(1)}, u32[]{:S(2)}, u32[]{:S(2)}) collective-permute-start(bf16[24,64,256]{2,1,0:T(8,128)(2,1)S(1)} %collective-permute-done.1), channel_id=1, source_target_pairs={{0,8},{4,12},{8,16},{12,20},{16,24},{20,28},{24,0},{28,4},{1,9},{5... | collective-permute-start | bytes 2359304 | tf_op jit(solution)/shard_map/ppermute | solution.py:1281
  57.2 15.3 %collective-permute-start.3 = (bf16[16,64,256]{2,1,0:T(8,128)(2,1)S(1)}, bf16[16,64,256]{2,1,0:T(8,128)(2,1)S(1)}, u32[]{:S(2)}, u32[]{:S(2)}) collective-permute-start(bf16[16,64,256]{2,1,0:T(8,128)(2,1)S(1)} %pad_maximum_fusion.19), channel_id=1, source_target_pairs={{0,2},{1,3},{2,0},{3,1},{4,6},{5,7},{6,4},{7,5},{8,10},{9,11},{10,... | collective-permute-start | bytes 1572872 | tf_op jit(solution)/shard_map/ppermute | solution.py:1337
  86.5 37.7 %collective-permute-start.5 = (bf16[64,64,256]{2,1,0:T(8,128)(2,1)S(1)}, bf16[64,64,256]{2,1,0:T(8,128)(2,1)S(1)}, u32[]{:S(2)}, u32[]{:S(2)}) collective-permute-start(bf16[64,64,256]{2,1,0:T(8,128)(2,1)S(1)} %get-tuple-element.648), channel_id=1, source_target_pairs={{0,1},{1,0},{2,3},{3,2},{4,5},{5,4},{6,7},{7,6},{8,9},{9,8},{10,11... | collective-permute-start | bytes 6291464 | tf_op jit(solution)/shard_map/ppermute | solution.py:1339
  102.2 19.2 %collective-permute-start.6 = (bf16[24,64,256]{2,1,0:T(8,128)(2,1)S(1)}, bf16[24,64,256]{2,1,0:T(8,128)(2,1)S(1)}, u32[]{:S(2)}, u32[]{:S(2)}) collective-permute-start(bf16[24,64,256]{2,1,0:T(8,128)(2,1)S(1)} %collective-permute-done.4), channel_id=1, source_target_pairs={{0,4},{4,0},{8,12},{12,8},{16,20},{20,16},{24,28},{28,24},{1,5},{5... | collective-permute-start | bytes 2359304 | tf_op jit(solution)/shard_map/ppermute | solution.py:1334
  102.2 21.9 %collective-permute-start.8 = (bf16[24,64,256]{2,1,0:T(8,128)(2,1)S(1)}, bf16[24,64,256]{2,1,0:T(8,128)(2,1)}, u32[]{:S(2)}, u32[]{:S(2)}) collective-permute-start(bf16[24,64,256]{2,1,0:T(8,128)(2,1)S(1)} %collective-permute-done.4), channel_id=1, source_target_pairs={{0,8},{4,12},{8,16},{12,20},{16,24},{20,28},{24,0},{28,4},{1,9},{5... | collective-permute-start | bytes 2359304 | tf_op jit(solution)/shard_map/ppermute | solution.py:1281
  105.9 13.0 %collective-permute-start.7 = (bf16[16,64,256]{2,1,0:T(8,128)(2,1)S(1)}, bf16[16,64,256]{2,1,0:T(8,128)(2,1)S(1)}, u32[]{:S(2)}, u32[]{:S(2)}) collective-permute-start(bf16[16,64,256]{2,1,0:T(8,128)(2,1)S(1)} %pad_maximum_fusion.20), channel_id=1, source_target_pairs={{0,2},{1,3},{2,0},{3,1},{4,6},{5,7},{6,4},{7,5},{8,10},{9,11},{10,... | collective-permute-start | bytes 1572872 | tf_op jit(solution)/shard_map/ppermute | solution.py:1337
  133.2 38.5 %collective-permute-start.9 = (bf16[64,64,256]{2,1,0:T(8,128)(2,1)}, bf16[64,64,256]{2,1,0:T(8,128)(2,1)}, u32[]{:S(2)}, u32[]{:S(2)}) collective-permute-start(bf16[64,64,256]{2,1,0:T(8,128)(2,1)} %get-tuple-element.644), channel_id=1, source_target_pairs={{0,1},{1,0},{2,3},{3,2},{4,5},{5,4},{6,7},{7,6},{8,9},{9,8},{10,11... | collective-permute-start | bytes 6291464 | tf_op jit(solution)/shard_map/ppermute | solution.py:1339
  134.0 25.2 %collective-permute-start.11 = (bf16[16,64,256]{2,1,0:T(8,128)(2,1)S(1)}, bf16[16,64,256]{2,1,0:T(8,128)(2,1)S(1)}, u32[]{:S(2)}, u32[]{:S(2)}) collective-permute-start(bf16[16,64,256]{2,1,0:T(8,128)(2,1)S(1)} %pad_maximum_fusion.21), channel_id=1, source_target_pairs={{0,2},{1,3},{2,0},{3,1},{4,6},{5,7},{6,4},{7,5},{8,10},{9,11},{10,... | collective-permute-start | bytes 1572872 | tf_op jit(solution)/shard_map/ppermute | solution.py:1337
  135.3 36.5 %collective-permute-start.10 = (bf16[24,64,256]{2,1,0:T(8,128)(2,1)}, bf16[24,64,256]{2,1,0:T(8,128)(2,1)S(1)}, u32[]{:S(2)}, u32[]{:S(2)}) collective-permute-start(bf16[24,64,256]{2,1,0:T(8,128)(2,1)} %collective-permute-done.8), channel_id=1, source_target_pairs={{0,4},{4,0},{8,12},{12,8},{16,20},{20,16},{24,28},{28,24},{1,5},{5... | collective-permute-start | bytes 2359304 | tf_op jit(solution)/shard_map/ppermute | solution.py:1334
  177.4 17.0 %collective-permute-start.12 = (bf16[64,64,256]{2,1,0:T(8,128)(2,1)}, bf16[64,64,256]{2,1,0:T(8,128)(2,1)}, u32[]{:S(2)}, u32[]{:S(2)}) collective-permute-start(bf16[64,64,256]{2,1,0:T(8,128)(2,1)} %get-tuple-element.640), channel_id=1, source_target_pairs={{0,1},{1,0},{2,3},{3,2},{4,5},{5,4},{6,7},{7,6},{8,9},{9,8},{10,11... | collective-permute-start | bytes 6291464 | tf_op jit(solution)/shard_map/ppermute | solution.py:1339
  179.6 14.8 %collective-permute-start.13 = (bf16[16,64,256]{2,1,0:T(8,128)(2,1)S(1)}, bf16[16,64,256]{2,1,0:T(8,128)(2,1)S(1)}, u32[]{:S(2)}, u32[]{:S(2)}) collective-permute-start(bf16[16,64,256]{2,1,0:T(8,128)(2,1)S(1)} %pad_maximum_fusion.22), channel_id=1, source_target_pairs={{0,2},{1,3},{2,0},{3,1},{4,6},{5,7},{6,4},{7,5},{8,10},{9,11},{10,... | collective-permute-start | bytes 1572872 | tf_op jit(solution)/shard_map/ppermute | solution.py:1337
  202.6 10.0 %collective-permute-start.14 = (bf16[64,64,256]{2,1,0:T(8,128)(2,1)}, bf16[64,64,256]{2,1,0:T(8,128)(2,1)}, u32[]{:S(2)}, u32[]{:S(2)}) collective-permute-start(bf16[64,64,256]{2,1,0:T(8,128)(2,1)} %get-tuple-element.636), channel_id=1, source_target_pairs={{0,1},{1,0},{2,3},{3,2},{4,5},{5,4},{6,7},{7,6},{8,9},{9,8},{10,11... | collective-permute-start | bytes 6291464 | tf_op jit(solution)/shard_map/ppermute | solution.py:1339
  274.1 149.2 %reduce-scatter.5.cloned.1.call-start = ((), (), s32[]{:S(2)}) async-start(), calls=%async_computation.4 | async-start | bytes 10485760 | tf_op jit(solution)/shard_map/reduce_scatter | solution.py:1548
  277.1 32.4 %collective-permute-start.15 = (bf16[32,64,256]{2,1,0:T(8,128)(2,1)}, bf16[32,64,256]{2,1,0:T(8,128)(2,1)S(1)}, u32[]{:S(2)}, u32[]{:S(2)}) collective-permute-start(bf16[32,64,256]{2,1,0:T(8,128)(2,1)} %get-tuple-element.370), channel_id=1, source_target_pairs={{0,1},{1,0},{2,3},{3,2},{4,5},{5,4},{6,7},{7,6},{8,9},{9,8},{10,11... | collective-permute-start | bytes 3145736 | tf_op jit(solution)/shard_map/ppermute | solution.py:1666
  337.4 28.8 %collective-permute-start.19 = (bf16[80,64,256]{2,1,0:T(8,128)(2,1)}, bf16[80,64,256]{2,1,0:T(8,128)(2,1)}, u32[]{:S(2)}, u32[]{:S(2)}) collective-permute-start(bf16[80,64,256]{2,1,0:T(8,128)(2,1)} %shard_map.233), channel_id=1, source_target_pairs={{0,1},{1,0},{2,3},{3,2},{4,5},{5,4},{6,7},{7,6},{8,9},{9,8},{10,11... | collective-permute-start | bytes 7864328 | tf_op jit(solution)/shard_map/ppermute | solution.py:1692
  341.0 25.3 %collective-permute-start.18 = (bf16[32,64,256]{2,1,0:T(8,128)(2,1)}, bf16[32,64,256]{2,1,0:T(8,128)(2,1)}, u32[]{:S(2)}, u32[]{:S(2)}) collective-permute-start(bf16[32,64,256]{2,1,0:T(8,128)(2,1)} %get-tuple-element.395), channel_id=1, source_target_pairs={{0,1},{1,0},{2,3},{3,2},{4,5},{5,4},{6,7},{7,6},{8,9},{9,8},{10,11... | collective-permute-start | bytes 3145736 | tf_op jit(solution)/shard_map/ppermute | solution.py:1666
  351.0 18.7 %collective-permute-start.16 = (bf16[24,64,256]{2,1,0:T(8,128)(2,1)}, bf16[24,64,256]{2,1,0:T(8,128)(2,1)}, u32[]{:S(2)}, u32[]{:S(2)}) collective-permute-start(bf16[24,64,256]{2,1,0:T(8,128)(2,1)} %pad_maximum_fusion.11), channel_id=1, source_target_pairs={{0,4},{4,0},{8,12},{12,8},{16,20},{20,16},{24,28},{28,24},{1,5},{5... | collective-permute-start | bytes 2359304 | tf_op jit(solution)/shard_map/ppermute | solution.py:1573
  351.3 15.0 %collective-permute-start.17 = (f32[2,5376]{1,0:T(2,128)S(1)}, f32[2,5376]{1,0:T(2,128)S(1)}, u32[]{:S(2)}, u32[]{:S(2)}) collective-permute-start(f32[2,5376]{1,0:T(2,128)S(1)} %constant_dynamic-update-slice_fusion.24), channel_id=1, source_target_pairs={{0,1},{1,0},{2,3},{3,2},{4,5},{5,4},{6,7},{7,6},{8,9},{9,8},{10,11... | collective-permute-start | bytes 129032 | tf_op jit(solution)/shard_map/ppermute | solution.py:1585
  369.7 25.6 %collective-permute-start.22 = (f32[2,5376]{1,0:T(2,128)S(1)}, f32[2,5376]{1,0:T(2,128)S(1)}, u32[]{:S(2)}, u32[]{:S(2)}) collective-permute-start(f32[2,5376]{1,0:T(2,128)S(1)} %add.383), channel_id=1, source_target_pairs={{0,2},{1,3},{2,0},{3,1},{4,6},{5,7},{6,4},{7,5},{8,10},{9,11},{10,... | collective-permute-start | bytes 129032 | tf_op jit(solution)/shard_map/ppermute | solution.py:1585
  371.5 26.0 %collective-permute-start.21 = (bf16[24,64,256]{2,1,0:T(8,128)(2,1)S(1)}, bf16[24,64,256]{2,1,0:T(8,128)(2,1)}, u32[]{:S(2)}, u32[]{:S(2)}) collective-permute-start(bf16[24,64,256]{2,1,0:T(8,128)(2,1)S(1)} %add_convert_fusion.29), channel_id=1, source_target_pairs={{24,16},{28,20},{0,8},{4,12},{25,17},{29,21},{1,9},{5,13},{26,18},... | collective-permute-start | bytes 2359304 | tf_op jit(solution)/shard_map/ppermute | solution.py:1281
  381.4 44.7 %collective-permute-start.27 = (bf16[80,64,256]{2,1,0:T(8,128)(2,1)}, bf16[80,64,256]{2,1,0:T(8,128)(2,1)}, u32[]{:S(2)}, u32[]{:S(2)}) collective-permute-start(bf16[80,64,256]{2,1,0:T(8,128)(2,1)} %shard_map.237), channel_id=1, source_target_pairs={{0,1},{1,0},{2,3},{3,2},{4,5},{5,4},{6,7},{7,6},{8,9},{9,8},{10,11... | collective-permute-start | bytes 7864328 | tf_op jit(solution)/shard_map/ppermute | solution.py:1692
  394.6 45.0 %collective-permute-start.25 = (bf16[80,64,256]{2,1,0:T(8,128)(2,1)}, bf16[80,64,256]{2,1,0:T(8,128)(2,1)}, u32[]{:S(2)}, u32[]{:S(2)}) collective-permute-start(bf16[80,64,256]{2,1,0:T(8,128)(2,1)} %get-tuple-element.412), channel_id=1, source_target_pairs={{0,1},{1,0},{2,3},{3,2},{4,5},{5,4},{6,7},{7,6},{8,9},{9,8},{10,11... | collective-permute-start | bytes 7864328 | tf_op jit(solution)/shard_map/ppermute | solution.py:1692
  394.8 44.8 %collective-permute-start.26 = (bf16[80,64,256]{2,1,0:T(8,128)(2,1)}, bf16[80,64,256]{2,1,0:T(8,128)(2,1)}, u32[]{:S(2)}, u32[]{:S(2)}) collective-permute-start(bf16[80,64,256]{2,1,0:T(8,128)(2,1)} %get-tuple-element.413), channel_id=1, source_target_pairs={{0,1},{1,0},{2,3},{3,2},{4,5},{5,4},{6,7},{7,6},{8,9},{9,8},{10,11... | collective-permute-start | bytes 7864328 | tf_op jit(solution)/shard_map/ppermute | solution.py:1692
  395.3 19.2 %collective-permute-start.20 = (bf16[24,64,256]{2,1,0:T(8,128)(2,1)S(1)}, bf16[24,64,256]{2,1,0:T(8,128)(2,1)}, u32[]{:S(2)}, u32[]{:S(2)}) collective-permute-start(bf16[24,64,256]{2,1,0:T(8,128)(2,1)S(1)} %pad_maximum_fusion.12), channel_id=1, source_target_pairs={{0,4},{4,0},{8,12},{12,8},{16,20},{20,16},{24,28},{28,24},{1,5},{5... | collective-permute-start | bytes 2359304 | tf_op jit(solution)/shard_map/ppermute | solution.py:1573
  416.8 21.8 %collective-permute-start.24 = (bf16[24,64,256]{2,1,0:T(8,128)(2,1)}, bf16[24,64,256]{2,1,0:T(8,128)(2,1)}, u32[]{:S(2)}, u32[]{:S(2)}) collective-permute-start(bf16[24,64,256]{2,1,0:T(8,128)(2,1)} %add_convert_fusion.27), channel_id=1, source_target_pairs={{24,16},{28,20},{0,8},{4,12},{25,17},{29,21},{1,9},{5,13},{26,18},... | collective-permute-start | bytes 2359304 | tf_op jit(solution)/shard_map/ppermute | solution.py:1281
  419.5 20.1 %collective-permute-start.23 = (bf16[24,64,256]{2,1,0:T(8,128)(2,1)S(1)}, bf16[24,64,256]{2,1,0:T(8,128)(2,1)}, u32[]{:S(2)}, u32[]{:S(2)}) collective-permute-start(bf16[24,64,256]{2,1,0:T(8,128)(2,1)S(1)} %add_convert_fusion.28), channel_id=1, source_target_pairs={{16,8},{20,12},{17,9},{21,13},{18,10},{22,14},{19,11},{23,15}} | collective-permute-start | bytes 2359304 | tf_op jit(solution)/shard_map/ppermute | solution.py:1281
  426.1 32.2 %collective-permute-start.29 = (bf16[24,64,256]{2,1,0:T(8,128)(2,1)}, bf16[24,64,256]{2,1,0:T(8,128)(2,1)}, u32[]{:S(2)}, u32[]{:S(2)}) collective-permute-start(bf16[24,64,256]{2,1,0:T(8,128)(2,1)} %pad_maximum_fusion.13), channel_id=1, source_target_pairs={{0,4},{4,0},{8,12},{12,8},{16,20},{20,16},{24,28},{28,24},{1,5},{5... | collective-permute-start | bytes 2359304 | tf_op jit(solution)/shard_map/ppermute | solution.py:1573
  441.9 23.1 %collective-permute-start.28 = (bf16[2,16,64,256]{3,2,1,0:T(8,128)(2,1)}, bf16[2,16,64,256]{3,2,1,0:T(8,128)(2,1)}, u32[]{:S(2)}, u32[]{:S(2)}) collective-permute-start(bf16[2,16,64,256]{3,2,1,0:T(8,128)(2,1)} %dynamic-slice_bitcast_fusion.3), channel_id=1, source_target_pairs={{0,2},{1,3},{2,0},{3,1},{4,6},{5,7},{6,4},{7,5},{8,10},{9,11},{10,... | collective-permute-start | bytes 3145736 | tf_op jit(solution)/shard_map/ppermute | solution.py:1570
  445.8 19.2 %collective-permute-start.30 = (bf16[24,64,256]{2,1,0:T(8,128)(2,1)}, bf16[24,64,256]{2,1,0:T(8,128)(2,1)}, u32[]{:S(2)}, u32[]{:S(2)}) collective-permute-start(bf16[24,64,256]{2,1,0:T(8,128)(2,1)} %add_convert_fusion.26), channel_id=1, source_target_pairs={{16,8},{20,12},{17,9},{21,13},{18,10},{22,14},{19,11},{23,15}} | collective-permute-start | bytes 2359304 | tf_op jit(solution)/shard_map/ppermute | solution.py:1281
  466.7 21.8 %collective-permute-start.33 = (bf16[24,64,256]{2,1,0:T(8,128)(2,1)S(1)}, bf16[24,64,256]{2,1,0:T(8,128)(2,1)S(1)}, u32[]{:S(2)}, u32[]{:S(2)}) collective-permute-start(bf16[24,64,256]{2,1,0:T(8,128)(2,1)S(1)} %add_convert_fusion.24), channel_id=1, source_target_pairs={{0,8},{4,12},{1,9},{5,13},{2,10},{6,14},{3,11},{7,15}} | collective-permute-start | bytes 2359304 | tf_op jit(solution)/shard_map/ppermute | solution.py:1281
  468.1 21.8 %collective-permute-start.31 = (bf16[2,16,64,256]{3,2,1,0:T(8,128)(2,1)S(1)}, bf16[2,16,64,256]{3,2,1,0:T(8,128)(2,1)S(1)}, u32[]{:S(2)}, u32[]{:S(2)}) collective-permute-start(bf16[2,16,64,256]{3,2,1,0:T(8,128)(2,1)S(1)} %dynamic-slice_bitcast_fusion.2), channel_id=1, source_target_pairs={{0,2},{1,3},{2,0},{3,1},{4,6},{5,7},{6,4},{7,5},{8,10},{9,11},{10,... | collective-permute-start | bytes 3145736 | tf_op jit(solution)/shard_map/ppermute | solution.py:1570
  471.4 17.1 %collective-permute-start.32 = (bf16[24,64,256]{2,1,0:T(8,128)(2,1)S(1)}, bf16[24,64,256]{2,1,0:T(8,128)(2,1)S(1)}, u32[]{:S(2)}, u32[]{:S(2)}) collective-permute-start(bf16[24,64,256]{2,1,0:T(8,128)(2,1)S(1)} %pad_maximum_fusion.14), channel_id=1, source_target_pairs={{0,4},{4,0},{8,12},{12,8},{16,20},{20,16},{24,28},{28,24},{1,5},{5... | collective-permute-start | bytes 2359304 | tf_op jit(solution)/shard_map/ppermute | solution.py:1573
  471.4 17.0 %collective-permute-start.34 = (f32[2,5376]{1,0:T(2,128)S(1)}, f32[2,5376]{1,0:T(2,128)S(1)}, u32[]{:S(2)}, u32[]{:S(2)}) collective-permute-start(f32[2,5376]{1,0:T(2,128)S(1)} %add.386), channel_id=1, source_target_pairs={{0,4},{4,0},{8,12},{12,8},{16,20},{20,16},{24,28},{28,24},{1,5},{5... | collective-permute-start | bytes 129032 | tf_op jit(solution)/shard_map/ppermute | solution.py:1585
  490.2 22.6 %collective-permute-start.50 = (bf16[24,64,256]{2,1,0:T(8,128)(2,1)S(1)}, bf16[24,64,256]{2,1,0:T(8,128)(2,1)S(1)}, u32[]{:S(2)}, u32[]{:S(2)}) collective-permute-start(bf16[24,64,256]{2,1,0:T(8,128)(2,1)S(1)} %add_convert_fusion.11), channel_id=1, source_target_pairs={{8,16},{12,20},{9,17},{13,21},{10,18},{14,22},{11,19},{15,23}} | collective-permute-start | bytes 2359304 | tf_op jit(solution)/shard_map/ppermute | solution.py:1281
  493.1 19.6 %collective-permute-start.49 = (bf16[24,64,256]{2,1,0:T(8,128)(2,1)S(1)}, bf16[24,64,256]{2,1,0:T(8,128)(2,1)S(1)}, u32[]{:S(2)}, u32[]{:S(2)}) collective-permute-start(bf16[24,64,256]{2,1,0:T(8,128)(2,1)S(1)} %add_convert_fusion.12), channel_id=1, source_target_pairs={{0,8},{4,12},{24,16},{28,20},{1,9},{5,13},{25,17},{29,21},{2,10},{... | collective-permute-start | bytes 2359304 | tf_op jit(solution)/shard_map/ppermute | solution.py:1281
  495.2 17.6 %collective-permute-start.48 = (bf16[24,64,256]{2,1,0:T(8,128)(2,1)S(1)}, bf16[24,64,256]{2,1,0:T(8,128)(2,1)S(1)}, u32[]{:S(2)}, u32[]{:S(2)}) collective-permute-start(bf16[24,64,256]{2,1,0:T(8,128)(2,1)S(1)} %pad_maximum_fusion.18), channel_id=1, source_target_pairs={{0,4},{4,0},{8,12},{12,8},{16,20},{20,16},{24,28},{28,24},{1,5},{5... | collective-permute-start | bytes 2359304 | tf_op jit(solution)/shard_map/ppermute | solution.py:1573
  495.5 16.0 %collective-permute-start.51 = (f32[2,5376]{1,0:T(2,128)S(1)}, f32[2,5376]{1,0:T(2,128)S(1)}, u32[]{:S(2)}, u32[]{:S(2)}) collective-permute-start(f32[2,5376]{1,0:T(2,128)S(1)} %add.410), channel_id=1, source_target_pairs={{0,8},{4,12},{8,0},{12,4},{16,24},{20,28},{24,16},{28,20},{1,9},{5... | collective-permute-start | bytes 129032 | tf_op jit(solution)/shard_map/ppermute | solution.py:1585
  497.9 29.7 %collective-permute-start.36 = (bf16[24,64,256]{2,1,0:T(8,128)(2,1)S(1)}, bf16[24,64,256]{2,1,0:T(8,128)(2,1)S(1)}, u32[]{:S(2)}, u32[]{:S(2)}) collective-permute-start(bf16[24,64,256]{2,1,0:T(8,128)(2,1)S(1)} %pad_maximum_fusion.15), channel_id=1, source_target_pairs={{0,4},{4,0},{8,12},{12,8},{16,20},{20,16},{24,28},{28,24},{1,5},{5... | collective-permute-start | bytes 2359304 | tf_op jit(solution)/shard_map/ppermute | solution.py:1573
  511.6 19.7 %collective-permute-start.35 = (bf16[2,16,64,256]{3,2,1,0:T(8,128)(2,1)S(1)}, bf16[2,16,64,256]{3,2,1,0:T(8,128)(2,1)S(1)}, u32[]{:S(2)}, u32[]{:S(2)}) collective-permute-start(bf16[2,16,64,256]{3,2,1,0:T(8,128)(2,1)S(1)} %dynamic-slice_bitcast_fusion.1), channel_id=1, source_target_pairs={{0,2},{1,3},{2,0},{3,1},{4,6},{5,7},{6,4},{7,5},{8,10},{9,11},{10,... | collective-permute-start | bytes 3145736 | tf_op jit(solution)/shard_map/ppermute | solution.py:1570
  512.8 24.1 %collective-permute-start.55 = (f32[2,5376]{1,0:T(2,128)S(1)}, f32[2,5376]{1,0:T(2,128)S(1)}, u32[]{:S(2)}, u32[]{:S(2)}) collective-permute-start(f32[2,5376]{1,0:T(2,128)S(1)} %add.414), channel_id=1, source_target_pairs={{0,16},{4,20},{8,24},{12,28},{16,0},{20,4},{24,8},{28,12},{1,17},{... | collective-permute-start | bytes 129032 | tf_op jit(solution)/shard_map/ppermute | solution.py:1585
  513.1 25.0 %collective-permute-start.54 = (bf16[24,64,256]{2,1,0:T(8,128)(2,1)S(1)}, bf16[24,64,256]{2,1,0:T(8,128)(2,1)S(1)}, u32[]{:S(2)}, u32[]{:S(2)}) collective-permute-start(bf16[24,64,256]{2,1,0:T(8,128)(2,1)S(1)} %add_convert_fusion.8), channel_id=1, source_target_pairs={{16,24},{20,28},{17,25},{21,29},{18,26},{22,30},{19,27},{23,31}} | collective-permute-start | bytes 2359304 | tf_op jit(solution)/shard_map/ppermute | solution.py:1281
  514.2 25.2 %collective-permute-start.53 = (bf16[24,64,256]{2,1,0:T(8,128)(2,1)S(1)}, bf16[24,64,256]{2,1,0:T(8,128)(2,1)}, u32[]{:S(2)}, u32[]{:S(2)}) collective-permute-start(bf16[24,64,256]{2,1,0:T(8,128)(2,1)S(1)} %add_convert_fusion.9), channel_id=1, source_target_pairs={{8,16},{12,20},{9,17},{13,21},{10,18},{14,22},{11,19},{15,23}} | collective-permute-start | bytes 2359304 | tf_op jit(solution)/shard_map/ppermute | solution.py:1281
  527.6 11.8 %collective-permute-start.52 = (bf16[24,64,256]{2,1,0:T(8,128)(2,1)S(1)}, bf16[24,64,256]{2,1,0:T(8,128)(2,1)}, u32[]{:S(2)}, u32[]{:S(2)}) collective-permute-start(bf16[24,64,256]{2,1,0:T(8,128)(2,1)S(1)} %add_convert_fusion.10), channel_id=1, source_target_pairs={{24,16},{28,20},{25,17},{29,21},{26,18},{30,22},{27,19},{31,23}} | collective-permute-start | bytes 2359304 | tf_op jit(solution)/shard_map/ppermute | solution.py:1281
  532.5 20.5 %collective-permute-start.37 = (bf16[2,16,64,256]{3,2,1,0:T(8,128)(2,1)}, bf16[2,16,64,256]{3,2,1,0:T(8,128)(2,1)}, u32[]{:S(2)}, u32[]{:S(2)}) collective-permute-start(bf16[2,16,64,256]{3,2,1,0:T(8,128)(2,1)} %dynamic-slice_bitcast_fusion), channel_id=1, source_target_pairs={{0,2},{1,3},{2,0},{3,1},{4,6},{5,7},{6,4},{7,5},{8,10},{9,11},{10,... | collective-permute-start | bytes 3145736 | tf_op jit(solution)/shard_map/ppermute | solution.py:1570
  536.9 13.8 %collective-permute-start.39 = (bf16[24,64,256]{2,1,0:T(8,128)(2,1)}, bf16[24,64,256]{2,1,0:T(8,128)(2,1)}, u32[]{:S(2)}, u32[]{:S(2)}) collective-permute-start(bf16[24,64,256]{2,1,0:T(8,128)(2,1)} %add_convert_fusion.22), channel_id=1, source_target_pairs={{0,8},{4,12},{1,9},{5,13},{2,10},{6,14},{3,11},{7,15}} | collective-permute-start | bytes 2359304 | tf_op jit(solution)/shard_map/ppermute | solution.py:1281
  539.0 11.9 %collective-permute-start.38 = (bf16[24,64,256]{2,1,0:T(8,128)(2,1)}, bf16[24,64,256]{2,1,0:T(8,128)(2,1)}, u32[]{:S(2)}, u32[]{:S(2)}) collective-permute-start(bf16[24,64,256]{2,1,0:T(8,128)(2,1)} %pad_maximum_fusion.16), channel_id=1, source_target_pairs={{0,4},{4,0},{8,12},{12,8},{16,20},{20,16},{24,28},{28,24},{1,5},{5... | collective-permute-start | bytes 2359304 | tf_op jit(solution)/shard_map/ppermute | solution.py:1573
  540.8 23.8 %collective-permute-start.56 = (bf16[24,64,256]{2,1,0:T(8,128)(2,1)S(1)}, bf16[24,64,256]{2,1,0:T(8,128)(2,1)S(1)}, u32[]{:S(2)}, u32[]{:S(2)}) collective-permute-start(bf16[24,64,256]{2,1,0:T(8,128)(2,1)S(1)} %add_convert_fusion.7), channel_id=1, source_target_pairs={{16,8},{20,12},{17,9},{21,13},{18,10},{22,14},{19,11},{23,15}} | collective-permute-start | bytes 2359304 | tf_op jit(solution)/shard_map/ppermute | solution.py:1281
  554.7 14.3 %collective-permute-start.42 = (bf16[24,64,256]{2,1,0:T(8,128)(2,1)S(1)}, bf16[24,64,256]{2,1,0:T(8,128)(2,1)S(1)}, u32[]{:S(2)}, u32[]{:S(2)}) collective-permute-start(bf16[24,64,256]{2,1,0:T(8,128)(2,1)S(1)} %add_convert_fusion.20), channel_id=1, source_target_pairs={{8,16},{12,20},{9,17},{13,21},{10,18},{14,22},{11,19},{15,23}} | collective-permute-start | bytes 2359304 | tf_op jit(solution)/shard_map/ppermute | solution.py:1281
  558.7 14.2 %collective-permute-start.41 = (bf16[24,64,256]{2,1,0:T(8,128)(2,1)S(1)}, bf16[24,64,256]{2,1,0:T(8,128)(2,1)S(1)}, u32[]{:S(2)}, u32[]{:S(2)}) collective-permute-start(bf16[24,64,256]{2,1,0:T(8,128)(2,1)S(1)} %add_convert_fusion.21), channel_id=1, source_target_pairs={{0,8},{4,12},{24,16},{28,20},{1,9},{5,13},{25,17},{29,21},{2,10},{... | collective-permute-start | bytes 2359304 | tf_op jit(solution)/shard_map/ppermute | solution.py:1281
  562.0 12.3 %collective-permute-start.40 = (bf16[24,64,256]{2,1,0:T(8,128)(2,1)S(1)}, bf16[24,64,256]{2,1,0:T(8,128)(2,1)S(1)}, u32[]{:S(2)}, u32[]{:S(2)}) collective-permute-start(bf16[24,64,256]{2,1,0:T(8,128)(2,1)S(1)} %pad_maximum_fusion.17), channel_id=1, source_target_pairs={{0,4},{4,0},{8,12},{12,8},{16,20},{20,16},{24,28},{28,24},{1,5},{5... | collective-permute-start | bytes 2359304 | tf_op jit(solution)/shard_map/ppermute | solution.py:1573
  564.9 16.5 %collective-permute-start.57 = (bf16[24,64,256]{2,1,0:T(8,128)(2,1)S(1)}, bf16[24,64,256]{2,1,0:T(8,128)(2,1)S(1)}, u32[]{:S(2)}, u32[]{:S(2)}) collective-permute-start(bf16[24,64,256]{2,1,0:T(8,128)(2,1)S(1)} %add_convert_fusion.4), channel_id=1, source_target_pairs={{8,0},{12,4},{9,1},{13,5},{10,2},{14,6},{11,3},{15,7}} | collective-permute-start | bytes 2359304 | tf_op jit(solution)/shard_map/ppermute | solution.py:1281
  574.5 9.5 %collective-permute-start.45 = (bf16[24,64,256]{2,1,0:T(8,128)(2,1)S(1)}, bf16[24,64,256]{2,1,0:T(8,128)(2,1)S(1)}, u32[]{:S(2)}, u32[]{:S(2)}) collective-permute-start(bf16[24,64,256]{2,1,0:T(8,128)(2,1)S(1)} %add_convert_fusion.17), channel_id=1, source_target_pairs={{16,24},{20,28},{17,25},{21,29},{18,26},{22,30},{19,27},{23,31}} | collective-permute-start | bytes 2359304 | tf_op jit(solution)/shard_map/ppermute | solution.py:1281
  575.5 13.7 %collective-permute-start.44 = (bf16[24,64,256]{2,1,0:T(8,128)(2,1)S(1)}, bf16[24,64,256]{2,1,0:T(8,128)(2,1)S(1)}, u32[]{:S(2)}, u32[]{:S(2)}) collective-permute-start(bf16[24,64,256]{2,1,0:T(8,128)(2,1)S(1)} %add_convert_fusion.18), channel_id=1, source_target_pairs={{8,16},{12,20},{9,17},{13,21},{10,18},{14,22},{11,19},{15,23}} | collective-permute-start | bytes 2359304 | tf_op jit(solution)/shard_map/ppermute | solution.py:1281
  582.1 11.3 %collective-permute-start.58 = (bf16[24,64,256]{2,1,0:T(8,128)(2,1)S(1)}, bf16[24,64,256]{2,1,0:T(8,128)(2,1)S(1)}, u32[]{:S(2)}, u32[]{:S(2)}) collective-permute-start(bf16[24,64,256]{2,1,0:T(8,128)(2,1)S(1)} %select_select_fusion.1), channel_id=1, source_target_pairs={{0,2},{1,3},{2,0},{3,1},{4,6},{5,7},{6,4},{7,5},{8,10},{9,11},{10,... | collective-permute-start | bytes 2359304 | tf_op jit(solution)/shard_map/ppermute | solution.py:1580
  589.5 14.5 %collective-permute-start.46 = (bf16[24,64,256]{2,1,0:T(8,128)(2,1)S(1)}, bf16[24,64,256]{2,1,0:T(8,128)(2,1)S(1)}, u32[]{:S(2)}, u32[]{:S(2)}) collective-permute-start(bf16[24,64,256]{2,1,0:T(8,128)(2,1)S(1)} %add_convert_fusion.16), channel_id=1, source_target_pairs={{16,8},{20,12},{17,9},{21,13},{18,10},{22,14},{19,11},{23,15}} | collective-permute-start | bytes 2359304 | tf_op jit(solution)/shard_map/ppermute | solution.py:1281
  593.7 14.1 %collective-permute-start.59 = (bf16[40,64,256]{2,1,0:T(8,128)(2,1)S(1)}, bf16[40,64,256]{2,1,0:T(8,128)(2,1)}, u32[]{:S(2)}, u32[]{:S(2)}) collective-permute-start(bf16[40,64,256]{2,1,0:T(8,128)(2,1)S(1)} %pad_maximum_fusion.1), channel_id=1, source_target_pairs={{0,1},{1,0},{2,3},{3,2},{4,5},{5,4},{6,7},{7,6},{8,9},{9,8},{10,11... | collective-permute-start | bytes 3932168 | tf_op jit(solution)/shard_map/ppermute | solution.py:1582
  605.2 20.2 %collective-permute-start.47 = (bf16[24,64,256]{2,1,0:T(8,128)(2,1)}, bf16[24,64,256]{2,1,0:T(8,128)(2,1)}, u32[]{:S(2)}, u32[]{:S(2)}) collective-permute-start(bf16[24,64,256]{2,1,0:T(8,128)(2,1)} %add_convert_fusion.13), channel_id=1, source_target_pairs={{8,0},{12,4},{9,1},{13,5},{10,2},{14,6},{11,3},{15,7}} | collective-permute-start | bytes 2359304 | tf_op jit(solution)/shard_map/ppermute | solution.py:1281
  627.5 18.4 %collective-permute-start.60 = (bf16[24,64,256]{2,1,0:T(8,128)(2,1)S(1)}, bf16[24,64,256]{2,1,0:T(8,128)(2,1)S(1)}, u32[]{:S(2)}, u32[]{:S(2)}) collective-permute-start(bf16[24,64,256]{2,1,0:T(8,128)(2,1)S(1)} %select_select_fusion), channel_id=1, source_target_pairs={{0,2},{1,3},{2,0},{3,1},{4,6},{5,7},{6,4},{7,5},{8,10},{9,11},{10,... | collective-permute-start | bytes 2359304 | tf_op jit(solution)/shard_map/ppermute | solution.py:1580
  646.2 12.2 %collective-permute-start.61 = (bf16[40,64,256]{2,1,0:T(8,128)(2,1)S(1)}, bf16[40,64,256]{2,1,0:T(8,128)(2,1)S(1)}, u32[]{:S(2)}, u32[]{:S(2)}) collective-permute-start(bf16[40,64,256]{2,1,0:T(8,128)(2,1)S(1)} %pad_maximum_fusion.2), channel_id=1, source_target_pairs={{0,1},{1,0},{2,3},{3,2},{4,5},{5,4},{6,7},{7,6},{8,9},{9,8},{10,11... | collective-permute-start | bytes 3932168 | tf_op jit(solution)/shard_map/ppermute | solution.py:1582
  (59 other events, 553.7 us)
Sparse Core Ops, SparseCore 0:
  13.1 202.3 all-gather.1
  274.2 73.9 reduce-scatter.2
  351.5 71.7 reduce-scatter.4
